TPU v7x, 32 devices: a whole 2x2x4 slice. The times are simulated.
32 devices in a mesh: dp: 8 (over y, x, core), tensor: 4 (over z).
Axes of the slice: x: 2, y: 2, z: 4, core: 2. Of those that a mesh axis runs over, the one named last changes fastest.
Arguments:
- tokens: bfloat16 [16384, 1536], P(('dp', 'tensor')), may hold values from -6 to 6
- perm: int32 [16384], P('dp'), may hold values from 0 to 16383, as said below
- routes: int32 [16384, 4], P('dp'), may hold values from 0 to 7, all different within a row
- gates: bfloat16 [16384, 4], P(('dp', 'tensor')), may hold values from 0.049804688 to 0.5
- lengths: int32 [8, 4], P('dp'), may hold values from 1 to 1024, 2048 in all within a row
- cotangent: bfloat16 [16384, 1536], P(('dp', 'tensor')), may hold values from -6 to 6
- gain_attn: float32 [1536], replicated, may hold values from 0.5 to 1.5
- w_query: bfloat16 [1536, 1536], P(None, 'tensor'), may hold values from -0.15625 to 0.15625
- w_keyval: bfloat16 [1536, 512], replicated, may hold values from -0.15625 to 0.15625
- w_out: bfloat16 [1536, 1536], P('tensor'), may hold values from -1.5 to 1.5
- gain_moe: float32 [1536], replicated, may hold values from 0.5 to 1.5
- w_gate: bfloat16 [8, 1536, 768], P(None, None, 'tensor'), may hold values from -0.15625 to 0.15625
- w_up: bfloat16 [8, 1536, 768], P(None, None, 'tensor'), may hold values from -0.15625 to 0.15625
- w_down: bfloat16 [8, 768, 1536], P(None, 'tensor'), may hold values from -0.21875 to 0.21875
Outputs:
- outputs: bfloat16 [16384, 1536], P(('dp', 'tensor'))
- grad_tokens: bfloat16 [16384, 1536], P(('dp', 'tensor'))
- grad_gain_attn: float32 [1536], P('dp')
- grad_query: float32 [1536, 1536], P('dp', 'tensor')
- grad_keyval: float32 [1536, 512], P('dp')
- grad_out: float32 [1536, 1536], P('tensor', 'dp')
- grad_gain_moe: float32 [1536], P('dp')
- grad_gate: float32 [8, 1536, 768], P(None, 'dp', 'tensor')
- grad_up: float32 [8, 1536, 768], P(None, 'dp', 'tensor')
- grad_down: float32 [8, 768, 1536], P(None, 'tensor', 'dp')
Inputs may be any that keep to these rules, and one draw needn't show every extreme that they name: `perm`: each value once. The 512 rows of aligned block b go to blocks b' with b' % 4 == b % 4, exactly 64 rows to each such block, where block b' holds rows b' * 512 to (b' + 1) * 512 - 1 of the dealt order.
All inputs are finite; a program needn't handle non-finite values.
Results may differ from a plain program's by a relative error of at most 0.02.
Values may be sent and summed in bfloat16 or wider, within the bound.
A program may use at most 448 MiB of HBM per device.

v0:
```python
import jax
import jax.numpy as jnp
from jax import lax
from jax.sharding import PartitionSpec as P

H = 12
KVH = 2
HD = 128
BQ = 512


eps_norm = 1e-06
rope_base = 1000000.0
masked_score = -1e30


def position_tables(seq_lengths, group_rows, head_dim):
    row_ids = jnp.arange(group_rows, dtype=jnp.int32)
    seq_ends = jnp.cumsum(seq_lengths, dtype=jnp.int32)
    segment = jnp.sum(
        (row_ids[:, None] >= seq_ends[None, :]).astype(jnp.int32), axis=1, dtype=jnp.int32
    )
    starts = seq_ends - seq_lengths
    seq_ids = jnp.arange(seq_lengths.shape[0], dtype=jnp.int32)
    first_row = jnp.sum(
        jnp.where(segment[:, None] == seq_ids[None, :], starts[None, :], 0), axis=1, dtype=jnp.int32
    )
    offset = (row_ids - first_row).astype(jnp.float32)
    half_dim = head_dim // 2
    frequency = rope_base ** (-2.0 * jnp.arange(half_dim, dtype=jnp.float32) / head_dim)
    angles = offset[:, None] * frequency[None, :]
    return (row_ids, segment, jnp.cos(angles)[:, None, :], jnp.sin(angles)[:, None, :])


def rotate(values, cosine_table, sine_table):
    half_dim = values.shape[-1] // 2
    first_half = values[..., :half_dim]
    second_half = values[..., half_dim:]
    return jnp.concatenate(
        [
            first_half * cosine_table - second_half * sine_table,
            second_half * cosine_table + first_half * sine_table,
        ],
        axis=-1,
    )


def pair_sum(table, slot_pairs, pair_weights):
    return jnp.sum(table[slot_pairs] * pair_weights[:, :, None], axis=1)


def per_device(
    tokens,
    perm,
    routes,
    gates,
    lengths,
    cotangent,
    gain_attn,
    w_query,
    w_keyval,
    w_out,
    gain_moe,
    w_gate,
    w_up,
    w_down,
):
    dp_count = lax.axis_size("dp")
    tensor_count = lax.axis_size("tensor")
    tensor_rank = lax.axis_index("tensor")
    own_rows, width = tokens.shape
    group_rows = perm.shape[0]
    share = own_rows // dp_count
    top_count = routes.shape[1]
    experts = w_gate.shape[0]
    capacity = 9 * group_rows * top_count // (8 * experts)
    heads_here = w_query.shape[1] // HD
    query_cols = heads_here * HD
    score_scale = HD ** (-0.5)
    block_count = group_rows // BQ
    dest_dp = perm // group_rows
    local_dest = perm % group_rows
    quarter = local_dest // own_rows
    bucket = quarter * dp_count + dest_dp
    onehot = (
        bucket[:, None] == jnp.arange(tensor_count * dp_count, dtype=jnp.int32)[None, :]
    ).astype(jnp.int32)
    earlier = jnp.sum(
        (jnp.cumsum(onehot, axis=0, dtype=jnp.int32) - onehot) * onehot, axis=1, dtype=jnp.int32
    )
    slot_all = dest_dp * (tensor_count * share) + quarter * share + earlier
    order_all = (
        jnp.zeros((group_rows,), jnp.int32)
        .at[slot_all]
        .set(jnp.arange(group_rows, dtype=jnp.int32))
    )
    packed = jnp.concatenate([local_dest[:, None], routes], axis=1)[order_all]
    arrived = lax.all_to_all(
        packed.reshape(dp_count, tensor_count * share, 1 + top_count),
        "dp",
        split_axis=0,
        concat_axis=0,
        tiled=True,
    )
    arrived = arrived.reshape(dp_count, tensor_count, share, 1 + top_count).transpose(1, 0, 2, 3)
    arrived = arrived.reshape(group_rows, 1 + top_count)
    where_to = arrived[:, 0]
    group_order = (
        jnp.zeros((group_rows,), jnp.int32)
        .at[where_to]
        .set(jnp.arange(group_rows, dtype=jnp.int32))
    )
    route_rows = arrived[group_order, 1:]
    own_slot = lax.dynamic_slice_in_dim(
        dest_dp * share + earlier, tensor_rank * own_rows, own_rows, 0
    )
    own_order = (
        jnp.zeros((own_rows,), jnp.int32).at[own_slot].set(jnp.arange(own_rows, dtype=jnp.int32))
    )
    x_in, dy_in, gate_in = (
        lax.all_to_all(
            tokens[own_order].reshape(dp_count, share, width),
            "dp",
            split_axis=0,
            concat_axis=0,
            tiled=True,
        ),
        lax.all_to_all(
            cotangent[own_order].reshape(dp_count, share, width),
            "dp",
            split_axis=0,
            concat_axis=0,
            tiled=True,
        ),
        lax.all_to_all(
            gates[own_order].reshape(dp_count, share, top_count),
            "dp",
            split_axis=0,
            concat_axis=0,
            tiled=True,
        ),
    )
    arrival_pos = (
        lax.dynamic_slice_in_dim(where_to, tensor_rank * own_rows, own_rows, 0)
        - tensor_rank * own_rows
    )
    arrival_order = (
        jnp.zeros((own_rows,), jnp.int32).at[arrival_pos].set(jnp.arange(own_rows, dtype=jnp.int32))
    )
    x_rows = x_in.reshape(own_rows, width)[arrival_order].astype(jnp.float32)
    dy_rows = dy_in.reshape(own_rows, width)[arrival_order]
    gate_rows = gate_in.reshape(own_rows, top_count)[arrival_order]
    row_ids, segment, cosine_table, sine_table = position_tables(lengths[0], group_rows, HD)
    inv_one = lax.rsqrt(jnp.mean(x_rows * x_rows, axis=1, keepdims=True) + eps_norm)
    normed_own = (x_rows * inv_one * gain_attn).astype(jnp.bfloat16)
    normed_one = lax.all_gather(normed_own, "tensor", axis=0, tiled=True)
    kv_head = tensor_rank * heads_here // (H // KVH)
    key_cols = lax.dynamic_slice_in_dim(w_keyval, kv_head * HD, HD, 1)
    value_cols = lax.dynamic_slice_in_dim(w_keyval, (KVH + kv_head) * HD, HD, 1)
    projection = jnp.concatenate([w_query, key_cols, value_cols], axis=1)
    projected = jnp.dot(normed_one, projection, preferred_element_type=jnp.float32)
    queries = rotate(
        projected[:, :query_cols].reshape(group_rows, heads_here, HD), cosine_table, sine_table
    ).astype(jnp.bfloat16)
    keys = rotate(projected[:, query_cols : query_cols + HD][:, None, :], cosine_table, sine_table)[
        :, 0
    ].astype(jnp.bfloat16)
    values = projected[:, query_cols + HD :].astype(jnp.bfloat16)

    def scores_of(block_index):
        start = block_index * BQ
        query_block = lax.dynamic_slice_in_dim(queries, start, BQ, 0)
        rows_q = start + jnp.arange(BQ, dtype=jnp.int32)
        seg_q = lax.dynamic_slice_in_dim(segment, start, BQ, 0)
        scores = (
            jnp.einsum("qhd,kd->hqk", query_block, keys, preferred_element_type=jnp.float32)
            * score_scale
        )
        allowed = (seg_q[:, None] == segment[None, :]) & (row_ids[None, :] <= rows_q[:, None])
        return (query_block, jnp.where(allowed[None], scores, masked_score))

    def attend(block_index):
        query_block, scores = scores_of(block_index)
        row_peak = jnp.max(scores, axis=2, keepdims=True)
        exponent = jnp.exp(scores - row_peak)
        total = jnp.sum(exponent, axis=2, keepdims=True)
        soft = (exponent / total).astype(jnp.bfloat16)
        mixed_rows = jnp.einsum("hqk,kd->qhd", soft, values, preferred_element_type=jnp.float32)
        return (mixed_rows.astype(jnp.bfloat16), (row_peak + jnp.log(total))[:, :, 0])

    mixed_blocks, lse_blocks = lax.map(attend, jnp.arange(block_count, dtype=jnp.int32))
    attended = mixed_blocks.reshape(group_rows, query_cols)
    hidden_state = x_rows + lax.psum_scatter(
        jnp.dot(attended, w_out, preferred_element_type=jnp.float32),
        "tensor",
        scatter_dimension=0,
        tiled=True,
    )
    inv_two = lax.rsqrt(jnp.mean(hidden_state * hidden_state, axis=1, keepdims=True) + eps_norm)
    normed_two_own = (hidden_state * inv_two * gain_moe).astype(jnp.bfloat16)
    normed_two, gate_group, dy_group = (
        lax.all_gather(normed_two_own, "tensor", axis=0, tiled=True),
        lax.all_gather(gate_rows, "tensor", axis=0, tiled=True),
        lax.all_gather(dy_rows, "tensor", axis=0, tiled=True),
    )
    route_flat = route_rows.reshape(-1)
    route_hot = (route_flat[:, None] == jnp.arange(experts, dtype=jnp.int32)[None, :]).astype(
        jnp.int32
    )
    position = jnp.sum(
        (jnp.cumsum(route_hot, axis=0, dtype=jnp.int32) - route_hot) * route_hot,
        axis=1,
        dtype=jnp.int32,
    )
    slot_of = jnp.where(position < capacity, route_flat * capacity + position, experts * capacity)
    pair_token = jnp.arange(group_rows * top_count, dtype=jnp.int32) // top_count
    slot_token = (
        jnp.full((experts * capacity + 1,), group_rows, jnp.int32)
        .at[slot_of]
        .set(pair_token)[: experts * capacity]
    )
    gate_flat = gate_group.astype(jnp.float32).reshape(-1)
    slot_weight = (
        jnp.zeros((experts * capacity + 1,), jnp.float32)
        .at[slot_of]
        .set(gate_flat)[: experts * capacity]
    )
    slot_pairs = slot_of.reshape(group_rows, top_count)
    pair_gates = gate_group.astype(jnp.float32)
    zero_row = jnp.zeros((1, width), jnp.bfloat16)
    slot_rows = jnp.concatenate([normed_two, zero_row], axis=0)[slot_token].reshape(
        experts, capacity, width
    )
    gate_val = jnp.einsum("ecd,edf->ecf", slot_rows, w_gate, preferred_element_type=jnp.float32)
    up_val = jnp.einsum("ecd,edf->ecf", slot_rows, w_up, preferred_element_type=jnp.float32)
    gate_pos = jax.nn.relu(gate_val)
    hidden = (gate_pos * gate_pos * up_val).astype(jnp.bfloat16)
    expert_out = jnp.einsum("ecf,efd->ecd", hidden, w_down, preferred_element_type=jnp.float32)
    expert_pad = jnp.concatenate(
        [expert_out.reshape(experts * capacity, width), jnp.zeros((1, width), jnp.float32)], axis=0
    )
    result_rows = hidden_state + lax.psum_scatter(
        pair_sum(expert_pad, slot_pairs, pair_gates).astype(jnp.bfloat16),
        "tensor",
        scatter_dimension=0,
        tiled=True,
    ).astype(jnp.float32)
    dy_pad = jnp.concatenate([dy_group, zero_row], axis=0)[slot_token].astype(jnp.float32)
    slot_grad = (
        (slot_weight[:, None] * dy_pad).astype(jnp.bfloat16).reshape(experts, capacity, width)
    )
    grad_down = jnp.einsum("ecf,ecd->efd", hidden, slot_grad, preferred_element_type=jnp.float32)
    hidden_grad = jnp.einsum("ecd,efd->ecf", slot_grad, w_down, preferred_element_type=jnp.float32)
    gate_grad = (hidden_grad * up_val * 2.0 * gate_pos).astype(jnp.bfloat16)
    up_grad = (hidden_grad * gate_pos * gate_pos).astype(jnp.bfloat16)
    grad_gate = jnp.einsum("ecd,ecf->edf", slot_rows, gate_grad, preferred_element_type=jnp.float32)
    grad_up = jnp.einsum("ecd,ecf->edf", slot_rows, up_grad, preferred_element_type=jnp.float32)
    rows_grad = jnp.einsum("ecf,edf->ecd", gate_grad, w_gate, preferred_element_type=jnp.float32)
    rows_grad = rows_grad + jnp.einsum(
        "ecf,edf->ecd", up_grad, w_up, preferred_element_type=jnp.float32
    )
    rows_pad = jnp.concatenate(
        [rows_grad.reshape(experts * capacity, width), jnp.zeros((1, width), jnp.float32)], axis=0
    )
    pair_ones = jnp.ones((group_rows, top_count), jnp.float32)
    normed_two_grad = lax.psum_scatter(
        pair_sum(rows_pad, slot_pairs, pair_ones).astype(jnp.bfloat16),
        "tensor",
        scatter_dimension=0,
        tiled=True,
    ).astype(jnp.float32)
    grad_gain_two = jnp.sum(normed_two_grad * hidden_state * inv_two, axis=0)
    scaled_two = normed_two_grad * gain_moe
    state_grad = dy_rows.astype(jnp.float32) + inv_two * (
        scaled_two
        - hidden_state
        * inv_two
        * inv_two
        * jnp.mean(scaled_two * hidden_state, axis=1, keepdims=True)
    )
    branch_grad = lax.all_gather(state_grad.astype(jnp.bfloat16), "tensor", axis=0, tiled=True)
    grad_out = jnp.dot(attended.T, branch_grad, preferred_element_type=jnp.float32)
    mixed_grad = jnp.dot(branch_grad, w_out.T, preferred_element_type=jnp.float32).astype(
        jnp.bfloat16
    )
    mixed_grad = mixed_grad.reshape(group_rows, heads_here, HD)

    def attend_back(carry, block_index):
        key_acc, value_acc = carry
        query_block, scores = scores_of(block_index)
        soft = jnp.exp(scores - lse_blocks[block_index][:, :, None])
        grad_block = lax.dynamic_slice_in_dim(mixed_grad, block_index * BQ, BQ, 0)
        value_acc = value_acc + jnp.einsum(
            "hqk,qhd->kd", soft.astype(jnp.bfloat16), grad_block, preferred_element_type=jnp.float32
        )
        soft_grad = jnp.einsum(
            "qhd,kd->hqk", grad_block, values, preferred_element_type=jnp.float32
        )
        centred = jnp.sum(soft * soft_grad, axis=2, keepdims=True)
        score_grad = (soft * (soft_grad - centred)).astype(jnp.bfloat16)
        query_grad = (
            jnp.einsum("hqk,kd->qhd", score_grad, keys, preferred_element_type=jnp.float32)
            * score_scale
        )
        key_acc = (
            key_acc
            + jnp.einsum("hqk,qhd->kd", score_grad, query_block, preferred_element_type=jnp.float32)
            * score_scale
        )
        return ((key_acc, value_acc), query_grad)

    zero_kv = jnp.zeros((group_rows, HD), jnp.float32)
    (key_grad, value_grad), query_blocks = lax.scan(
        attend_back, (zero_kv, zero_kv), jnp.arange(block_count, dtype=jnp.int32)
    )
    query_grad = query_blocks.reshape(group_rows, heads_here, HD)
    query_raw = (
        rotate(query_grad, cosine_table, -sine_table)
        .reshape(group_rows, query_cols)
        .astype(jnp.bfloat16)
    )
    key_raw = rotate(key_grad[:, None, :], cosine_table, -sine_table)[:, 0].astype(jnp.bfloat16)
    projected_grad = jnp.concatenate([query_raw, key_raw, value_grad.astype(jnp.bfloat16)], axis=1)
    normed_one_grad = lax.psum_scatter(
        jnp.dot(projected_grad, projection.T, preferred_element_type=jnp.float32).astype(
            jnp.bfloat16
        ),
        "tensor",
        scatter_dimension=0,
        tiled=True,
    ).astype(jnp.float32)
    projection_grad = jnp.dot(normed_one.T, projected_grad, preferred_element_type=jnp.float32)
    grad_query = projection_grad[:, :query_cols]
    grad_keyval = jnp.zeros((width, 2 * KVH * HD), jnp.float32)
    grad_keyval = lax.dynamic_update_slice_in_dim(
        grad_keyval, projection_grad[:, query_cols : query_cols + HD], kv_head * HD, 1
    )
    grad_keyval = lax.dynamic_update_slice_in_dim(
        grad_keyval, projection_grad[:, query_cols + HD :], (KVH + kv_head) * HD, 1
    )
    grad_gain_one = jnp.sum(normed_one_grad * x_rows * inv_one, axis=0)
    scaled_one = normed_one_grad * gain_attn
    input_grad = state_grad + inv_one * (
        scaled_one
        - x_rows * inv_one * inv_one * jnp.mean(scaled_one * x_rows, axis=1, keepdims=True)
    )
    back_out, back_grad = (
        lax.all_to_all(
            result_rows.astype(jnp.bfloat16)[arrival_pos].reshape(dp_count, share, width),
            "dp",
            split_axis=0,
            concat_axis=0,
            tiled=True,
        ),
        lax.all_to_all(
            input_grad.astype(jnp.bfloat16)[arrival_pos].reshape(dp_count, share, width),
            "dp",
            split_axis=0,
            concat_axis=0,
            tiled=True,
        ),
    )
    outputs = back_out.reshape(own_rows, width)[own_slot]
    grad_tokens = back_grad.reshape(own_rows, width)[own_slot]
    sum_one, sum_two, sum_keyval, sum_query, sum_out, sum_gate, sum_up, sum_down = (
        lax.psum_scatter(grad_gain_one, "dp", scatter_dimension=0, tiled=True),
        lax.psum_scatter(grad_gain_two, "dp", scatter_dimension=0, tiled=True),
        lax.psum_scatter(grad_keyval, "dp", scatter_dimension=0, tiled=True),
        lax.psum_scatter(grad_query, "dp", scatter_dimension=0, tiled=True),
        lax.psum_scatter(grad_out, "dp", scatter_dimension=1, tiled=True),
        lax.psum_scatter(grad_gate, "dp", scatter_dimension=1, tiled=True),
        lax.psum_scatter(grad_up, "dp", scatter_dimension=1, tiled=True),
        lax.psum_scatter(grad_down, "dp", scatter_dimension=2, tiled=True),
    )
    sum_one, sum_two, sum_keyval = (
        lax.psum(sum_one.astype(jnp.bfloat16), "tensor").astype(jnp.float32),
        lax.psum(sum_two.astype(jnp.bfloat16), "tensor").astype(jnp.float32),
        lax.psum(sum_keyval.astype(jnp.bfloat16), "tensor").astype(jnp.float32),
    )
    return (
        outputs,
        grad_tokens,
        sum_one,
        sum_query,
        sum_keyval,
        sum_out,
        sum_two,
        sum_gate,
        sum_up,
        sum_down,
    )


def solution(mesh):
    in_specs = (
        P(("dp", "tensor"), None),
        P("dp"),
        P("dp", None),
        P(("dp", "tensor"), None),
        P("dp", None),
        P(("dp", "tensor"), None),
        P(),
        P(None, "tensor"),
        P(),
        P("tensor", None),
        P(),
        P(None, None, "tensor"),
        P(None, None, "tensor"),
        P(None, "tensor", None),
    )
    out_specs = (
        P(("dp", "tensor"), None),
        P(("dp", "tensor"), None),
        P("dp"),
        P("dp", "tensor"),
        P("dp", None),
        P("tensor", "dp"),
        P("dp"),
        P(None, "dp", "tensor"),
        P(None, "dp", "tensor"),
        P(None, "tensor", "dp"),
    )
    return jax.shard_map(
        per_device, mesh=mesh, in_specs=in_specs, out_specs=out_specs, check_vma=False
    )
```

profile of v0, /device:TPU:0, one launch (start us, length us, event | category | flops | bytes accessed | tf_op | source)
XLA Modules:
  0.0 2435.7 jit_solution(9070633839762562727)
XLA Ops:
  88.7 108.5 %all-gather.7.cloned.1.call-done = bf16[2048,1536]{1,0:T(8,128)(2,1)} async-done(((bf16[512,1536]{1,0:T(8,128)(2,1)}), bf16[2048,1536]{1,0:T(8,128)(2,1)}) %all-gather.7.cloned.1.call-update) | async-done | bytes 6291472 | tf_op jit(solution)/shard_map/all_gather | solution.py:156
  223.4 96.8 %while.28 = (s32[]{:T(128)}, bf16[4,512,3,128]{3,1,2,0:T(8,128)(2,1)}, f32[4,3,512]{2,1,0:T(4,128)}, s32[4]{0:T(128)S(1)}, s32[2048]{0:T(1024)S(1)}, /*index=5*/...) while((s32[]{:T(128)}, ...), condition=%wide.region_13.14_spmd.clone, body=%wide.region_10.13_spmd.clone.sunk | while | flops 1651702784 | bytes 43847884 | solution.py:191
  337.5 24.4 %all_to_all.30 = bf16[8,64,1536]{2,1,0:T(8,128)(2,1)S(1)} all-to-all(bf16[8,64,1536]{2,1,0:T(8,128)(2,1)S(1)} %bitcast.308), channel_id=1, replica_groups=mesh['dp'=8,'tensor'=4] {'dp'}, dimensions={0} | all-to-all | bytes 3145728 | tf_op jit(solution)/shard_map/all_to_all | solution.py:128
  365.0 179.3 %reduce-scatter.13.cloned.1.call-done = f32[512,1536]{1,0:T(8,128)} async-done(((f32[2048,1536]{1,0:T(8,128)}), f32[512,1536]{1,0:T(8,128)}) %reduce-scatter.13.cloned.1.call-update) | async-done | bytes 3145744 | tf_op jit(solution)/shard_map/reduce_scatter | solution.py:193
  622.7 24.5 %all-gather = bf16[2048,4]{1,0:T(8,128)(2,1)S(1)} all-gather(bf16[512,4]{1,0:T(8,128)(2,1)S(1)} %gather_fusion.6), channel_id=2, replica_groups=mesh['dp'=8,'tensor'=4] {'tensor'}, dimensions={0}, use_global_device_ids=true | all-gather | bytes 20480 | tf_op jit(solution)/shard_map/all_gather | solution.py:203
  653.6 30.5 %scatter_custom_fusion.4 = s32[9217]{0:T(1024)S(1)} fusion(s32[8192]{0:T(1024)S(1)} %bitcast.328, s32[8192]{0:T(1024)S(1)} %add_select_fusion, s32[]{:T(128)} %constant.161.clone.1), kind=kCustom, calls=%fused_computation.208 | custom fusion | bytes 36872 | tf_op jit(solution)/shard_map/scatter | solution.py:220
  684.1 30.6 %scatter_custom_fusion.5 = f32[9217]{0:T(1024)S(1)} fusion(s32[8192]{0:T(1024)S(1)} %bitcast.329, f32[8192]{0:T(1024)S(1)} %reshape.762, f32[]{:T(128)} %constant.169.clone.1), kind=kCustom, calls=%fused_computation.206 | custom fusion | bytes 36872 | tf_op jit(solution)/shard_map/scatter | solution.py:226
  723.3 59.0 %gather_fusion.11 = bf16[9216,1536]{1,0:T(8,128)(2,1)} fusion(bf16[2049,1536]{1,0:T(8,128)(2,1)} %concatenate.47, s32[9216]{0:T(1024)S(1)} %fusion.105), kind=kCustom, calls=%fused_computation.11 | custom fusion | bytes 56659968 | tf_op jit(solution)/shard_map/gather | solution.py:248
  792.6 58.9 %gather_fusion.3 = bf16[9216,1536]{1,0:T(8,128)(2,1)} fusion(bf16[2049,1536]{1,0:T(8,128)(2,1)} %concatenate.44, s32[9216]{0:T(1024)S(1)} %fusion.105), kind=kCustom, calls=%fused_computation.3 | custom fusion | bytes 56659968 | tf_op jit(solution)/shard_map/gather | solution.py:231
  886.3 22.2 fusion.57
  908.5 23.8 fusion.149
  932.3 40.6 %convolution_add_fusion = f32[8,1152,1536]{2,1,0:T(8,128)} fusion(f32[8,1152,1536]{2,1,0:T(8,128)} %fusion.149, bf16[8,1152,192]{1,2,0:T(8,128)(2,1)} %get-tuple-element.332, bf16[8,1536,192]{1,2,0:T(8,128)(2,1)} %param.30), kind=kOutput, calls=%fused_computation.85 | convolution fusion | flops 5449973760 | bytes 121503744 | tf_op jit(solution)/shard_map/ecf,edf->ecd/dot_general | solution.py:259
  972.9 38.1 %concatenate.48 = f32[9217,1536]{1,0:T(8,128)} pad(f32[9216,1536]{1,0:T(8,128)} %bitcast.282, f32[]{:T(128)} %constant.169.clone.1), padding=0_1x0_0 | pad | bytes 113252352 | tf_op jit(solution)/shard_map/concatenate | solution.py:262
  1011.0 70.2 %gather_fusion.12 = f32[8192,1536]{1,0:T(8,128)} fusion(f32[9217,1536]{1,0:T(8,128)} %concatenate.48, s32[8192]{0:T(1024)S(1)} %copy-done.4), kind=kCustom, calls=%fused_computation.12 | custom fusion | bytes 100696064 | tf_op jit(solution)/shard_map/gather | solution.py:49
  1081.2 56.2 %reshape.671 = f32[2048,4,1536]{2,1,0:T(4,128)} reshape(f32[8192,1536]{1,0:T(8,128)} %gather_fusion.12) | data formatting | bytes 100663296 | tf_op jit(solution)/shard_map/gather | solution.py:49
  1137.5 41.6 %reduce_sum.139 = bf16[2048,1536]{1,0:T(8,128)(2,1)} reduce(f32[2048,4,1536]{2,1,0:T(4,128)} %reshape.671, f32[]{:T(128)} %constant.169.clone.1), dimensions={1}, to_apply=%region_24.25 | reduce | flops 9437184 | bytes 56623108 | tf_op jit(solution)/shard_map/reduce_sum | solution.py:49
  1179.2 109.0 %reduce-scatter.17.cloned.1.call-done = bf16[512,1536]{1,0:T(8,128)(2,1)} async-done(((bf16[2048,1536]{1,0:T(8,128)(2,1)}), bf16[512,1536]{1,0:T(8,128)(2,1)}) %reduce-scatter.17.cloned.1.call-update) | async-done | bytes 1572880 | tf_op jit(solution)/shard_map/reduce_scatter | solution.py:266
  1297.1 115.9 %all-gather.11.cloned.1.call-done = bf16[2048,1536]{1,0:T(8,128)(2,1)} async-done(((bf16[512,1536]{1,0:T(8,128)(2,1)}), bf16[2048,1536]{1,0:T(8,128)(2,1)}) %all-gather.11.cloned.1.call-update) | async-done | bytes 6291472 | tf_op jit(solution)/shard_map/all_gather | solution.py:281
  1419.9 130.1 %while.29 = (s32[]{:T(128)}, f32[2048,128]{1,0:T(8,128)S(1)}, f32[2048,128]{1,0:T(8,128)}, f32[4,512,3,128]{3,1,0,2:T(8,128)}, s32[4]{0:T(128)S(1)}, /*index=5*/...) while((s32[]{:T(128)}, f32[2048,128]{1,0:T(8,128)S(1)}, ...), condition=%wide.region_29.30_spmd.clone, body=%wide.region_27.29_spmd.clone.sunk | while | flops 4078369792 | bytes 121438584 | solution.py:313
  1583.6 24.7 %fusion.148 = f32[8,1152,1536]{2,1,0:T(8,128)} fusion(bf16[8,1152,192]{1,2,0:T(8,128)(2,1)} %get-tuple-element.334, bf16[8,192,1536]{2,1,0:T(8,128)(2,1)} %param.31), kind=kOutput, calls=%fused_computation.291 | convolution fusion | flops 5435817984 | bytes 64880640 | tf_op jit(solution)/shard_map/ecf,efd->ecd/dot_general | solution.py:238
  1608.2 39.7 %concatenate.46 = f32[9217,1536]{1,0:T(8,128)} pad(f32[9216,1536]{1,0:T(8,128)} %bitcast.281, f32[]{:T(128)} %constant.169.clone.1), padding=0_1x0_0 | pad | bytes 113252352 | tf_op jit(solution)/shard_map/concatenate | solution.py:239
  1648.0 70.2 %gather_fusion.4 = f32[8192,1536]{1,0:T(8,128)} fusion(f32[9217,1536]{1,0:T(8,128)} %concatenate.46, s32[8192]{0:T(1024)S(1)} %copy-done.5), kind=kCustom, calls=%fused_computation.4 | custom fusion | bytes 100696064 | tf_op jit(solution)/shard_map/gather | solution.py:49
  1718.2 56.4 %reshape.603 = f32[2048,4,1536]{2,1,0:T(4,128)} reshape(f32[8192,1536]{1,0:T(8,128)} %gather_fusion.4) | data formatting | bytes 100663296 | tf_op jit(solution)/shard_map/gather | solution.py:49
  1774.6 124.2 %multiply_reduce_fusion = bf16[2048,1536]{1,0:T(8,128)(2,1)} fusion(f32[2048,4,1536]{2,1,0:T(4,128)} %reshape.603, f32[2048,4]{1,0:T(8,128)S(1)} %copy-done.22), kind=kLoop, calls=%fused_computation.88 | loop fusion | flops 22020096 | bytes 56655872 | tf_op jit(solution)/shard_map/reduce_sum | solution.py:49
  1944.7 20.1 fusion.151
  2045.9 59.7 %reduce-scatter.31.cloned.1.call-done = f32[192,1536]{1,0:T(8,128)} async-done(((f32[1536,1536]{1,0:T(8,128)}), f32[192,1536]{1,0:T(8,128)}) %reduce-scatter.31.cloned.1.call-update) | async-done | bytes 1179664
  2111.5 31.9 %all-reduce.11.cloned.1.call-done = bf16[192,512]{1,0:T(8,128)(2,1)} async-done(((bf16[192,512]{1,0:T(8,128)(2,1)}), bf16[192,512]{1,0:T(8,128)(2,1)}) %all-reduce.11.cloned.1.call-update) | async-done | bytes 196624 | tf_op jit(solution)/shard_map/psum | solution.py:378
  2145.2 22.3 all-reduce.7
  2185.1 54.4 %reduce-scatter.27.cloned.1.call-done = f32[8,192,192]{2,1,0:T(8,128)} async-done(((f32[8,1536,192]{2,1,0:T(8,128)}), f32[8,192,192]{2,1,0:T(8,128)}) %reduce-scatter.27.cloned.1.call-update) | async-done | bytes 1179664 | tf_op jit(solution)/shard_map/reduce_scatter | solution.py:371
  2239.5 96.5 %reduce-scatter.29.cloned.1.call-done = f32[8,192,192]{2,1,0:T(8,128)} async-done(((f32[8,1536,192]{2,1,0:T(8,128)}), f32[8,192,192]{2,1,0:T(8,128)}) %reduce-scatter.29.cloned.1.call-update) | async-done | bytes 1179664 | tf_op jit(solution)/shard_map/reduce_scatter | solution.py:372
  2336.0 46.3 %reduce-scatter.25.cloned.1.call-done = f32[384,192]{0,1:T(8,128)} async-done(((f32[384,1536]{0,1:T(8,128)}), f32[384,192]{0,1:T(8,128)}) %reduce-scatter.25.cloned.1.call-update) | async-done | bytes 294928 | tf_op jit(solution)/shard_map/reduce_scatter | solution.py:370
  2382.3 46.6 %reduce-scatter.21.cloned.1.call-done = f32[192,384]{1,0:T(8,128)} async-done(((f32[1536,384]{1,0:T(8,128)}), f32[192,384]{1,0:T(8,128)}) %reduce-scatter.21.cloned.1.call-update) | async-done | bytes 294928 | tf_op jit(solution)/shard_map/reduce_scatter | solution.py:369
  (436 shorter events, 679.8 us)
Async XLA Ops:
  38.5 10.7 all-to-all-start.1
  49.1 25.2 %all-to-all-start = ((bf16[8,64,1536]{2,1,0:T(8,128)(2,1)}), bf16[8,64,1536]{2,1,0:T(8,128)(2,1)S(1)}, u32[]{:S(2)}, u32[]{:S(2)}) async-start(bf16[8,64,1536]{2,1,0:T(8,128)(2,1)} %bitcast.306), calls=%async_computation | async-start | bytes 3145728 | tf_op jit(solution)/shard_map/all_to_all | solution.py:121
  53.4 143.8 %all-gather.7.cloned.1.call-start = ((), (), s32[]{:S(2)}) async-start(), calls=%async_computation.16 | async-start | bytes 7864320 | tf_op jit(solution)/shard_map/all_gather | solution.py:156
  82.3 461.9 %reduce-scatter.13.cloned.1.call-start = ((), (), s32[]{:S(2)}) async-start(), calls=%async_computation.17 | async-start | bytes 15728640 | tf_op jit(solution)/shard_map/reduce_scatter | solution.py:193
  82.8 121.2 %copy-start.61 = (f32[64]{0:T(128)}, f32[64]{0:T(128)S(1)}, u32[]{:S(2)}) copy-start(f32[64]{0:T(128)S(1)} %multiply_power_fusion) | copy-start | bytes 772
  83.0 123.4 %copy-start.36 = (f32[2048]{0:T(1024)}, f32[2048]{0:T(1024)S(1)}, u32[]{:S(2)}) copy-start(f32[2048]{0:T(1024)S(1)} %subtract_convert_fusion.2) | copy-start | bytes 24580
  83.1 120.8 %copy-start.32 = (bf16[1536,128]{1,0:T(8,128)(2,1)}, bf16[1536,128]{1,0:T(8,128)(2,1)S(1)}, u32[]{:S(2)}) copy-start(bf16[1536,128]{1,0:T(8,128)(2,1)S(1)} %get-tuple-element.343) | copy-start | bytes 1179652
  83.1 120.8 %copy-start.34 = (bf16[1536,128]{1,0:T(8,128)(2,1)}, bf16[1536,128]{1,0:T(8,128)(2,1)S(1)}, u32[]{:S(2)}) copy-start(bf16[1536,128]{1,0:T(8,128)(2,1)S(1)} %get-tuple-element.344) | copy-start | bytes 1179652
  88.7 129.9 %copy-start.16 = (f32[2048,64]{1,0:T(8,128)}, f32[2048,64]{1,0:T(8,128)S(1)}, u32[]{:S(2)}) copy-start(f32[2048,64]{1,0:T(8,128)S(1)} %get-tuple-element.357) | copy-start | bytes 1572868
  334.0 383.5 %all-gather.13.cloned.1.call-start = ((), (), s32[]{:S(2)}) async-start(), calls=%async_computation.29 | async-start | bytes 7864320 | tf_op jit(solution)/shard_map/all_gather | solution.py:204
  361.9 182.3 %copy-start.8 = (bf16[512,1536]{1,0:T(8,128)(2,1)S(1)}, bf16[512,1536]{1,0:T(8,128)(2,1)}, u32[]{:S(2)}) copy-start(bf16[512,1536]{1,0:T(8,128)(2,1)} %gather_fusion.2) | copy-start | bytes 4718596
  364.9 183.3 %copy-start.38 = (f32[1536]{0:T(1024)S(1)}, f32[1536]{0:T(1024)}, u32[]{:S(2)}) copy-start(f32[1536]{0:T(1024)} %param.28) | copy-start | bytes 18436
  364.9 421.8 %all-gather.9.cloned.1.call-start = ((), (), s32[]{:S(2)}) async-start(), calls=%async_computation.18 | async-start | bytes 7864320 | tf_op jit(solution)/shard_map/all_gather | solution.py:202
  552.1 8.3 all-to-all-start.2
  555.7 732.5 %reduce-scatter.17.cloned.1.call-start = ((), (), s32[]{:S(2)}) async-start(), calls=%async_computation.20 | async-start | bytes 7864320 | tf_op jit(solution)/shard_map/reduce_scatter | solution.py:266
  1179.1 113.7 %copy-start.10 = (bf16[512,1536]{1,0:T(8,128)(2,1)S(1)}, bf16[512,1536]{1,0:T(8,128)(2,1)}, u32[]{:S(2)}) copy-start(bf16[512,1536]{1,0:T(8,128)(2,1)} %gather_fusion.10) | copy-start | bytes 4718596
  1179.1 233.9 %all-gather.11.cloned.1.call-start = ((), (), s32[]{:S(2)}) async-start(), calls=%async_computation.21 | async-start | bytes 7864320 | tf_op jit(solution)/shard_map/all_gather | solution.py:281
  1297.0 645.9 %reduce-scatter.23.cloned.1.call-start = ((), (), s32[]{:S(2)}) async-start(), calls=%async_computation.24 | async-start | bytes 3538944 | tf_op jit(solution)/shard_map/reduce_scatter | solution.py:368
  1297.0 122.8 %copy-start.13 = (bf16[2048,128]{1,0:T(8,128)(2,1)S(1)}, bf16[2048,128]{1,0:T(8,128)(2,1)}, u32[]{:S(2)}) copy-start(bf16[2048,128]{1,0:T(8,128)(2,1)} %copy-done.12) | copy-start | bytes 1572868
  1297.1 122.8 %copy-start.14 = (bf16[2048,128]{1,0:T(8,128)(2,1)S(1)}, bf16[2048,128]{1,0:T(8,128)(2,1)}, u32[]{:S(2)}) copy-start(bf16[2048,128]{1,0:T(8,128)(2,1)} %get-tuple-element.603) | copy-start | bytes 1572868
  1297.1 122.8 %copy-start.26 = (s32[2048]{0:T(1024)S(1)}, s32[2048]{0:T(1024)}, u32[]{:S(2)}) copy-start(s32[2048]{0:T(1024)} %copy-done.25) | copy-start | bytes 24580
  1573.1 424.4 %reduce-scatter.19.cloned.1.call-start = ((), (), s32[]{:S(2)}) async-start(), calls=%async_computation.22 | async-start | bytes 7864320 | tf_op jit(solution)/shard_map/reduce_scatter | solution.py:324
  1581.5 426.4 %reduce-scatter.15.cloned.1.call-start = ((), (), s32[]{:S(2)}) async-start(), calls=%async_computation.19 | async-start | bytes 7864320 | tf_op jit(solution)/shard_map/reduce_scatter | solution.py:242
  1898.8 206.8 %reduce-scatter.31.cloned.1.call-start = ((), (), s32[]{:S(2)}) async-start(), calls=%async_computation.30 | async-start | bytes 10616832
  1942.8 200.6 %all-reduce.11.cloned.1.call-start = ((), (), s32[]{:S(2)}) async-start(), calls=%async_computation.25 | async-start | bytes 393216 | tf_op jit(solution)/shard_map/psum | solution.py:378
  1944.6 294.9 %reduce-scatter.27.cloned.1.call-start = ((), (), s32[]{:S(2)}) async-start(), calls=%async_computation.27 | async-start | bytes 14155776 | tf_op jit(solution)/shard_map/reduce_scatter | solution.py:371
  1964.8 371.2 %reduce-scatter.29.cloned.1.call-start = ((), (), s32[]{:S(2)}) async-start(), calls=%async_computation.28 | async-start | bytes 14155776 | tf_op jit(solution)/shard_map/reduce_scatter | solution.py:372
  1984.8 397.5 %reduce-scatter.25.cloned.1.call-start = ((), (), s32[]{:S(2)}) async-start(), calls=%async_computation.26 | async-start | bytes 2654208 | tf_op jit(solution)/shard_map/reduce_scatter | solution.py:370
  1993.9 435.0 %reduce-scatter.21.cloned.1.call-start = ((), (), s32[]{:S(2)}) async-start(), calls=%async_computation.23 | async-start | bytes 2654208 | tf_op jit(solution)/shard_map/reduce_scatter | solution.py:369
  2016.3 24.7 %all-to-all-start.5 = ((bf16[8,64,1536]{2,1,0:T(8,128)(2,1)}), bf16[8,64,1536]{2,1,0:T(8,128)(2,1)S(1)}, u32[]{:S(2)}, u32[]{:S(2)}) async-start(bf16[8,64,1536]{2,1,0:T(8,128)(2,1)} %bitcast.307), calls=%async_computation.9 | async-start | bytes 3145728 | tf_op jit(solution)/shard_map/all_to_all | solution.py:355
  2041.0 141.2 %all-to-all-start.3 = ((bf16[8,64,1536]{2,1,0:T(8,128)(2,1)}), bf16[8,64,1536]{2,1,0:T(8,128)(2,1)S(1)}, u32[]{:S(2)}, u32[]{:S(2)}) async-start(bf16[8,64,1536]{2,1,0:T(8,128)(2,1)} %bitcast.305), calls=%async_computation.5 | async-start | bytes 3145728 | tf_op jit(solution)/shard_map/all_to_all | solution.py:348
  2182.2 246.7 %copy-start.1 = (bf16[512,1536]{1,0:T(8,128)(2,1)S(1)}, bf16[512,1536]{1,0:T(8,128)(2,1)}, u32[]{:S(2)}) copy-start(bf16[512,1536]{1,0:T(8,128)(2,1)} %param.18) | copy-start | bytes 4718596
  (65 other events, 944.0 us)
Sparse Core Ops, SparseCore 0:
  82.4 114.7 all-gather.6
  334.1 210.0 reduce-scatter.12
  546.4 124.7 all-gather.12
  673.2 113.4 all-gather.8
  1179.2 108.9 reduce-scatter.16
  1297.1 115.8 all-gather.10
  1573.2 44.4 reduce-scatter.22
  1620.1 110.7 reduce-scatter.18
  1898.9 108.9 reduce-scatter.14
  2011.6 93.9 reduce-scatter.30
  2108.6 34.7 all-reduce.10
  2147.4 92.1 reduce-scatter.26
  2243.6 92.3 reduce-scatter.28
  2339.8 42.4 reduce-scatter.24
  2386.4 42.4 reduce-scatter.20
where the time goes:
time: 2450 us; the launch traced here: 2440 us
  waiting for transfers between devices  901 us (37%)
  local copies, waits for them, and re-layouts  716 us (29%)
  matrix products  386 us (16%)
  other arithmetic  301 us (12%)
  blocking collectives  81.8 us (3%)
    gather x4, local copies, waits for them, and re-layouts, pair_sum(): return jnp.sum(table[slot_pairs] * pair_weights[:, :, None], axis=1)  253 us
    reduce_scatter x1, waiting for transfers between devices, per_device(): lax.psum_scatter(jnp.dot(attended, w_out, preferred_element_type=jnp.floa...  179 us
    reduce_sum x2, other arithmetic, pair_sum(): return jnp.sum(table[slot_pairs] * pair_weights[:, :, None], axis=1)  166 us
    all_gather x1, waiting for transfers between devices, per_device(): lax.all_gather(state_grad.astype(jnp.bfloat16), 'tensor', axis=0, tiled=T...  116 us
    reduce_scatter x1, waiting for transfers between devices, per_device(): lax.psum_scatter(pair_sum(rows_pad, slot_pairs, pair_ones).astype(jnp.bfl...  109 us
    all_gather x1, waiting for transfers between devices, per_device(): normed_one = lax.all_gather(normed_own, 'tensor', axis=0, tiled=True)  109 us
    reduce_scatter x1, waiting for transfers between devices, per_device(): lax.psum_scatter(grad_up, 'dp', scatter_dimension=1, tiled=True)  96.5 us
    unnamed x16, waiting for transfers between devices  60 us
  transfers between devices with their start and end apart: 20, of which 15 were waited for; matrix products, arithmetic and copies ran while one was open for 28% of the time, Pallas kernels for 0%

commit v1 on v0

v1 whole, which is shorter than its diff:
```python
import functools

import jax
import jax.numpy as jnp
from jax import lax
from jax.experimental import pallas as pl
from jax.experimental.pallas import tpu as pltpu
from jax.sharding import PartitionSpec as P

HD = 128
EPS = 1e-06
ROPE_BASE = 1000000.0
MASKED = -1e30
LOG2E = 1.4426950408889634
F32 = jnp.float32
BF16 = jnp.bfloat16
META = 128


def mm(a, b):
    return lax.dot_general(a, b, (((1,), (0,)), ((), ())), preferred_element_type=F32)


def mm_nt(a, b):
    return lax.dot_general(a, b, (((1,), (1,)), ((), ())), preferred_element_type=F32)


def mm_tn(a, b):
    return lax.dot_general(a, b, (((0,), (0,)), ((), ())), preferred_element_type=F32)


def params(mb=56):
    return pltpu.CompilerParams(vmem_limit_bytes=mb * 2**20)


def swap_halves(u):
    return pltpu.roll(u, HD // 2, 1)


def project_kernel(rotated, x_ref, w_ref, cos_ref, sin_ref, out_ref):
    step = pl.program_id(0)
    raw = mm(x_ref[...], w_ref[...])
    halves = []
    for i in range(raw.shape[1] // HD):
        u = raw[:, i * HD : (i + 1) * HD]
        turned = u * cos_ref[...] + swap_halves(u) * sin_ref[...]
        halves.append(jnp.where(step < rotated, turned, u))
    out_ref[...] = jnp.concatenate(halves, axis=1).astype(BF16)


def project(x, w, cos_full, sin_full, rotated):
    rows, width = x.shape
    columns = w.shape[1]
    return pl.pallas_call(
        functools.partial(project_kernel, rotated),
        grid=(columns // 256,),
        in_specs=[
            pl.BlockSpec((rows, width), lambda i: (0, 0)),
            pl.BlockSpec((width, 256), lambda i: (0, i)),
            pl.BlockSpec((rows, HD), lambda i: (0, 0)),
            pl.BlockSpec((rows, HD), lambda i: (0, 0)),
        ],
        out_specs=pl.BlockSpec((rows, 256), lambda i: (0, i)),
        out_shape=jax.ShapeDtypeStruct((rows, columns), BF16),
        compiler_params=params(),
        name="project",
        cost_estimate=pl.CostEstimate(
            flops=2 * rows * width * columns,
            bytes_accessed=2 * (rows * width + width * columns + rows * columns),
            transcendentals=0,
        ),
    )(x, w, cos_full, sin_full)


def make_bias(z_ref, start_ref, bias_ref):
    rows = start_ref.shape[0]
    blocks = bias_ref.shape[0]
    z = z_ref[0]
    for j in range(blocks):
        key = (z - (blocks - 1) + j) * rows + lax.broadcasted_iota(jnp.int32, (rows, rows), 1)
        query = z * rows + lax.broadcasted_iota(jnp.int32, (rows, rows), 0)
        allowed = (key >= start_ref[...]) & (key <= query)
        bias_ref[j] = jnp.where(allowed, 0.0, MASKED)


def attend_kernel(kv_heads, z_ref, start_ref, q_ref, kv0_ref, kv1_ref, kv2_ref, o_ref, lse_ref, bias_ref):
    head = pl.program_id(0)
    heads = pl.num_programs(0)

    @pl.when(head == 0)
    def _():
        make_bias(z_ref, start_ref, bias_ref)

    kvh = head // (heads // kv_heads)
    scale = HD**-0.5 * LOG2E
    q = q_ref[...]
    kvs = (kv0_ref, kv1_ref, kv2_ref)
    kcol = pl.ds(pl.multiple_of(kvh * HD, HD), HD)
    vcol = pl.ds(pl.multiple_of((kv_heads + kvh) * HD, HD), HD)
    scores = [mm_nt(q, ref[:, kcol]) * scale + bias_ref[j] for j, ref in enumerate(kvs)]
    peak = functools.reduce(
        jnp.maximum, [jnp.max(s, axis=1, keepdims=True) for s in scores]
    )
    soft = [jnp.exp2(s - peak) for s in scores]
    total = sum(jnp.sum(s, axis=1, keepdims=True) for s in soft)
    mixed = sum(mm(s.astype(BF16), ref[:, vcol]) for s, ref in zip(soft, kvs))
    o_ref[...] = (mixed / total).astype(BF16)
    lse_ref[0] = peak + jnp.log2(total)


def attend(z, start, q, kvs, kv_heads):
    rows, columns = q.shape
    heads = columns // HD
    blocks = len(kvs)
    kv_spec = pl.BlockSpec(kvs[0].shape, lambda h, s: (0, 0))
    return pl.pallas_call(
        functools.partial(attend_kernel, kv_heads),
        grid_spec=pltpu.PrefetchScalarGridSpec(
            num_scalar_prefetch=1,
            grid=(heads,),
            in_specs=[
                pl.BlockSpec((rows, 1), lambda h, s: (0, 0)),
                pl.BlockSpec((rows, HD), lambda h, s: (0, h)),
                *[kv_spec] * blocks,
            ],
            out_specs=[
                pl.BlockSpec((rows, HD), lambda h, s: (0, h)),
                pl.BlockSpec((1, rows, 1), lambda h, s: (h, 0, 0)),
            ],
            scratch_shapes=[pltpu.VMEM((blocks, rows, rows), F32)],
        ),
        out_shape=[
            jax.ShapeDtypeStruct((rows, columns), BF16),
            jax.ShapeDtypeStruct((heads, rows, 1), F32),
        ],
        compiler_params=params(),
        name="attend",
        cost_estimate=pl.CostEstimate(
            flops=4 * rows * rows * blocks * columns,
            bytes_accessed=8 * rows * columns,
            transcendentals=rows * rows * blocks * heads,
        ),
    )(z, start, q, *kvs)


def attend_back_kernel(
    kv_heads,
    z_ref,
    start_ref,
    q_ref,
    o_ref,
    do_ref,
    lse_ref,
    cos_ref,
    sin_ref,
    kv0_ref,
    kv1_ref,
    kv2_ref,
    dq_ref,
    d0_ref,
    d1_ref,
    d2_ref,
    bias_ref,
    acc_ref,
):
    head = pl.program_id(0)
    heads = pl.num_programs(0)

    @pl.when(head == 0)
    def _():
        make_bias(z_ref, start_ref, bias_ref)
        acc_ref[...] = jnp.zeros_like(acc_ref)

    kvh = head // (heads // kv_heads)
    scale = HD**-0.5 * LOG2E
    q = q_ref[...]
    do = do_ref[...]
    centre = jnp.sum(do.astype(F32) * o_ref[...].astype(F32), axis=1, keepdims=True)
    lse = lse_ref[0]
    kcol = pl.ds(pl.multiple_of(kvh * HD, HD), HD)
    vcol = pl.ds(pl.multiple_of((kv_heads + kvh) * HD, HD), HD)
    dq = jnp.zeros(q.shape, F32)
    for j, ref in enumerate((kv0_ref, kv1_ref, kv2_ref)):
        keys = ref[:, kcol]
        soft = jnp.exp2(mm_nt(q, keys) * scale + (bias_ref[j] - lse))
        acc_ref[j, :, vcol] += mm_tn(soft.astype(BF16), do)
        dsoft = mm_nt(do, ref[:, vcol])
        dscore = (soft * (dsoft - centre)).astype(BF16)
        dq += mm(dscore, keys)
        acc_ref[j, :, kcol] += mm_tn(dscore, q) * (HD**-0.5)
    dq = dq * (HD**-0.5)
    dq_ref[...] = (dq * cos_ref[...] - swap_halves(dq) * sin_ref[...]).astype(BF16)

    @pl.when(head == heads - 1)
    def _():
        d0_ref[...] = acc_ref[0].astype(BF16)
        d1_ref[...] = acc_ref[1].astype(BF16)
        d2_ref[...] = acc_ref[2]


def attend_back(z, start, q, o, do, lse, cos_full, sin_full, kvs, kv_heads):
    rows, columns = q.shape
    heads = columns // HD
    blocks = len(kvs)
    kv_columns = kvs[0].shape[1]
    kv_spec = pl.BlockSpec((rows, kv_columns), lambda h, s: (0, 0))
    head_spec = pl.BlockSpec((rows, HD), lambda h, s: (0, h))
    table_spec = pl.BlockSpec((rows, HD), lambda h, s: (0, 0))
    return pl.pallas_call(
        functools.partial(attend_back_kernel, kv_heads),
        grid_spec=pltpu.PrefetchScalarGridSpec(
            num_scalar_prefetch=1,
            grid=(heads,),
            in_specs=[
                pl.BlockSpec((rows, 1), lambda h, s: (0, 0)),
                head_spec,
                head_spec,
                head_spec,
                pl.BlockSpec((1, rows, 1), lambda h, s: (h, 0, 0)),
                table_spec,
                table_spec,
                *[kv_spec] * blocks,
            ],
            out_specs=[head_spec, *[kv_spec] * blocks],
            scratch_shapes=[
                pltpu.VMEM((blocks, rows, rows), F32),
                pltpu.VMEM((blocks, rows, kv_columns), F32),
            ],
        ),
        out_shape=[
            jax.ShapeDtypeStruct((rows, columns), BF16),
            jax.ShapeDtypeStruct((rows, kv_columns), BF16),
            jax.ShapeDtypeStruct((rows, kv_columns), BF16),
            jax.ShapeDtypeStruct((rows, kv_columns), F32),
        ],
        compiler_params=params(),
        name="attend_back",
        cost_estimate=pl.CostEstimate(
            flops=10 * rows * rows * blocks * columns,
            bytes_accessed=12 * rows * columns,
            transcendentals=rows * rows * blocks * heads,
        ),
    )(z, start, q, o, do, lse, cos_full, sin_full, *kvs)


def expert_kernel(first, x_ref, dy_ref, gate_ref, wg_ref, wu_ref, wd_ref, *refs):
    if first:
        y_ref, dn_ref, hs_ref, dg_ref, du_ref = refs
    else:
        y0_ref, dn0_ref, y_ref, dn_ref, hs_ref, dg_ref, du_ref = refs
    step = pl.program_id(0)

    @pl.when(step == 0)
    def _():
        if first:
            y_ref[...] = jnp.zeros_like(y_ref)
            dn_ref[...] = jnp.zeros_like(dn_ref)
        else:
            y_ref[...] = y0_ref[...]
            dn_ref[...] = dn0_ref[...]

    x = x_ref[...]
    gate = gate_ref[...].astype(F32)
    g = jnp.maximum(mm(x, wg_ref[...]), 0.0)
    u = mm(x, wu_ref[...])
    square = g * g
    hs = ((square * u).astype(BF16).astype(F32) * gate).astype(BF16)
    hs_ref[...] = hs
    dh = mm_nt(dy_ref[...], wd_ref[...]) * gate
    dg = (dh * u * (2.0 * g)).astype(BF16)
    du = (dh * square).astype(BF16)
    dg_ref[...] = dg
    du_ref[...] = du
    dn_ref[...] += mm_nt(dg, wg_ref[...]) + mm_nt(du, wu_ref[...])
    y_ref[...] += mm(hs, wd_ref[...])


def experts(x, dy, gate, wg, wu, wd, before=None, chunk=256):
    rows, width = x.shape
    hidden = gate.shape[1]
    full = pl.BlockSpec((rows, width), lambda i: (0, 0))
    part = pl.BlockSpec((rows, chunk), lambda i: (0, i))
    columns = pl.BlockSpec((width, chunk), lambda i: (0, i))
    extra = () if before is None else tuple(before)
    return pl.pallas_call(
        functools.partial(expert_kernel, before is None),
        grid=(hidden // chunk,),
        in_specs=[
            full,
            full,
            part,
            columns,
            columns,
            pl.BlockSpec((chunk, width), lambda i: (i, 0)),
            *[full] * len(extra),
        ],
        out_specs=[full, full, part, part, part],
        out_shape=[
            jax.ShapeDtypeStruct((rows, width), F32),
            jax.ShapeDtypeStruct((rows, width), F32),
            *[jax.ShapeDtypeStruct((rows, hidden), BF16)] * 3,
        ],
        compiler_params=params(),
        name="experts",
        cost_estimate=pl.CostEstimate(
            flops=12 * rows * width * hidden,
            bytes_accessed=6 * width * hidden + 16 * rows * width,
            transcendentals=0,
        ),
    )(x, dy, gate, wg, wu, wd, *extra)


def per_device(
    tokens,
    perm,
    routes,
    gates,
    lengths,
    cotangent,
    gain_attn,
    w_query,
    w_keyval,
    w_out,
    gain_moe,
    w_gate,
    w_up,
    w_down,
):
    dp_count = lax.axis_size("dp")
    tensor_count = lax.axis_size("tensor")
    d = lax.axis_index("dp")
    z = lax.axis_index("tensor")
    rows, width = tokens.shape
    group_rows = perm.shape[0]
    share = rows // dp_count
    top = routes.shape[1]
    experts_n, _, part_hidden = w_gate.shape
    hidden = experts_n * part_hidden
    capacity = 9 * group_rows * top // (8 * experts_n)
    kv_heads = w_keyval.shape[1] // (2 * HD)
    query_cols = w_query.shape[1]
    team = 8
    teams = [[t * team + i for i in range(team)] for t in range(dp_count // team)]
    teams = None if len(teams) == 1 else teams
    piece_rows = width // team
    member = d % team

    def z_move(x, pairs):
        return lax.ppermute(x, "tensor", pairs)

    near = [(i, i ^ 1) for i in range(tensor_count)]
    far = [(i, i ^ 2) for i in range(tensor_count)]

    def deal(x):
        return lax.all_to_all(
            x.reshape(dp_count, share, x.shape[1]), "dp", split_axis=0, concat_axis=0, tiled=True
        ).reshape(rows, x.shape[1])

    own_perm = lax.dynamic_slice_in_dim(perm, z * rows, rows, 0)
    own_routes = lax.dynamic_slice_in_dim(routes, z * rows, rows, 0)
    dest = own_perm // group_rows
    place = own_perm % rows
    row_index = jnp.arange(rows, dtype=jnp.int32)
    lower = (row_index[:, None] > row_index[None, :]).astype(BF16)
    dest_hot = (dest[:, None] == jnp.arange(dp_count, dtype=jnp.int32)[None, :]).astype(BF16)
    earlier = jnp.sum(mm(lower, dest_hot) * dest_hot.astype(F32), axis=1).astype(jnp.int32)
    slot = dest * share + earlier
    pack = (row_index[:, None] == slot[None, :]).astype(BF16)
    meta = jnp.concatenate(
        [
            (place // 16)[:, None].astype(BF16),
            (place % 16)[:, None].astype(BF16),
            own_routes.astype(BF16),
            gates,
            jnp.zeros((rows, META - 2 - 2 * top), BF16),
        ],
        axis=1,
    )
    packed = mm(pack, jnp.concatenate([tokens, meta], axis=1)).astype(BF16)
    arrived = deal(packed)
    packed_dy = mm(pack, cotangent).astype(BF16)
    arrived_dy = deal(packed_dy)
    meta_in = arrived[:, width:].astype(F32)
    place_in = (meta_in[:, 0] * 16.0 + meta_in[:, 1]).astype(jnp.int32)
    unpack = (row_index[:, None] == place_in[None, :]).astype(BF16)
    dealt = mm(unpack, arrived)
    x_rows = dealt[:, :width]
    meta_rows = dealt[:, width:]
    dy_rows = mm(unpack, arrived_dy).astype(BF16)

    expert_ids = jnp.arange(experts_n, dtype=jnp.int32).astype(F32)
    route_rows = meta_rows[:, 2 : 2 + top]
    gate_rows = meta_rows[:, 2 + top : 2 + 2 * top]
    hot = route_rows[:, :, None] == expert_ids[None, None, :]
    routed = jnp.sum(hot.astype(F32), axis=1)
    counts = lax.all_gather(jnp.sum(routed, axis=0)[None, :], "tensor", axis=0, tiled=True)
    z_ids = jnp.arange(tensor_count, dtype=jnp.int32)
    base = jnp.sum(jnp.where(z_ids[:, None] < z, counts, 0.0), axis=0)
    position = mm(lower, routed.astype(BF16)) + base[None, :]
    weight = jnp.sum(jnp.where(hot, gate_rows[:, :, None], 0.0), axis=1)
    weight = jnp.where(position < capacity, weight, 0.0).astype(BF16)
    weight_near = z_move(weight, near)
    gate_own = jnp.repeat(weight, part_hidden, axis=1)
    gate_near = jnp.repeat(weight_near, part_hidden, axis=1)
    dy_near = z_move(dy_rows, near)

    def team_gather(x):
        return lax.all_gather(x, "dp", axis=0, tiled=True, axis_index_groups=teams)

    def flat(w):
        return w.transpose(1, 0, 2).reshape(w.shape[1], hidden)

    def piece(w):
        return lax.dynamic_slice_in_dim(w, member * piece_rows, piece_rows, 1)

    wq_piece = lax.dynamic_slice_in_dim(w_query, member * piece_rows, piece_rows, 0)
    wq_piece = lax.all_gather(wq_piece, "tensor", axis=0, tiled=True)
    wq_all = team_gather(wq_piece).reshape(team, tensor_count, piece_rows, query_cols)
    wq = wq_all.transpose(0, 2, 1, 3).reshape(width, tensor_count * query_cols)
    out_rows = query_cols // team
    wo_piece = lax.dynamic_slice_in_dim(w_out, member * out_rows, out_rows, 0)
    wo_piece = lax.all_gather(wo_piece, "tensor", axis=0, tiled=True)
    wo_all = team_gather(wo_piece).reshape(team, tensor_count, out_rows, width)
    wo = wo_all.transpose(1, 0, 2, 3).reshape(tensor_count * query_cols, width)

    wd_own = w_down.reshape(hidden, width)
    wg_own = flat(w_gate)
    wu_own = flat(w_up)
    gu_piece = jnp.concatenate([flat(piece(w_gate)), flat(piece(w_up))], axis=1)
    hidden_piece = hidden // team
    wd_piece = lax.dynamic_slice_in_dim(wd_own, member * hidden_piece, hidden_piece, 0)
    gu_far = team_gather(z_move(gu_piece, far))
    wd_far = team_gather(z_move(wd_piece, far))
    wg_far = gu_far[:, :hidden]
    wu_far = gu_far[:, hidden:]

    seq_lengths = lengths[0]
    seq_index = jnp.arange(seq_lengths.shape[0], dtype=jnp.int32)
    seq_ends = jnp.sum(
        jnp.where(seq_index[None, :] <= seq_index[:, None], seq_lengths[None, :], 0), axis=1
    ).astype(jnp.int32)
    global_row = z * rows + row_index
    start = jnp.max(
        jnp.where(global_row[:, None] >= seq_ends[None, :], seq_ends[None, :], 0), axis=1
    ).astype(jnp.int32)
    offset = (global_row - start).astype(F32)
    frequency = ROPE_BASE ** (-2.0 * jnp.arange(HD // 2, dtype=F32) / HD)
    angles = offset[:, None] * frequency[None, :]
    cosine, sine = jnp.cos(angles), jnp.sin(angles)
    cos_full = jnp.concatenate([cosine, cosine], axis=1)
    sin_full = jnp.concatenate([-sine, sine], axis=1)
    start = start[:, None]
    z_arg = z.astype(jnp.int32)[None]

    inv_one = lax.rsqrt(jnp.mean(x_rows * x_rows, axis=1, keepdims=True) + EPS)
    n1 = (x_rows * inv_one * gain_attn).astype(BF16)
    kv = project(n1, w_keyval, cos_full, sin_full, 1)
    up_one = [(i, i + 1) for i in range(tensor_count - 1)]
    up_two = [(i, i + 2) for i in range(tensor_count - 2)]
    kv_one = z_move(kv, up_one)
    kv_two = z_move(kv, up_two)
    q = project(n1, wq, cos_full, sin_full, wq.shape[1] // 256)
    kvs = (kv_two, kv_one, kv)
    o, lse = attend(z_arg, start, q, kvs, kv_heads)
    h = x_rows + mm(o, wo)
    inv_two = lax.rsqrt(jnp.mean(h * h, axis=1, keepdims=True) + EPS)
    n2 = (h * inv_two * gain_moe).astype(BF16)

    n2_near = z_move(n2, near)
    y, dn2, hs_oo, dg_oo, du_oo = experts(n2, dy_rows, gate_own, wg_own, wu_own, wd_own)
    y, dn2, hs_of, dg_of, du_of = experts(
        n2, dy_rows, gate_own, wg_far, wu_far, wd_far, (y, dn2)
    )
    yn, dnn, hs_no, dg_no, du_no = experts(n2_near, dy_near, gate_near, wg_own, wu_own, wd_own)
    yn, dnn, hs_nf, dg_nf, du_nf = experts(
        n2_near, dy_near, gate_near, wg_far, wu_far, wd_far, (yn, dnn)
    )
    dn2 = dn2 + z_move(dnn.astype(BF16), near).astype(F32)
    result = h + y + z_move(yn.astype(BF16), near).astype(F32)

    def two(a, b, c, e):
        return (mm_tn(a, b) + mm_tn(c, e)).astype(BF16)

    grads_own = [
        two(n2, dg_oo, n2_near, dg_no),
        two(n2, du_oo, n2_near, du_no),
        two(dy_rows, hs_oo, dy_near, hs_no),
    ]
    grads_far = [
        two(n2, dg_of, n2_near, dg_nf),
        two(n2, du_of, n2_near, du_nf),
        two(dy_rows, hs_of, dy_near, hs_nf),
    ]

    def dp_sum(x):
        return lax.psum_scatter(x, "dp", scatter_dimension=0, tiled=True)

    sums_far = [z_move(dp_sum(g), far) for g in grads_far]
    sums = [dp_sum(g).astype(F32) + f.astype(F32) for g, f in zip(grads_own, sums_far)]
    out_w = width // dp_count
    sum_gate, sum_up, sum_down = [g.reshape(out_w, experts_n, part_hidden) for g in sums]
    sum_gate = sum_gate.transpose(1, 0, 2)
    sum_up = sum_up.transpose(1, 0, 2)
    sum_down = sum_down.transpose(1, 2, 0)

    gain_two_part = jnp.sum(dn2 * h * inv_two, axis=0)
    u2 = dn2 * gain_moe
    dh = dy_rows.astype(F32) + inv_two * (
        u2 - h * inv_two * inv_two * jnp.mean(u2 * h, axis=1, keepdims=True)
    )
    dhb = dh.astype(BF16)
    do = mm_nt(dhb, wo).astype(BF16)
    grad_out_part = mm_tn(dhb, o).astype(BF16)

    dq, dkv_two, dkv_one, dkv = attend_back(
        z_arg, start, q, o, do, lse, cos_full, sin_full, kvs, kv_heads
    )
    dkv = dkv + z_move(dkv_one, [(b, a) for a, b in up_one]).astype(F32)
    dkv = dkv + z_move(dkv_two, [(b, a) for a, b in up_two]).astype(F32)

    def unrotate(u):
        swapped = jnp.concatenate([u[:, HD // 2 :], u[:, : HD // 2]], axis=1)
        return u * cos_full - swapped * sin_full

    dkv = jnp.concatenate(
        [unrotate(dkv[:, i * HD : (i + 1) * HD]) for i in range(kv_heads)]
        + [dkv[:, kv_heads * HD :]],
        axis=1,
    ).astype(BF16)
    dn1 = mm_nt(dq, wq) + mm_nt(dkv, w_keyval)
    grad_query_part = mm_tn(n1, dq).astype(BF16)
    grad_keyval_part = mm_tn(n1, dkv).astype(BF16)
    gain_one_part = jnp.sum(dn1 * x_rows * inv_one, axis=0)
    u1 = dn1 * gain_attn
    dx = dh + inv_one * (
        u1 - x_rows * inv_one * inv_one * jnp.mean(u1 * x_rows, axis=1, keepdims=True)
    )

    def give_back(values):
        back = deal(mm_tn(unpack, values.astype(BF16)).astype(BF16))
        return mm_tn(pack, back).astype(BF16)

    outputs = give_back(result)
    grad_tokens = give_back(dx)

    def tensor_sum(x):
        parts = x.reshape(x.shape[0], tensor_count, x.shape[1] // tensor_count).transpose(1, 0, 2)
        return lax.psum_scatter(parts, "tensor", scatter_dimension=0, tiled=True)[0].astype(F32)

    sum_out = tensor_sum(dp_sum(grad_out_part)).T
    sum_query = tensor_sum(dp_sum(grad_query_part))
    small = jnp.concatenate(
        [
            grad_keyval_part,
            gain_one_part[:, None].astype(BF16),
            gain_two_part[:, None].astype(BF16),
            jnp.zeros((width, HD - 2), BF16),
        ],
        axis=1,
    )
    small = lax.psum(dp_sum(small), "tensor").astype(F32)
    kv_cols = w_keyval.shape[1]
    return (
        outputs,
        grad_tokens,
        small[:, kv_cols],
        sum_query,
        small[:, :kv_cols],
        sum_out,
        small[:, kv_cols + 1],
        sum_gate,
        sum_up,
        sum_down,
    )


def solution(mesh):
    in_specs = (
        P(("dp", "tensor"), None),
        P("dp"),
        P("dp", None),
        P(("dp", "tensor"), None),
        P("dp", None),
        P(("dp", "tensor"), None),
        P(),
        P(None, "tensor"),
        P(),
        P("tensor", None),
        P(),
        P(None, None, "tensor"),
        P(None, None, "tensor"),
        P(None, "tensor", None),
    )
    out_specs = (
        P(("dp", "tensor"), None),
        P(("dp", "tensor"), None),
        P("dp"),
        P("dp", "tensor"),
        P("dp", None),
        P("tensor", "dp"),
        P("dp"),
        P(None, "dp", "tensor"),
        P(None, "dp", "tensor"),
        P(None, "tensor", "dp"),
    )
    return jax.shard_map(
        per_device, mesh=mesh, in_specs=in_specs, out_specs=out_specs, check_vma=False
    )
```

time: 2450 us -> 1160 us (0.47)
  local copies, waits for them, and re-layouts: 716 us -> 89 us
  waiting for transfers between devices: 901 us -> 595 us
  other arithmetic: 301 us -> 29.4 us
  matrix products: 386 us -> 125 us
  Pallas kernels: 0 us -> 188 us
    gather x22 -> x0, local copies, waits for them, and re-layouts: 454 us -> none  [the longest x4 253 us: pair_sum(): return jnp.sum(table[slot_pairs] * pair_weights[:, :, None], axis=1)]
    dot_general x43 -> x29, matrix products: 386 us -> 125 us  [the longest x19 101 us: mm_tn(): lax.dot_general(a, b, (((0,), (0,)), ((), ())), preferred_element_type=F32)]
    all_gather x4, waiting for transfers between devices: 229 us -> 0.03 us  [team_gather(): return lax.all_gather(x, 'dp', axis=0, tiled=True, axis_index_groups=teams)]
    reduce_sum x14 -> x5, other arithmetic: 204 us -> 3.7 us  [the longest x1 3 us: per_device(): gain_two_part = jnp.sum(dn2 * h * inv_two, axis=0)]
    reduce_scatter x9 -> x10, waiting for transfers between devices: 540 us -> 346 us  [the longest x8 304 us: dp_sum(): return lax.psum_scatter(x, 'dp', scatter_dimension=0, tiled=True)]
    pallas_call x0 -> x8, Pallas kernels: none -> 188 us  [the longest x4 109 us: experts(): pl.pallas_call(functools.partial(expert_kernel, before is None), grid=(hi...]
    ppermute x0 -> x14, waiting for transfers between devices: none -> 125 us  [z_move(): return lax.ppermute(x, 'tensor', pairs)]
    concatenate x6 -> x2, local copies, waits for them, and re-layouts: 91.4 us -> 2.62 us  [the longest x1 2.55 us: per_device(): packed = mm(pack, jnp.concatenate([tokens, meta], axis=1)).astype(BF16)]
  transfers between devices with their start and end apart: 20 -> 34, of which waited for: 15 -> 18; matrix products, arithmetic and copies ran while one was open for 28% -> 18% of each run, Pallas kernels for 0% -> 11%
where the time goes in v1:
time: 1160 us; the launch traced here: 1150 us
  waiting for transfers between devices  595 us (51%)
  Pallas kernels  188 us (16%)
  matrix products  125 us (11%)
  local copies, waits for them, and re-layouts  89 us (8%)
  blocking collectives  66.3 us (6%)
  starting transfers between devices  39.7 us (3%)
  other arithmetic  29.4 us (3%)
  between operations  15.6 us (1%)
    reduce_scatter x8, waiting for transfers between devices, dp_sum(): return lax.psum_scatter(x, 'dp', scatter_dimension=0, tiled=True)  304 us
    ppermute x14, waiting for transfers between devices, z_move(): return lax.ppermute(x, 'tensor', pairs)  125 us
    pallas_call x4, Pallas kernels, experts(): pl.pallas_call(functools.partial(expert_kernel, before is None), grid=(hi...  109 us
    dot_general x19, matrix products, mm_tn(): lax.dot_general(a, b, (((0,), (0,)), ((), ())), preferred_element_type=F32)  101 us
    all_to_all x4, waiting for transfers between devices, deal(): lax.all_to_all(x.reshape(dp_count, share, x.shape[1]), 'dp', split_axis=0...  59.4 us
    psum x1, waiting for transfers between devices, per_device(): small = lax.psum(dp_sum(small), 'tensor').astype(F32)  52.2 us
    reduce_scatter x2, waiting for transfers between devices, tensor_sum(): lax.psum_scatter(parts, 'tensor', scatter_dimension=0, tiled=True)[0]  41.9 us
    pallas_call x1, Pallas kernels, attend_back(): pl.pallas_call(functools.partial(attend_back_kernel, kv_heads), grid_spec...  37.7 us
  transfers between devices with their start and end apart: 34, of which 18 were waited for; matrix products, arithmetic and copies ran while one was open for 18% of the time, Pallas kernels for 11%

profile of v1, /device:TPU:0, one launch (start us, length us, event | category | flops | bytes accessed | tf_op | source)
XLA Modules:
  0.0 1148.4 jit_solution(616775260848965478)
XLA Ops:
  8.3 18.4 %all_gather.21 = bf16[768,384]{1,0:T(8,128)(2,1)} all-gather(bf16[192,384]{1,0:T(8,128)(2,1)S(1)} %constant_dynamic-slice_fusion.4), channel_id=1, replica_groups=mesh['dp'=8,'tensor'=4] {'tensor'}, dimensions={0}, use_global_device_ids=true | all-gather | bytes 737280 | tf_op jit(solution)/shard_map/all_gather | solution.py:417
  27.7 17.4 %all_gather.23 = bf16[192,1536]{1,0:T(8,128)(2,1)} all-gather(bf16[48,1536]{1,0:T(8,128)(2,1)S(1)} %constant_dynamic-slice_fusion.3), channel_id=1, replica_groups=mesh['dp'=8,'tensor'=4] {'tensor'}, dimensions={0}, use_global_device_ids=true | all-gather | bytes 737280 | tf_op jit(solution)/shard_map/all_gather | solution.py:422
  50.7 46.9 %collective-permute-done.2 = bf16[192,3072]{1,0:T(8,128)(2,1)S(1)} collective-permute-done((bf16[192,3072]{1,0:T(8,128)(2,1)S(1)}, bf16[192,3072]{1,0:T(8,128)(2,1)S(1)}, u32[]{:S(2)}, u32[]{:S(2)}) %collective-permute-start.2) | collective-permute-done | bytes 1179680 | tf_op jit(solution)/shard_map/ppermute | solution.py:349
  119.6 23.2 %collective-permute-done.3 = bf16[192,1536]{1,0:T(8,128)(2,1)S(1)} collective-permute-done((bf16[192,1536]{1,0:T(8,128)(2,1)}, bf16[192,1536]{1,0:T(8,128)(2,1)S(1)}, u32[]{:S(2)}, u32[]{:S(2)}) %collective-permute-start.3) | collective-permute-done | bytes 589856 | tf_op jit(solution)/shard_map/ppermute | solution.py:349
  167.3 21.8 %all-to-all-done.1 = bf16[8,64,1536]{2,1,0:T(8,128)(2,1)S(1)} async-done(((bf16[8,64,1536]{2,1,0:T(8,128)(2,1)}), bf16[8,64,1536]{2,1,0:T(8,128)(2,1)S(1)}, u32[]{:S(2)}, u32[]{:S(2)}) %all-to-all-start.1) | async-done | bytes 1572896 | tf_op jit(solution)/shard_map/all_to_all | solution.py:355
  205.2 7.9 project.2.q_ref
  214.1 28.8 %attend.1 = (bf16[512,1536]{1,0:T(8,128)(2,1)}, f32[12,512,1]{2,1,0:T(8,128)}) custom-call(s32[1]{0:T(128)} %bitcast.2.z_ref, s32[512,1]{1,0:T(8,128)} %copy.116.start_ref, bf16[512,1536]{1,0:T(8,128)(2,1)} %project.2.q_ref, bf16[512,512]{1,0:T(8,128)(2,1)} %copy-done.22, bf16[512,512]{1,0:T(8,128)(2,1)} %copy-done.23, bf16[512,512]{1,0:T(8,128)(2,1)} %project.3.kv2_ref), custom_call_target="tpu_custom_call" | custom-call | flops 4831838208 | bytes 6291456 | tf_op jit(solution)/shard_map/attend/pallas_call | solution.py:116
  257.5 30.5 %all-reduce = f32[32]{0:T(128)S(1)} all-reduce(f32[32]{0:T(128)S(1)} %dynamic-update-slice), channel_id=2, replica_groups=mesh['dp'=8,'tensor'=4] {'tensor'}, use_global_device_ids=true, to_apply=%add | all-reduce | flops 32 | bytes 256
  309.4 26.3 %experts.6 = (f32[512,1536]{1,0:T(8,128)}, f32[512,1536]{1,0:T(8,128)}, bf16[512,1536]{1,0:T(8,128)(2,1)}, bf16[512,1536]{1,0:T(8,128)(2,1)}, bf16[512,1536]{1,0:T(8,128)(2,1)}) custom-call(bf16[512,1536]{1,0:T(8,128)(2,1)} %collective-permute-done.4.x_ref, bf16[512,1536]{1,0:T(8,128)(2,1)} %collective-permute-done.5.dy_ref, ...), custom_call_target="tpu_custom_call" | custom-call | flops 14495514624 | bytes 26738688 | tf_op jit(solution)/shard_map/experts/pallas_call | solution.py:285
  335.8 8.0 fusion.37
  343.7 28.1 %experts.7 = (f32[512,1536]{1,0:T(8,128)}, f32[512,1536]{1,0:T(8,128)}, bf16[512,1536]{1,0:T(8,128)(2,1)}, bf16[512,1536]{1,0:T(8,128)(2,1)}, bf16[512,1536]{1,0:T(8,128)(2,1)}) custom-call(bf16[512,1536]{1,0:T(8,128)(2,1)} %collective-permute-done.4.x_ref, bf16[512,1536]{1,0:T(8,128)(2,1)} %collective-permute-done.5.dy_ref, ...), custom_call_target="tpu_custom_call" | custom-call | flops 14495514624 | bytes 26738688 | tf_op jit(solution)/shard_map/experts/pallas_call | solution.py:285
  376.0 26.7 %experts.4 = (f32[512,1536]{1,0:T(8,128)}, f32[512,1536]{1,0:T(8,128)}, bf16[512,1536]{1,0:T(8,128)(2,1)}, bf16[512,1536]{1,0:T(8,128)(2,1)}, bf16[512,1536]{1,0:T(8,128)(2,1)}) custom-call(bf16[512,1536]{1,0:T(8,128)(2,1)} %multiply_convert_fusion.x_ref, bf16[512,1536]{1,0:T(8,128)(2,1)} %convolution_convert_fusion.7.dy_ref, ...), custom_call_target="tpu_custom_call" | custom-call | flops 14495514624 | bytes 26738688 | tf_op jit(solution)/shard_map/experts/pallas_call | solution.py:285
  402.7 28.2 %experts.5 = (f32[512,1536]{1,0:T(8,128)}, f32[512,1536]{1,0:T(8,128)}, bf16[512,1536]{1,0:T(8,128)(2,1)}, bf16[512,1536]{1,0:T(8,128)(2,1)}, bf16[512,1536]{1,0:T(8,128)(2,1)}) custom-call(bf16[512,1536]{1,0:T(8,128)(2,1)} %multiply_convert_fusion.x_ref, bf16[512,1536]{1,0:T(8,128)(2,1)} %convolution_convert_fusion.7.dy_ref, ...), custom_call_target="tpu_custom_call" | custom-call | flops 14495514624 | bytes 26738688 | tf_op jit(solution)/shard_map/experts/pallas_call | solution.py:285
  440.6 37.7 %attend_back.1 = (bf16[512,1536]{1,0:T(8,128)(2,1)}, bf16[512,512]{1,0:T(8,128)(2,1)}, bf16[512,512]{1,0:T(8,128)(2,1)}, f32[512,512]{1,0:T(8,128)}) custom-call(s32[1]{0:T(128)} %bitcast.2.z_ref, s32[512,1]{1,0:T(8,128)} %copy.116.start_ref, bf16[512,1536]{1,0:T(8,128)(2,1)} %project.2.q_ref, bf16[512,1536]{1,0:T(8,128)(2,1)} %get-tuple-element.36.o_ref, ...), custom_call_target="tpu_custom_call" | custom-call | flops 12079595520 | bytes 9437184 | tf_op jit(solution)/shard_map/attend_back/pallas_call | solution.py:209
  481.0 20.6 %collective-permute-done.10 = bf16[512,512]{1,0:T(8,128)(2,1)S(1)} collective-permute-done((bf16[512,512]{1,0:T(8,128)(2,1)}, bf16[512,512]{1,0:T(8,128)(2,1)S(1)}, u32[]{:S(2)}, u32[]{:S(2)}) %collective-permute-start.10) | collective-permute-done | bytes 524320 | tf_op jit(solution)/shard_map/ppermute | solution.py:349
  530.0 6.7 convolution_convert_fusion.1
  547.7 8.5 fusion.46
  556.2 12.5 %reduce-scatter.34.cloned.1.call-done = bf16[192,640]{1,0:T(8,128)(2,1)} async-done(((bf16[1536,640]{1,0:T(8,128)(2,1)}), bf16[192,640]{1,0:T(8,128)(2,1)}) %reduce-scatter.34.cloned.1.call-update) | async-done | bytes 245776
  571.0 9.4 add_convert_fusion
  591.7 7.2 convolution_convert_fusion
  624.7 34.7 %collective-permute-done.7 = bf16[512,1536]{1,0:T(8,128)(2,1)S(1)} collective-permute-done((bf16[512,1536]{1,0:T(8,128)(2,1)S(1)}, bf16[512,1536]{1,0:T(8,128)(2,1)S(1)}, u32[]{:S(2)}, u32[]{:S(2)}) %collective-permute-start.7) | collective-permute-done | bytes 1572896 | tf_op jit(solution)/shard_map/ppermute | solution.py:349
  671.8 21.8 %all-to-all-done.2 = bf16[8,64,1536]{2,1,0:T(8,128)(2,1)} async-done(((bf16[8,64,1536]{2,1,0:T(8,128)(2,1)}), bf16[8,64,1536]{2,1,0:T(8,128)(2,1)}, u32[]{:S(2)}, u32[]{:S(2)}) %all-to-all-start.2) | async-done | bytes 1572896 | tf_op jit(solution)/shard_map/all_to_all | solution.py:355
  706.3 12.0 %all-to-all-done.3 = bf16[8,64,1536]{2,1,0:T(8,128)(2,1)S(1)} async-done(((bf16[8,64,1536]{2,1,0:T(8,128)(2,1)}), bf16[8,64,1536]{2,1,0:T(8,128)(2,1)S(1)}, u32[]{:S(2)}, u32[]{:S(2)}) %all-to-all-start.3) | async-done | bytes 1572896 | tf_op jit(solution)/shard_map/all_to_all | solution.py:355
  720.5 31.3 %reduce-scatter.28.cloned.1.call-done = bf16[192,1536]{1,0:T(8,128)(2,1)} async-done(((bf16[1536,1536]{1,0:T(8,128)(2,1)}), bf16[192,1536]{1,0:T(8,128)(2,1)}) %reduce-scatter.28.cloned.1.call-update) | async-done | bytes 589840 | tf_op jit(solution)/shard_map/reduce_scatter | solution.py:496
  754.1 52.2 %all-reduce.3.cloned.1.call-done = bf16[192,640]{0,1:T(8,128)(2,1)} async-done(((bf16[192,640]{0,1:T(8,128)(2,1)}), bf16[192,640]{0,1:T(8,128)(2,1)}) %all-reduce.3.cloned.1.call-update) | async-done | bytes 245776 | tf_op jit(solution)/shard_map/psum | solution.py:561
  809.6 53.7 %reduce-scatter.32.cloned.1.call-done = bf16[192,1536]{1,0:T(8,128)(2,1)} async-done(((bf16[1536,1536]{1,0:T(8,128)(2,1)}), bf16[192,1536]{1,0:T(8,128)(2,1)}) %reduce-scatter.32.cloned.1.call-update) | async-done | bytes 589840 | tf_op jit(solution)/shard_map/reduce_scatter | solution.py:496
  865.7 55.3 %reduce-scatter.22.cloned.1.call-done = bf16[192,1536]{1,0:T(8,128)(2,1)} async-done(((bf16[1536,1536]{1,0:T(8,128)(2,1)}), bf16[192,1536]{1,0:T(8,128)(2,1)}) %reduce-scatter.22.cloned.1.call-update) | async-done | bytes 589840 | tf_op jit(solution)/shard_map/reduce_scatter | solution.py:496
  924.4 53.9 %reduce-scatter.18.cloned.1.call-done = bf16[192,1536]{1,0:T(8,128)(2,1)} async-done(((bf16[1536,1536]{1,0:T(8,128)(2,1)}), bf16[192,1536]{1,0:T(8,128)(2,1)}) %reduce-scatter.18.cloned.1.call-update) | async-done | bytes 589840 | tf_op jit(solution)/shard_map/reduce_scatter | solution.py:496
  980.3 55.7 %reduce-scatter.26.cloned.1.call-done = bf16[192,1536]{1,0:T(8,128)(2,1)} async-done(((bf16[1536,1536]{1,0:T(8,128)(2,1)}), bf16[192,1536]{1,0:T(8,128)(2,1)}) %reduce-scatter.26.cloned.1.call-update) | async-done | bytes 589840 | tf_op jit(solution)/shard_map/reduce_scatter | solution.py:496
  1039.5 53.7 %reduce-scatter.30.cloned.1.call-done = bf16[192,1536]{1,0:T(8,128)(2,1)} async-done(((bf16[1536,1536]{1,0:T(8,128)(2,1)}), bf16[192,1536]{1,0:T(8,128)(2,1)}) %reduce-scatter.30.cloned.1.call-update) | async-done | bytes 589840 | tf_op jit(solution)/shard_map/reduce_scatter | solution.py:496
  1096.4 21.0 %reduce-scatter.16.cloned.1.call-done = bf16[1,192,384]{2,1,0:T(8,128)(2,1)} async-done(((bf16[4,192,384]{2,1,0:T(8,128)(2,1)}), bf16[1,192,384]{2,1,0:T(8,128)(2,1)}) %reduce-scatter.16.cloned.1.call-update) | async-done | bytes 147472 | tf_op jit(solution)/shard_map/reduce_scatter | solution.py:548
  1119.1 20.9 %reduce-scatter.20.cloned.1.call-done = bf16[1,192,384]{2,1,0:T(8,128)(2,1)} async-done(((bf16[4,192,384]{2,1,0:T(8,128)(2,1)}), bf16[1,192,384]{2,1,0:T(8,128)(2,1)}) %reduce-scatter.20.cloned.1.call-update) | async-done | bytes 147472 | tf_op jit(solution)/shard_map/reduce_scatter | solution.py:548
  (250 shorter events, 251.7 us)
Async XLA Ops:
  7.2 184.0 %all-gather.6.cloned.1.call-start = ((), (), s32[]{:S(2)}) async-start(), calls=%async_computation.15 | async-start | bytes 5308416 | tf_op jit(solution)/shard_map/all_gather | solution.py:408
  26.7 173.6 %all-gather.8.cloned.1.call-start = ((), (), s32[]{:S(2)}) async-start(), calls=%async_computation.16 | async-start | bytes 5308416 | tf_op jit(solution)/shard_map/all_gather | solution.py:408
  45.2 290.6 %all-gather.10.cloned.1.call-start = ((), (), s32[]{:S(2)}) async-start(), calls=%async_computation.17 | async-start | bytes 10616832 | tf_op jit(solution)/shard_map/all_gather | solution.py:408
  49.9 47.8 %collective-permute-start.2 = (bf16[192,3072]{1,0:T(8,128)(2,1)S(1)}, bf16[192,3072]{1,0:T(8,128)(2,1)S(1)}, u32[]{:S(2)}, u32[]{:S(2)}) collective-permute-start(bf16[192,3072]{1,0:T(8,128)(2,1)S(1)} %pad_maximum_fusion), channel_id=1, source_target_pairs={{0,2},{1,3},{2,0},{3,1},{4,6},{5,7},{6,4},{7,5},{8,10},{9,11},{10,... | collective-permute-start | bytes 3538952 | tf_op jit(solution)/shard_map/ppermute | solution.py:349
  107.9 39.5 %all-to-all-start = ((bf16[8,64,1664]{2,1,0:T(8,128)(2,1)}), bf16[8,64,1664]{2,1,0:T(8,128)(2,1)}, u32[]{:S(2)}, u32[]{:S(2)}) async-start(bf16[8,64,1664]{2,1,0:T(8,128)(2,1)} %bitcast), calls=%async_computation | async-start | bytes 3407872 | tf_op jit(solution)/shard_map/all_to_all | solution.py:355
  112.4 231.4 %all-gather.12.cloned.1.call-start = ((), (), s32[]{:S(2)}) async-start(), calls=%async_computation.18 | async-start | bytes 5308416 | tf_op jit(solution)/shard_map/all_gather | solution.py:408
  114.3 28.4 %collective-permute-start.3 = (bf16[192,1536]{1,0:T(8,128)(2,1)}, bf16[192,1536]{1,0:T(8,128)(2,1)S(1)}, u32[]{:S(2)}, u32[]{:S(2)}) collective-permute-start(bf16[192,1536]{1,0:T(8,128)(2,1)} %constant_dynamic-slice_fusion), channel_id=1, source_target_pairs={{0,2},{1,3},{2,0},{3,1},{4,6},{5,7},{6,4},{7,5},{8,10},{9,11},{10,... | collective-permute-start | bytes 1769480 | tf_op jit(solution)/shard_map/ppermute | solution.py:349
  147.4 41.6 %all-to-all-start.1 = ((bf16[8,64,1536]{2,1,0:T(8,128)(2,1)}), bf16[8,64,1536]{2,1,0:T(8,128)(2,1)S(1)}, u32[]{:S(2)}, u32[]{:S(2)}) async-start(bf16[8,64,1536]{2,1,0:T(8,128)(2,1)} %bitcast.10), calls=%async_computation.1 | async-start | bytes 3145728 | tf_op jit(solution)/shard_map/all_to_all | solution.py:355
  151.0 417.7 %reduce-scatter.34.cloned.1.call-start = ((), (), s32[]{:S(2)}) async-start(), calls=%async_computation.30 | async-start | bytes 2211840
  161.9 51.2 %collective-permute-start = (bf16[512,512]{1,0:T(8,128)(2,1)}, bf16[512,512]{1,0:T(8,128)(2,1)S(1)}, u32[]{:S(2)}, u32[]{:S(2)}) collective-permute-start(bf16[512,512]{1,0:T(8,128)(2,1)} %project.3.kv2_ref), channel_id=1, source_target_pairs={{0,2},{1,3},{4,6},{5,7},{8,10},{9,11},{12,14},{13,15},{16,18},{17,... | collective-permute-start | bytes 1572872 | tf_op jit(solution)/shard_map/ppermute | solution.py:349
  163.2 49.9 %collective-permute-start.1 = (bf16[512,512]{1,0:T(8,128)(2,1)}, bf16[512,512]{1,0:T(8,128)(2,1)S(1)}, u32[]{:S(2)}, u32[]{:S(2)}) collective-permute-start(bf16[512,512]{1,0:T(8,128)(2,1)} %project.3.kv2_ref), channel_id=1, source_target_pairs={{0,1},{1,2},{2,3},{4,5},{5,6},{6,7},{8,9},{9,10},{10,11},{12,13},{... | collective-permute-start | bytes 1572872 | tf_op jit(solution)/shard_map/ppermute | solution.py:349
  191.2 118.2 %collective-permute-start.5 = (bf16[512,1536]{1,0:T(8,128)(2,1)}, bf16[512,1536]{1,0:T(8,128)(2,1)}, u32[]{:S(2)}, u32[]{:S(2)}) collective-permute-start(bf16[512,1536]{1,0:T(8,128)(2,1)} %convolution_convert_fusion.7.dy_ref), channel_id=1, source_target_pairs={{0,1},{1,0},{2,3},{3,2},{4,5},{5,4},{6,7},{7,6},{8,9},{9,8},{10,11... | collective-permute-start | bytes 4718600 | tf_op jit(solution)/shard_map/ppermute | solution.py:349
  249.5 59.9 %collective-permute-start.4 = (bf16[512,1536]{1,0:T(8,128)(2,1)}, bf16[512,1536]{1,0:T(8,128)(2,1)}, u32[]{:S(2)}, u32[]{:S(2)}) collective-permute-start(bf16[512,1536]{1,0:T(8,128)(2,1)} %multiply_convert_fusion.x_ref), channel_id=1, source_target_pairs={{0,1},{1,0},{2,3},{3,2},{4,5},{5,4},{6,7},{7,6},{8,9},{9,8},{10,11... | collective-permute-start | bytes 4718600 | tf_op jit(solution)/shard_map/ppermute | solution.py:349
  373.9 57.0 %collective-permute-start.8 = (bf16[512,1536]{1,0:T(8,128)(2,1)S(1)}, bf16[512,1536]{1,0:T(8,128)(2,1)S(1)}, u32[]{:S(2)}, u32[]{:S(2)}) collective-permute-start(bf16[512,1536]{1,0:T(8,128)(2,1)S(1)} %convert_element_type.237), channel_id=1, source_target_pairs={{0,1},{1,0},{2,3},{3,2},{4,5},{5,4},{6,7},{7,6},{8,9},{9,8},{10,11... | collective-permute-start | bytes 4718600 | tf_op jit(solution)/shard_map/ppermute | solution.py:349
  478.3 23.3 %collective-permute-start.10 = (bf16[512,512]{1,0:T(8,128)(2,1)}, bf16[512,512]{1,0:T(8,128)(2,1)S(1)}, u32[]{:S(2)}, u32[]{:S(2)}) collective-permute-start(bf16[512,512]{1,0:T(8,128)(2,1)} %get-tuple-element.49), channel_id=1, source_target_pairs={{2,0},{3,1},{6,4},{7,5},{10,8},{11,9},{14,12},{15,13},{18,16},{19,... | collective-permute-start | bytes 1572872 | tf_op jit(solution)/shard_map/ppermute | solution.py:349
  519.0 178.4 %reduce-scatter.24.cloned.1.call-start = ((), (), s32[]{:S(2)}) async-start(), calls=%async_computation.25 | async-start | bytes 5308416 | tf_op jit(solution)/shard_map/reduce_scatter | solution.py:496
  529.9 170.1 %reduce-scatter.14.cloned.1.call-start = ((), (), s32[]{:S(2)}) async-start(), calls=%async_computation.20 | async-start | bytes 5308416 | tf_op jit(solution)/shard_map/reduce_scatter | solution.py:496
  536.7 215.0 %reduce-scatter.28.cloned.1.call-start = ((), (), s32[]{:S(2)}) async-start(), calls=%async_computation.27 | async-start | bytes 5308416 | tf_op jit(solution)/shard_map/reduce_scatter | solution.py:496
  547.6 258.7 %all-reduce.3.cloned.1.call-start = ((), (), s32[]{:S(2)}) async-start(), calls=%async_computation.19 | async-start | bytes 655360 | tf_op jit(solution)/shard_map/psum | solution.py:561
  570.5 292.8 %reduce-scatter.32.cloned.1.call-start = ((), (), s32[]{:S(2)}) async-start(), calls=%async_computation.29 | async-start | bytes 5308416 | tf_op jit(solution)/shard_map/reduce_scatter | solution.py:496
  580.5 340.6 %reduce-scatter.22.cloned.1.call-start = ((), (), s32[]{:S(2)}) async-start(), calls=%async_computation.24 | async-start | bytes 5308416 | tf_op jit(solution)/shard_map/reduce_scatter | solution.py:496
  591.6 386.7 %reduce-scatter.18.cloned.1.call-start = ((), (), s32[]{:S(2)}) async-start(), calls=%async_computation.22 | async-start | bytes 5308416 | tf_op jit(solution)/shard_map/reduce_scatter | solution.py:496
  598.9 437.2 %reduce-scatter.26.cloned.1.call-start = ((), (), s32[]{:S(2)}) async-start(), calls=%async_computation.26 | async-start | bytes 5308416 | tf_op jit(solution)/shard_map/reduce_scatter | solution.py:496
  609.8 483.4 %reduce-scatter.30.cloned.1.call-start = ((), (), s32[]{:S(2)}) async-start(), calls=%async_computation.28 | async-start | bytes 5308416 | tf_op jit(solution)/shard_map/reduce_scatter | solution.py:496
  623.1 36.2 %collective-permute-start.7 = (bf16[512,1536]{1,0:T(8,128)(2,1)S(1)}, bf16[512,1536]{1,0:T(8,128)(2,1)S(1)}, u32[]{:S(2)}, u32[]{:S(2)}) collective-permute-start(bf16[512,1536]{1,0:T(8,128)(2,1)S(1)} %convert_element_type.231), channel_id=1, source_target_pairs={{0,1},{1,0},{2,3},{3,2},{4,5},{5,4},{6,7},{7,6},{8,9},{9,8},{10,11... | collective-permute-start | bytes 4718600 | tf_op jit(solution)/shard_map/ppermute | solution.py:349
  661.7 31.9 %all-to-all-start.2 = ((bf16[8,64,1536]{2,1,0:T(8,128)(2,1)}), bf16[8,64,1536]{2,1,0:T(8,128)(2,1)}, u32[]{:S(2)}, u32[]{:S(2)}) async-start(bf16[8,64,1536]{2,1,0:T(8,128)(2,1)} %bitcast.112), calls=%async_computation.2 | async-start | bytes 3145728 | tf_op jit(solution)/shard_map/all_to_all | solution.py:355
  693.6 24.7 %all-to-all-start.3 = ((bf16[8,64,1536]{2,1,0:T(8,128)(2,1)}), bf16[8,64,1536]{2,1,0:T(8,128)(2,1)S(1)}, u32[]{:S(2)}, u32[]{:S(2)}) async-start(bf16[8,64,1536]{2,1,0:T(8,128)(2,1)} %bitcast.115), calls=%async_computation.3 | async-start | bytes 3145728 | tf_op jit(solution)/shard_map/all_to_all | solution.py:355
  697.3 420.1 %reduce-scatter.16.cloned.1.call-start = ((), (), s32[]{:S(2)}) async-start(), calls=%async_computation.21 | async-start | bytes 737280 | tf_op jit(solution)/shard_map/reduce_scatter | solution.py:548
  697.4 223.7 %collective-permute-start.11 = (bf16[192,1536]{1,0:T(8,128)(2,1)}, bf16[192,1536]{1,0:T(8,128)(2,1)S(1)}, u32[]{:S(2)}, u32[]{:S(2)}) collective-permute-start(bf16[192,1536]{1,0:T(8,128)(2,1)} %reduce-scatter.24.cloned.1.call-done), channel_id=1, source_target_pairs={{0,2},{1,3},{2,0},{3,1},{4,6},{5,7},{6,4},{7,5},{8,10},{9,11},{10,... | collective-permute-start | bytes 1769480 | tf_op jit(solution)/shard_map/ppermute | solution.py:349
  702.1 437.9 %reduce-scatter.20.cloned.1.call-start = ((), (), s32[]{:S(2)}) async-start(), calls=%async_computation.23 | async-start | bytes 737280 | tf_op jit(solution)/shard_map/reduce_scatter | solution.py:548
  751.7 284.3 %collective-permute-start.12 = (bf16[192,1536]{1,0:T(8,128)(2,1)}, bf16[192,1536]{1,0:T(8,128)(2,1)}, u32[]{:S(2)}, u32[]{:S(2)}) collective-permute-start(bf16[192,1536]{1,0:T(8,128)(2,1)} %reduce-scatter.28.cloned.1.call-done), channel_id=1, source_target_pairs={{0,2},{1,3},{2,0},{3,1},{4,6},{5,7},{6,4},{7,5},{8,10},{9,11},{10,... | collective-permute-start | bytes 1769480 | tf_op jit(solution)/shard_map/ppermute | solution.py:349
  863.3 230.0 %collective-permute-start.13 = (bf16[192,1536]{1,0:T(8,128)(2,1)}, bf16[192,1536]{1,0:T(8,128)(2,1)}, u32[]{:S(2)}, u32[]{:S(2)}) collective-permute-start(bf16[192,1536]{1,0:T(8,128)(2,1)} %reduce-scatter.32.cloned.1.call-done), channel_id=1, source_target_pairs={{0,2},{1,3},{2,0},{3,1},{4,6},{5,7},{6,4},{7,5},{8,10},{9,11},{10,... | collective-permute-start | bytes 1769480 | tf_op jit(solution)/shard_map/ppermute | solution.py:349
  (38 other events, 631.0 us)
Sparse Core Ops, SparseCore 0:
  26.9 40.6 all-gather.5
  69.5 38.9 all-gather.7
  110.3 86.4 all-gather.9
  198.5 37.9 all-gather.11
  519.1 49.5 reduce-scatter.33
  572.4 53.8 reduce-scatter.23
  629.7 60.2 reduce-scatter.13
  693.8 57.8 reduce-scatter.27
  754.7 51.6 all-reduce.2
  809.6 53.6 reduce-scatter.31
  867.1 53.8 reduce-scatter.21
  924.4 53.8 reduce-scatter.17
  982.1 53.8 reduce-scatter.25
  1039.3 53.8 reduce-scatter.29
  1095.5 21.8 reduce-scatter.15
  1119.7 20.2 reduce-scatter.19

commit v2 on v1

--- a/solution.py
+++ b/solution.py
@@ -4,6 +4,7 @@
 import jax.numpy as jnp
 from jax import lax
 from jax.experimental import pallas as pl
+from jax.experimental.layout import Layout, with_layout_constraint
 from jax.experimental.pallas import tpu as pltpu
 from jax.sharding import PartitionSpec as P
 
@@ -37,39 +38,171 @@
     return pltpu.roll(u, HD // 2, 1)
 
 
-def project_kernel(rotated, x_ref, w_ref, cos_ref, sin_ref, out_ref):
-    step = pl.program_id(0)
+def keyval_kernel(
+    x_ref,
+    w_ref,
+    cos_ref,
+    sin_ref,
+    count_ref,
+    mark_ref,
+    deal_ref,
+    kv_ref,
+    one_ref,
+    two_ref,
+    counts_ref,
+    near_ref,
+    dealt_ref,
+    send,
+    recv,
+    deal_send,
+    deal_recv,
+):
+    z = lax.axis_index("tensor")
+    d = lax.axis_index("dp")
+    d_count = deal_ref.shape[0]
+    z_count = counts_ref.shape[0]
+    others = [{"tensor": (z + m) % z_count} for m in range(1, z_count)]
+    barrier = pltpu.get_barrier_semaphore()
+    peers = [{"dp": (d + p) % d_count} for p in range(1, d_count)]
+    for other in others + peers:
+        pl.semaphore_signal(barrier, inc=1, device_id=other, device_id_type=pl.DeviceIdType.MESH)
     raw = mm(x_ref[...], w_ref[...])
-    halves = []
+    turned = raw.shape[1] // 2
+    for i in range(turned // HD):
+        u = raw[:, i * HD : (i + 1) * HD]
+        u = u * cos_ref[...] + swap_halves(u) * sin_ref[...]
+        kv_ref[:, i * HD : (i + 1) * HD] = u.astype(BF16)
+    kv_ref[:, turned:] = raw[:, turned:].astype(BF16)
+    pl.semaphore_wait(barrier, z_count - 1 + d_count - 1)
+    moves = [(count_ref, counts_ref.at[m], others[m]) for m in range(z_count - 1)]
+    moves += [(mark_ref, near_ref, {"tensor": flip(z, 1)})]
+    moves += [(kv_ref, one_ref, others[0]), (kv_ref, two_ref, others[1])]
+    copies = []
+    for at, (src, dst, to) in enumerate(moves):
+        copy = pltpu.make_async_remote_copy(
+            src_ref=src,
+            dst_ref=dst,
+            send_sem=send.at[at],
+            recv_sem=recv.at[at],
+            device_id=to,
+            device_id_type=pl.DeviceIdType.MESH,
+        )
+        copy.start()
+        copies.append(copy)
+    for p, peer in enumerate(peers):
+        copy = pltpu.make_async_remote_copy(
+            src_ref=deal_ref.at[(d + p + 1) % d_count],
+            dst_ref=dealt_ref.at[d],
+            send_sem=deal_send.at[p],
+            recv_sem=deal_recv.at[p],
+            device_id=peer,
+            device_id_type=pl.DeviceIdType.MESH,
+        )
+        copy.start()
+        copies.append(copy)
+    counts_ref[z_count - 1] = count_ref[...]
+    dealt_ref[d] = deal_ref[d]
+    for copy in copies:
+        copy.wait()
+
+
+def keyval(x, w, cos_full, sin_full, counts, marks, deals, z_count):
+    rows = x.shape[0]
+    columns = w.shape[1]
+    vmem = pl.BlockSpec(memory_space=pltpu.VMEM)
+    block = jax.ShapeDtypeStruct((rows, columns), BF16)
+    return pl.pallas_call(
+        keyval_kernel,
+        in_specs=[vmem] * 7,
+        out_specs=[vmem] * 6,
+        out_shape=[block] * 3
+        + [
+            jax.ShapeDtypeStruct((z_count, *counts.shape), counts.dtype),
+            jax.ShapeDtypeStruct(marks.shape, marks.dtype),
+            jax.ShapeDtypeStruct(deals.shape, deals.dtype),
+        ],
+        scratch_shapes=[
+            pltpu.SemaphoreType.DMA((z_count + 2,)),
+            pltpu.SemaphoreType.DMA((z_count + 2,)),
+            pltpu.SemaphoreType.DMA((deals.shape[0] - 1,)),
+            pltpu.SemaphoreType.DMA((deals.shape[0] - 1,)),
+        ],
+        compiler_params=pltpu.CompilerParams(
+            vmem_limit_bytes=40 * 2**20, collective_id=1, has_side_effects=True
+        ),
+        name="keyval",
+    )(x, w, cos_full, sin_full, counts, marks, deals)
+
+
+def project_query_kernel(x_ref, w_ref, cos_ref, sin_ref, out_ref):
+    raw = mm(x_ref[...], w_ref[...].reshape(x_ref.shape[1], out_ref.shape[1]))
     for i in range(raw.shape[1] // HD):
         u = raw[:, i * HD : (i + 1) * HD]
         turned = u * cos_ref[...] + swap_halves(u) * sin_ref[...]
-        halves.append(jnp.where(step < rotated, turned, u))
-    out_ref[...] = jnp.concatenate(halves, axis=1).astype(BF16)
-
-
-def project(x, w, cos_full, sin_full, rotated):
+        out_ref[:, i * HD : (i + 1) * HD] = turned.astype(BF16)
+
+
+def project_query(x, w, cos_full, sin_full):
     rows, width = x.shape
-    columns = w.shape[1]
+    pieces, blocks, piece, columns = w.shape
     return pl.pallas_call(
-        functools.partial(project_kernel, rotated),
-        grid=(columns // 256,),
+        project_query_kernel,
+        grid=(blocks,),
         in_specs=[
             pl.BlockSpec((rows, width), lambda i: (0, 0)),
-            pl.BlockSpec((width, 256), lambda i: (0, i)),
+            pl.BlockSpec((pieces, 1, piece, columns), lambda i: (0, i, 0, 0)),
             pl.BlockSpec((rows, HD), lambda i: (0, 0)),
             pl.BlockSpec((rows, HD), lambda i: (0, 0)),
         ],
-        out_specs=pl.BlockSpec((rows, 256), lambda i: (0, i)),
-        out_shape=jax.ShapeDtypeStruct((rows, columns), BF16),
+        out_specs=pl.BlockSpec((rows, columns), lambda i: (0, i)),
+        out_shape=jax.ShapeDtypeStruct((rows, blocks * columns), BF16),
         compiler_params=params(),
-        name="project",
+        name="project_query",
         cost_estimate=pl.CostEstimate(
-            flops=2 * rows * width * columns,
-            bytes_accessed=2 * (rows * width + width * columns + rows * columns),
+            flops=2 * rows * width * blocks * columns,
+            bytes_accessed=2 * (2 * rows * width + width * blocks * columns),
             transcendentals=0,
         ),
     )(x, w, cos_full, sin_full)
+
+
+def project_back_kernel(dq_ref, w_ref, dkv_ref, wkv_ref, out_ref):
+    step = pl.program_id(0)
+    width = out_ref.shape[1]
+    part = mm_nt(dq_ref[...], w_ref[...].reshape(width, dq_ref.shape[1]))
+
+    @pl.when(step == 0)
+    def _():
+        out_ref[...] = part + mm_nt(dkv_ref[...], wkv_ref[...])
+
+    @pl.when(step > 0)
+    def _():
+        out_ref[...] += part
+
+
+def project_back(dq, w, dkv, wkv):
+    rows = dq.shape[0]
+    pieces, blocks, piece, columns = w.shape
+    width = pieces * piece
+    return pl.pallas_call(
+        project_back_kernel,
+        grid=(blocks,),
+        in_specs=[
+            pl.BlockSpec((rows, columns), lambda i: (0, i)),
+            pl.BlockSpec((pieces, 1, piece, columns), lambda i: (0, i, 0, 0)),
+            pl.BlockSpec(dkv.shape, lambda i: (0, 0)),
+            pl.BlockSpec(wkv.shape, lambda i: (0, 0)),
+        ],
+        out_specs=pl.BlockSpec((rows, width), lambda i: (0, 0)),
+        out_shape=jax.ShapeDtypeStruct((rows, width), F32),
+        compiler_params=params(),
+        name="project_back",
+        cost_estimate=pl.CostEstimate(
+            flops=2 * rows * width * (blocks * columns + dkv.shape[1]),
+            bytes_accessed=2 * width * (3 * rows + blocks * columns),
+            transcendentals=0,
+        ),
+    )(dq, w, dkv, wkv)
 
 
 def make_bias(z_ref, start_ref, bias_ref):
@@ -243,11 +376,8 @@
     )(z, start, q, o, do, lse, cos_full, sin_full, *kvs)
 
 
-def expert_kernel(first, x_ref, dy_ref, gate_ref, wg_ref, wu_ref, wd_ref, *refs):
-    if first:
-        y_ref, dn_ref, hs_ref, dg_ref, du_ref = refs
-    else:
-        y0_ref, dn0_ref, y_ref, dn_ref, hs_ref, dg_ref, du_ref = refs
+def expert_kernel(chunk, first, x_ref, dy_ref, gate_ref, wg_ref, wu_ref, wd_ref, *refs):
+    y_ref, dn_ref, hs_ref, dgu_ref = refs[-4:]
     step = pl.program_id(0)
 
     @pl.when(step == 0)
@@ -256,8 +386,8 @@
             y_ref[...] = jnp.zeros_like(y_ref)
             dn_ref[...] = jnp.zeros_like(dn_ref)
         else:
-            y_ref[...] = y0_ref[...]
-            dn_ref[...] = dn0_ref[...]
+            y_ref[...] = refs[0][...]
+            dn_ref[...] = refs[1][...]
 
     x = x_ref[...]
     gate = gate_ref[...].astype(F32)
@@ -269,37 +399,51 @@
     dh = mm_nt(dy_ref[...], wd_ref[...]) * gate
     dg = (dh * u * (2.0 * g)).astype(BF16)
     du = (dh * square).astype(BF16)
-    dg_ref[...] = dg
-    du_ref[...] = du
+    dgu_ref[:, :chunk] = dg
+    dgu_ref[:, chunk:] = du
     dn_ref[...] += mm_nt(dg, wg_ref[...]) + mm_nt(du, wu_ref[...])
     y_ref[...] += mm(hs, wd_ref[...])
 
 
-def experts(x, dy, gate, wg, wu, wd, before=None, chunk=256):
+def experts(tile, x, dy, gate, wg, wu, wd, before=None, filled=None, up_at=0, chunk=512):
     rows, width = x.shape
     hidden = gate.shape[1]
     full = pl.BlockSpec((rows, width), lambda i: (0, 0))
     part = pl.BlockSpec((rows, chunk), lambda i: (0, i))
-    columns = pl.BlockSpec((width, chunk), lambda i: (0, i))
-    extra = () if before is None else tuple(before)
+    operands = [x, dy, gate, wg, wu, wd]
+    in_specs = [
+        full,
+        full,
+        part,
+        pl.BlockSpec((width, chunk), lambda i: (0, i)),
+        pl.BlockSpec((width, chunk), lambda i: (0, i + up_at)),
+        pl.BlockSpec((chunk, width), lambda i: (i, 0)),
+    ]
+    aliases = {}
+    if before is not None:
+        operands += list(before)
+        in_specs += [full] * 2
+    if filled is not None:
+        aliases = {len(operands): 2, len(operands) + 1: 3}
+        operands += list(filled)
+        in_specs += [pl.BlockSpec(memory_space=pl.ANY)] * 2
     return pl.pallas_call(
-        functools.partial(expert_kernel, before is None),
+        functools.partial(expert_kernel, chunk, before is None),
         grid=(hidden // chunk,),
-        in_specs=[
+        in_specs=in_specs,
+        out_specs=[
             full,
             full,
-            part,
-            columns,
-            columns,
-            pl.BlockSpec((chunk, width), lambda i: (i, 0)),
-            *[full] * len(extra),
-        ],
-        out_specs=[full, full, part, part, part],
+            pl.BlockSpec((rows, chunk), lambda i: (tile, i)),
+            pl.BlockSpec((rows, 2 * chunk), lambda i: (tile, i)),
+        ],
         out_shape=[
             jax.ShapeDtypeStruct((rows, width), F32),
             jax.ShapeDtypeStruct((rows, width), F32),
-            *[jax.ShapeDtypeStruct((rows, hidden), BF16)] * 3,
-        ],
+            jax.ShapeDtypeStruct((2 * rows, hidden), BF16),
+            jax.ShapeDtypeStruct((2 * rows, 2 * hidden), BF16),
+        ],
+        input_output_aliases=aliases,
         compiler_params=params(),
         name="experts",
         cost_estimate=pl.CostEstimate(
@@ -307,7 +451,313 @@
             bytes_accessed=6 * width * hidden + 16 * rows * width,
             transcendentals=0,
         ),
-    )(x, dy, gate, wg, wu, wd, *extra)
+    )(*operands)
+
+
+def gradient_kernel(jobs, lefts, rights, keep, *refs):
+    left_refs, right_refs, rest = refs[:lefts], refs[lefts : lefts + rights], refs[lefts + rights :]
+    step = pl.program_id(0)
+    each = len(jobs[0])
+    for i, (left, right, _) in enumerate(jobs[0] + jobs[1]):
+
+        @pl.when(step == i)
+        def _(i=i, left=left, right=right):
+            side = i // each
+            value = mm(left_refs[left][...], right_refs[right][...])
+            if keep:
+                value = value + rest[0][0].astype(F32)
+                half = value.shape[0] // 2
+                rest[1 + 2 * side][...] = value[:half].astype(BF16)
+                rest[2 + 2 * side][...] = value[half:].astype(BF16)
+            else:
+                rest[0][0] = value.astype(BF16)
+
+
+def pick(i, values):
+    result = values[0]
+    for at, value in enumerate(values):
+        if at and value != values[at - 1]:
+            result = jnp.where(i >= at, value, result)
+    return result
+
+
+def gradients(jobs, lefts, rights, got=None, chunk=768):
+    rows, tokens = lefts[0].shape
+    each = len(jobs[0])
+    first = lambda i: (0, jnp.minimum(i, each - 1))
+    second = lambda i: (0, jnp.maximum(i - each, 0))
+    whole = [pl.BlockSpec((1, rows, chunk), lambda i: (i // each, 0, i % each))]
+    if got is None:
+        out_specs = whole[0]
+        out_shape = jax.ShapeDtypeStruct((2, rows, each * chunk), BF16)
+    else:
+        out_specs = [pl.BlockSpec((rows // 2, chunk), at) for at in (first, first, second, second)]
+        out_shape = [jax.ShapeDtypeStruct((rows // 2, each * chunk), BF16)] * 4
+    right_specs = []
+    for r in range(len(rights)):
+        at, blocks = None, []
+        for _, right, block in jobs[0] + jobs[1]:
+            at = block if right == r else at
+            blocks.append(at)
+        known = next(block for block in blocks if block is not None)
+        blocks = tuple(known if block is None else block for block in blocks)
+        right_specs.append(
+            pl.BlockSpec((tokens, chunk), lambda i, blocks=blocks: (0, pick(i, blocks)))
+        )
+    return pl.pallas_call(
+        functools.partial(gradient_kernel, jobs, len(lefts), len(rights), got is not None),
+        grid=(2 * each,),
+        in_specs=[
+            *[pl.BlockSpec((rows, tokens), lambda i: (0, 0))] * len(lefts),
+            *right_specs,
+            *(() if got is None else whole),
+        ],
+        out_specs=out_specs,
+        out_shape=out_shape,
+        compiler_params=params(),
+        name="gradients",
+        cost_estimate=pl.CostEstimate(
+            flops=4 * each * rows * tokens * chunk,
+            bytes_accessed=4 * each * (rows + tokens) * chunk,
+            transcendentals=0,
+        ),
+    )(*lefts, *rights, *(() if got is None else (got,)))
+
+
+EXPERT_JOBS = (((0, 0, 0), (0, 0, 1), (1, 1, 0)), ((2, 0, 2), (2, 0, 3), (3, 1, 1)))
+ATTENTION_JOBS = (((0, 0, 0), (0, 0, 1)), ((1, 1, 0), (1, 1, 1)))
+
+
+def flip(index, mask):
+    for bit in (1, 2, 4):
+        if mask & bit:
+            index = index + bit - 2 * bit * (index // bit % 2)
+    return index
+
+
+def finish_kernel(
+    dx_ref,
+    q_keep,
+    q_send,
+    o_keep,
+    o_send,
+    s_send,
+    s_keep,
+    back_ref,
+    qo_ref,
+    s_ref,
+    q_got,
+    o_got,
+    q_half,
+    o_half,
+    q_last,
+    o_last,
+    s_got,
+    s_half,
+    s_got2,
+    s_quarter,
+    s_last,
+    z_mine,
+    z_got,
+    k_mine,
+    k_got,
+    deal_send,
+    deal_recv,
+    send,
+    recv,
+):
+    d = lax.axis_index("dp")
+    z = lax.axis_index("tensor")
+    count = dx_ref.shape[0]
+    z_count = z_mine.shape[0]
+    barrier = pltpu.get_barrier_semaphore()
+    for p in range(1, count):
+        pl.semaphore_signal(
+            barrier, inc=1, device_id={"dp": flip(d, p)}, device_id_type=pl.DeviceIdType.MESH
+        )
+    for m in range(1, z_count):
+        pl.semaphore_signal(
+            barrier, inc=1, device_id={"tensor": flip(z, m)}, device_id_type=pl.DeviceIdType.MESH
+        )
+    pl.semaphore_wait(barrier, count - 1 + z_count - 1)
+
+    def start(src, dst, at, to):
+        copy = pltpu.make_async_remote_copy(
+            src_ref=src,
+            dst_ref=dst,
+            send_sem=send.at[at],
+            recv_sem=recv.at[at],
+            device_id=to,
+            device_id_type=pl.DeviceIdType.MESH,
+        )
+        copy.start()
+        return copy
+
+    one, two, four = [{"dp": flip(d, bit)} for bit in (1, 2, 4)]
+    s_one = start(s_send, s_got, 0, one)
+    q_one = start(q_send, q_got, 1, two)
+    o_one = start(o_send, o_got, 2, four)
+    deals = []
+    for p in range(1, count):
+        copy = pltpu.make_async_remote_copy(
+            src_ref=dx_ref.at[flip(d, p)],
+            dst_ref=back_ref.at[d],
+            send_sem=deal_send.at[p - 1],
+            recv_sem=deal_recv.at[p - 1],
+            device_id={"dp": flip(d, p)},
+            device_id_type=pl.DeviceIdType.MESH,
+        )
+        copy.start()
+        deals.append(copy)
+    back_ref[d] = dx_ref[d]
+
+    rows = q_last.shape[0]
+    s_one.wait()
+    total = s_keep[...].astype(F32) + s_got[...].astype(F32)
+    s_keep2 = total[: 2 * rows]
+    s_half[...] = total[2 * rows :].astype(BF16)
+    s_two = start(s_half, s_got2, 3, four)
+    q_one.wait()
+    q_half[...] = (q_keep[rows:].astype(F32) + q_got[rows:].astype(F32)).astype(BF16)
+    q_two = start(q_half, q_last, 4, four)
+    o_one.wait()
+    o_half[...] = (o_keep[rows:].astype(F32) + o_got[rows:].astype(F32)).astype(BF16)
+    o_two = start(o_half, o_last, 5, two)
+    s_two.wait()
+    total = s_keep2 + s_got2[...].astype(F32)
+    s_quarter[...] = total[rows:].astype(BF16)
+    s_three = start(s_quarter, s_last, 6, two)
+    s_own = total[:rows]
+    s_three.wait()
+    s_own = s_own + s_last[...].astype(F32)
+    k_mine[...] = s_own.astype(BF16)
+    finals = [
+        start(k_mine, k_got.at[m - 1], 6 + m, {"tensor": flip(z, m)}) for m in range(1, z_count)
+    ]
+    part = qo_ref.shape[1] // 2
+    for two_copy, keep, got, last, side in (
+        (q_two, q_keep, q_got, q_last, 0),
+        (o_two, o_keep, o_got, o_last, 1),
+    ):
+        two_copy.wait()
+        total = (
+            keep[:rows].astype(F32) + got[:rows].astype(F32) + last[...].astype(F32)
+        )
+        for i in range(z_count):
+            block = total[:, i * part : (i + 1) * part]
+            z_mine[i, :, side * part : (side + 1) * part] = block.astype(BF16)
+    for m in range(1, z_count):
+        at = 5 + z_count + m
+        finals.append(start(z_mine.at[flip(z, m)], z_got.at[m - 1], at, {"tensor": flip(z, m)}))
+    for copy in finals[: z_count - 1]:
+        copy.wait()
+    for m in range(z_count - 1):
+        s_own = s_own + k_got[m].astype(F32)
+    s_ref[...] = s_own
+    for copy in finals[z_count - 1 :]:
+        copy.wait()
+    total = z_mine[z].astype(F32)
+    for m in range(z_count - 1):
+        total = total + z_got[m].astype(F32)
+    qo_ref[...] = total
+    for copy in deals:
+        copy.wait()
+
+
+def finish(dx, q_keep, q_send, o_keep, o_send, s_send, s_keep, z_count):
+    count = dx.shape[0]
+    rows = q_keep.shape[0] // 2
+    columns = q_keep.shape[1]
+    small = s_keep.shape[1]
+    part = columns // z_count
+    vmem = pl.BlockSpec(memory_space=pltpu.VMEM)
+    dma = pltpu.SemaphoreType.DMA
+    return pl.pallas_call(
+        finish_kernel,
+        in_specs=[vmem] * 7,
+        out_specs=[vmem] * 3,
+        out_shape=[
+            jax.ShapeDtypeStruct(dx.shape, BF16),
+            jax.ShapeDtypeStruct((rows, 2 * part), F32),
+            jax.ShapeDtypeStruct((rows, small), F32),
+        ],
+        scratch_shapes=[
+            pltpu.VMEM((2 * rows, columns), BF16),
+            pltpu.VMEM((2 * rows, columns), BF16),
+            pltpu.VMEM((rows, columns), BF16),
+            pltpu.VMEM((rows, columns), BF16),
+            pltpu.VMEM((rows, columns), BF16),
+            pltpu.VMEM((rows, columns), BF16),
+            pltpu.VMEM((4 * rows, small), BF16),
+            pltpu.VMEM((2 * rows, small), BF16),
+            pltpu.VMEM((2 * rows, small), BF16),
+            pltpu.VMEM((rows, small), BF16),
+            pltpu.VMEM((rows, small), BF16),
+            pltpu.VMEM((z_count, rows, 2 * part), BF16),
+            pltpu.VMEM((z_count - 1, rows, 2 * part), BF16),
+            pltpu.VMEM((rows, small), BF16),
+            pltpu.VMEM((z_count - 1, rows, small), BF16),
+            dma((count - 1,)),
+            dma((count - 1,)),
+            dma((7 + 2 * z_count,)),
+            dma((7 + 2 * z_count,)),
+        ],
+        compiler_params=pltpu.CompilerParams(
+            vmem_limit_bytes=56 * 2**20, collective_id=0, has_side_effects=True
+        ),
+        name="finish",
+    )(dx, q_keep, q_send, o_keep, o_send, s_send, s_keep)
+
+
+def turn_kernel(orders, d_ref, *refs):
+    tiles = len(refs) - 1 - len(orders)
+    scratch_ref = refs[-1]
+    step = pl.program_id(0)
+    for t in range(tiles):
+
+        @pl.when(step == t)
+        def _(t=t):
+            scratch_ref[...] = refs[t][...].T
+
+    for order, out_ref in zip(orders, refs[tiles:-1]):
+        size = out_ref.shape[0] // len(order)
+        for i, p in enumerate(order):
+            block = jnp.bitwise_xor(d_ref[0], p)
+            at = pl.multiple_of(block * size, size)
+            out_ref[i * size : (i + 1) * size, :] = scratch_ref[pl.ds(at, size), :]
+
+
+def turn(d, tiles, orders, blocks):
+    rows, width = tiles[0].shape
+    size = width // blocks
+    return pl.pallas_call(
+        functools.partial(turn_kernel, orders),
+        grid_spec=pltpu.PrefetchScalarGridSpec(
+            num_scalar_prefetch=1,
+            grid=(len(tiles),),
+            in_specs=[pl.BlockSpec((rows, width), lambda t, s: (0, 0))] * len(tiles),
+            out_specs=[
+                pl.BlockSpec((len(order) * size, rows), lambda t, s: (0, t)) for order in orders
+            ],
+            scratch_shapes=[pltpu.VMEM((width, rows), BF16)],
+        ),
+        out_shape=[
+            jax.ShapeDtypeStruct((len(order) * size, rows * len(tiles)), BF16) for order in orders
+        ],
+        compiler_params=params(),
+        name="turn",
+        cost_estimate=pl.CostEstimate(
+            flops=0, bytes_accessed=6 * rows * width * len(tiles), transcendentals=0
+        ),
+    )(d, *tiles)
+
+
+def tie(*values):
+    return lax.optimization_barrier(values)
+
+
+def row_major(x):
+    return with_layout_constraint(x, Layout(major_to_minor=tuple(range(x.ndim))))
 
 
 def per_device(
@@ -348,13 +798,28 @@
     def z_move(x, pairs):
         return lax.ppermute(x, "tensor", pairs)
 
-    near = [(i, i ^ 1) for i in range(tensor_count)]
-    far = [(i, i ^ 2) for i in range(tensor_count)]
+    def dp_move(x, bit):
+        return lax.ppermute(x, "dp", [(i, i ^ bit) for i in range(dp_count)])
+
+    near, far, across = [[(i, i ^ m) for i in range(tensor_count)] for m in (1, 2, 3)]
+    up_one, up_two = [[(i, i + m) for i in range(tensor_count - m)] for m in (1, 2)]
 
     def deal(x):
         return lax.all_to_all(
             x.reshape(dp_count, share, x.shape[1]), "dp", split_axis=0, concat_axis=0, tiled=True
         ).reshape(rows, x.shape[1])
+
+    def team_gather(x):
+        return lax.all_gather(x, "dp", axis=0, tiled=True, axis_index_groups=teams)
+
+    def flat(w):
+        return row_major(w.transpose(1, 0, 2).reshape(w.shape[1], hidden))
+
+    def z_gather(x):
+        parts = jnp.zeros((tensor_count, *x.shape), x.dtype)
+        for m, part in enumerate((x, z_move(x, near), z_move(x, far), z_move(x, across))):
+            parts = lax.dynamic_update_slice_in_dim(parts, part[None], z ^ m, 0)
+        return parts
 
     own_perm = lax.dynamic_slice_in_dim(perm, z * rows, rows, 0)
     own_routes = lax.dynamic_slice_in_dim(routes, z * rows, rows, 0)
@@ -377,62 +842,50 @@
         axis=1,
     )
     packed = mm(pack, jnp.concatenate([tokens, meta], axis=1)).astype(BF16)
+    packed, pack, w_query, w_out, w_gate, w_up, w_down = tie(
+        packed, pack, w_query, w_out, w_gate, w_up, w_down
+    )
     arrived = deal(packed)
     packed_dy = mm(pack, cotangent).astype(BF16)
-    arrived_dy = deal(packed_dy)
+    wg_own = flat(w_gate)
+    wq_piece = lax.dynamic_slice_in_dim(w_query, member * piece_rows, piece_rows, 0)
+    wq_z = z_gather(wq_piece)
+
+    out_rows = query_cols // team
+    wo_piece = lax.dynamic_slice_in_dim(w_out, member * out_rows, out_rows, 0)
+    wo_z = z_gather(wo_piece)
+    wd_own = w_down.reshape(hidden, width)
+    wu_own = flat(w_up)
+    gu_piece = jnp.concatenate(
+        [
+            lax.dynamic_slice_in_dim(w, member * piece_rows, piece_rows, 0)
+            for w in (wg_own, wu_own)
+        ],
+        axis=1,
+    )
+    hidden_piece = hidden // team
+    wd_piece = lax.dynamic_slice_in_dim(wd_own, member * hidden_piece, hidden_piece, 0)
+    gu_moved = z_move(gu_piece, far)
+    arrived, packed_dy, wq_z, wo_z, wg_own, wu_own, wd_piece = tie(
+        arrived, packed_dy, wq_z, wo_z, wg_own, wu_own, wd_piece
+    )
+    wq_all = team_gather(wq_z).reshape(team, tensor_count, piece_rows, query_cols)
+    wo_all = team_gather(wo_z).reshape(team, tensor_count, out_rows, width)
+    wo = wo_all.transpose(1, 0, 2, 3).reshape(tensor_count * query_cols, width)
+
     meta_in = arrived[:, width:].astype(F32)
     place_in = (meta_in[:, 0] * 16.0 + meta_in[:, 1]).astype(jnp.int32)
     unpack = (row_index[:, None] == place_in[None, :]).astype(BF16)
     dealt = mm(unpack, arrived)
     x_rows = dealt[:, :width]
     meta_rows = dealt[:, width:]
-    dy_rows = mm(unpack, arrived_dy).astype(BF16)
 
     expert_ids = jnp.arange(experts_n, dtype=jnp.int32).astype(F32)
     route_rows = meta_rows[:, 2 : 2 + top]
     gate_rows = meta_rows[:, 2 + top : 2 + 2 * top]
     hot = route_rows[:, :, None] == expert_ids[None, None, :]
     routed = jnp.sum(hot.astype(F32), axis=1)
-    counts = lax.all_gather(jnp.sum(routed, axis=0)[None, :], "tensor", axis=0, tiled=True)
-    z_ids = jnp.arange(tensor_count, dtype=jnp.int32)
-    base = jnp.sum(jnp.where(z_ids[:, None] < z, counts, 0.0), axis=0)
-    position = mm(lower, routed.astype(BF16)) + base[None, :]
-    weight = jnp.sum(jnp.where(hot, gate_rows[:, :, None], 0.0), axis=1)
-    weight = jnp.where(position < capacity, weight, 0.0).astype(BF16)
-    weight_near = z_move(weight, near)
-    gate_own = jnp.repeat(weight, part_hidden, axis=1)
-    gate_near = jnp.repeat(weight_near, part_hidden, axis=1)
-    dy_near = z_move(dy_rows, near)
-
-    def team_gather(x):
-        return lax.all_gather(x, "dp", axis=0, tiled=True, axis_index_groups=teams)
-
-    def flat(w):
-        return w.transpose(1, 0, 2).reshape(w.shape[1], hidden)
-
-    def piece(w):
-        return lax.dynamic_slice_in_dim(w, member * piece_rows, piece_rows, 1)
-
-    wq_piece = lax.dynamic_slice_in_dim(w_query, member * piece_rows, piece_rows, 0)
-    wq_piece = lax.all_gather(wq_piece, "tensor", axis=0, tiled=True)
-    wq_all = team_gather(wq_piece).reshape(team, tensor_count, piece_rows, query_cols)
-    wq = wq_all.transpose(0, 2, 1, 3).reshape(width, tensor_count * query_cols)
-    out_rows = query_cols // team
-    wo_piece = lax.dynamic_slice_in_dim(w_out, member * out_rows, out_rows, 0)
-    wo_piece = lax.all_gather(wo_piece, "tensor", axis=0, tiled=True)
-    wo_all = team_gather(wo_piece).reshape(team, tensor_count, out_rows, width)
-    wo = wo_all.transpose(1, 0, 2, 3).reshape(tensor_count * query_cols, width)
-
-    wd_own = w_down.reshape(hidden, width)
-    wg_own = flat(w_gate)
-    wu_own = flat(w_up)
-    gu_piece = jnp.concatenate([flat(piece(w_gate)), flat(piece(w_up))], axis=1)
-    hidden_piece = hidden // team
-    wd_piece = lax.dynamic_slice_in_dim(wd_own, member * hidden_piece, hidden_piece, 0)
-    gu_far = team_gather(z_move(gu_piece, far))
-    wd_far = team_gather(z_move(wd_piece, far))
-    wg_far = gu_far[:, :hidden]
-    wu_far = gu_far[:, hidden:]
+    counts = jnp.pad(jnp.sum(routed, axis=0)[None, :], ((0, 7), (0, HD - experts_n)))
 
     seq_lengths = lengths[0]
     seq_index = jnp.arange(seq_lengths.shape[0], dtype=jnp.int32)
@@ -454,54 +907,119 @@
 
     inv_one = lax.rsqrt(jnp.mean(x_rows * x_rows, axis=1, keepdims=True) + EPS)
     n1 = (x_rows * inv_one * gain_attn).astype(BF16)
-    kv = project(n1, w_keyval, cos_full, sin_full, 1)
-    up_one = [(i, i + 1) for i in range(tensor_count - 1)]
-    up_two = [(i, i + 2) for i in range(tensor_count - 2)]
-    kv_one = z_move(kv, up_one)
-    kv_two = z_move(kv, up_two)
-    q = project(n1, wq, cos_full, sin_full, wq.shape[1] // 256)
+    weight = jnp.sum(jnp.where(hot, gate_rows[:, :, None], 0.0), axis=1)
+    marks = jnp.pad(
+        jnp.concatenate([routed, weight], axis=1).astype(BF16), ((0, 0), (0, HD - 2 * experts_n))
+    )
+    kv, kv_one, kv_two, counts, marks_near, arrived_dy = keyval(
+        n1,
+        w_keyval,
+        cos_full,
+        sin_full,
+        counts,
+        marks,
+        packed_dy.reshape(dp_count, share, width),
+        tensor_count,
+    )
+    arrived_dy = arrived_dy.reshape(rows, width)
+    kv, n1, gu_moved = tie(kv, n1, gu_moved)
+
+    def kept_gates(routed, weight, at):
+        block = (z - 1 - jnp.arange(tensor_count, dtype=jnp.int32)) % tensor_count
+        base = jnp.sum(
+            jnp.where((block < at)[:, None], counts[:, 0, :experts_n], 0.0), axis=0
+        )
+        position = mm(lower, routed.astype(BF16)) + base[None, :]
+        weight = jnp.where(position < capacity, weight, 0.0).astype(BF16)
+        return row_major(jnp.repeat(weight, part_hidden, axis=1))
+
+    gate_own = kept_gates(routed, weight, z)
+    marks_near = marks_near.astype(F32)
+    gate_near = kept_gates(
+        marks_near[:, :experts_n], marks_near[:, experts_n : 2 * experts_n], z + 1 - 2 * (z % 2)
+    )
+    q = project_query(n1, wq_all, cos_full, sin_full)
+    dy_rows = mm(unpack, arrived_dy).astype(BF16)
+    q, dy_rows, gate_own, gate_near = tie(q, dy_rows, gate_own, gate_near)
+    dy_near = z_move(dy_rows, near)
     kvs = (kv_two, kv_one, kv)
     o, lse = attend(z_arg, start, q, kvs, kv_heads)
+    o, wd_piece, gu_moved, dy_near = tie(o, wd_piece, gu_moved, dy_near)
+    gu_far = team_gather(gu_moved)
     h = x_rows + mm(o, wo)
     inv_two = lax.rsqrt(jnp.mean(h * h, axis=1, keepdims=True) + EPS)
     n2 = (h * inv_two * gain_moe).astype(BF16)
 
-    n2_near = z_move(n2, near)
-    y, dn2, hs_oo, dg_oo, du_oo = experts(n2, dy_rows, gate_own, wg_own, wu_own, wd_own)
-    y, dn2, hs_of, dg_of, du_of = experts(
-        n2, dy_rows, gate_own, wg_far, wu_far, wd_far, (y, dn2)
-    )
-    yn, dnn, hs_no, dg_no, du_no = experts(n2_near, dy_near, gate_near, wg_own, wu_own, wd_own)
-    yn, dnn, hs_nf, dg_nf, du_nf = experts(
-        n2_near, dy_near, gate_near, wg_far, wu_far, wd_far, (yn, dnn)
-    )
-    dn2 = dn2 + z_move(dnn.astype(BF16), near).astype(F32)
-    result = h + y + z_move(yn.astype(BF16), near).astype(F32)
-
-    def two(a, b, c, e):
-        return (mm_tn(a, b) + mm_tn(c, e)).astype(BF16)
-
-    grads_own = [
-        two(n2, dg_oo, n2_near, dg_no),
-        two(n2, du_oo, n2_near, du_no),
-        two(dy_rows, hs_oo, dy_near, hs_no),
-    ]
-    grads_far = [
-        two(n2, dg_of, n2_near, dg_nf),
-        two(n2, du_of, n2_near, du_nf),
-        two(dy_rows, hs_of, dy_near, hs_nf),
-    ]
+    halving = dp_count == 8
+    d_arg = d.astype(jnp.int32)[None]
+    out_w = width // dp_count
+    orders_a = ((1, 5, 3, 7), (0, 4, 2, 6))
+    orders_b = ((1, 3, 5, 7), (0, 2, 4, 6))
+
+    def turned(tiles, *orders):
+        if halving:
+            return turn(d_arg, tiles, orders, dp_count)
+        return [jnp.concatenate(tiles, axis=0).T] * len(orders)
 
     def dp_sum(x):
         return lax.psum_scatter(x, "dp", scatter_dimension=0, tiled=True)
 
-    sums_far = [z_move(dp_sum(g), far) for g in grads_far]
-    sums = [dp_sum(g).astype(F32) + f.astype(F32) for g, f in zip(grads_own, sums_far)]
-    out_w = width // dp_count
-    sum_gate, sum_up, sum_down = [g.reshape(out_w, experts_n, part_hidden) for g in sums]
-    sum_gate = sum_gate.transpose(1, 0, 2)
-    sum_up = sum_up.transpose(1, 0, 2)
-    sum_down = sum_down.transpose(1, 2, 0)
+    def unit_start(jobs, send_lefts, rights):
+        return dp_move(gradients(jobs, send_lefts, rights), 1)
+
+    def unit_keep(jobs, keep_lefts, rights, got):
+        return gradients(jobs, keep_lefts, rights, got)
+
+    def first_moves(parts):
+        return parts[0], dp_move(parts[1], xy[0]), parts[2], dp_move(parts[3], yx[0])
+
+    def second_moves(moved):
+        halves = []
+        for keep, got, bit in ((*moved[:2], xy[1]), (*moved[2:], yx[1])):
+            x = keep.astype(F32) + got.astype(F32)
+            half = x.shape[0] // 2
+            halves += [x[:half], dp_move(x[half:].astype(BF16), bit)]
+        return halves
+
+    def unit_end(moved):
+        return moved[0] + moved[1].astype(F32), moved[2] + moved[3].astype(F32)
+
+    def expert_lefts(n_a, d_a, keep):
+        return n_a[keep], d_a[keep], n_a[2 + keep], d_a[2 + keep]
+
+    xy, yx = (2, 4), (4, 2)
+    n2_near = z_move(n2, near)
+    ff = gu_far.shape[1] // 1024
+    y, dn2, *own_grads = experts(0, n2, dy_rows, gate_own, wg_own, wu_own, wd_own)
+    n2_near, y, dy_near, wd_piece = tie(n2_near, y, dy_near, wd_piece)
+    wd_moved = z_move(wd_piece, far)
+    wd_far = team_gather(wd_moved)
+    yn, dnn, *own_grads = experts(
+        1, n2_near, dy_near, gate_near, wg_own, wu_own, wd_own, filled=own_grads
+    )
+    dy_a = turned((dy_rows, dy_near), *orders_a, *orders_b)
+    n2_a = turned((n2, n2_near), *orders_a, *orders_b)
+    if halving:
+        own_grads = own_grads[::-1]
+        got = unit_start(EXPERT_JOBS, expert_lefts(n2_a, dy_a, 0), own_grads)
+        own = unit_keep(EXPERT_JOBS, expert_lefts(n2_a, dy_a, 1), own_grads, got)
+        gu_far, *own = tie(gu_far, *own)
+        own = first_moves(own)
+    yn, dnn, *far_grads = experts(
+        1, n2_near, dy_near, gate_near, gu_far, gu_far, wd_far, (yn, dnn), up_at=ff
+    )
+    dnn_moved = z_move(dnn.astype(BF16), near)
+    yn_moved = z_move(yn.astype(BF16), near)
+    y, dn2, *far_grads = experts(
+        0, n2, dy_rows, gate_own, gu_far, gu_far, wd_far, (y, dn2), far_grads, up_at=ff
+    )
+    if halving:
+        far_grads = far_grads[::-1]
+        far_sent = gradients(EXPERT_JOBS, expert_lefts(n2_a, dy_a, 0), far_grads)
+        dnn_moved, far_sent, *own = tie(dnn_moved, far_sent, *own)
+        got = dp_move(far_sent, 1)
+        own = second_moves(own)
+    dn2 = dn2 + dnn_moved.astype(F32)
 
     gain_two_part = jnp.sum(dn2 * h * inv_two, axis=0)
     u2 = dn2 * gain_moe
@@ -510,13 +1028,34 @@
     )
     dhb = dh.astype(BF16)
     do = mm_nt(dhb, wo).astype(BF16)
-    grad_out_part = mm_tn(dhb, o).astype(BF16)
+    if halving:
+        far_w = unit_keep(EXPERT_JOBS, expert_lefts(n2_a, dy_a, 1), far_grads, got)
+        do, *far_w = tie(do, *far_w)
+        far_w = first_moves(far_w)
+    result = h + y + yn_moved.astype(F32)
+    result_out = mm_tn(unpack, result.astype(BF16)).astype(BF16)
+    do, result_out = tie(do, result_out)
 
     dq, dkv_two, dkv_one, dkv = attend_back(
         z_arg, start, q, o, do, lse, cos_full, sin_full, kvs, kv_heads
     )
-    dkv = dkv + z_move(dkv_one, [(b, a) for a, b in up_one]).astype(F32)
-    dkv = dkv + z_move(dkv_two, [(b, a) for a, b in up_two]).astype(F32)
+    dkv_one = z_move(dkv_one, [(b, a) for a, b in up_one])
+    dkv_two = z_move(dkv_two, [(b, a) for a, b in up_two])
+    n1_t = turned((n1,), *orders_a, *orders_b)
+    dhb_t = turned((dhb,), *orders_b)
+    if halving:
+        dq, *far_w = tie(dq, *far_w)
+        far_w = second_moves(far_w)
+        got = unit_start(ATTENTION_JOBS, (n1_t[0], dhb_t[0]), (dq, o))
+        parts = unit_keep(ATTENTION_JOBS, (n1_t[1], dhb_t[1]), (dq, o), got)
+        dkv_one, dkv_two, *rest = tie(dkv_one, dkv_two, *parts, *far_w)
+        parts, far_w = rest[:4], rest[4:]
+        far_sums = [z_move(part.astype(BF16), far) for part in unit_end(far_w)]
+    else:
+        sum_q, sum_o = [
+            dp_sum(mm_tn(a, b).astype(BF16)).astype(F32) for a, b in ((n1, dq), (dhb, o))
+        ]
+    dkv = dkv + dkv_one.astype(F32) + dkv_two.astype(F32)
 
     def unrotate(u):
         swapped = jnp.concatenate([u[:, HD // 2 :], u[:, : HD // 2]], axis=1)
@@ -527,38 +1066,67 @@
         + [dkv[:, kv_heads * HD :]],
         axis=1,
     ).astype(BF16)
-    dn1 = mm_nt(dq, wq) + mm_nt(dkv, w_keyval)
-    grad_query_part = mm_tn(n1, dq).astype(BF16)
-    grad_keyval_part = mm_tn(n1, dkv).astype(BF16)
+    dn1 = project_back(dq, wq_all, dkv, w_keyval)
     gain_one_part = jnp.sum(dn1 * x_rows * inv_one, axis=0)
     u1 = dn1 * gain_attn
     dx = dh + inv_one * (
         u1 - x_rows * inv_one * inv_one * jnp.mean(u1 * x_rows, axis=1, keepdims=True)
     )
 
-    def give_back(values):
-        back = deal(mm_tn(unpack, values.astype(BF16)).astype(BF16))
-        return mm_tn(pack, back).astype(BF16)
-
-    outputs = give_back(result)
-    grad_tokens = give_back(dx)
-
-    def tensor_sum(x):
-        parts = x.reshape(x.shape[0], tensor_count, x.shape[1] // tensor_count).transpose(1, 0, 2)
-        return lax.psum_scatter(parts, "tensor", scatter_dimension=0, tiled=True)[0].astype(F32)
-
-    sum_out = tensor_sum(dp_sum(grad_out_part)).T
-    sum_query = tensor_sum(dp_sum(grad_query_part))
-    small = jnp.concatenate(
-        [
-            grad_keyval_part,
-            gain_one_part[:, None].astype(BF16),
-            gain_two_part[:, None].astype(BF16),
-            jnp.zeros((width, HD - 2), BF16),
-        ],
-        axis=1,
-    )
-    small = lax.psum(dp_sum(small), "tensor").astype(F32)
+    outputs = mm_tn(pack, deal(result_out)).astype(BF16)
+
+    if halving:
+        first, second = [a + b.astype(F32) for a, b in zip(unit_end(own), far_sums)]
+        sum_gu = jnp.concatenate([first[:, :hidden], second[:, :hidden]], axis=1)
+        sum_down = jnp.concatenate([first[:, hidden:], second[:, hidden:]], axis=1)
+    else:
+        lefts = (n2_a[0], dy_a[0])
+        far_sums = [dp_sum(mm(a, b).astype(BF16)) for a, b in zip(lefts, far_grads[::-1])]
+        own_sums = [dp_sum(mm(a, b).astype(BF16)) for a, b in zip(lefts, own_grads[::-1])]
+        sum_gu, sum_down = [
+            a.astype(F32) + z_move(b, far).astype(F32) for a, b in zip(own_sums, far_sums)
+        ]
+    sum_gu = sum_gu.reshape(out_w, hidden // 512, 2, 512)
+    sum_gate, sum_up = [
+        sum_gu[:, :, i].reshape(out_w, experts_n, part_hidden).transpose(1, 0, 2) for i in (0, 1)
+    ]
+    sum_down = sum_down.reshape(out_w, experts_n, part_hidden).transpose(1, 2, 0)
+
+    gains = jnp.stack([gain_one_part, gain_two_part])
+
+    def gain_columns(order):
+        blocks = gains.reshape(2, dp_count, out_w)
+        if halving:
+            blocks = jnp.stack(
+                [lax.dynamic_index_in_dim(blocks, d ^ p, 1, keepdims=False) for p in order], 1
+            )
+        return jnp.pad(blocks.reshape(2, -1).T, ((0, 0), (dkv.shape[1], HD - 2)))
+
+    columns = [gain_columns(order) for order in orders_b]
+    dkv_wide = jnp.pad(dkv, ((0, 0), (0, HD)))
+    if halving:
+        kv_send, kv_keep = [
+            (mm(left, dkv_wide) + column).astype(BF16) for left, column in zip(n1_t[2:], columns)
+        ]
+        dx_out = mm_tn(unpack, dx.astype(BF16)).astype(BF16).reshape(dp_count, share, width)
+        back, total, small = finish(dx_out, *parts, kv_send, kv_keep, tensor_count)
+        grad_tokens = mm_tn(pack, back.reshape(rows, width)).astype(BF16)
+    else:
+        grad_tokens = mm_tn(pack, deal(mm_tn(unpack, dx.astype(BF16)).astype(BF16))).astype(BF16)
+        small = dp_sum((mm(n1_t[3], dkv_wide) + columns[0]).astype(BF16))
+        small = small.astype(F32) + sum(
+            z_move(small, move).astype(F32) for move in (near, far, across)
+        )
+
+        def z_block(x, m):
+            return lax.dynamic_slice_in_dim(x, (z ^ m) * query_cols, query_cols, 1)
+
+        both = [jnp.concatenate([z_block(sum_q, m), z_block(sum_o, m)], axis=1) for m in range(4)]
+        total = both[0] + sum(
+            z_move(part.astype(BF16), move).astype(F32)
+            for part, move in zip(both[1:], (near, far, across))
+        )
+    sum_query, sum_out = total[:, :query_cols], total[:, query_cols:].T
     kv_cols = w_keyval.shape[1]
     return (
         outputs,

time: 1160 us -> 791 us (0.68)
  waiting for transfers between devices: 595 us -> 99.1 us
  Pallas kernels: 188 us -> 458 us
  matrix products: 125 us -> 34.7 us
  blocking collectives: 66.3 us -> 0 us
  other arithmetic: 29.4 us -> 43.1 us
    reduce_scatter x10 -> x0, waiting for transfers between devices: 346 us -> none  [the longest x8 304 us: dp_sum(): return lax.psum_scatter(x, 'dp', scatter_dimension=0, tiled=True)]
    pallas_call x6 -> x18, Pallas kernels: 121 us -> 392 us  [the longest x1 111 us: finish(): pl.pallas_call(finish_kernel, in_specs=[vmem] * 7, out_specs=[vmem] * 3,...]
    dot_general x19 -> x4, matrix products: 101 us -> 16 us  [mm_tn(): lax.dot_general(a, b, (((0,), (0,)), ((), ())), preferred_element_type=F32)]
    all_to_all x4 -> x2, waiting for transfers between devices: 59.4 us -> 3.9 us  [deal(): lax.all_to_all(x.reshape(dp_count, share, x.shape[1]), 'dp', split_axis=0...]
    psum x1 -> x0, waiting for transfers between devices: 52.2 us -> none  [per_device(): small = lax.psum(dp_sum(small), 'tensor').astype(F32)]
    ppermute x14 -> x16, waiting for transfers between devices: 125 us -> 82.7 us  [z_move(): return lax.ppermute(x, 'tensor', pairs)]
    all_gather x2 -> x0, blocking collectives: 35.8 us -> none  [the longest x1 18.4 us: per_device(): wq_piece = lax.all_gather(wq_piece, 'tensor', axis=0, tiled=True)]
    unnamed x1 -> x0, blocking collectives: 30.5 us -> none
  transfers between devices with their start and end apart: 34 -> 33, of which waited for: 18 -> 7; matrix products, arithmetic and copies ran while one was open for 18% -> 14% of each run, Pallas kernels for 11% -> 54%
where the time goes in v2:
time: 791 us; the launch traced here: 783 us
  Pallas kernels  458 us (58%)
  waiting for transfers between devices  99.1 us (13%)
  local copies, waits for them, and re-layouts  93.4 us (12%)
  other arithmetic  43.1 us (5%)
  starting transfers between devices  39.9 us (5%)
  matrix products  34.7 us (4%)
  between operations  15 us (2%)
    pallas_call x1, Pallas kernels, finish(): pl.pallas_call(finish_kernel, in_specs=[vmem] * 7, out_specs=[vmem] * 3,...  111 us
    pallas_call x4, Pallas kernels, experts(): pl.pallas_call(functools.partial(expert_kernel, chunk, before is None), g...  94.8 us
    ppermute x16, waiting for transfers between devices, z_move(): return lax.ppermute(x, 'tensor', pairs)  82.7 us
    pallas_call x6, Pallas kernels, gradients(): pl.pallas_call(functools.partial(gradient_kernel, jobs, len(lefts), len(r...  76.8 us
    pallas_call x1, Pallas kernels, keyval(): pl.pallas_call(keyval_kernel, in_specs=[vmem] * 7, out_specs=[vmem] * 6,...  73.7 us
    pallas_call x1, Pallas kernels, attend_back(): pl.pallas_call(functools.partial(attend_back_kernel, kv_heads), grid_spec...  37.7 us
    pallas_call x1, Pallas kernels, attend(): pl.pallas_call(functools.partial(attend_kernel, kv_heads), grid_spec=pltp...  28.6 us
    unnamed x128, local copies, waits for them, and re-layouts  24.1 us
  transfers between devices with their start and end apart: 33, of which 7 were waited for; matrix products, arithmetic and copies ran while one was open for 14% of the time, Pallas kernels for 54%

profile of v2, /device:TPU:0, one launch (start us, length us, event | category | flops | bytes accessed | tf_op | source)
XLA Modules:
  0.0 783.4 jit_solution(18383313579596534392)
XLA Ops:
  33.0 4.3 all-to-all-start
  37.4 6.6 copy.133.wg_ref
  44.1 6.7 copy.134.wu_ref
  83.6 73.7 %keyval.1 = (bf16[512,512]{1,0:T(8,128)(2,1)S(1)}, bf16[512,512]{1,0:T(8,128)(2,1)S(1)}, bf16[512,512]{1,0:T(8,128)(2,1)S(1)}, f32[4,8,128]{2,1,0:T(8,128)S(1)},...) custom-call(bf16[512,1536]{1,0:T(8,128)(2,1)S(1)} %multiply_convert_fusion.1.x_ref.refs_0_, ...), custom_call_target="tpu_custom_call" | custom-call | tf_op jit(solution)/shard_map/keyval/pallas_call | solution.py:114
  166.3 8.0 %project_query.1.q_ref = bf16[512,1536]{1,0:T(8,128)(2,1)} custom-call(bf16[512,1536]{1,0:T(8,128)(2,1)} %copy-done.2, bf16[8,4,192,384]{3,2,1,0:T(8,128)(2,1)} %bitcast.101, f32[512,128]{1,0:T(8,128)} %get-tuple-element.345.cos_ref, f32[512,128]{1,0:T(8,128)} %copy-done.3), custom_call_target="tpu_custom_call" | custom-call | flops 2415919104 | bytes 7864320 | tf_op jit(solution)/shard_map/project_query/pallas_call | solution.py:148
  175.2 28.6 %attend.1 = (bf16[512,1536]{1,0:T(8,128)(2,1)}, f32[12,512,1]{2,1,0:T(8,128)}) custom-call(s32[1]{0:T(128)} %bitcast.23.z_ref, s32[512,1]{1,0:T(8,128)} %copy.146.start_ref, bf16[512,1536]{1,0:T(8,128)(2,1)} %project_query.1.q_ref, bf16[512,512]{1,0:T(8,128)(2,1)} %copy-done.11, bf16[512,512]{1,0:T(8,128)(2,1)} %copy-done.10, bf16[512,512]{1,0:T(8,128)(2,1)} %copy-done.9), custom_call_target="tpu_custom_call" | custom-call | flops 4831838208 | bytes 6291456 | tf_op jit(solution)/shard_map/attend/pallas_call | solution.py:249
  203.8 6.0 collective-permute-done.7.refs_1_.dy_ref
  220.6 22.7 %experts.4 = (f32[512,1536]{1,0:T(8,128)}, f32[512,1536]{1,0:T(8,128)}, bf16[1024,1536]{1,0:T(8,128)(2,1)}, bf16[1024,3072]{1,0:T(8,128)(2,1)}) custom-call(bf16[512,1536]{1,0:T(8,128)(2,1)} %copy-done.30, bf16[512,1536]{1,0:T(8,128)(2,1)} %copy-done.27, bf16[512,1536]{1,0:T(8,128)(2,1)} %copy.142.gate_ref, bf16[1536,1536]{1,0:T(8,128)(2,1)} %copy.133.wg_ref, ...), custom_call_target="tpu_custom_call" | custom-call | flops 14495514624 | bytes 26738688 | tf_op jit(solution)/shard_map/experts/pallas_call | solution.py:430
  243.3 10.6 %collective-permute-done.8.refs_1_.x_ref = bf16[512,1536]{1,0:T(8,128)(2,1)S(1)} collective-permute-done((bf16[512,1536]{1,0:T(8,128)(2,1)S(1)}, bf16[512,1536]{1,0:T(8,128)(2,1)S(1)}, u32[]{:S(2)}, u32[]{:S(2)}) %collective-permute-start.8) | collective-permute-done | bytes 1572896 | tf_op jit(solution)/shard_map/ppermute | solution.py:799
  257.2 22.6 %experts.5 = (f32[512,1536]{1,0:T(8,128)}, f32[512,1536]{1,0:T(8,128)}, bf16[1024,1536]{1,0:T(8,128)(2,1)}, bf16[1024,3072]{1,0:T(8,128)(2,1)}) custom-call(bf16[512,1536]{1,0:T(8,128)(2,1)} %copy-done.43, bf16[512,1536]{1,0:T(8,128)(2,1)} %copy-done.42, bf16[512,1536]{1,0:T(8,128)(2,1)} %copy.145.gate_ref, ...), custom_call_target="tpu_custom_call", output_to_operand_aliasing={{2}: (6, {}), {3}: (7, {})} | custom-call | flops 14495514624 | bytes 26738688 | tf_op jit(solution)/shard_map/experts/pallas_call | solution.py:430
  279.8 5.2 turn.5
  285.0 5.3 turn.4
  291.2 14.8 %gradients.6 = bf16[2,768,2304]{2,1,0:T(8,128)(2,1)} custom-call(bf16[768,1024]{1,0:T(8,128)(2,1)} %get-tuple-element.172.refs_0_, bf16[768,1024]{1,0:T(8,128)(2,1)} %get-tuple-element.173.refs_1_, bf16[768,1024]{1,0:T(8,128)(2,1)} %get-tuple-element.174.refs_2_, bf16[768,1024]{1,0:T(8,128)(2,1)} %get-tuple-element.175.refs_3_, ...), custom_call_target="tpu_custom_call" | custom-call | flops 7247757312 | bytes 16515072 | tf_op jit(solution)/shard_map/gradients/pallas_call | solution.py:507
  306.0 11.6 %collective-permute-done.9.refs_6_ = bf16[2,768,2304]{2,1,0:T(8,128)(2,1)} collective-permute-done((bf16[2,768,2304]{2,1,0:T(8,128)(2,1)}, bf16[2,768,2304]{2,1,0:T(8,128)(2,1)}, u32[]{:S(2)}, u32[]{:S(2)}) %collective-permute-start.9) | collective-permute-done | bytes 7077920 | tf_op jit(solution)/shard_map/ppermute | solution.py:802
  317.6 16.0 %gradients.7 = (bf16[384,2304]{1,0:T(8,128)(2,1)}, bf16[384,2304]{1,0:T(8,128)(2,1)}, bf16[384,2304]{1,0:T(8,128)(2,1)}, bf16[384,2304]{1,0:T(8,128)(2,1)}) custom-call(bf16[768,1024]{1,0:T(8,128)(2,1)} %get-tuple-element.162.refs_0_, bf16[768,1024]{1,0:T(8,128)(2,1)} %get-tuple-element.164.refs_1_, bf16[768,1024]{1,0:T(8,128)(2,1)} %get-tuple-element.165.refs_2_, ...), custom_call_target="tpu_custom_call" | custom-call | flops 7247757312 | bytes 16515072 | tf_op jit(solution)/shard_map/gradients/pallas_call | solution.py:507
  333.7 24.7 %experts.6 = (f32[512,1536]{1,0:T(8,128)}, f32[512,1536]{1,0:T(8,128)}, bf16[1024,1536]{1,0:T(8,128)(2,1)}, bf16[1024,3072]{1,0:T(8,128)(2,1)}) custom-call(bf16[512,1536]{1,0:T(8,128)(2,1)} %copy-done.43, bf16[512,1536]{1,0:T(8,128)(2,1)} %copy-done.42, bf16[512,1536]{1,0:T(8,128)(2,1)} %copy.145.gate_ref, ...), custom_call_target="tpu_custom_call" | custom-call | flops 14495514624 | bytes 26738688 | tf_op jit(solution)/shard_map/experts/pallas_call | solution.py:430
  365.8 24.8 %experts.7 = (f32[512,1536]{1,0:T(8,128)}, f32[512,1536]{1,0:T(8,128)}, bf16[1024,1536]{1,0:T(8,128)(2,1)}, bf16[1024,3072]{1,0:T(8,128)(2,1)}) custom-call(bf16[512,1536]{1,0:T(8,128)(2,1)} %copy-done.30, bf16[512,1536]{1,0:T(8,128)(2,1)} %copy-done.27, bf16[512,1536]{1,0:T(8,128)(2,1)} %copy.142.gate_ref, ...), custom_call_target="tpu_custom_call", output_to_operand_aliasing={{2}: (8, {}), {3}: (9, {})} | custom-call | flops 14495514624 | bytes 26738688 | tf_op jit(solution)/shard_map/experts/pallas_call | solution.py:430
  390.6 14.9 %gradients.8 = bf16[2,768,2304]{2,1,0:T(8,128)(2,1)} custom-call(bf16[768,1024]{1,0:T(8,128)(2,1)} %get-tuple-element.172.refs_0_, bf16[768,1024]{1,0:T(8,128)(2,1)} %get-tuple-element.173.refs_1_, bf16[768,1024]{1,0:T(8,128)(2,1)} %get-tuple-element.174.refs_2_, bf16[768,1024]{1,0:T(8,128)(2,1)} %get-tuple-element.175.refs_3_, ...), custom_call_target="tpu_custom_call" | custom-call | flops 7247757312 | bytes 16515072 | tf_op jit(solution)/shard_map/gradients/pallas_call | solution.py:507
  415.0 3.7 convolution_convert_fusion.6.do_ref
  418.7 15.9 %gradients.9 = (bf16[384,2304]{1,0:T(8,128)(2,1)}, bf16[384,2304]{1,0:T(8,128)(2,1)}, bf16[384,2304]{1,0:T(8,128)(2,1)}, bf16[384,2304]{1,0:T(8,128)(2,1)}) custom-call(bf16[768,1024]{1,0:T(8,128)(2,1)} %get-tuple-element.162.refs_0_, bf16[768,1024]{1,0:T(8,128)(2,1)} %get-tuple-element.164.refs_1_, bf16[768,1024]{1,0:T(8,128)(2,1)} %get-tuple-element.165.refs_2_, ...), custom_call_target="tpu_custom_call" | custom-call | flops 7247757312 | bytes 16515072 | tf_op jit(solution)/shard_map/gradients/pallas_call | solution.py:507
  439.5 6.6 collective-permute-done.15
  452.8 37.7 %attend_back.1 = (bf16[512,1536]{1,0:T(8,128)(2,1)}, bf16[512,512]{1,0:T(8,128)(2,1)}, bf16[512,512]{1,0:T(8,128)(2,1)}, f32[512,512]{1,0:T(8,128)}) custom-call(s32[1]{0:T(128)} %bitcast.23.z_ref, s32[512,1]{1,0:T(8,128)} %copy.146.start_ref, bf16[512,1536]{1,0:T(8,128)(2,1)} %project_query.1.q_ref, bf16[512,1536]{1,0:T(8,128)(2,1)} %get-tuple-element.152.o_ref.refs_3_, ...), custom_call_target="tpu_custom_call" | custom-call | flops 12079595520 | bytes 9437184 | tf_op jit(solution)/shard_map/attend_back/pallas_call | solution.py:342
  490.5 7.1 gradients.10
  515.1 3.8 slice.229
  522.6 3.9 all-to-all-done.1
  530.2 8.0 %gradients.11 = (bf16[384,1536]{1,0:T(8,128)(2,1)}, bf16[384,1536]{1,0:T(8,128)(2,1)}, bf16[384,1536]{1,0:T(8,128)(2,1)}, bf16[384,1536]{1,0:T(8,128)(2,1)}) custom-call(bf16[768,512]{1,0:T(8,128)(2,1)} %get-tuple-element.217.refs_0_, bf16[768,512]{1,0:T(8,128)(2,1)} %get-tuple-element.218.refs_1_, bf16[512,1536]{1,0:T(8,128)(2,1)} %get-tuple-element.213.refs_2_.dq_ref, ...), custom_call_target="tpu_custom_call" | custom-call | flops 2415919104 | bytes 7864320 | tf_op jit(solution)/shard_map/gradients/pallas_call | solution.py:507
  538.9 57.9 %collective-permute-done.19 = bf16[512,512]{1,0:T(8,128)(2,1)} collective-permute-done((bf16[512,512]{1,0:T(8,128)(2,1)}, bf16[512,512]{1,0:T(8,128)(2,1)}, u32[]{:S(2)}, u32[]{:S(2)}) %collective-permute-start.19) | collective-permute-done | bytes 524320 | tf_op jit(solution)/shard_map/ppermute | solution.py:799
  606.6 10.1 %project_back.1 = f32[512,1536]{1,0:T(8,128)} custom-call(bf16[512,1536]{1,0:T(8,128)(2,1)} %get-tuple-element.213.refs_2_.dq_ref, bf16[8,4,192,384]{3,2,1,0:T(8,128)(2,1)} %bitcast.102, bf16[512,512]{1,0:T(8,128)(2,1)} %pad_maximum_fusion.3.dkv_ref, bf16[1536,512]{1,0:T(8,128)(2,1)} %wkv_ref.1), custom_call_target="tpu_custom_call" | custom-call | flops 3221225472 | bytes 9437184 | tf_op jit(solution)/shard_map/project_back/pallas_call | solution.py:187
  622.5 5.5 convolution_convert_fusion.1
  629.7 111.3 %finish.1 = (bf16[8,64,1536]{2,1,0:T(8,128)(2,1)}, f32[192,768]{1,0:T(8,128)}, f32[192,640]{1,0:T(8,128)}) custom-call(bf16[8,64,1536]{2,1,0:T(8,128)(2,1)} %bitcast.83, bf16[384,1536]{1,0:T(8,128)(2,1)} %get-tuple-element.231.q_keep, bf16[384,1536]{1,0:T(8,128)(2,1)} %get-tuple-element.232.q_send, bf16[384,1536]{1,0:T(8,128)(2,1)} %get-tuple-element.233.o_keep, ...), custom_call_target="tpu_custom_call" | custom-call | tf_op jit(solution)/shard_map/finish/pallas_call | solution.py:675
  759.4 4.2 reshape.192
  763.7 5.4 fusion.40
  (313 shorter events, 179.9 us)
Async XLA Ops:
  20.6 34.1 %collective-permute-start.3 = (bf16[48,1536]{1,0:T(8,128)(2,1)S(1)}, bf16[48,1536]{1,0:T(8,128)(2,1)}, u32[]{:S(2)}, u32[]{:S(2)}) collective-permute-start(bf16[48,1536]{1,0:T(8,128)(2,1)S(1)} %get-tuple-element.312), channel_id=1, source_target_pairs={{0,1},{1,0},{2,3},{3,2},{4,5},{5,4},{6,7},{7,6},{8,9},{9,8},{10,11... | collective-permute-start | bytes 442376 | tf_op jit(solution)/shard_map/ppermute | solution.py:799
  23.6 32.7 %collective-permute-start.4 = (bf16[48,1536]{1,0:T(8,128)(2,1)S(1)}, bf16[48,1536]{1,0:T(8,128)(2,1)}, u32[]{:S(2)}, u32[]{:S(2)}) collective-permute-start(bf16[48,1536]{1,0:T(8,128)(2,1)S(1)} %get-tuple-element.312), channel_id=1, source_target_pairs={{0,2},{1,3},{2,0},{3,1},{4,6},{5,7},{6,4},{7,5},{8,10},{9,11},{10,... | collective-permute-start | bytes 442376 | tf_op jit(solution)/shard_map/ppermute | solution.py:799
  26.2 37.2 %collective-permute-start.5 = (bf16[48,1536]{1,0:T(8,128)(2,1)S(1)}, bf16[48,1536]{1,0:T(8,128)(2,1)}, u32[]{:S(2)}, u32[]{:S(2)}) collective-permute-start(bf16[48,1536]{1,0:T(8,128)(2,1)S(1)} %get-tuple-element.312), channel_id=1, source_target_pairs={{0,3},{1,2},{2,1},{3,0},{4,7},{5,6},{6,5},{7,4},{8,11},{9,10},{10,... | collective-permute-start | bytes 442376 | tf_op jit(solution)/shard_map/ppermute | solution.py:799
  28.7 29.2 %collective-permute-start = (bf16[192,384]{1,0:T(8,128)(2,1)S(1)}, bf16[192,384]{1,0:T(8,128)(2,1)}, u32[]{:S(2)}, u32[]{:S(2)}) collective-permute-start(bf16[192,384]{1,0:T(8,128)(2,1)S(1)} %get-tuple-element.314), channel_id=1, source_target_pairs={{0,1},{1,0},{2,3},{3,2},{4,5},{5,4},{6,7},{7,6},{8,9},{9,8},{10,11... | collective-permute-start | bytes 442376 | tf_op jit(solution)/shard_map/ppermute | solution.py:799
  29.6 29.9 %collective-permute-start.1 = (bf16[192,384]{1,0:T(8,128)(2,1)S(1)}, bf16[192,384]{1,0:T(8,128)(2,1)}, u32[]{:S(2)}, u32[]{:S(2)}) collective-permute-start(bf16[192,384]{1,0:T(8,128)(2,1)S(1)} %get-tuple-element.314), channel_id=1, source_target_pairs={{0,2},{1,3},{2,0},{3,1},{4,6},{5,7},{6,4},{7,5},{8,10},{9,11},{10,... | collective-permute-start | bytes 442376 | tf_op jit(solution)/shard_map/ppermute | solution.py:799
  33.0 31.9 %all-to-all-start = ((bf16[8,64,1664]{2,1,0:T(8,128)(2,1)}), bf16[8,64,1664]{2,1,0:T(8,128)(2,1)}, u32[]{:S(2)}, u32[]{:S(2)}) async-start(bf16[8,64,1664]{2,1,0:T(8,128)(2,1)} %bitcast), calls=%async_computation | async-start | bytes 3407872 | tf_op jit(solution)/shard_map/all_to_all | solution.py:808
  37.4 128.9 %all-gather.5.cloned.1.call-start = ((), (), s32[]{:S(2)}) async-start(), calls=%async_computation.2 | async-start | bytes 5308416 | tf_op jit(solution)/shard_map/all_gather | solution.py:813
  64.9 145.1 %all-gather.7.cloned.1.call-start = ((), (), s32[]{:S(2)}) async-start(), calls=%async_computation.3 | async-start | bytes 5308416 | tf_op jit(solution)/shard_map/all_gather | solution.py:813
  65.7 268.0 %all-gather.9.cloned.1.call-start = ((), (), s32[]{:S(2)}) async-start(), calls=%async_computation.4 | async-start | bytes 10616832 | tf_op jit(solution)/shard_map/all_gather | solution.py:813
  69.3 95.9 %collective-permute-start.6 = (bf16[192,3072]{1,0:T(8,128)(2,1)}, bf16[192,3072]{1,0:T(8,128)(2,1)}, u32[]{:S(2)}, u32[]{:S(2)}) collective-permute-start(bf16[192,3072]{1,0:T(8,128)(2,1)} %pad_maximum_fusion.1), channel_id=1, source_target_pairs={{0,2},{1,3},{2,0},{3,1},{4,6},{5,7},{6,4},{7,5},{8,10},{9,11},{10,... | collective-permute-start | bytes 3538952 | tf_op jit(solution)/shard_map/ppermute | solution.py:799
  174.3 35.5 %collective-permute-start.7 = (bf16[512,1536]{1,0:T(8,128)(2,1)S(1)}, bf16[512,1536]{1,0:T(8,128)(2,1)S(1)}, u32[]{:S(2)}, u32[]{:S(2)}) collective-permute-start(bf16[512,1536]{1,0:T(8,128)(2,1)S(1)} %convolution_convert_fusion.4.dy_ref.refs_0_), channel_id=1, source_target_pairs={{0,1},{1,0},{2,3},{3,2},{4,5},{5,4},{6,7},{7,6},{8,9},{9,8},{10,11... | collective-permute-start | bytes 4718600 | tf_op jit(solution)/shard_map/ppermute | solution.py:799
  209.8 123.9 %all-gather.11.cloned.1.call-start = ((), (), s32[]{:S(2)}) async-start(), calls=%async_computation.5 | async-start | bytes 5308416 | tf_op jit(solution)/shard_map/all_gather | solution.py:813
  219.4 34.5 %collective-permute-start.8 = (bf16[512,1536]{1,0:T(8,128)(2,1)S(1)}, bf16[512,1536]{1,0:T(8,128)(2,1)S(1)}, u32[]{:S(2)}, u32[]{:S(2)}) collective-permute-start(bf16[512,1536]{1,0:T(8,128)(2,1)S(1)} %multiply_convert_fusion.x_ref.refs_0_), channel_id=1, source_target_pairs={{0,1},{1,0},{2,3},{3,2},{4,5},{5,4},{6,7},{7,6},{8,9},{9,8},{10,11... | collective-permute-start | bytes 4718600 | tf_op jit(solution)/shard_map/ppermute | solution.py:799
  254.0 36.4 %collective-permute-start.10 = (bf16[192,1536]{1,0:T(8,128)(2,1)S(1)}, bf16[192,1536]{1,0:T(8,128)(2,1)S(1)}, u32[]{:S(2)}, u32[]{:S(2)}) collective-permute-start(bf16[192,1536]{1,0:T(8,128)(2,1)S(1)} %copy-done.47), channel_id=1, source_target_pairs={{0,2},{1,3},{2,0},{3,1},{4,6},{5,7},{6,4},{7,5},{8,10},{9,11},{10,... | collective-permute-start | bytes 1769480 | tf_op jit(solution)/shard_map/ppermute | solution.py:799
  306.0 11.6 %collective-permute-start.9 = (bf16[2,768,2304]{2,1,0:T(8,128)(2,1)}, bf16[2,768,2304]{2,1,0:T(8,128)(2,1)}, u32[]{:S(2)}, u32[]{:S(2)}) collective-permute-start(bf16[2,768,2304]{2,1,0:T(8,128)(2,1)} %gradients.6), channel_id=1, source_target_pairs={{0,4},{4,0},{8,12},{12,8},{16,20},{20,16},{24,28},{28,24},{1,5},{5... | collective-permute-start | bytes 21233672 | tf_op jit(solution)/shard_map/ppermute | solution.py:802
  361.6 43.9 %collective-permute-start.11 = (bf16[512,1536]{1,0:T(8,128)(2,1)}, bf16[512,1536]{1,0:T(8,128)(2,1)S(1)}, u32[]{:S(2)}, u32[]{:S(2)}) collective-permute-start(bf16[512,1536]{1,0:T(8,128)(2,1)} %convert_element_type.220), channel_id=1, source_target_pairs={{0,1},{1,0},{2,3},{3,2},{4,5},{5,4},{6,7},{7,6},{8,9},{9,8},{10,11... | collective-permute-start | bytes 4718600 | tf_op jit(solution)/shard_map/ppermute | solution.py:799
  362.9 42.6 %collective-permute-start.12 = (bf16[384,2304]{1,0:T(8,128)(2,1)}, bf16[384,2304]{1,0:T(8,128)(2,1)}, u32[]{:S(2)}, u32[]{:S(2)}) collective-permute-start(bf16[384,2304]{1,0:T(8,128)(2,1)} %get-tuple-element.193), channel_id=1, source_target_pairs={{0,8},{4,12},{8,0},{12,4},{16,24},{20,28},{24,16},{28,20},{1,9},{5... | collective-permute-start | bytes 5308424 | tf_op jit(solution)/shard_map/ppermute | solution.py:802
  364.4 41.1 %collective-permute-start.13 = (bf16[384,2304]{1,0:T(8,128)(2,1)}, bf16[384,2304]{1,0:T(8,128)(2,1)S(1)}, u32[]{:S(2)}, u32[]{:S(2)}) collective-permute-start(bf16[384,2304]{1,0:T(8,128)(2,1)} %get-tuple-element.195), channel_id=1, source_target_pairs={{0,16},{4,20},{8,24},{12,28},{16,0},{20,4},{24,8},{28,12},{1,17},{... | collective-permute-start | bytes 5308424 | tf_op jit(solution)/shard_map/ppermute | solution.py:802
  405.5 13.2 %collective-permute-start.14 = (bf16[2,768,2304]{2,1,0:T(8,128)(2,1)}, bf16[2,768,2304]{2,1,0:T(8,128)(2,1)}, u32[]{:S(2)}, u32[]{:S(2)}) collective-permute-start(bf16[2,768,2304]{2,1,0:T(8,128)(2,1)} %gradients.8), channel_id=1, source_target_pairs={{0,4},{4,0},{8,12},{12,8},{16,20},{20,16},{24,28},{28,24},{1,5},{5... | collective-permute-start | bytes 21233672 | tf_op jit(solution)/shard_map/ppermute | solution.py:802
  410.1 35.9 %collective-permute-start.15 = (bf16[512,1536]{1,0:T(8,128)(2,1)}, bf16[512,1536]{1,0:T(8,128)(2,1)}, u32[]{:S(2)}, u32[]{:S(2)}) collective-permute-start(bf16[512,1536]{1,0:T(8,128)(2,1)} %convert_element_type.224), channel_id=1, source_target_pairs={{0,1},{1,0},{2,3},{3,2},{4,5},{5,4},{6,7},{7,6},{8,9},{9,8},{10,11... | collective-permute-start | bytes 4718600 | tf_op jit(solution)/shard_map/ppermute | solution.py:799
  434.7 55.8 %collective-permute-start.16 = (bf16[384,2304]{1,0:T(8,128)(2,1)}, bf16[384,2304]{1,0:T(8,128)(2,1)}, u32[]{:S(2)}, u32[]{:S(2)}) collective-permute-start(bf16[384,2304]{1,0:T(8,128)(2,1)} %get-tuple-element.210), channel_id=1, source_target_pairs={{0,8},{4,12},{8,0},{12,4},{16,24},{20,28},{24,16},{28,20},{1,9},{5... | collective-permute-start | bytes 5308424 | tf_op jit(solution)/shard_map/ppermute | solution.py:802
  435.2 55.2 %collective-permute-start.17 = (bf16[384,2304]{1,0:T(8,128)(2,1)}, bf16[384,2304]{1,0:T(8,128)(2,1)}, u32[]{:S(2)}, u32[]{:S(2)}) collective-permute-start(bf16[384,2304]{1,0:T(8,128)(2,1)} %get-tuple-element.212), channel_id=1, source_target_pairs={{0,16},{4,20},{8,24},{12,28},{16,0},{20,4},{24,8},{28,12},{1,17},{... | collective-permute-start | bytes 5308424 | tf_op jit(solution)/shard_map/ppermute | solution.py:802
  497.6 32.1 %collective-permute-start.20 = (bf16[2,768,1536]{2,1,0:T(8,128)(2,1)}, bf16[2,768,1536]{2,1,0:T(8,128)(2,1)}, u32[]{:S(2)}, u32[]{:S(2)}) collective-permute-start(bf16[2,768,1536]{2,1,0:T(8,128)(2,1)} %gradients.10), channel_id=1, source_target_pairs={{0,4},{4,0},{8,12},{12,8},{16,20},{20,16},{24,28},{28,24},{1,5},{5... | collective-permute-start | bytes 14155784 | tf_op jit(solution)/shard_map/ppermute | solution.py:802
  501.3 25.2 %all-to-all-start.1 = ((bf16[8,64,1536]{2,1,0:T(8,128)(2,1)}), bf16[8,64,1536]{2,1,0:T(8,128)(2,1)S(1)}, u32[]{:S(2)}, u32[]{:S(2)}) async-start(bf16[8,64,1536]{2,1,0:T(8,128)(2,1)} %bitcast.29), calls=%async_computation.1 | async-start | bytes 3145728 | tf_op jit(solution)/shard_map/all_to_all | solution.py:808
  507.9 88.8 %collective-permute-start.22 = (bf16[192,2304]{1,0:T(8,128)(2,1)}, bf16[192,2304]{1,0:T(8,128)(2,1)S(1)}, u32[]{:S(2)}, u32[]{:S(2)}) collective-permute-start(bf16[192,2304]{1,0:T(8,128)(2,1)} %slice.230), channel_id=1, source_target_pairs={{0,8},{4,12},{8,0},{12,4},{16,24},{20,28},{24,16},{28,20},{1,9},{5... | collective-permute-start | bytes 2654216 | tf_op jit(solution)/shard_map/ppermute | solution.py:802
  513.0 83.8 %collective-permute-start.21 = (bf16[192,2304]{1,0:T(8,128)(2,1)}, bf16[192,2304]{1,0:T(8,128)(2,1)S(1)}, u32[]{:S(2)}, u32[]{:S(2)}) collective-permute-start(bf16[192,2304]{1,0:T(8,128)(2,1)} %slice.231), channel_id=1, source_target_pairs={{0,16},{4,20},{8,24},{12,28},{16,0},{20,4},{24,8},{28,12},{1,17},{... | collective-permute-start | bytes 2654216 | tf_op jit(solution)/shard_map/ppermute | solution.py:802
  520.0 18.2 %collective-permute-start.18 = (bf16[512,512]{1,0:T(8,128)(2,1)}, bf16[512,512]{1,0:T(8,128)(2,1)}, u32[]{:S(2)}, u32[]{:S(2)}) collective-permute-start(bf16[512,512]{1,0:T(8,128)(2,1)} %get-tuple-element.215), channel_id=1, source_target_pairs={{1,0},{2,1},{3,2},{5,4},{6,5},{7,6},{9,8},{10,9},{11,10},{13,12},{... | collective-permute-start | bytes 1572872 | tf_op jit(solution)/shard_map/ppermute | solution.py:799
  521.3 75.4 %collective-permute-start.19 = (bf16[512,512]{1,0:T(8,128)(2,1)}, bf16[512,512]{1,0:T(8,128)(2,1)}, u32[]{:S(2)}, u32[]{:S(2)}) collective-permute-start(bf16[512,512]{1,0:T(8,128)(2,1)} %get-tuple-element.216), channel_id=1, source_target_pairs={{2,0},{3,1},{6,4},{7,5},{10,8},{11,9},{14,12},{15,13},{18,16},{19,... | collective-permute-start | bytes 1572872 | tf_op jit(solution)/shard_map/ppermute | solution.py:799
  529.7 218.5 %collective-permute-start.23 = (bf16[192,2304]{1,0:T(8,128)(2,1)}, bf16[192,2304]{1,0:T(8,128)(2,1)}, u32[]{:S(2)}, u32[]{:S(2)}) collective-permute-start(bf16[192,2304]{1,0:T(8,128)(2,1)} %slice.229), channel_id=1, source_target_pairs={{0,16},{4,20},{8,24},{12,28},{16,0},{20,4},{24,8},{28,12},{1,17},{... | collective-permute-start | bytes 2654216 | tf_op jit(solution)/shard_map/ppermute | solution.py:802
  538.2 211.9 %collective-permute-start.25 = (bf16[192,2304]{1,0:T(8,128)(2,1)}, bf16[192,2304]{1,0:T(8,128)(2,1)}, u32[]{:S(2)}, u32[]{:S(2)}) collective-permute-start(bf16[192,2304]{1,0:T(8,128)(2,1)} %slice.228), channel_id=1, source_target_pairs={{0,8},{4,12},{8,0},{12,4},{16,24},{20,28},{24,16},{28,20},{1,9},{5... | collective-permute-start | bytes 2654216 | tf_op jit(solution)/shard_map/ppermute | solution.py:802
  601.4 146.9 %collective-permute-start.24 = (bf16[192,2304]{1,0:T(8,128)(2,1)S(1)}, bf16[192,2304]{1,0:T(8,128)(2,1)}, u32[]{:S(2)}, u32[]{:S(2)}) collective-permute-start(bf16[192,2304]{1,0:T(8,128)(2,1)S(1)} %add_convert_fusion.5), channel_id=1, source_target_pairs={{0,2},{1,3},{2,0},{3,1},{4,6},{5,7},{6,4},{7,5},{8,10},{9,11},{10,... | collective-permute-start | bytes 2654216 | tf_op jit(solution)/shard_map/ppermute | solution.py:799
  602.6 147.6 %collective-permute-start.26 = (bf16[192,2304]{1,0:T(8,128)(2,1)}, bf16[192,2304]{1,0:T(8,128)(2,1)}, u32[]{:S(2)}, u32[]{:S(2)}) collective-permute-start(bf16[192,2304]{1,0:T(8,128)(2,1)} %add_convert_fusion.4), channel_id=1, source_target_pairs={{0,2},{1,3},{2,0},{3,1},{4,6},{5,7},{6,4},{7,5},{8,10},{9,11},{10,... | collective-permute-start | bytes 2654216 | tf_op jit(solution)/shard_map/ppermute | solution.py:799
  (66 other events, 589.8 us)
Sparse Core Ops, SparseCore 0:
  65.1 53.8 all-gather.4
  120.9 38.1 all-gather.6
  209.9 59.5 all-gather.8
  291.3 38.5 all-gather.10

commit v3 on v2

--- a/solution.py
+++ b/solution.py
@@ -36,6 +36,82 @@
 
 def swap_halves(u):
     return pltpu.roll(u, HD // 2, 1)
+
+
+def open_kernel(
+    deal_ref,
+    q_ref,
+    o_ref,
+    dealt_ref,
+    q_all,
+    o_all,
+    send,
+    recv,
+    deal_send,
+    deal_recv,
+):
+    z = lax.axis_index("tensor")
+    d = lax.axis_index("dp")
+    d_count = deal_ref.shape[0]
+    z_count = q_all.shape[0]
+    others = [{"tensor": flip(z, m)} for m in range(1, z_count)]
+    peers = [{"dp": (d + p) % d_count} for p in range(1, d_count)]
+    barrier = pltpu.get_barrier_semaphore()
+    for other in others + peers:
+        pl.semaphore_signal(barrier, inc=1, device_id=other, device_id_type=pl.DeviceIdType.MESH)
+    pl.semaphore_wait(barrier, len(others) + len(peers))
+    moves = [(q_ref, q_all.at[m], others[m - 1]) for m in range(1, z_count)]
+    moves += [(o_ref, o_all.at[z], other) for other in others]
+    copies = []
+    for p, peer in enumerate(peers):
+        copy = pltpu.make_async_remote_copy(
+            src_ref=deal_ref.at[(d + p + 1) % d_count],
+            dst_ref=dealt_ref.at[d],
+            send_sem=deal_send.at[p],
+            recv_sem=deal_recv.at[p],
+            device_id=peer,
+            device_id_type=pl.DeviceIdType.MESH,
+        )
+        copy.start()
+        copies.append(copy)
+    for at, (src, dst, to) in enumerate(moves):
+        copy = pltpu.make_async_remote_copy(
+            src_ref=src,
+            dst_ref=dst,
+            send_sem=send.at[at],
+            recv_sem=recv.at[at],
+            device_id=to,
+            device_id_type=pl.DeviceIdType.MESH,
+        )
+        copy.start()
+        copies.append(copy)
+    dealt_ref[d] = deal_ref[d]
+    q_all[0] = q_ref[...]
+    o_all[z] = o_ref[...]
+    for copy in copies:
+        copy.wait()
+
+
+def open_moves(deals, q, o, z_count):
+    vmem = pl.BlockSpec(memory_space=pltpu.VMEM)
+    shapes = [deals.shape, (z_count, *q.shape), (z_count, *o.shape)]
+    moves = 2 * (z_count - 1)
+    return pl.pallas_call(
+        open_kernel,
+        in_specs=[vmem] * 3,
+        out_specs=[vmem] * 3,
+        out_shape=[jax.ShapeDtypeStruct(shape, BF16) for shape in shapes],
+        scratch_shapes=[
+            pltpu.SemaphoreType.DMA((moves,)),
+            pltpu.SemaphoreType.DMA((moves,)),
+            pltpu.SemaphoreType.DMA((deals.shape[0] - 1,)),
+            pltpu.SemaphoreType.DMA((deals.shape[0] - 1,)),
+        ],
+        compiler_params=pltpu.CompilerParams(
+            vmem_limit_bytes=40 * 2**20, collective_id=4, has_side_effects=True
+        ),
+        name="open_moves",
+    )(deals, q, o)
 
 
 def keyval_kernel(
@@ -76,7 +152,7 @@
     pl.semaphore_wait(barrier, z_count - 1 + d_count - 1)
     moves = [(count_ref, counts_ref.at[m], others[m]) for m in range(z_count - 1)]
     moves += [(mark_ref, near_ref, {"tensor": flip(z, 1)})]
-    moves += [(kv_ref, one_ref, others[0]), (kv_ref, two_ref, others[1])]
+    moves += [(kv_ref, one_ref, others[0]), (one_ref, two_ref, others[0])]
     copies = []
     for at, (src, dst, to) in enumerate(moves):
         copy = pltpu.make_async_remote_copy(
@@ -87,8 +163,9 @@
             device_id=to,
             device_id_type=pl.DeviceIdType.MESH,
         )
+        copies.append(copy)
+    for copy in copies[:-1]:
         copy.start()
-        copies.append(copy)
     for p, peer in enumerate(peers):
         copy = pltpu.make_async_remote_copy(
             src_ref=deal_ref.at[(d + p + 1) % d_count],
@@ -102,7 +179,10 @@
         copies.append(copy)
     counts_ref[z_count - 1] = count_ref[...]
     dealt_ref[d] = deal_ref[d]
-    for copy in copies:
+    step_one, step_two = copies[z_count], copies[z_count + 1]
+    step_one.wait()
+    step_two.start()
+    for copy in copies[:z_count] + copies[z_count + 1 :]:
         copy.wait()
 
 
@@ -134,27 +214,32 @@
     )(x, w, cos_full, sin_full, counts, marks, deals)
 
 
-def project_query_kernel(x_ref, w_ref, cos_ref, sin_ref, out_ref):
+def project_query_kernel(z_ref, x_ref, w_ref, cos_ref, sin_ref, out_ref):
     raw = mm(x_ref[...], w_ref[...].reshape(x_ref.shape[1], out_ref.shape[1]))
     for i in range(raw.shape[1] // HD):
         u = raw[:, i * HD : (i + 1) * HD]
         turned = u * cos_ref[...] + swap_halves(u) * sin_ref[...]
-        out_ref[:, i * HD : (i + 1) * HD] = turned.astype(BF16)
-
-
-def project_query(x, w, cos_full, sin_full):
+        out_ref[:, i * HD : (i + 1) * HD] = (turned * SCALE).astype(BF16)
+
+
+def project_query(z, x, w, cos_full, sin_full):
     rows, width = x.shape
     pieces, blocks, piece, columns = w.shape
     return pl.pallas_call(
         project_query_kernel,
-        grid=(blocks,),
-        in_specs=[
-            pl.BlockSpec((rows, width), lambda i: (0, 0)),
-            pl.BlockSpec((pieces, 1, piece, columns), lambda i: (0, i, 0, 0)),
-            pl.BlockSpec((rows, HD), lambda i: (0, 0)),
-            pl.BlockSpec((rows, HD), lambda i: (0, 0)),
-        ],
-        out_specs=pl.BlockSpec((rows, columns), lambda i: (0, i)),
+        grid_spec=pltpu.PrefetchScalarGridSpec(
+            num_scalar_prefetch=1,
+            grid=(blocks,),
+            in_specs=[
+                pl.BlockSpec((rows, width), lambda i, s: (0, 0)),
+                pl.BlockSpec(
+                    (pieces, 1, piece, columns), lambda i, s: (0, jnp.bitwise_xor(i, s[0]), 0, 0)
+                ),
+                pl.BlockSpec((rows, HD), lambda i, s: (0, 0)),
+                pl.BlockSpec((rows, HD), lambda i, s: (0, 0)),
+            ],
+            out_specs=pl.BlockSpec((rows, columns), lambda i, s: (0, i)),
+        ),
         out_shape=jax.ShapeDtypeStruct((rows, blocks * columns), BF16),
         compiler_params=params(),
         name="project_query",
@@ -163,10 +248,10 @@
             bytes_accessed=2 * (2 * rows * width + width * blocks * columns),
             transcendentals=0,
         ),
-    )(x, w, cos_full, sin_full)
-
-
-def project_back_kernel(dq_ref, w_ref, dkv_ref, wkv_ref, out_ref):
+    )(z, x, w, cos_full, sin_full)
+
+
+def project_back_kernel(z_ref, dq_ref, w_ref, dkv_ref, wkv_ref, out_ref):
     step = pl.program_id(0)
     width = out_ref.shape[1]
     part = mm_nt(dq_ref[...], w_ref[...].reshape(width, dq_ref.shape[1]))
@@ -180,20 +265,25 @@
         out_ref[...] += part
 
 
-def project_back(dq, w, dkv, wkv):
+def project_back(z, dq, w, dkv, wkv):
     rows = dq.shape[0]
     pieces, blocks, piece, columns = w.shape
     width = pieces * piece
     return pl.pallas_call(
         project_back_kernel,
-        grid=(blocks,),
-        in_specs=[
-            pl.BlockSpec((rows, columns), lambda i: (0, i)),
-            pl.BlockSpec((pieces, 1, piece, columns), lambda i: (0, i, 0, 0)),
-            pl.BlockSpec(dkv.shape, lambda i: (0, 0)),
-            pl.BlockSpec(wkv.shape, lambda i: (0, 0)),
-        ],
-        out_specs=pl.BlockSpec((rows, width), lambda i: (0, 0)),
+        grid_spec=pltpu.PrefetchScalarGridSpec(
+            num_scalar_prefetch=1,
+            grid=(blocks,),
+            in_specs=[
+                pl.BlockSpec((rows, columns), lambda i, s: (0, i)),
+                pl.BlockSpec(
+                    (pieces, 1, piece, columns), lambda i, s: (0, jnp.bitwise_xor(i, s[0]), 0, 0)
+                ),
+                pl.BlockSpec(dkv.shape, lambda i, s: (0, 0)),
+                pl.BlockSpec(wkv.shape, lambda i, s: (0, 0)),
+            ],
+            out_specs=pl.BlockSpec((rows, width), lambda i, s: (0, 0)),
+        ),
         out_shape=jax.ShapeDtypeStruct((rows, width), F32),
         compiler_params=params(),
         name="project_back",
@@ -202,49 +292,58 @@
             bytes_accessed=2 * width * (3 * rows + blocks * columns),
             transcendentals=0,
         ),
-    )(dq, w, dkv, wkv)
-
-
-def make_bias(z_ref, start_ref, bias_ref):
-    rows = start_ref.shape[0]
-    blocks = bias_ref.shape[0]
-    z = z_ref[0]
-    for j in range(blocks):
-        key = (z - (blocks - 1) + j) * rows + lax.broadcasted_iota(jnp.int32, (rows, rows), 1)
-        query = z * rows + lax.broadcasted_iota(jnp.int32, (rows, rows), 0)
-        allowed = (key >= start_ref[...]) & (key <= query)
-        bias_ref[j] = jnp.where(allowed, 0.0, MASKED)
-
-
-def attend_kernel(kv_heads, z_ref, start_ref, q_ref, kv0_ref, kv1_ref, kv2_ref, o_ref, lse_ref, bias_ref):
+    )(z, dq, w, dkv, wkv)
+
+
+ATTEND_TILE = 256
+SCALE = HD**-0.5 * LOG2E
+
+
+def make_bias(z, start_ref, bias_ref):
+    tiles, tile, width = bias_ref.shape
+    rows = tiles * tile
+    for i in range(tiles):
+        key = (z - 2) * rows + i * tile + lax.broadcasted_iota(jnp.int32, (tile, width), 1)
+        query = z * rows + i * tile + lax.broadcasted_iota(jnp.int32, (tile, width), 0)
+        allowed = (key >= start_ref[i * tile : (i + 1) * tile]) & (key <= query)
+        bias_ref[i] = jnp.where(allowed, 0.0, MASKED)
+
+
+def attend_kernel(
+    kv_heads, z_ref, start_ref, q_ref, kv0_ref, kv1_ref, kv2_ref, o_ref, lse_ref, bias_ref, k_ref, v_ref
+):
     head = pl.program_id(0)
-    heads = pl.num_programs(0)
+    each = pl.num_programs(0) // kv_heads
+    rows = q_ref.shape[0]
+    tiles, tile, width = bias_ref.shape
 
     @pl.when(head == 0)
     def _():
-        make_bias(z_ref, start_ref, bias_ref)
-
-    kvh = head // (heads // kv_heads)
-    scale = HD**-0.5 * LOG2E
-    q = q_ref[...]
-    kvs = (kv0_ref, kv1_ref, kv2_ref)
-    kcol = pl.ds(pl.multiple_of(kvh * HD, HD), HD)
-    vcol = pl.ds(pl.multiple_of((kv_heads + kvh) * HD, HD), HD)
-    scores = [mm_nt(q, ref[:, kcol]) * scale + bias_ref[j] for j, ref in enumerate(kvs)]
-    peak = functools.reduce(
-        jnp.maximum, [jnp.max(s, axis=1, keepdims=True) for s in scores]
-    )
-    soft = [jnp.exp2(s - peak) for s in scores]
-    total = sum(jnp.sum(s, axis=1, keepdims=True) for s in soft)
-    mixed = sum(mm(s.astype(BF16), ref[:, vcol]) for s, ref in zip(soft, kvs))
-    o_ref[...] = (mixed / total).astype(BF16)
-    lse_ref[0] = peak + jnp.log2(total)
+        make_bias(z_ref[0], start_ref, bias_ref)
+        v_ref[:, HD:] = jnp.ones((v_ref.shape[0], HD), BF16)
+
+    @pl.when(head % each == 0)
+    def _():
+        kvh = head // each
+        for j, ref in enumerate((kv0_ref, kv1_ref, kv2_ref)):
+            at = slice(j * rows, (j + 1) * rows)
+            k_ref[at] = ref[:, pl.ds(pl.multiple_of(kvh * HD, HD), HD)]
+            v_ref[at, :HD] = ref[:, pl.ds(pl.multiple_of((kv_heads + kvh) * HD, HD), HD)]
+
+    for i in range(tiles):
+        at, window = slice(i * tile, (i + 1) * tile), slice(i * tile, i * tile + width)
+        score = mm_nt(q_ref[at], k_ref[window]) + bias_ref[i]
+        peak = jnp.max(score, axis=1, keepdims=True)
+        mixed = mm(jnp.exp2(score - peak).astype(BF16), v_ref[window])
+        total = mixed[:, HD : HD + 1]
+        o_ref[at] = (mixed[:, :HD] / total).astype(BF16)
+        lse_ref[0, at] = peak + jnp.log2(total)
 
 
 def attend(z, start, q, kvs, kv_heads):
     rows, columns = q.shape
     heads = columns // HD
-    blocks = len(kvs)
+    tile = ATTEND_TILE
     kv_spec = pl.BlockSpec(kvs[0].shape, lambda h, s: (0, 0))
     return pl.pallas_call(
         functools.partial(attend_kernel, kv_heads),
@@ -254,13 +353,17 @@
             in_specs=[
                 pl.BlockSpec((rows, 1), lambda h, s: (0, 0)),
                 pl.BlockSpec((rows, HD), lambda h, s: (0, h)),
-                *[kv_spec] * blocks,
+                *[kv_spec] * 3,
             ],
             out_specs=[
                 pl.BlockSpec((rows, HD), lambda h, s: (0, h)),
                 pl.BlockSpec((1, rows, 1), lambda h, s: (h, 0, 0)),
             ],
-            scratch_shapes=[pltpu.VMEM((blocks, rows, rows), F32)],
+            scratch_shapes=[
+                pltpu.VMEM((rows // tile, tile, 2 * rows + tile), F32),
+                pltpu.VMEM((3 * rows, HD), BF16),
+                pltpu.VMEM((3 * rows, 2 * HD), BF16),
+            ],
         ),
         out_shape=[
             jax.ShapeDtypeStruct((rows, columns), BF16),
@@ -269,9 +372,9 @@
         compiler_params=params(),
         name="attend",
         cost_estimate=pl.CostEstimate(
-            flops=4 * rows * rows * blocks * columns,
+            flops=12 * rows * rows * columns,
             bytes_accessed=8 * rows * columns,
-            transcendentals=rows * rows * blocks * heads,
+            transcendentals=rows * rows * 3 * heads,
         ),
     )(z, start, q, *kvs)
 
@@ -294,47 +397,55 @@
     d1_ref,
     d2_ref,
     bias_ref,
-    acc_ref,
+    k_ref,
+    v_ref,
+    dk_ref,
+    dv_ref,
 ):
     head = pl.program_id(0)
-    heads = pl.num_programs(0)
+    each = pl.num_programs(0) // kv_heads
+    rows = q_ref.shape[0]
+    tiles, tile, width = bias_ref.shape
+    kvh = head // each
+    kcol = pl.ds(pl.multiple_of(kvh * HD, HD), HD)
+    vcol = pl.ds(pl.multiple_of((kv_heads + kvh) * HD, HD), HD)
 
     @pl.when(head == 0)
     def _():
-        make_bias(z_ref, start_ref, bias_ref)
-        acc_ref[...] = jnp.zeros_like(acc_ref)
-
-    kvh = head // (heads // kv_heads)
-    scale = HD**-0.5 * LOG2E
-    q = q_ref[...]
-    do = do_ref[...]
-    centre = jnp.sum(do.astype(F32) * o_ref[...].astype(F32), axis=1, keepdims=True)
-    lse = lse_ref[0]
-    kcol = pl.ds(pl.multiple_of(kvh * HD, HD), HD)
-    vcol = pl.ds(pl.multiple_of((kv_heads + kvh) * HD, HD), HD)
-    dq = jnp.zeros(q.shape, F32)
-    for j, ref in enumerate((kv0_ref, kv1_ref, kv2_ref)):
-        keys = ref[:, kcol]
-        soft = jnp.exp2(mm_nt(q, keys) * scale + (bias_ref[j] - lse))
-        acc_ref[j, :, vcol] += mm_tn(soft.astype(BF16), do)
-        dsoft = mm_nt(do, ref[:, vcol])
-        dscore = (soft * (dsoft - centre)).astype(BF16)
-        dq += mm(dscore, keys)
-        acc_ref[j, :, kcol] += mm_tn(dscore, q) * (HD**-0.5)
-    dq = dq * (HD**-0.5)
-    dq_ref[...] = (dq * cos_ref[...] - swap_halves(dq) * sin_ref[...]).astype(BF16)
-
-    @pl.when(head == heads - 1)
+        make_bias(z_ref[0], start_ref, bias_ref)
+
+    @pl.when(head % each == 0)
     def _():
-        d0_ref[...] = acc_ref[0].astype(BF16)
-        d1_ref[...] = acc_ref[1].astype(BF16)
-        d2_ref[...] = acc_ref[2]
+        for j, ref in enumerate((kv0_ref, kv1_ref, kv2_ref)):
+            k_ref[j * rows : (j + 1) * rows] = ref[:, kcol]
+            v_ref[j * rows : (j + 1) * rows] = ref[:, vcol]
+        dk_ref[...] = jnp.zeros_like(dk_ref)
+        dv_ref[...] = jnp.zeros_like(dv_ref)
+
+    for i in range(tiles):
+        at, window = slice(i * tile, (i + 1) * tile), slice(i * tile, i * tile + width)
+        q = q_ref[at]
+        do = do_ref[at]
+        centre = jnp.sum(do.astype(F32) * o_ref[at].astype(F32), axis=1, keepdims=True)
+        soft = jnp.exp2(mm_nt(q, k_ref[window]) + (bias_ref[i] - lse_ref[0, at]))
+        dv_ref[window] += mm_tn(soft.astype(BF16), do)
+        dscore = (soft * (mm_nt(do, v_ref[window]) - centre)).astype(BF16)
+        dk_ref[window] += mm_tn(dscore, q)
+        dq = mm(dscore, k_ref[window]) * (HD**-0.5)
+        dq_ref[at] = (dq * cos_ref[at] - swap_halves(dq) * sin_ref[at]).astype(BF16)
+
+    @pl.when(head % each == each - 1)
+    def _():
+        for j, ref in enumerate((d0_ref, d1_ref, d2_ref)):
+            at = slice(j * rows, (j + 1) * rows)
+            ref[:, kcol] = (dk_ref[at] * (1 / LOG2E)).astype(ref.dtype)
+            ref[:, vcol] = dv_ref[at].astype(ref.dtype)
 
 
 def attend_back(z, start, q, o, do, lse, cos_full, sin_full, kvs, kv_heads):
     rows, columns = q.shape
     heads = columns // HD
-    blocks = len(kvs)
+    tile = ATTEND_TILE
     kv_columns = kvs[0].shape[1]
     kv_spec = pl.BlockSpec((rows, kv_columns), lambda h, s: (0, 0))
     head_spec = pl.BlockSpec((rows, HD), lambda h, s: (0, h))
@@ -352,12 +463,15 @@
                 pl.BlockSpec((1, rows, 1), lambda h, s: (h, 0, 0)),
                 table_spec,
                 table_spec,
-                *[kv_spec] * blocks,
+                *[kv_spec] * 3,
             ],
-            out_specs=[head_spec, *[kv_spec] * blocks],
+            out_specs=[head_spec, *[kv_spec] * 3],
             scratch_shapes=[
-                pltpu.VMEM((blocks, rows, rows), F32),
-                pltpu.VMEM((blocks, rows, kv_columns), F32),
+                pltpu.VMEM((rows // tile, tile, 2 * rows + tile), F32),
+                pltpu.VMEM((3 * rows, HD), BF16),
+                pltpu.VMEM((3 * rows, HD), BF16),
+                pltpu.VMEM((3 * rows, HD), F32),
+                pltpu.VMEM((3 * rows, HD), F32),
             ],
         ),
         out_shape=[
@@ -369,9 +483,9 @@
         compiler_params=params(),
         name="attend_back",
         cost_estimate=pl.CostEstimate(
-            flops=10 * rows * rows * blocks * columns,
+            flops=30 * rows * rows * columns,
             bytes_accessed=12 * rows * columns,
-            transcendentals=rows * rows * blocks * heads,
+            transcendentals=rows * rows * 3 * heads,
         ),
     )(z, start, q, o, do, lse, cos_full, sin_full, *kvs)
 
@@ -391,8 +505,8 @@
 
     x = x_ref[...]
     gate = gate_ref[...].astype(F32)
-    g = jnp.maximum(mm(x, wg_ref[...]), 0.0)
-    u = mm(x, wu_ref[...])
+    g = jnp.maximum(mm_nt(x, wg_ref[...]), 0.0)
+    u = mm_nt(x, wu_ref[...])
     square = g * g
     hs = ((square * u).astype(BF16).astype(F32) * gate).astype(BF16)
     hs_ref[...] = hs
@@ -401,11 +515,11 @@
     du = (dh * square).astype(BF16)
     dgu_ref[:, :chunk] = dg
     dgu_ref[:, chunk:] = du
-    dn_ref[...] += mm_nt(dg, wg_ref[...]) + mm_nt(du, wu_ref[...])
+    dn_ref[...] += mm(dg, wg_ref[...]) + mm(du, wu_ref[...])
     y_ref[...] += mm(hs, wd_ref[...])
 
 
-def experts(tile, x, dy, gate, wg, wu, wd, before=None, filled=None, up_at=0, chunk=512):
+def experts(tile, x, dy, gate, wg, wu, wd, before=None, filled=None, chunk=512):
     rows, width = x.shape
     hidden = gate.shape[1]
     full = pl.BlockSpec((rows, width), lambda i: (0, 0))
@@ -415,9 +529,7 @@
         full,
         full,
         part,
-        pl.BlockSpec((width, chunk), lambda i: (0, i)),
-        pl.BlockSpec((width, chunk), lambda i: (0, i + up_at)),
-        pl.BlockSpec((chunk, width), lambda i: (i, 0)),
+        *[pl.BlockSpec((chunk, width), lambda i: (i, 0))] * 3,
     ]
     aliases = {}
     if before is not None:
@@ -454,11 +566,102 @@
     )(*operands)
 
 
-def gradient_kernel(jobs, lefts, rights, keep, *refs):
+def pick(i, values):
+    result = values[0]
+    for at, value in enumerate(values):
+        if at and value != values[at - 1]:
+            result = jnp.where(i >= at, value, result)
+    return result
+
+
+def gradient_kernel(jobs, lefts, rights, *refs):
+    send_refs, keep_refs, right_refs = refs[:lefts], refs[lefts : 2 * lefts], refs[2 * lefts :]
+    outs, (sent, got, send, recv) = right_refs[rights:-4], refs[-4:]
+    d = lax.axis_index("dp")
+    step = pl.program_id(0)
+    count = len(jobs)
+
+    @pl.when(step == 0)
+    def _():
+        barrier = pltpu.get_barrier_semaphore()
+        pl.semaphore_signal(
+            barrier, inc=1, device_id={"dp": flip(d, 1)}, device_id_type=pl.DeviceIdType.MESH
+        )
+        pl.semaphore_wait(barrier, 1)
+
+    def copy(i):
+        return pltpu.make_async_remote_copy(
+            src_ref=sent.at[i],
+            dst_ref=got.at[i],
+            send_sem=send.at[i],
+            recv_sem=recv.at[i],
+            device_id={"dp": flip(d, 1)},
+            device_id_type=pl.DeviceIdType.MESH,
+        )
+
+    for i, (left, right, _) in enumerate(jobs):
+
+        @pl.when(step == i)
+        def _(i=i, left=left, right=right):
+            sent[i] = mm(send_refs[left][...], right_refs[right][...]).astype(BF16)
+            copy(i).start()
+
+        @pl.when(step == count + i)
+        def _(i=i, left=left, right=right):
+            value = mm(keep_refs[left][...], right_refs[right][...])
+            copy(i).wait()
+            value = value + got[i].astype(F32)
+            half = value.shape[0] // 2
+            side = 2 * (i // (count // 2))
+            outs[side][...] = value[:half].astype(BF16)
+            outs[side + 1][...] = value[half:].astype(BF16)
+
+
+def gradients(jobs, send_lefts, keep_lefts, rights, ident, chunk=768):
+    rows, tokens = keep_lefts[0].shape
+    count = len(jobs)
+    each = count // 2
+    first = lambda i: (0, jnp.clip(i - count, 0, each - 1))
+    second = lambda i: (0, jnp.maximum(i - count - each, 0))
+    right_specs = []
+    for r in range(len(rights)):
+        blocks, at = [], None
+        for _, right, block in jobs + jobs:
+            at = block if right == r else at
+            blocks.append(at)
+        known = next(block for block in blocks if block is not None)
+        blocks = tuple(known if block is None else block for block in blocks)
+        right_specs.append(
+            pl.BlockSpec((tokens, chunk), lambda i, blocks=blocks: (0, pick(i, blocks)))
+        )
+    left = pl.BlockSpec((rows, tokens), lambda i: (0, 0), pipeline_mode=pl.Buffered(1))
+    return pl.pallas_call(
+        functools.partial(gradient_kernel, jobs, len(keep_lefts), len(rights)),
+        grid=(2 * count,),
+        in_specs=[*[left] * (2 * len(keep_lefts)), *right_specs],
+        out_specs=[
+            pl.BlockSpec((rows // 2, chunk), at) for at in (first, first, second, second)
+        ],
+        out_shape=[jax.ShapeDtypeStruct((rows // 2, each * chunk), BF16)] * 4,
+        scratch_shapes=[
+            pltpu.VMEM((count, rows, chunk), BF16),
+            pltpu.VMEM((count, rows, chunk), BF16),
+            pltpu.SemaphoreType.DMA((count,)),
+            pltpu.SemaphoreType.DMA((count,)),
+        ],
+        compiler_params=pltpu.CompilerParams(
+            vmem_limit_bytes=56 * 2**20, collective_id=ident, has_side_effects=True
+        ),
+        name="gradients",
+        cost_estimate=pl.CostEstimate(flops=10**9, bytes_accessed=10**6, transcendentals=0),
+    )(*send_lefts, *keep_lefts, *rights)
+
+
+def part_kernel(jobs, lefts, rights, keep, *refs):
     left_refs, right_refs, rest = refs[:lefts], refs[lefts : lefts + rights], refs[lefts + rights :]
     step = pl.program_id(0)
-    each = len(jobs[0])
-    for i, (left, right, _) in enumerate(jobs[0] + jobs[1]):
+    each = len(jobs) // 2
+    for i, (left, right, _) in enumerate(jobs):
 
         @pl.when(step == i)
         def _(i=i, left=left, right=right):
@@ -473,17 +676,9 @@
                 rest[0][0] = value.astype(BF16)
 
 
-def pick(i, values):
-    result = values[0]
-    for at, value in enumerate(values):
-        if at and value != values[at - 1]:
-            result = jnp.where(i >= at, value, result)
-    return result
-
-
-def gradients(jobs, lefts, rights, got=None, chunk=768):
+def gradient_parts(jobs, lefts, rights, got=None, chunk=768):
     rows, tokens = lefts[0].shape
-    each = len(jobs[0])
+    each = len(jobs) // 2
     first = lambda i: (0, jnp.minimum(i, each - 1))
     second = lambda i: (0, jnp.maximum(i - each, 0))
     whole = [pl.BlockSpec((1, rows, chunk), lambda i: (i // each, 0, i % each))]
@@ -496,7 +691,7 @@
     right_specs = []
     for r in range(len(rights)):
         at, blocks = None, []
-        for _, right, block in jobs[0] + jobs[1]:
+        for _, right, block in jobs:
             at = block if right == r else at
             blocks.append(at)
         known = next(block for block in blocks if block is not None)
@@ -505,7 +700,7 @@
             pl.BlockSpec((tokens, chunk), lambda i, blocks=blocks: (0, pick(i, blocks)))
         )
     return pl.pallas_call(
-        functools.partial(gradient_kernel, jobs, len(lefts), len(rights), got is not None),
+        functools.partial(part_kernel, jobs, len(lefts), len(rights), got is not None),
         grid=(2 * each,),
         in_specs=[
             *[pl.BlockSpec((rows, tokens), lambda i: (0, 0))] * len(lefts),
@@ -515,7 +710,7 @@
         out_specs=out_specs,
         out_shape=out_shape,
         compiler_params=params(),
-        name="gradients",
+        name="gradient_parts",
         cost_estimate=pl.CostEstimate(
             flops=4 * each * rows * tokens * chunk,
             bytes_accessed=4 * each * (rows + tokens) * chunk,
@@ -524,8 +719,7 @@
     )(*lefts, *rights, *(() if got is None else (got,)))
 
 
-EXPERT_JOBS = (((0, 0, 0), (0, 0, 1), (1, 1, 0)), ((2, 0, 2), (2, 0, 3), (3, 1, 1)))
-ATTENTION_JOBS = (((0, 0, 0), (0, 0, 1)), ((1, 1, 0), (1, 1, 1)))
+EXPERT_JOBS = ((0, 0, 0), (0, 0, 1), (1, 1, 0), (2, 0, 2), (2, 0, 3), (3, 1, 1))
 
 
 def flip(index, mask):
@@ -533,6 +727,132 @@
         if mask & bit:
             index = index + bit - 2 * bit * (index // bit % 2)
     return index
+
+
+def mix_kernel(
+    dq_ref,
+    o_ref,
+    n_send,
+    n_keep,
+    d_send,
+    d_keep,
+    one_ref,
+    two_ref,
+    fa_keep,
+    fa_got,
+    fb_keep,
+    fb_got,
+    q_keep,
+    q_send,
+    o_keep,
+    o_send,
+    got_one,
+    far_ref,
+    got_two,
+    both_ref,
+    sent,
+    got,
+    halves,
+    lasts,
+    send,
+    recv,
+):
+    d = lax.axis_index("dp")
+    z = lax.axis_index("tensor")
+    z_count = lax.axis_size("tensor")
+    pairs = [{"dp": flip(d, bit)} for bit in (1, 2, 4)]
+    others = [{"tensor": (z + m) % z_count} for m in range(1, z_count)]
+    barrier = pltpu.get_barrier_semaphore()
+    for peer in pairs + others:
+        pl.semaphore_signal(barrier, inc=1, device_id=peer, device_id_type=pl.DeviceIdType.MESH)
+    pl.semaphore_wait(barrier, len(pairs) + len(others))
+
+    def start(src, dst, at, to):
+        copy = pltpu.make_async_remote_copy(
+            src_ref=src,
+            dst_ref=dst,
+            send_sem=send.at[at],
+            recv_sem=recv.at[at],
+            device_id=to,
+            device_id_type=pl.DeviceIdType.MESH,
+        )
+        copy.start()
+        return copy
+
+    step_two = start(two_ref, got_two, 1, others[-1])
+    rows = halves.shape[1]
+    far_copies = []
+    for side, (keep, arrived) in enumerate(((fa_keep, fa_got), (fb_keep, fb_got))):
+        total = keep[rows:].astype(F32) + arrived[rows:].astype(F32)
+        halves[side] = total.astype(BF16)
+        far_copies.append(start(halves.at[side], lasts.at[side], 2 + side, pairs[2 - side]))
+
+    step_two.wait()
+    both_ref[...] = (one_ref[...].astype(F32) + got_two[...].astype(F32)).astype(BF16)
+    step_one = start(both_ref, got_one, 0, others[-1])
+    columns = dq_ref.shape[1]
+    chunk = columns // 4
+
+    def at_chunk(i):
+        return pl.ds(pl.multiple_of(i * chunk, chunk), chunk)
+
+    sides = ((dq_ref, n_send, n_keep, q_keep, q_send), (o_ref, d_send, d_keep, o_keep, o_send))
+    core_copies = []
+    for side, (right, left, _, _, _) in enumerate(sides):
+
+        def compute_send(i, carry, side=side, right=right, left=left):
+            at = at_chunk(i)
+            sent[side, :, at] = mm(left[...], right[:, at]).astype(BF16)
+            return carry
+
+        lax.fori_loop(0, 4, compute_send, 0)
+        core_copies.append(start(sent.at[side], got.at[side], 4 + side, pairs[0]))
+    for side, (right, _, left, keep, away) in enumerate(sides):
+        core_copies[side].wait()
+
+        def compute_keep(i, carry, side=side, right=right, left=left, keep=keep, away=away):
+            at = at_chunk(i)
+            value = mm(left[...], right[:, at]) + got[side, :, at].astype(F32)
+            half = value.shape[0] // 2
+            keep[:, at] = value[:half].astype(BF16)
+            away[:, at] = value[half:].astype(BF16)
+            return carry
+
+        lax.fori_loop(0, 4, compute_keep, 0)
+    for side, (keep, arrived) in enumerate(((fa_keep, fa_got), (fb_keep, fb_got))):
+        far_copies[side].wait()
+        total = keep[:rows].astype(F32) + arrived[:rows].astype(F32) + lasts[side].astype(F32)
+        far_ref[side] = total.astype(BF16)
+    step_one.wait()
+
+
+def mix(dq, o, lefts, dkv_one, dkv_two, far_parts):
+    rows2, columns = far_parts[0].shape
+    rows = rows2 // 2
+    wide = dq.shape[1]
+    vmem = pl.BlockSpec(memory_space=pltpu.VMEM)
+    half = jax.ShapeDtypeStruct((rows2, wide), BF16)
+    block = jax.ShapeDtypeStruct(dkv_one.shape, BF16)
+    return pl.pallas_call(
+        mix_kernel,
+        in_specs=[vmem] * 12,
+        out_specs=[vmem] * 6,
+        out_shape=[half] * 4 + [block] + [jax.ShapeDtypeStruct((2, rows, columns), BF16)],
+        scratch_shapes=[
+            pltpu.VMEM(block.shape, BF16),
+            pltpu.VMEM(block.shape, BF16),
+            pltpu.VMEM((2, 2 * rows2, wide), BF16),
+            pltpu.VMEM((2, 2 * rows2, wide), BF16),
+            pltpu.VMEM((2, rows, columns), BF16),
+            pltpu.VMEM((2, rows, columns), BF16),
+            pltpu.SemaphoreType.DMA((6,)),
+            pltpu.SemaphoreType.DMA((6,)),
+        ],
+        compiler_params=pltpu.CompilerParams(
+            vmem_limit_bytes=56 * 2**20, collective_id=2, has_side_effects=True
+        ),
+        name="mix",
+    )(dq, o, *lefts, dkv_one, dkv_two, *far_parts)
 
 
 def finish_kernel(
@@ -560,6 +880,7 @@
     z_mine,
     z_got,
     k_mine,
+    k_half,
     k_got,
     deal_send,
     deal_recv,
@@ -594,23 +915,10 @@
         return copy
 
     one, two, four = [{"dp": flip(d, bit)} for bit in (1, 2, 4)]
-    s_one = start(s_send, s_got, 0, one)
     q_one = start(q_send, q_got, 1, two)
     o_one = start(o_send, o_got, 2, four)
-    deals = []
-    for p in range(1, count):
-        copy = pltpu.make_async_remote_copy(
-            src_ref=dx_ref.at[flip(d, p)],
-            dst_ref=back_ref.at[d],
-            send_sem=deal_send.at[p - 1],
-            recv_sem=deal_recv.at[p - 1],
-            device_id={"dp": flip(d, p)},
-            device_id_type=pl.DeviceIdType.MESH,
-        )
-        copy.start()
-        deals.append(copy)
+    s_one = start(s_send, s_got, 0, one)
     back_ref[d] = dx_ref[d]
-
     rows = q_last.shape[0]
     s_one.wait()
     total = s_keep[...].astype(F32) + s_got[...].astype(F32)
@@ -627,13 +935,24 @@
     total = s_keep2 + s_got2[...].astype(F32)
     s_quarter[...] = total[rows:].astype(BF16)
     s_three = start(s_quarter, s_last, 6, two)
+    deals = []
+    for p in range(1, count):
+        copy = pltpu.make_async_remote_copy(
+            src_ref=dx_ref.at[flip(d, p)],
+            dst_ref=back_ref.at[d],
+            send_sem=deal_send.at[p - 1],
+            recv_sem=deal_recv.at[p - 1],
+            device_id={"dp": flip(d, p)},
+            device_id_type=pl.DeviceIdType.MESH,
+        )
+        copy.start()
+        deals.append(copy)
     s_own = total[:rows]
     s_three.wait()
     s_own = s_own + s_last[...].astype(F32)
     k_mine[...] = s_own.astype(BF16)
-    finals = [
-        start(k_mine, k_got.at[m - 1], 6 + m, {"tensor": flip(z, m)}) for m in range(1, z_count)
-    ]
+    k_near = start(k_mine, k_got.at[0], 7, {"tensor": flip(z, 1)})
+    finals = []
     part = qo_ref.shape[1] // 2
     for two_copy, keep, got, last, side in (
         (q_two, q_keep, q_got, q_last, 0),
@@ -647,19 +966,19 @@
             block = total[:, i * part : (i + 1) * part]
             z_mine[i, :, side * part : (side + 1) * part] = block.astype(BF16)
     for m in range(1, z_count):
-        at = 5 + z_count + m
-        finals.append(start(z_mine.at[flip(z, m)], z_got.at[m - 1], at, {"tensor": flip(z, m)}))
-    for copy in finals[: z_count - 1]:
-        copy.wait()
-    for m in range(z_count - 1):
-        s_own = s_own + k_got[m].astype(F32)
-    s_ref[...] = s_own
-    for copy in finals[z_count - 1 :]:
+        finals.append(start(z_mine.at[flip(z, m)], z_got.at[m - 1], 8 + m, {"tensor": flip(z, m)}))
+    k_near.wait()
+    s_own = s_own + k_got[0].astype(F32)
+    k_half[...] = s_own.astype(BF16)
+    k_far = start(k_half, k_got.at[1], 8, {"tensor": flip(z, 2)})
+    for copy in finals:
         copy.wait()
     total = z_mine[z].astype(F32)
     for m in range(z_count - 1):
         total = total + z_got[m].astype(F32)
     qo_ref[...] = total
+    k_far.wait()
+    s_ref[...] = s_own + k_got[1].astype(F32)
     for copy in deals:
         copy.wait()
 
@@ -696,7 +1015,8 @@
             pltpu.VMEM((z_count, rows, 2 * part), BF16),
             pltpu.VMEM((z_count - 1, rows, 2 * part), BF16),
             pltpu.VMEM((rows, small), BF16),
-            pltpu.VMEM((z_count - 1, rows, small), BF16),
+            pltpu.VMEM((rows, small), BF16),
+            pltpu.VMEM((2, rows, small), BF16),
             dma((count - 1,)),
             dma((count - 1,)),
             dma((7 + 2 * z_count,)),
@@ -813,13 +1133,7 @@
         return lax.all_gather(x, "dp", axis=0, tiled=True, axis_index_groups=teams)
 
     def flat(w):
-        return row_major(w.transpose(1, 0, 2).reshape(w.shape[1], hidden))
-
-    def z_gather(x):
-        parts = jnp.zeros((tensor_count, *x.shape), x.dtype)
-        for m, part in enumerate((x, z_move(x, near), z_move(x, far), z_move(x, across))):
-            parts = lax.dynamic_update_slice_in_dim(parts, part[None], z ^ m, 0)
-        return parts
+        return w.transpose(0, 2, 1).reshape(hidden, w.shape[1])
 
     own_perm = lax.dynamic_slice_in_dim(perm, z * rows, rows, 0)
     own_routes = lax.dynamic_slice_in_dim(routes, z * rows, rows, 0)
@@ -842,33 +1156,24 @@
         axis=1,
     )
     packed = mm(pack, jnp.concatenate([tokens, meta], axis=1)).astype(BF16)
-    packed, pack, w_query, w_out, w_gate, w_up, w_down = tie(
-        packed, pack, w_query, w_out, w_gate, w_up, w_down
+    wg_own, wu_own = flat(w_gate), flat(w_up)
+    wd_own = w_down.reshape(hidden, width)
+    out_rows = query_cols // team
+    hidden_piece = hidden // team
+
+    def piece(w, count):
+        return lax.dynamic_slice_in_dim(w, member * count, count, 0)
+
+    wg_piece, wu_piece, wd_piece = [piece(w, hidden_piece) for w in (wg_own, wu_own, wd_own)]
+    packed_dy = mm(pack, cotangent).astype(BF16)
+    packed, packed_dy = tie(packed, packed_dy)
+    arrived, wq_z, wo_z = open_moves(
+        packed.reshape(dp_count, share, width + META),
+        piece(w_query, piece_rows),
+        piece(w_out, out_rows),
+        tensor_count,
     )
-    arrived = deal(packed)
-    packed_dy = mm(pack, cotangent).astype(BF16)
-    wg_own = flat(w_gate)
-    wq_piece = lax.dynamic_slice_in_dim(w_query, member * piece_rows, piece_rows, 0)
-    wq_z = z_gather(wq_piece)
-
-    out_rows = query_cols // team
-    wo_piece = lax.dynamic_slice_in_dim(w_out, member * out_rows, out_rows, 0)
-    wo_z = z_gather(wo_piece)
-    wd_own = w_down.reshape(hidden, width)
-    wu_own = flat(w_up)
-    gu_piece = jnp.concatenate(
-        [
-            lax.dynamic_slice_in_dim(w, member * piece_rows, piece_rows, 0)
-            for w in (wg_own, wu_own)
-        ],
-        axis=1,
-    )
-    hidden_piece = hidden // team
-    wd_piece = lax.dynamic_slice_in_dim(wd_own, member * hidden_piece, hidden_piece, 0)
-    gu_moved = z_move(gu_piece, far)
-    arrived, packed_dy, wq_z, wo_z, wg_own, wu_own, wd_piece = tie(
-        arrived, packed_dy, wq_z, wo_z, wg_own, wu_own, wd_piece
-    )
+    arrived = arrived.reshape(rows, width + META)
     wq_all = team_gather(wq_z).reshape(team, tensor_count, piece_rows, query_cols)
     wo_all = team_gather(wo_z).reshape(team, tensor_count, out_rows, width)
     wo = wo_all.transpose(1, 0, 2, 3).reshape(tensor_count * query_cols, width)
@@ -922,7 +1227,8 @@
         tensor_count,
     )
     arrived_dy = arrived_dy.reshape(rows, width)
-    kv, n1, gu_moved = tie(kv, n1, gu_moved)
+    kv, n1, wg_piece, wu_piece = tie(kv, n1, wg_piece, wu_piece)
+    wg_moved, wu_moved = z_move(wg_piece, far), z_move(wu_piece, far)
 
     def kept_gates(routed, weight, at):
         block = (z - 1 - jnp.arange(tensor_count, dtype=jnp.int32)) % tensor_count
@@ -938,14 +1244,15 @@
     gate_near = kept_gates(
         marks_near[:, :experts_n], marks_near[:, experts_n : 2 * experts_n], z + 1 - 2 * (z % 2)
     )
-    q = project_query(n1, wq_all, cos_full, sin_full)
+    q = project_query(z_arg, n1, wq_all, cos_full, sin_full)
     dy_rows = mm(unpack, arrived_dy).astype(BF16)
     q, dy_rows, gate_own, gate_near = tie(q, dy_rows, gate_own, gate_near)
     dy_near = z_move(dy_rows, near)
     kvs = (kv_two, kv_one, kv)
     o, lse = attend(z_arg, start, q, kvs, kv_heads)
-    o, wd_piece, gu_moved, dy_near = tie(o, wd_piece, gu_moved, dy_near)
-    gu_far = team_gather(gu_moved)
+    o, wd_piece, wg_moved, wu_moved = tie(o, wd_piece, wg_moved, wu_moved)
+    wg_far = team_gather(wg_moved)
+    wu_far = team_gather(wu_moved)
     h = x_rows + mm(o, wo)
     inv_two = lax.rsqrt(jnp.mean(h * h, axis=1, keepdims=True) + EPS)
     n2 = (h * inv_two * gain_moe).astype(BF16)
@@ -963,12 +1270,6 @@
 
     def dp_sum(x):
         return lax.psum_scatter(x, "dp", scatter_dimension=0, tiled=True)
-
-    def unit_start(jobs, send_lefts, rights):
-        return dp_move(gradients(jobs, send_lefts, rights), 1)
-
-    def unit_keep(jobs, keep_lefts, rights, got):
-        return gradients(jobs, keep_lefts, rights, got)
 
     def first_moves(parts):
         return parts[0], dp_move(parts[1], xy[0]), parts[2], dp_move(parts[3], yx[0])
@@ -989,36 +1290,41 @@
 
     xy, yx = (2, 4), (4, 2)
     n2_near = z_move(n2, near)
-    ff = gu_far.shape[1] // 1024
     y, dn2, *own_grads = experts(0, n2, dy_rows, gate_own, wg_own, wu_own, wd_own)
     n2_near, y, dy_near, wd_piece = tie(n2_near, y, dy_near, wd_piece)
     wd_moved = z_move(wd_piece, far)
-    wd_far = team_gather(wd_moved)
     yn, dnn, *own_grads = experts(
         1, n2_near, dy_near, gate_near, wg_own, wu_own, wd_own, filled=own_grads
     )
+    yn, wd_moved, *own_grads = tie(yn, wd_moved, *own_grads)
+    wd_far = team_gather(wd_moved)
     dy_a = turned((dy_rows, dy_near), *orders_a, *orders_b)
     n2_a = turned((n2, n2_near), *orders_a, *orders_b)
     if halving:
-        own_grads = own_grads[::-1]
-        got = unit_start(EXPERT_JOBS, expert_lefts(n2_a, dy_a, 0), own_grads)
-        own = unit_keep(EXPERT_JOBS, expert_lefts(n2_a, dy_a, 1), own_grads, got)
-        gu_far, *own = tie(gu_far, *own)
+        own = gradients(
+            EXPERT_JOBS,
+            expert_lefts(n2_a, dy_a, 0),
+            expert_lefts(n2_a, dy_a, 1),
+            own_grads[::-1],
+            3,
+        )
+        wg_far, *own = tie(wg_far, *own)
         own = first_moves(own)
     yn, dnn, *far_grads = experts(
-        1, n2_near, dy_near, gate_near, gu_far, gu_far, wd_far, (yn, dnn), up_at=ff
+        1, n2_near, dy_near, gate_near, wg_far, wu_far, wd_far, (yn, dnn)
     )
     dnn_moved = z_move(dnn.astype(BF16), near)
-    yn_moved = z_move(yn.astype(BF16), near)
     y, dn2, *far_grads = experts(
-        0, n2, dy_rows, gate_own, gu_far, gu_far, wd_far, (y, dn2), far_grads, up_at=ff
+        0, n2, dy_rows, gate_own, wg_far, wu_far, wd_far, (y, dn2), far_grads
     )
     if halving:
         far_grads = far_grads[::-1]
-        far_sent = gradients(EXPERT_JOBS, expert_lefts(n2_a, dy_a, 0), far_grads)
+        far_sent = gradient_parts(EXPERT_JOBS, expert_lefts(n2_a, dy_a, 0), far_grads)
         dnn_moved, far_sent, *own = tie(dnn_moved, far_sent, *own)
         got = dp_move(far_sent, 1)
         own = second_moves(own)
+    yn, dnn_moved = tie(yn, dnn_moved)
+    yn_moved = z_move(yn.astype(BF16), near)
     dn2 = dn2 + dnn_moved.astype(F32)
 
     gain_two_part = jnp.sum(dn2 * h * inv_two, axis=0)
@@ -1029,33 +1335,35 @@
     dhb = dh.astype(BF16)
     do = mm_nt(dhb, wo).astype(BF16)
     if halving:
-        far_w = unit_keep(EXPERT_JOBS, expert_lefts(n2_a, dy_a, 1), far_grads, got)
+        far_w = gradient_parts(EXPERT_JOBS, expert_lefts(n2_a, dy_a, 1), far_grads, got)
         do, *far_w = tie(do, *far_w)
         far_w = first_moves(far_w)
     result = h + y + yn_moved.astype(F32)
     result_out = mm_tn(unpack, result.astype(BF16)).astype(BF16)
-    do, result_out = tie(do, result_out)
+    if halving:
+        do, result_out, *own = tie(do, result_out, *own)
+    else:
+        do, result_out = tie(do, result_out)
 
     dq, dkv_two, dkv_one, dkv = attend_back(
         z_arg, start, q, o, do, lse, cos_full, sin_full, kvs, kv_heads
     )
-    dkv_one = z_move(dkv_one, [(b, a) for a, b in up_one])
-    dkv_two = z_move(dkv_two, [(b, a) for a, b in up_two])
     n1_t = turned((n1,), *orders_a, *orders_b)
     dhb_t = turned((dhb,), *orders_b)
     if halving:
         dq, *far_w = tie(dq, *far_w)
-        far_w = second_moves(far_w)
-        got = unit_start(ATTENTION_JOBS, (n1_t[0], dhb_t[0]), (dq, o))
-        parts = unit_keep(ATTENTION_JOBS, (n1_t[1], dhb_t[1]), (dq, o), got)
-        dkv_one, dkv_two, *rest = tie(dkv_one, dkv_two, *parts, *far_w)
-        parts, far_w = rest[:4], rest[4:]
-        far_sums = [z_move(part.astype(BF16), far) for part in unit_end(far_w)]
+        *parts, dkv_sum, far_sum = mix(
+            dq, o, (n1_t[0], n1_t[1], *dhb_t), dkv_one, dkv_two, far_w
+        )
+        far_sum = z_move(far_sum, far)
     else:
+        dkv_one = z_move(dkv_one, [(b, a) for a, b in up_one])
+        dkv_two = z_move(dkv_two, [(b, a) for a, b in up_two])
+        dkv_sum = dkv_one.astype(F32) + dkv_two.astype(F32)
         sum_q, sum_o = [
             dp_sum(mm_tn(a, b).astype(BF16)).astype(F32) for a, b in ((n1, dq), (dhb, o))
         ]
-    dkv = dkv + dkv_one.astype(F32) + dkv_two.astype(F32)
+    dkv = dkv + dkv_sum.astype(F32)
 
     def unrotate(u):
         swapped = jnp.concatenate([u[:, HD // 2 :], u[:, : HD // 2]], axis=1)
@@ -1066,7 +1374,7 @@
         + [dkv[:, kv_heads * HD :]],
         axis=1,
     ).astype(BF16)
-    dn1 = project_back(dq, wq_all, dkv, w_keyval)
+    dn1 = project_back(z_arg, dq, wq_all, dkv, w_keyval)
     gain_one_part = jnp.sum(dn1 * x_rows * inv_one, axis=0)
     u1 = dn1 * gain_attn
     dx = dh + inv_one * (
@@ -1076,7 +1384,7 @@
     outputs = mm_tn(pack, deal(result_out)).astype(BF16)
 
     if halving:
-        first, second = [a + b.astype(F32) for a, b in zip(unit_end(own), far_sums)]
+        first, second = [a + b.astype(F32) for a, b in zip(unit_end(own), far_sum)]
         sum_gu = jnp.concatenate([first[:, :hidden], second[:, :hidden]], axis=1)
         sum_down = jnp.concatenate([first[:, hidden:], second[:, hidden:]], axis=1)
     else:

time: 791 us -> 673 us (0.85)
  waiting for transfers between devices: 99.1 us -> 72.8 us
  local copies, waits for them, and re-layouts: 93.4 us -> 67.4 us
  starting transfers between devices: 39.9 us -> 17 us
  Pallas kernels: 458 us -> 438 us
  other arithmetic: 43.1 us -> 26.2 us
    pallas_call x8 -> x7, Pallas kernels: 95 us -> 144 us  [the longest x1 35.4 us: mix(): pl.pallas_call(mix_kernel, in_specs=[vmem] * 12, out_specs=[vmem] * 6, ou...]
    pallas_call x1, Pallas kernels: 73.7 us -> 33.9 us  [keyval(): pl.pallas_call(keyval_kernel, in_specs=[vmem] * 7, out_specs=[vmem] * 6,...]
    ppermute x16 -> x8, waiting for transfers between devices: 82.7 us -> 67.6 us  [z_move(): return lax.ppermute(x, 'tensor', pairs)]
    ppermute x16 -> x8, starting transfers between devices: 22.3 us -> 7.35 us  [z_move(): return lax.ppermute(x, 'tensor', pairs)]
    pallas_call x1, Pallas kernels: 111 us -> 96.7 us  [finish(): pl.pallas_call(finish_kernel, in_specs=[vmem] * 7, out_specs=[vmem] * 3,...]
    reshape x2 -> x0, local copies, waits for them, and re-layouts: 13.3 us -> none  [flat(): return row_major(w.transpose(1, 0, 2).reshape(w.shape[1], hidden))]
    dynamic_update_slice x8 -> x0, local copies, waits for them, and re-layouts: 11.8 us -> none  [z_gather(): parts = lax.dynamic_update_slice_in_dim(parts, part[None], z ^ m, 0)]
    ppermute x11 -> x7, waiting for transfers between devices: 11.6 us -> 0.02 us  [dp_move(): return lax.ppermute(x, 'dp', [(i, i ^ bit) for i in range(dp_count)])]
  transfers between devices with their start and end apart: 33 -> 21, of which waited for: 7 -> 6; matrix products, arithmetic and copies ran while one was open for 14% -> 10% of each run, Pallas kernels for 54% -> 56%
where the time goes in v3:
time: 673 us; the launch traced here: 668 us
  Pallas kernels  438 us (65%)
  waiting for transfers between devices  72.8 us (11%)
  local copies, waits for them, and re-layouts  67.4 us (10%)
  matrix products  31.3 us (5%)
  other arithmetic  26.2 us (4%)
  starting transfers between devices  17 us (3%)
  between operations  14.9 us (2%)
    pallas_call x1, Pallas kernels, finish(): pl.pallas_call(finish_kernel, in_specs=[vmem] * 7, out_specs=[vmem] * 3,...  96.7 us
    pallas_call x4, Pallas kernels, experts(): pl.pallas_call(functools.partial(expert_kernel, chunk, before is None), g...  94.6 us
    ppermute x8, waiting for transfers between devices, z_move(): return lax.ppermute(x, 'tensor', pairs)  67.6 us
    pallas_call x1, Pallas kernels, mix(): pl.pallas_call(mix_kernel, in_specs=[vmem] * 12, out_specs=[vmem] * 6, ou...  35.4 us
    pallas_call x1, Pallas kernels, keyval(): pl.pallas_call(keyval_kernel, in_specs=[vmem] * 7, out_specs=[vmem] * 6,...  33.9 us
    pallas_call x1, Pallas kernels, open_moves(): pl.pallas_call(open_kernel, in_specs=[vmem] * 3, out_specs=[vmem] * 3, ou...  31.5 us
    pallas_call x2, Pallas kernels, gradient_parts(): pl.pallas_call(functools.partial(part_kernel, jobs, len(lefts), len(right...  31.3 us
    pallas_call x1, Pallas kernels, attend_back(): pl.pallas_call(functools.partial(attend_back_kernel, kv_heads), grid_spec...  29.9 us
  transfers between devices with their start and end apart: 21, of which 6 were waited for; matrix products, arithmetic and copies ran while one was open for 10% of the time, Pallas kernels for 56%

profile of v3, /device:TPU:0, one launch (start us, length us, event | category | flops | bytes accessed | tf_op | source)
XLA Modules:
  0.0 668.0 jit_solution(2268045346327616734)
XLA Ops:
  10.5 3.8 concatenate.30
  20.9 31.5 %open_moves.1 = (bf16[8,64,1664]{2,1,0:T(8,128)(2,1)S(1)}, bf16[4,192,384]{2,1,0:T(8,128)(2,1)}, bf16[4,48,1536]{2,1,0:T(8,128)(2,1)}) custom-call(bf16[8,64,1664]{2,1,0:T(8,128)(2,1)S(1)} %bitcast.69, bf16[192,384]{1,0:T(8,128)(2,1)S(1)} %constant_dynamic-slice_fusion.12.q_ref, bf16[48,1536]{1,0:T(8,128)(2,1)S(1)} %constant_dynamic-slice_fusion.11.o_ref), custom_call_target="tpu_custom_call" | custom-call | tf_op jit(solution)/shard_map/open_moves/pallas_call | solution.py:99
  66.6 33.9 %keyval.1 = (bf16[512,512]{1,0:T(8,128)(2,1)S(1)}, bf16[512,512]{1,0:T(8,128)(2,1)S(1)}, bf16[512,512]{1,0:T(8,128)(2,1)S(1)}, f32[4,8,128]{2,1,0:T(8,128)S(1)},...) custom-call(bf16[512,1536]{1,0:T(8,128)(2,1)S(1)} %multiply_convert_fusion.1.x_ref.refs_0_, ...), custom_call_target="tpu_custom_call" | custom-call | tf_op jit(solution)/shard_map/keyval/pallas_call | solution.py:194
  117.6 8.1 %project_query.1.q_ref = bf16[512,1536]{1,0:T(8,128)(2,1)} custom-call(s32[1]{0:T(128)} %bitcast.z_ref, bf16[512,1536]{1,0:T(8,128)(2,1)} %copy-done.2, bf16[8,4,192,384]{3,2,1,0:T(8,128)(2,1)} %bitcast.104, f32[512,128]{1,0:T(8,128)} %copy-done.7, f32[512,128]{1,0:T(8,128)} %copy-done.3), custom_call_target="tpu_custom_call" | custom-call | flops 2415919104 | bytes 7864320 | tf_op jit(solution)/shard_map/project_query/pallas_call | solution.py:228
  125.7 22.1 %attend.1 = (bf16[512,1536]{1,0:T(8,128)(2,1)}, f32[12,512,1]{2,1,0:T(8,128)}) custom-call(s32[1]{0:T(128)} %bitcast.z_ref, s32[512,1]{1,0:T(8,128)} %copy.140.start_ref, bf16[512,1536]{1,0:T(8,128)(2,1)} %project_query.1.q_ref, bf16[512,512]{1,0:T(8,128)(2,1)} %copy-done.14, bf16[512,512]{1,0:T(8,128)(2,1)} %copy-done.13, bf16[512,512]{1,0:T(8,128)(2,1)} %copy-done.12), custom_call_target="tpu_custom_call" | custom-call | flops 4831838208 | bytes 6291456 | tf_op jit(solution)/shard_map/attend/pallas_call | solution.py:348
  147.8 10.0 %collective-permute-done.1 = bf16[192,1536]{1,0:T(8,128)(2,1)} collective-permute-done((bf16[192,1536]{1,0:T(8,128)(2,1)}, bf16[192,1536]{1,0:T(8,128)(2,1)}, u32[]{:S(2)}, u32[]{:S(2)}) %collective-permute-start.1) | collective-permute-done | bytes 589856 | tf_op jit(solution)/shard_map/ppermute | solution.py:1119
  169.2 23.0 %experts.4 = (f32[512,1536]{1,0:T(8,128)}, f32[512,1536]{1,0:T(8,128)}, bf16[1024,1536]{1,0:T(8,128)(2,1)}, bf16[1024,3072]{1,0:T(8,128)(2,1)}) custom-call(bf16[512,1536]{1,0:T(8,128)(2,1)} %copy-done.29, bf16[512,1536]{1,0:T(8,128)(2,1)} %copy-done.26, bf16[512,1536]{1,0:T(8,128)(2,1)} %copy.136.gate_ref, bf16[1536,1536]{1,0:T(8,128)(2,1)} %bitcast.92, ...), custom_call_target="tpu_custom_call" | custom-call | flops 14495514624 | bytes 26738688 | tf_op jit(solution)/shard_map/experts/pallas_call | solution.py:542
  192.3 12.2 %collective-permute-done.2.refs_1_.x_ref = bf16[512,1536]{1,0:T(8,128)(2,1)S(1)} collective-permute-done((bf16[512,1536]{1,0:T(8,128)(2,1)S(1)}, bf16[512,1536]{1,0:T(8,128)(2,1)S(1)}, u32[]{:S(2)}, u32[]{:S(2)}) %collective-permute-start.2) | collective-permute-done | bytes 1572896 | tf_op jit(solution)/shard_map/ppermute | solution.py:1119
  204.5 32.5 %collective-permute-done.3.refs_1_.dy_ref = bf16[512,1536]{1,0:T(8,128)(2,1)S(1)} collective-permute-done((bf16[512,1536]{1,0:T(8,128)(2,1)S(1)}, bf16[512,1536]{1,0:T(8,128)(2,1)S(1)}, u32[]{:S(2)}, u32[]{:S(2)}) %collective-permute-start.3) | collective-permute-done | bytes 1572896 | tf_op jit(solution)/shard_map/ppermute | solution.py:1119
  238.1 22.7 %experts.5 = (f32[512,1536]{1,0:T(8,128)}, f32[512,1536]{1,0:T(8,128)}, bf16[1024,1536]{1,0:T(8,128)(2,1)}, bf16[1024,3072]{1,0:T(8,128)(2,1)}) custom-call(bf16[512,1536]{1,0:T(8,128)(2,1)} %copy-done.38, bf16[512,1536]{1,0:T(8,128)(2,1)} %copy-done.39, bf16[512,1536]{1,0:T(8,128)(2,1)} %copy.139.gate_ref, ...), custom_call_target="tpu_custom_call", output_to_operand_aliasing={{2}: (6, {}), {3}: (7, {})} | custom-call | flops 14495514624 | bytes 26738688 | tf_op jit(solution)/shard_map/experts/pallas_call | solution.py:542
  260.8 3.8 collective-permute-done.4
  265.5 5.3 turn.5
  270.8 5.2 turn.4
  276.1 27.5 %gradients.1 = (bf16[384,2304]{1,0:T(8,128)(2,1)}, bf16[384,2304]{1,0:T(8,128)(2,1)}, bf16[384,2304]{1,0:T(8,128)(2,1)}, bf16[384,2304]{1,0:T(8,128)(2,1)}) custom-call(bf16[768,1024]{1,0:T(8,128)(2,1)} %get-tuple-element.147.refs_0_, bf16[768,1024]{1,0:T(8,128)(2,1)} %get-tuple-element.149.refs_1_, bf16[768,1024]{1,0:T(8,128)(2,1)} %get-tuple-element.150.refs_2_, ...), custom_call_target="tpu_custom_call" | custom-call | flops 1000000000 | bytes 1000000 | tf_op jit(solution)/shard_map/gradients/pallas_call | solution.py:638
  305.0 24.4 %experts.6 = (f32[512,1536]{1,0:T(8,128)}, f32[512,1536]{1,0:T(8,128)}, bf16[1024,1536]{1,0:T(8,128)(2,1)}, bf16[1024,3072]{1,0:T(8,128)(2,1)}) custom-call(bf16[512,1536]{1,0:T(8,128)(2,1)} %copy-done.38, bf16[512,1536]{1,0:T(8,128)(2,1)} %copy-done.39, bf16[512,1536]{1,0:T(8,128)(2,1)} %copy.139.gate_ref, ...), custom_call_target="tpu_custom_call" | custom-call | flops 14495514624 | bytes 26738688 | tf_op jit(solution)/shard_map/experts/pallas_call | solution.py:542
  331.5 24.5 %experts.7 = (f32[512,1536]{1,0:T(8,128)}, f32[512,1536]{1,0:T(8,128)}, bf16[1024,1536]{1,0:T(8,128)(2,1)}, bf16[1024,3072]{1,0:T(8,128)(2,1)}) custom-call(bf16[512,1536]{1,0:T(8,128)(2,1)} %copy-done.29, bf16[512,1536]{1,0:T(8,128)(2,1)} %copy-done.26, bf16[512,1536]{1,0:T(8,128)(2,1)} %copy.136.gate_ref, ...), custom_call_target="tpu_custom_call", output_to_operand_aliasing={{2}: (8, {}), {3}: (9, {})} | custom-call | flops 14495514624 | bytes 26738688 | tf_op jit(solution)/shard_map/experts/pallas_call | solution.py:542
  356.1 14.7 %gradient_parts.2 = bf16[2,768,2304]{2,1,0:T(8,128)(2,1)} custom-call(bf16[768,1024]{1,0:T(8,128)(2,1)} %get-tuple-element.147.refs_0_, bf16[768,1024]{1,0:T(8,128)(2,1)} %get-tuple-element.149.refs_1_, bf16[768,1024]{1,0:T(8,128)(2,1)} %get-tuple-element.150.refs_2_, bf16[768,1024]{1,0:T(8,128)(2,1)} %get-tuple-element.151.refs_3_, ...), custom_call_target="tpu_custom_call" | custom-call | flops 7247757312 | bytes 16515072 | tf_op jit(solution)/shard_map/gradient_parts/pallas_call | solution.py:702
  388.7 3.8 convolution_convert_fusion.6.do_ref
  392.4 16.6 %gradient_parts.3 = (bf16[384,2304]{1,0:T(8,128)(2,1)}, bf16[384,2304]{1,0:T(8,128)(2,1)}, bf16[384,2304]{1,0:T(8,128)(2,1)}, bf16[384,2304]{1,0:T(8,128)(2,1)}) custom-call(bf16[768,1024]{1,0:T(8,128)(2,1)} %get-tuple-element.152.refs_4_.refs_0_, bf16[768,1024]{1,0:T(8,128)(2,1)} %get-tuple-element.153.refs_5_.refs_1_, ...), custom_call_target="tpu_custom_call" | custom-call | flops 7247757312 | bytes 16515072 | tf_op jit(solution)/shard_map/gradient_parts/pallas_call | solution.py:702
  410.3 9.0 %collective-permute-done.9 = bf16[512,1536]{1,0:T(8,128)(2,1)} collective-permute-done((bf16[512,1536]{1,0:T(8,128)(2,1)}, bf16[512,1536]{1,0:T(8,128)(2,1)}, u32[]{:S(2)}, u32[]{:S(2)}) %collective-permute-start.9) | collective-permute-done | bytes 1572896 | tf_op jit(solution)/shard_map/ppermute | solution.py:1119
  419.3 3.6 convolution_convert_fusion.3
  422.9 3.8 all-to-all-start
  426.7 3.6 turn.6
  430.2 3.1 turn.7
  433.4 29.9 %attend_back.1 = (bf16[512,1536]{1,0:T(8,128)(2,1)}, bf16[512,512]{1,0:T(8,128)(2,1)}, bf16[512,512]{1,0:T(8,128)(2,1)}, f32[512,512]{1,0:T(8,128)}) custom-call(s32[1]{0:T(128)} %bitcast.z_ref, s32[512,1]{1,0:T(8,128)} %copy.140.start_ref, bf16[512,1536]{1,0:T(8,128)(2,1)} %project_query.1.q_ref, bf16[512,1536]{1,0:T(8,128)(2,1)} %get-tuple-element.140.o_ref, ...), custom_call_target="tpu_custom_call" | custom-call | flops 12079595520 | bytes 9437184 | tf_op jit(solution)/shard_map/attend_back/pallas_call | solution.py:453
  463.3 3.9 all-to-all-done
  469.4 35.4 %mix.1 = (bf16[384,1536]{1,0:T(8,128)(2,1)}, bf16[384,1536]{1,0:T(8,128)(2,1)}, bf16[384,1536]{1,0:T(8,128)(2,1)}, bf16[384,1536]{1,0:T(8,128)(2,1)}, bf16[512,5...) custom-call(bf16[512,1536]{1,0:T(8,128)(2,1)} %get-tuple-element.209.dq_ref, bf16[512,1536]{1,0:T(8,128)(2,1)} %get-tuple-element.140.o_ref, ...), custom_call_target="tpu_custom_call" | custom-call | tf_op jit(solution)/shard_map/mix/pallas_call | solution.py:836
  508.2 10.2 %project_back.1 = f32[512,1536]{1,0:T(8,128)} custom-call(s32[1]{0:T(128)} %bitcast.z_ref, bf16[512,1536]{1,0:T(8,128)(2,1)} %get-tuple-element.209.dq_ref, bf16[8,4,192,384]{3,2,1,0:T(8,128)(2,1)} %bitcast.105, bf16[512,512]{1,0:T(8,128)(2,1)} %pad_maximum_fusion.2.dkv_ref, bf16[1536,512]{1,0:T(8,128)(2,1)} %wkv_ref.1), custom_call_target="tpu_custom_call" | custom-call | flops 3221225472 | bytes 9437184 | tf_op jit(solution)/shard_map/project_back/pallas_call | solution.py:272
  527.0 4.5 convolution_convert_fusion.1
  531.5 96.7 %finish.1 = (bf16[8,64,1536]{2,1,0:T(8,128)(2,1)}, f32[192,768]{1,0:T(8,128)}, f32[192,640]{1,0:T(8,128)}) custom-call(bf16[8,64,1536]{2,1,0:T(8,128)(2,1)} %bitcast.78, bf16[384,1536]{1,0:T(8,128)(2,1)} %get-tuple-element.222.q_keep, bf16[384,1536]{1,0:T(8,128)(2,1)} %get-tuple-element.223.q_send, bf16[384,1536]{1,0:T(8,128)(2,1)} %get-tuple-element.224.o_keep, ...), custom_call_target="tpu_custom_call" | custom-call | tf_op jit(solution)/shard_map/finish/pallas_call | solution.py:994
  644.0 4.2 reshape.196
  648.2 5.4 fusion.39
  (258 shorter events, 114.2 us)
Async XLA Ops:
  7.2 110.4 %all-gather.6.cloned.1.call-start = ((), (), s32[]{:S(2)}) async-start(), calls=%async_computation.1 | async-start | bytes 5308416 | tf_op jit(solution)/shard_map/all_gather | solution.py:1133
  53.6 104.9 %all-gather.8.cloned.1.call-start = ((), (), s32[]{:S(2)}) async-start(), calls=%async_computation.2 | async-start | bytes 5308416 | tf_op jit(solution)/shard_map/all_gather | solution.py:1133
  54.3 249.3 %all-gather.10.cloned.1.call-start = ((), (), s32[]{:S(2)}) async-start(), calls=%async_computation.3 | async-start | bytes 5308416 | tf_op jit(solution)/shard_map/all_gather | solution.py:1133
  64.7 35.8 %copy-start.2 = (bf16[512,1536]{1,0:T(8,128)(2,1)}, bf16[512,1536]{1,0:T(8,128)(2,1)S(1)}, u32[]{:S(2)}) copy-start(bf16[512,1536]{1,0:T(8,128)(2,1)S(1)} %multiply_convert_fusion.1.x_ref.refs_0_) | copy-start | bytes 4718596
  106.4 41.4 %collective-permute-start = (bf16[192,1536]{1,0:T(8,128)(2,1)}, bf16[192,1536]{1,0:T(8,128)(2,1)}, u32[]{:S(2)}, u32[]{:S(2)}) collective-permute-start(bf16[192,1536]{1,0:T(8,128)(2,1)} %get-tuple-element.138), channel_id=1, source_target_pairs={{0,2},{1,3},{2,0},{3,1},{4,6},{5,7},{6,4},{7,5},{8,10},{9,11},{10,... | collective-permute-start | bytes 1769480 | tf_op jit(solution)/shard_map/ppermute | solution.py:1119
  106.4 51.5 %collective-permute-start.1 = (bf16[192,1536]{1,0:T(8,128)(2,1)}, bf16[192,1536]{1,0:T(8,128)(2,1)}, u32[]{:S(2)}, u32[]{:S(2)}) collective-permute-start(bf16[192,1536]{1,0:T(8,128)(2,1)} %get-tuple-element.139), channel_id=1, source_target_pairs={{0,2},{1,3},{2,0},{3,1},{4,6},{5,7},{6,4},{7,5},{8,10},{9,11},{10,... | collective-permute-start | bytes 1769480 | tf_op jit(solution)/shard_map/ppermute | solution.py:1119
  117.5 49.7 %copy-start.26 = (bf16[512,1536]{1,0:T(8,128)(2,1)}, bf16[512,1536]{1,0:T(8,128)(2,1)S(1)}, u32[]{:S(2)}) copy-start(bf16[512,1536]{1,0:T(8,128)(2,1)S(1)} %convolution_convert_fusion.4.dy_ref.refs_0_) | copy-start | bytes 4718596
  157.9 147.1 %all-gather.12.cloned.1.call-start = ((), (), s32[]{:S(2)}) async-start(), calls=%async_computation.4 | async-start | bytes 5308416 | tf_op jit(solution)/shard_map/all_gather | solution.py:1133
  158.5 146.5 %all-gather.14.cloned.1.call-start = ((), (), s32[]{:S(2)}) async-start(), calls=%async_computation.5 | async-start | bytes 5308416 | tf_op jit(solution)/shard_map/all_gather | solution.py:1133
  167.2 69.8 %copy-start.41 = (bf16[192,1536]{1,0:T(8,128)(2,1)S(1)}, bf16[192,1536]{1,0:T(8,128)(2,1)}, u32[]{:S(2)}) copy-start(bf16[192,1536]{1,0:T(8,128)(2,1)} %constant_dynamic-slice_fusion.8) | copy-start | bytes 1769476
  167.2 37.3 %collective-permute-start.2 = (bf16[512,1536]{1,0:T(8,128)(2,1)S(1)}, bf16[512,1536]{1,0:T(8,128)(2,1)S(1)}, u32[]{:S(2)}, u32[]{:S(2)}) collective-permute-start(bf16[512,1536]{1,0:T(8,128)(2,1)S(1)} %multiply_convert_fusion.x_ref.refs_0_), channel_id=1, source_target_pairs={{0,1},{1,0},{2,3},{3,2},{4,5},{5,4},{6,7},{7,6},{8,9},{9,8},{10,11... | collective-permute-start | bytes 4718600 | tf_op jit(solution)/shard_map/ppermute | solution.py:1119
  167.2 69.8 %collective-permute-start.3 = (bf16[512,1536]{1,0:T(8,128)(2,1)S(1)}, bf16[512,1536]{1,0:T(8,128)(2,1)S(1)}, u32[]{:S(2)}, u32[]{:S(2)}) collective-permute-start(bf16[512,1536]{1,0:T(8,128)(2,1)S(1)} %convolution_convert_fusion.4.dy_ref.refs_0_), channel_id=1, source_target_pairs={{0,1},{1,0},{2,3},{3,2},{4,5},{5,4},{6,7},{7,6},{8,9},{9,8},{10,11... | collective-permute-start | bytes 4718600 | tf_op jit(solution)/shard_map/ppermute | solution.py:1119
  204.5 32.5 %copy-start.38 = (bf16[512,1536]{1,0:T(8,128)(2,1)}, bf16[512,1536]{1,0:T(8,128)(2,1)S(1)}, u32[]{:S(2)}) copy-start(bf16[512,1536]{1,0:T(8,128)(2,1)S(1)} %collective-permute-done.2.refs_1_.x_ref) | copy-start | bytes 4718596
  237.0 27.7 %collective-permute-start.4 = (bf16[192,1536]{1,0:T(8,128)(2,1)S(1)}, bf16[192,1536]{1,0:T(8,128)(2,1)S(1)}, u32[]{:S(2)}, u32[]{:S(2)}) collective-permute-start(bf16[192,1536]{1,0:T(8,128)(2,1)S(1)} %copy-done.41), channel_id=1, source_target_pairs={{0,2},{1,3},{2,0},{3,1},{4,6},{5,7},{6,4},{7,5},{8,10},{9,11},{10,... | collective-permute-start | bytes 1769480 | tf_op jit(solution)/shard_map/ppermute | solution.py:1119
  303.6 67.1 %collective-permute-start.6 = (bf16[384,2304]{1,0:T(8,128)(2,1)}, bf16[384,2304]{1,0:T(8,128)(2,1)S(1)}, u32[]{:S(2)}, u32[]{:S(2)}) collective-permute-start(bf16[384,2304]{1,0:T(8,128)(2,1)} %get-tuple-element.184), channel_id=1, source_target_pairs={{0,8},{4,12},{8,0},{12,4},{16,24},{20,28},{24,16},{28,20},{1,9},{5... | collective-permute-start | bytes 5308424 | tf_op jit(solution)/shard_map/ppermute | solution.py:1122
  304.9 65.8 %collective-permute-start.7 = (bf16[384,2304]{1,0:T(8,128)(2,1)}, bf16[384,2304]{1,0:T(8,128)(2,1)}, u32[]{:S(2)}, u32[]{:S(2)}) collective-permute-start(bf16[384,2304]{1,0:T(8,128)(2,1)} %get-tuple-element.186), channel_id=1, source_target_pairs={{0,16},{4,20},{8,24},{12,28},{16,0},{20,4},{24,8},{28,12},{1,17},{... | collective-permute-start | bytes 5308424 | tf_op jit(solution)/shard_map/ppermute | solution.py:1122
  331.5 39.3 %collective-permute-start.5 = (bf16[512,1536]{1,0:T(8,128)(2,1)S(1)}, bf16[512,1536]{1,0:T(8,128)(2,1)S(1)}, u32[]{:S(2)}, u32[]{:S(2)}) collective-permute-start(bf16[512,1536]{1,0:T(8,128)(2,1)S(1)} %convert_element_type.194), channel_id=1, source_target_pairs={{0,1},{1,0},{2,3},{3,2},{4,5},{5,4},{6,7},{7,6},{8,9},{9,8},{10,11... | collective-permute-start | bytes 4718600 | tf_op jit(solution)/shard_map/ppermute | solution.py:1119
  356.1 14.8 %copy-start.36 = (bf16[384,2304]{1,0:T(8,128)(2,1)S(1)}, bf16[384,2304]{1,0:T(8,128)(2,1)}, u32[]{:S(2)}) copy-start(bf16[384,2304]{1,0:T(8,128)(2,1)} %get-tuple-element.199) | copy-start | bytes 5308420
  370.8 21.7 %collective-permute-start.8 = (bf16[2,768,2304]{2,1,0:T(8,128)(2,1)}, bf16[2,768,2304]{2,1,0:T(8,128)(2,1)}, u32[]{:S(2)}, u32[]{:S(2)}) collective-permute-start(bf16[2,768,2304]{2,1,0:T(8,128)(2,1)} %gradient_parts.2), channel_id=1, source_target_pairs={{0,4},{4,0},{8,12},{12,8},{16,20},{20,16},{24,28},{28,24},{1,5},{5... | collective-permute-start | bytes 21233672 | tf_op jit(solution)/shard_map/ppermute | solution.py:1122
  378.4 44.5 %collective-permute-start.11 = (bf16[192,2304]{1,0:T(8,128)(2,1)}, bf16[192,2304]{1,0:T(8,128)(2,1)}, u32[]{:S(2)}, u32[]{:S(2)}) collective-permute-start(bf16[192,2304]{1,0:T(8,128)(2,1)} %slice.196), channel_id=1, source_target_pairs={{0,8},{4,12},{8,0},{12,4},{16,24},{20,28},{24,16},{28,20},{1,9},{5... | collective-permute-start | bytes 2654216 | tf_op jit(solution)/shard_map/ppermute | solution.py:1122
  380.3 42.6 %collective-permute-start.10 = (bf16[192,2304]{1,0:T(8,128)(2,1)}, bf16[192,2304]{1,0:T(8,128)(2,1)}, u32[]{:S(2)}, u32[]{:S(2)}) collective-permute-start(bf16[192,2304]{1,0:T(8,128)(2,1)} %slice.197), channel_id=1, source_target_pairs={{0,16},{4,20},{8,24},{12,28},{16,0},{20,4},{24,8},{28,12},{1,17},{... | collective-permute-start | bytes 2654216 | tf_op jit(solution)/shard_map/ppermute | solution.py:1122
  382.5 36.8 %collective-permute-start.9 = (bf16[512,1536]{1,0:T(8,128)(2,1)}, bf16[512,1536]{1,0:T(8,128)(2,1)}, u32[]{:S(2)}, u32[]{:S(2)}) collective-permute-start(bf16[512,1536]{1,0:T(8,128)(2,1)} %convert_element_type.198), channel_id=1, source_target_pairs={{0,1},{1,0},{2,3},{3,2},{4,5},{5,4},{6,7},{7,6},{8,9},{9,8},{10,11... | collective-permute-start | bytes 4718600 | tf_op jit(solution)/shard_map/ppermute | solution.py:1119
  392.4 26.9 %copy-start.32 = (f32[512,1536]{1,0:T(8,128)S(1)}, f32[512,1536]{1,0:T(8,128)}, u32[]{:S(2)}) copy-start(f32[512,1536]{1,0:T(8,128)} %get-tuple-element.195) | copy-start | bytes 9437188
  409.0 60.3 %collective-permute-start.12 = (bf16[384,2304]{1,0:T(8,128)(2,1)}, bf16[384,2304]{1,0:T(8,128)(2,1)}, u32[]{:S(2)}, u32[]{:S(2)}) collective-permute-start(bf16[384,2304]{1,0:T(8,128)(2,1)} %get-tuple-element.206), channel_id=1, source_target_pairs={{0,8},{4,12},{8,0},{12,4},{16,24},{20,28},{24,16},{28,20},{1,9},{5... | collective-permute-start | bytes 5308424 | tf_op jit(solution)/shard_map/ppermute | solution.py:1122
  410.2 59.1 %collective-permute-start.13 = (bf16[384,2304]{1,0:T(8,128)(2,1)}, bf16[384,2304]{1,0:T(8,128)(2,1)}, u32[]{:S(2)}, u32[]{:S(2)}) collective-permute-start(bf16[384,2304]{1,0:T(8,128)(2,1)} %get-tuple-element.208), channel_id=1, source_target_pairs={{0,16},{4,20},{8,24},{12,28},{16,0},{20,4},{24,8},{28,12},{1,17},{... | collective-permute-start | bytes 5308424 | tf_op jit(solution)/shard_map/ppermute | solution.py:1122
  422.9 44.3 %all-to-all-start = ((bf16[8,64,1536]{2,1,0:T(8,128)(2,1)}), bf16[8,64,1536]{2,1,0:T(8,128)(2,1)S(1)}, u32[]{:S(2)}, u32[]{:S(2)}) async-start(bf16[8,64,1536]{2,1,0:T(8,128)(2,1)} %bitcast.24), calls=%async_computation | async-start | bytes 3145728 | tf_op jit(solution)/shard_map/all_to_all | solution.py:1128
  433.4 33.8 %copy-start.50 = (s32[512]{0:T(512)S(1)}, s32[512]{0:T(512)}, u32[]{:S(2)}) copy-start(s32[512]{0:T(512)} %copy-done.49) | copy-start | bytes 6148
  469.3 35.4 %copy-start.40 = (f32[512,512]{1,0:T(8,128)S(1)}, f32[512,512]{1,0:T(8,128)}, u32[]{:S(2)}) copy-start(f32[512,512]{1,0:T(8,128)} %get-tuple-element.210) | copy-start | bytes 3145732
  506.3 129.7 %collective-permute-start.14 = (bf16[2,192,2304]{2,1,0:T(8,128)(2,1)}, bf16[2,192,2304]{2,1,0:T(8,128)(2,1)S(1)}, u32[]{:S(2)}, u32[]{:S(2)}) collective-permute-start(bf16[2,192,2304]{2,1,0:T(8,128)(2,1)} %get-tuple-element.233), channel_id=1, source_target_pairs={{0,2},{1,3},{2,0},{3,1},{4,6},{5,7},{6,4},{7,5},{8,10},{9,11},{10,... | collective-permute-start | bytes 5308424 | tf_op jit(solution)/shard_map/ppermute | solution.py:1119
  508.2 10.2 %copy-start.18 = (f32[512,1664]{1,0:T(8,128)S(1)}, f32[512,1664]{1,0:T(8,128)}, u32[]{:S(2)}) copy-start(f32[512,1664]{1,0:T(8,128)} %copy-done.15) | copy-start | bytes 10223620
  508.2 10.2 %copy-start.46 = (f32[1536]{0:T(1024)S(1)}, f32[1536]{0:T(1024)}, u32[]{:S(2)}) copy-start(f32[1536]{0:T(1024)} %param.20) | copy-start | bytes 18436
  508.2 10.2 %copy-start.48 = (f32[512]{0:T(512)S(1)}, f32[512]{0:T(512)}, u32[]{:S(2)}) copy-start(f32[512]{0:T(512)} %copy-done.47) | copy-start | bytes 6148
  (47 other events, 138.3 us)
Sparse Core Ops, SparseCore 0:
  53.7 48.4 all-gather.5
  104.1 38.9 all-gather.7
  158.0 36.4 all-gather.9
  196.3 38.9 all-gather.11
  265.7 35.5 all-gather.13

commit v4 on v3

--- a/solution.py
+++ b/solution.py
@@ -490,8 +490,11 @@
     )(z, start, q, o, do, lse, cos_full, sin_full, *kvs)
 
 
-def expert_kernel(chunk, first, x_ref, dy_ref, gate_ref, wg_ref, wu_ref, wd_ref, *refs):
-    y_ref, dn_ref, hs_ref, dgu_ref = refs[-4:]
+def expert_kernel(chunk, first, last, x_ref, dy_ref, gate_ref, wg_ref, wu_ref, wd_ref, *refs):
+    if last:
+        y_out, dn_out, hs_ref, dgu_ref, y_ref, dn_ref = refs[-6:]
+    else:
+        y_ref, dn_ref, hs_ref, dgu_ref = refs[-4:]
     step = pl.program_id(0)
 
     @pl.when(step == 0)
@@ -517,9 +520,15 @@
     dgu_ref[:, chunk:] = du
     dn_ref[...] += mm(dg, wg_ref[...]) + mm(du, wu_ref[...])
     y_ref[...] += mm(hs, wd_ref[...])
-
-
-def experts(tile, x, dy, gate, wg, wu, wd, before=None, filled=None, chunk=512):
+    if last:
+
+        @pl.when(step == pl.num_programs(0) - 1)
+        def _():
+            y_out[...] = y_ref[...].astype(BF16)
+            dn_out[...] = dn_ref[...].astype(BF16)
+
+
+def experts(tile, x, dy, gate, wg, wu, wd, before=None, filled=None, last=False, chunk=512):
     rows, width = x.shape
     hidden = gate.shape[1]
     full = pl.BlockSpec((rows, width), lambda i: (0, 0))
@@ -540,7 +549,7 @@
         operands += list(filled)
         in_specs += [pl.BlockSpec(memory_space=pl.ANY)] * 2
     return pl.pallas_call(
-        functools.partial(expert_kernel, chunk, before is None),
+        functools.partial(expert_kernel, chunk, before is None, last),
         grid=(hidden // chunk,),
         in_specs=in_specs,
         out_specs=[
@@ -550,11 +559,11 @@
             pl.BlockSpec((rows, 2 * chunk), lambda i: (tile, i)),
         ],
         out_shape=[
-            jax.ShapeDtypeStruct((rows, width), F32),
-            jax.ShapeDtypeStruct((rows, width), F32),
+            *[jax.ShapeDtypeStruct((rows, width), BF16 if last else F32)] * 2,
             jax.ShapeDtypeStruct((2 * rows, hidden), BF16),
             jax.ShapeDtypeStruct((2 * rows, 2 * hidden), BF16),
         ],
+        scratch_shapes=[pltpu.VMEM((rows, width), F32)] * (2 if last else 0),
         input_output_aliases=aliases,
         compiler_params=params(),
         name="experts",
@@ -787,9 +796,6 @@
         halves[side] = total.astype(BF16)
         far_copies.append(start(halves.at[side], lasts.at[side], 2 + side, pairs[2 - side]))
 
-    step_two.wait()
-    both_ref[...] = (one_ref[...].astype(F32) + got_two[...].astype(F32)).astype(BF16)
-    step_one = start(both_ref, got_one, 0, others[-1])
     columns = dq_ref.shape[1]
     chunk = columns // 4
 
@@ -807,6 +813,10 @@
 
         lax.fori_loop(0, 4, compute_send, 0)
         core_copies.append(start(sent.at[side], got.at[side], 4 + side, pairs[0]))
+        if side == 0:
+            step_two.wait()
+            both_ref[...] = (one_ref[...].astype(F32) + got_two[...].astype(F32)).astype(BF16)
+            step_one = start(both_ref, got_one, 0, others[-1])
     for side, (right, _, left, keep, away) in enumerate(sides):
         core_copies[side].wait()
 
@@ -857,15 +867,25 @@
 
 def finish_kernel(
     dx_ref,
+    out_ref,
     q_keep,
     q_send,
     o_keep,
     o_send,
     s_send,
     s_keep,
+    a_keep,
+    a_got,
+    b_keep,
+    b_got,
     back_ref,
-    qo_ref,
+    back_out_ref,
+    q_ref,
+    o_ref,
     s_ref,
+    own_ref,
+    own_half,
+    own_last,
     q_got,
     o_got,
     q_half,
@@ -919,6 +939,7 @@
     o_one = start(o_send, o_got, 2, four)
     s_one = start(s_send, s_got, 0, one)
     back_ref[d] = dx_ref[d]
+    back_out_ref[d] = out_ref[d]
     rows = q_last.shape[0]
     s_one.wait()
     total = s_keep[...].astype(F32) + s_got[...].astype(F32)
@@ -935,25 +956,33 @@
     total = s_keep2 + s_got2[...].astype(F32)
     s_quarter[...] = total[rows:].astype(BF16)
     s_three = start(s_quarter, s_last, 6, two)
+    own_copies = []
+    for side, (keep, got, to) in enumerate(((a_keep, a_got, four), (b_keep, b_got, two))):
+        total = keep[...].astype(F32) + got[...].astype(F32)
+        own_ref[side] = total[:rows]
+        own_half[side] = total[rows:].astype(BF16)
+        own_copies.append(start(own_half.at[side], own_last.at[side], 12 + side, to))
+    total = s_keep2 + s_got2[...].astype(F32)
     deals = []
-    for p in range(1, count):
-        copy = pltpu.make_async_remote_copy(
-            src_ref=dx_ref.at[flip(d, p)],
-            dst_ref=back_ref.at[d],
-            send_sem=deal_send.at[p - 1],
-            recv_sem=deal_recv.at[p - 1],
-            device_id={"dp": flip(d, p)},
-            device_id_type=pl.DeviceIdType.MESH,
-        )
-        copy.start()
-        deals.append(copy)
+    for i, (src, dst) in enumerate(((dx_ref, back_ref), (out_ref, back_out_ref))):
+        for p in range(1, count):
+            copy = pltpu.make_async_remote_copy(
+                src_ref=src.at[flip(d, p)],
+                dst_ref=dst.at[d],
+                send_sem=deal_send.at[i, p - 1],
+                recv_sem=deal_recv.at[i, p - 1],
+                device_id={"dp": flip(d, p)},
+                device_id_type=pl.DeviceIdType.MESH,
+            )
+            copy.start()
+            deals.append(copy)
     s_own = total[:rows]
     s_three.wait()
     s_own = s_own + s_last[...].astype(F32)
     k_mine[...] = s_own.astype(BF16)
     k_near = start(k_mine, k_got.at[0], 7, {"tensor": flip(z, 1)})
     finals = []
-    part = qo_ref.shape[1] // 2
+    part = q_ref.shape[1]
     for two_copy, keep, got, last, side in (
         (q_two, q_keep, q_got, q_last, 0),
         (o_two, o_keep, o_got, o_last, 1),
@@ -976,14 +1005,18 @@
     total = z_mine[z].astype(F32)
     for m in range(z_count - 1):
         total = total + z_got[m].astype(F32)
-    qo_ref[...] = total
+    q_ref[...] = total[:, :part]
+    o_ref[...] = total[:, part:]
     k_far.wait()
     s_ref[...] = s_own + k_got[1].astype(F32)
+    for side, copy in enumerate(own_copies):
+        copy.wait()
+        own_ref[side] += own_last[side].astype(F32)
     for copy in deals:
         copy.wait()
 
 
-def finish(dx, q_keep, q_send, o_keep, o_send, s_send, s_keep, z_count):
+def finish(dx, out, q_keep, q_send, o_keep, o_send, s_send, s_keep, own, z_count):
     count = dx.shape[0]
     rows = q_keep.shape[0] // 2
     columns = q_keep.shape[1]
@@ -993,14 +1026,19 @@
     dma = pltpu.SemaphoreType.DMA
     return pl.pallas_call(
         finish_kernel,
-        in_specs=[vmem] * 7,
-        out_specs=[vmem] * 3,
+        in_specs=[vmem] * 12,
+        out_specs=[vmem] * 6,
         out_shape=[
             jax.ShapeDtypeStruct(dx.shape, BF16),
-            jax.ShapeDtypeStruct((rows, 2 * part), F32),
+            jax.ShapeDtypeStruct(dx.shape, BF16),
+            jax.ShapeDtypeStruct((rows, part), F32),
+            jax.ShapeDtypeStruct((rows, part), F32),
             jax.ShapeDtypeStruct((rows, small), F32),
+            jax.ShapeDtypeStruct((2, rows, own[0].shape[1]), F32),
         ],
         scratch_shapes=[
+            pltpu.VMEM((2, rows, own[0].shape[1]), BF16),
+            pltpu.VMEM((2, rows, own[0].shape[1]), BF16),
             pltpu.VMEM((2 * rows, columns), BF16),
             pltpu.VMEM((2 * rows, columns), BF16),
             pltpu.VMEM((rows, columns), BF16),
@@ -1017,8 +1055,8 @@
             pltpu.VMEM((rows, small), BF16),
             pltpu.VMEM((rows, small), BF16),
             pltpu.VMEM((2, rows, small), BF16),
-            dma((count - 1,)),
-            dma((count - 1,)),
+            dma((2, count - 1)),
+            dma((2, count - 1)),
             dma((7 + 2 * z_count,)),
             dma((7 + 2 * z_count,)),
         ],
@@ -1026,7 +1064,37 @@
             vmem_limit_bytes=56 * 2**20, collective_id=0, has_side_effects=True
         ),
         name="finish",
-    )(dx, q_keep, q_send, o_keep, o_send, s_send, s_keep)
+    )(dx, out, q_keep, q_send, o_keep, o_send, s_send, s_keep, *own)
+
+
+def assemble_kernel(own_ref, far_ref, gate_ref, up_ref, down_ref):
+    count, rows, columns = gate_ref.shape
+    a, b = [own_ref[side] + far_ref[side].astype(F32) for side in (0, 1)]
+    gate = jnp.concatenate([a[:, :512], a[:, 1024:1536], b[:, 512:1024]], axis=1)
+    up = jnp.concatenate([a[:, 512:1024], b[:, :512], b[:, 1024:1536]], axis=1)
+    down = jnp.concatenate([a[:, 1536:], b[:, 1536:]], axis=1)
+    pad = jnp.zeros((256 - rows, down.shape[1]), F32)
+    down = jnp.concatenate([down, pad], axis=0).T[:, :rows]
+    for e in range(count):
+        at = slice(e * columns, (e + 1) * columns)
+        gate_ref[e] = gate[:, at]
+        up_ref[e] = up[:, at]
+        down_ref[e] = down[at]
+
+
+def assemble(own, far_sum, count):
+    _, rows, columns = own.shape
+    part = columns * 2 // (3 * count)
+    vmem = pl.BlockSpec(memory_space=pltpu.VMEM)
+    wide = jax.ShapeDtypeStruct((count, rows, part), F32)
+    return pl.pallas_call(
+        assemble_kernel,
+        in_specs=[vmem] * 2,
+        out_specs=[vmem] * 3,
+        out_shape=[wide, wide, jax.ShapeDtypeStruct((count, part, rows), F32)],
+        compiler_params=params(),
+        name="assemble",
+    )(own, far_sum)
 
 
 def turn_kernel(orders, d_ref, *refs):
@@ -1173,7 +1241,8 @@
         piece(w_out, out_rows),
         tensor_count,
     )
-    arrived = arrived.reshape(rows, width + META)
+    arrived, wg_piece, wu_piece = tie(arrived.reshape(rows, width + META), wg_piece, wu_piece)
+    wg_moved, wu_moved = z_move(wg_piece, far), z_move(wu_piece, far)
     wq_all = team_gather(wq_z).reshape(team, tensor_count, piece_rows, query_cols)
     wo_all = team_gather(wo_z).reshape(team, tensor_count, out_rows, width)
     wo = wo_all.transpose(1, 0, 2, 3).reshape(tensor_count * query_cols, width)
@@ -1227,8 +1296,17 @@
         tensor_count,
     )
     arrived_dy = arrived_dy.reshape(rows, width)
-    kv, n1, wg_piece, wu_piece = tie(kv, n1, wg_piece, wu_piece)
-    wg_moved, wu_moved = z_move(wg_piece, far), z_move(wu_piece, far)
+    kv, n1, wg_moved, wu_moved = tie(kv, n1, wg_moved, wu_moved)
+
+    dy_rows = mm(unpack, arrived_dy).astype(BF16)
+    n1, dy_rows = tie(n1, dy_rows)
+    q = project_query(z_arg, n1, wq_all, cos_full, sin_full)
+    dy_near = z_move(dy_rows, near)
+    kvs = (kv_two, kv_one, kv)
+    o, lse = attend(z_arg, start, q, kvs, kv_heads)
+    o, wd_piece, dy_near, counts, weight, marks_near = tie(
+        o, wd_piece, dy_near, counts, weight, marks_near
+    )
 
     def kept_gates(routed, weight, at):
         block = (z - 1 - jnp.arange(tensor_count, dtype=jnp.int32)) % tensor_count
@@ -1244,13 +1322,6 @@
     gate_near = kept_gates(
         marks_near[:, :experts_n], marks_near[:, experts_n : 2 * experts_n], z + 1 - 2 * (z % 2)
     )
-    q = project_query(z_arg, n1, wq_all, cos_full, sin_full)
-    dy_rows = mm(unpack, arrived_dy).astype(BF16)
-    q, dy_rows, gate_own, gate_near = tie(q, dy_rows, gate_own, gate_near)
-    dy_near = z_move(dy_rows, near)
-    kvs = (kv_two, kv_one, kv)
-    o, lse = attend(z_arg, start, q, kvs, kv_heads)
-    o, wd_piece, wg_moved, wu_moved = tie(o, wd_piece, wg_moved, wu_moved)
     wg_far = team_gather(wg_moved)
     wu_far = team_gather(wu_moved)
     h = x_rows + mm(o, wo)
@@ -1274,24 +1345,17 @@
     def first_moves(parts):
         return parts[0], dp_move(parts[1], xy[0]), parts[2], dp_move(parts[3], yx[0])
 
-    def second_moves(moved):
-        halves = []
-        for keep, got, bit in ((*moved[:2], xy[1]), (*moved[2:], yx[1])):
-            x = keep.astype(F32) + got.astype(F32)
-            half = x.shape[0] // 2
-            halves += [x[:half], dp_move(x[half:].astype(BF16), bit)]
-        return halves
-
-    def unit_end(moved):
-        return moved[0] + moved[1].astype(F32), moved[2] + moved[3].astype(F32)
-
     def expert_lefts(n_a, d_a, keep):
         return n_a[keep], d_a[keep], n_a[2 + keep], d_a[2 + keep]
 
     xy, yx = (2, 4), (4, 2)
     n2_near = z_move(n2, near)
     y, dn2, *own_grads = experts(0, n2, dy_rows, gate_own, wg_own, wu_own, wd_own)
-    n2_near, y, dy_near, wd_piece = tie(n2_near, y, dy_near, wd_piece)
+    n2_near, y, wd_piece = tie(n2_near, y, wd_piece)
+    n2_a = turned((n2, n2_near), *orders_a, *orders_b)
+    n1_t = turned((n1,), *orders_a, *orders_b)
+    dy_near, *turns = tie(dy_near, *n2_a, *n1_t)
+    n2_a, n1_t = turns[:4], turns[4:]
     wd_moved = z_move(wd_piece, far)
     yn, dnn, *own_grads = experts(
         1, n2_near, dy_near, gate_near, wg_own, wu_own, wd_own, filled=own_grads
@@ -1299,7 +1363,6 @@
     yn, wd_moved, *own_grads = tie(yn, wd_moved, *own_grads)
     wd_far = team_gather(wd_moved)
     dy_a = turned((dy_rows, dy_near), *orders_a, *orders_b)
-    n2_a = turned((n2, n2_near), *orders_a, *orders_b)
     if halving:
         own = gradients(
             EXPERT_JOBS,
@@ -1311,9 +1374,9 @@
         wg_far, *own = tie(wg_far, *own)
         own = first_moves(own)
     yn, dnn, *far_grads = experts(
-        1, n2_near, dy_near, gate_near, wg_far, wu_far, wd_far, (yn, dnn)
+        1, n2_near, dy_near, gate_near, wg_far, wu_far, wd_far, (yn, dnn), last=True
     )
-    dnn_moved = z_move(dnn.astype(BF16), near)
+    dnn_moved = z_move(dnn, near)
     y, dn2, *far_grads = experts(
         0, n2, dy_rows, gate_own, wg_far, wu_far, wd_far, (y, dn2), far_grads
     )
@@ -1322,9 +1385,8 @@
         far_sent = gradient_parts(EXPERT_JOBS, expert_lefts(n2_a, dy_a, 0), far_grads)
         dnn_moved, far_sent, *own = tie(dnn_moved, far_sent, *own)
         got = dp_move(far_sent, 1)
-        own = second_moves(own)
     yn, dnn_moved = tie(yn, dnn_moved)
-    yn_moved = z_move(yn.astype(BF16), near)
+    yn_moved = z_move(yn, near)
     dn2 = dn2 + dnn_moved.astype(F32)
 
     gain_two_part = jnp.sum(dn2 * h * inv_two, axis=0)
@@ -1338,24 +1400,18 @@
         far_w = gradient_parts(EXPERT_JOBS, expert_lefts(n2_a, dy_a, 1), far_grads, got)
         do, *far_w = tie(do, *far_w)
         far_w = first_moves(far_w)
-    result = h + y + yn_moved.astype(F32)
-    result_out = mm_tn(unpack, result.astype(BF16)).astype(BF16)
-    if halving:
-        do, result_out, *own = tie(do, result_out, *own)
-    else:
-        do, result_out = tie(do, result_out)
-
     dq, dkv_two, dkv_one, dkv = attend_back(
         z_arg, start, q, o, do, lse, cos_full, sin_full, kvs, kv_heads
     )
-    n1_t = turned((n1,), *orders_a, *orders_b)
     dhb_t = turned((dhb,), *orders_b)
     if halving:
         dq, *far_w = tie(dq, *far_w)
         *parts, dkv_sum, far_sum = mix(
             dq, o, (n1_t[0], n1_t[1], *dhb_t), dkv_one, dkv_two, far_w
         )
-        far_sum = z_move(far_sum, far)
+        far_sum = [z_move(part, far) for part in jnp.split(far_sum.reshape(-1, far_sum.shape[2]), 2, axis=0)]
+        far_sum = jnp.concatenate(far_sum, axis=0).reshape(2, out_w, -1)
+        dkv_sum, yn_moved = tie(dkv_sum, yn_moved)
     else:
         dkv_one = z_move(dkv_one, [(b, a) for a, b in up_one])
         dkv_two = z_move(dkv_two, [(b, a) for a, b in up_two])
@@ -1381,24 +1437,21 @@
         u1 - x_rows * inv_one * inv_one * jnp.mean(u1 * x_rows, axis=1, keepdims=True)
     )
 
-    outputs = mm_tn(pack, deal(result_out)).astype(BF16)
-
-    if halving:
-        first, second = [a + b.astype(F32) for a, b in zip(unit_end(own), far_sum)]
-        sum_gu = jnp.concatenate([first[:, :hidden], second[:, :hidden]], axis=1)
-        sum_down = jnp.concatenate([first[:, hidden:], second[:, hidden:]], axis=1)
-    else:
+    result = h + y + yn_moved.astype(F32)
+    result_out = mm_tn(unpack, result.astype(BF16)).astype(BF16)
+
+    if not halving:
         lefts = (n2_a[0], dy_a[0])
         far_sums = [dp_sum(mm(a, b).astype(BF16)) for a, b in zip(lefts, far_grads[::-1])]
         own_sums = [dp_sum(mm(a, b).astype(BF16)) for a, b in zip(lefts, own_grads[::-1])]
         sum_gu, sum_down = [
             a.astype(F32) + z_move(b, far).astype(F32) for a, b in zip(own_sums, far_sums)
         ]
-    sum_gu = sum_gu.reshape(out_w, hidden // 512, 2, 512)
-    sum_gate, sum_up = [
-        sum_gu[:, :, i].reshape(out_w, experts_n, part_hidden).transpose(1, 0, 2) for i in (0, 1)
-    ]
-    sum_down = sum_down.reshape(out_w, experts_n, part_hidden).transpose(1, 2, 0)
+        sum_gu = sum_gu.reshape(out_w, hidden // 512, 2, 512)
+        sum_gate, sum_up = [
+            sum_gu[:, :, i].reshape(out_w, experts_n, part_hidden).transpose(1, 0, 2) for i in (0, 1)
+        ]
+        sum_down = sum_down.reshape(out_w, experts_n, part_hidden).transpose(1, 2, 0)
 
     gains = jnp.stack([gain_one_part, gain_two_part])
 
@@ -1417,9 +1470,20 @@
             (mm(left, dkv_wide) + column).astype(BF16) for left, column in zip(n1_t[2:], columns)
         ]
         dx_out = mm_tn(unpack, dx.astype(BF16)).astype(BF16).reshape(dp_count, share, width)
-        back, total, small = finish(dx_out, *parts, kv_send, kv_keep, tensor_count)
+        back, back_out, sum_query, sum_out, small, own_sum = finish(
+            dx_out,
+            result_out.reshape(dp_count, share, width),
+            *parts,
+            kv_send,
+            kv_keep,
+            own,
+            tensor_count,
+        )
+        sum_gate, sum_up, sum_down = assemble(own_sum, far_sum, experts_n)
         grad_tokens = mm_tn(pack, back.reshape(rows, width)).astype(BF16)
+        outputs = mm_tn(pack, back_out.reshape(rows, width)).astype(BF16)
     else:
+        outputs = mm_tn(pack, deal(result_out)).astype(BF16)
         grad_tokens = mm_tn(pack, deal(mm_tn(unpack, dx.astype(BF16)).astype(BF16))).astype(BF16)
         small = dp_sum((mm(n1_t[3], dkv_wide) + columns[0]).astype(BF16))
         small = small.astype(F32) + sum(
@@ -1434,7 +1498,8 @@
             z_move(part.astype(BF16), move).astype(F32)
             for part, move in zip(both[1:], (near, far, across))
         )
-    sum_query, sum_out = total[:, :query_cols], total[:, query_cols:].T
+        sum_query, sum_out = total[:, :query_cols], total[:, query_cols:]
+    sum_out = sum_out.T
     kv_cols = w_keyval.shape[1]
     return (
         outputs,

time: 673 us -> 655 us (0.973)
  waiting for transfers between devices: 72.8 us -> 16.3 us
  Pallas kernels: 438 us -> 494 us
  local copies, waits for them, and re-layouts: 67.4 us -> 38.5 us
  matrix products: 31.3 us -> 40.1 us
    ppermute x8 -> x9, waiting for transfers between devices: 67.6 us -> 7.41 us  [z_move(): return lax.ppermute(x, 'tensor', pairs)]
    pallas_call x1, Pallas kernels: 33.9 us -> 61 us  [keyval(): pl.pallas_call(keyval_kernel, in_specs=[vmem] * 7, out_specs=[vmem] * 6,...]
    pallas_call x5 -> x6, Pallas kernels: 191 us -> 214 us  [the longest x1 113 us: finish(): pl.pallas_call(finish_kernel, in_specs=[vmem] * 12, out_specs=[vmem] * 6,...]
    unnamed x119 -> x108, local copies, waits for them, and re-layouts: 26.9 us -> 8.46 us
    slice x12 -> x0, local copies, waits for them, and re-layouts: 8.8 us -> none  [the longest x1 5.41 us: per_device(): sum_gu[:, :, i].reshape(out_w, experts_n, part_hidden).transpose(1, 0, 2)]
    pallas_call x1, Pallas kernels: 27.5 us -> 36.2 us  [gradients(): pl.pallas_call(functools.partial(gradient_kernel, jobs, len(keep_lefts),...]
    ppermute x7 -> x5, waiting for transfers between devices: 0.02 us -> 7.57 us  [dp_move(): return lax.ppermute(x, 'dp', [(i, i ^ bit) for i in range(dp_count)])]
    reshape x2 -> x0, local copies, waits for them, and re-layouts: 7.12 us -> none  [the longest x1 4.24 us: per_device(): sum_gu = sum_gu.reshape(out_w, hidden // 512, 2, 512)]
  transfers between devices with their start and end apart: 21 -> 19, of which waited for: 6 -> 5; matrix products, arithmetic and copies ran while one was open for 10% -> 12% of each run, Pallas kernels for 56% -> 69%
where the time goes in v4:
time: 655 us; the launch traced here: 645 us
  Pallas kernels  494 us (75%)
  matrix products  40.1 us (6%)
  local copies, waits for them, and re-layouts  38.5 us (6%)
  other arithmetic  24.3 us (4%)
  starting transfers between devices  16.8 us (3%)
  waiting for transfers between devices  16.3 us (2%)
  between operations  15 us (2%)
    pallas_call x1, Pallas kernels, finish(): pl.pallas_call(finish_kernel, in_specs=[vmem] * 12, out_specs=[vmem] * 6,...  113 us
    pallas_call x4, Pallas kernels, experts(): pl.pallas_call(functools.partial(expert_kernel, chunk, before is None, la...  95.5 us
    pallas_call x1, Pallas kernels, keyval(): pl.pallas_call(keyval_kernel, in_specs=[vmem] * 7, out_specs=[vmem] * 6,...  61 us
    pallas_call x1, Pallas kernels, gradients(): pl.pallas_call(functools.partial(gradient_kernel, jobs, len(keep_lefts),...  36.2 us
    pallas_call x1, Pallas kernels, mix(): pl.pallas_call(mix_kernel, in_specs=[vmem] * 12, out_specs=[vmem] * 6, ou...  34.6 us
    pallas_call x2, Pallas kernels, gradient_parts(): pl.pallas_call(functools.partial(part_kernel, jobs, len(lefts), len(right...  30.8 us
    pallas_call x1, Pallas kernels, open_moves(): pl.pallas_call(open_kernel, in_specs=[vmem] * 3, out_specs=[vmem] * 3, ou...  30.4 us
    pallas_call x1, Pallas kernels, attend_back(): pl.pallas_call(functools.partial(attend_back_kernel, kv_heads), grid_spec...  29.9 us
  transfers between devices with their start and end apart: 19, of which 5 were waited for; matrix products, arithmetic and copies ran while one was open for 12% of the time, Pallas kernels for 69%

profile of v4, /device:TPU:0, one launch (start us, length us, event | category | flops | bytes accessed | tf_op | source)
XLA Modules:
  0.0 644.8 jit_solution(10964649943974221702)
XLA Ops:
  10.5 3.8 concatenate.27
  20.9 30.4 %open_moves.1 = (bf16[8,64,1664]{2,1,0:T(8,128)(2,1)S(1)}, bf16[4,192,384]{2,1,0:T(8,128)(2,1)S(1)}, bf16[4,48,1536]{2,1,0:T(8,128)(2,1)S(1)}) custom-call(bf16[8,64,1664]{2,1,0:T(8,128)(2,1)S(1)} %bitcast.56, bf16[192,384]{1,0:T(8,128)(2,1)S(1)} %constant_dynamic-slice_fusion.12.q_ref, bf16[48,1536]{1,0:T(8,128)(2,1)S(1)} %constant_dynamic-slice_fusion.11.o_ref), custom_call_target="tpu_custom_call" | custom-call | tf_op jit(solution)/shard_map/open_moves/pallas_call | solution.py:99
  56.2 3.2 collective-permute-start
  72.5 61.0 %keyval.1 = (bf16[512,512]{1,0:T(8,128)(2,1)S(1)}, bf16[512,512]{1,0:T(8,128)(2,1)S(1)}, bf16[512,512]{1,0:T(8,128)(2,1)S(1)}, f32[4,8,128]{2,1,0:T(8,128)S(1)},...) custom-call(bf16[512,1536]{1,0:T(8,128)(2,1)S(1)} %multiply_convert_fusion.1.x_ref.refs_0_, ...), custom_call_target="tpu_custom_call" | custom-call | tf_op jit(solution)/shard_map/keyval/pallas_call | solution.py:194
  143.6 3.6 turn.5
  147.2 7.8 %project_query.1.q_ref = bf16[512,1536]{1,0:T(8,128)(2,1)} custom-call(s32[1]{0:T(128)} %bitcast.11.z_ref, bf16[512,1536]{1,0:T(8,128)(2,1)} %copy-done.2, bf16[8,4,192,384]{3,2,1,0:T(8,128)(2,1)} %bitcast.88, f32[512,128]{1,0:T(8,128)} %copy-done.7, f32[512,128]{1,0:T(8,128)} %copy-done.3), custom_call_target="tpu_custom_call" | custom-call | flops 2415919104 | bytes 7864320 | tf_op jit(solution)/shard_map/project_query/pallas_call | solution.py:228
  155.1 21.9 %attend.1 = (bf16[512,1536]{1,0:T(8,128)(2,1)}, f32[12,512,1]{2,1,0:T(8,128)}) custom-call(s32[1]{0:T(128)} %bitcast.11.z_ref, s32[512,1]{1,0:T(8,128)} %copy.113.start_ref, bf16[512,1536]{1,0:T(8,128)(2,1)} %project_query.1.q_ref, bf16[512,512]{1,0:T(8,128)(2,1)} %copy-done.13, bf16[512,512]{1,0:T(8,128)(2,1)} %copy-done.12, bf16[512,512]{1,0:T(8,128)(2,1)} %copy-done.11), custom_call_target="tpu_custom_call" | custom-call | flops 4831838208 | bytes 6291456 | tf_op jit(solution)/shard_map/attend/pallas_call | solution.py:348
  182.0 6.3 multiply_reduce_fusion.4
  195.5 23.4 %experts.4 = (f32[512,1536]{1,0:T(8,128)}, f32[512,1536]{1,0:T(8,128)}, bf16[1024,1536]{1,0:T(8,128)(2,1)}, bf16[1024,3072]{1,0:T(8,128)(2,1)}) custom-call(bf16[512,1536]{1,0:T(8,128)(2,1)} %multiply_convert_fusion.x_ref.refs_0_, bf16[512,1536]{1,0:T(8,128)(2,1)} %copy-done.17, bf16[512,1536]{1,0:T(8,128)(2,1)} %copy.119.gate_ref, ...), custom_call_target="tpu_custom_call" | custom-call | flops 14495514624 | bytes 26738688 | tf_op jit(solution)/shard_map/experts/pallas_call | solution.py:551
  219.0 6.0 collective-permute-done.3.refs_1_.x_ref
  225.0 5.3 turn.4
  232.5 22.8 %experts.5 = (f32[512,1536]{1,0:T(8,128)}, f32[512,1536]{1,0:T(8,128)}, bf16[1024,1536]{1,0:T(8,128)(2,1)}, bf16[1024,3072]{1,0:T(8,128)(2,1)}) custom-call(bf16[512,1536]{1,0:T(8,128)(2,1)} %collective-permute-done.3.refs_1_.x_ref, bf16[512,1536]{1,0:T(8,128)(2,1)} %copy-done.26, ...), custom_call_target="tpu_custom_call", output_to_operand_aliasing={{2}: (6, {}), {3}: (7, {})} | custom-call | flops 14495514624 | bytes 26738688 | tf_op jit(solution)/shard_map/experts/pallas_call | solution.py:551
  256.7 5.3 turn.6
  262.0 36.2 %gradients.1 = (bf16[384,2304]{1,0:T(8,128)(2,1)}, bf16[384,2304]{1,0:T(8,128)(2,1)}, bf16[384,2304]{1,0:T(8,128)(2,1)}, bf16[384,2304]{1,0:T(8,128)(2,1)}) custom-call(bf16[768,1024]{1,0:T(8,128)(2,1)} %get-tuple-element.171.refs_0_, bf16[768,1024]{1,0:T(8,128)(2,1)} %get-tuple-element.173.refs_1_, bf16[768,1024]{1,0:T(8,128)(2,1)} %get-tuple-element.174.refs_2_, ...), custom_call_target="tpu_custom_call" | custom-call | flops 1000000000 | bytes 1000000 | tf_op jit(solution)/shard_map/gradients/pallas_call | solution.py:647
  300.4 24.8 %experts.6 = (bf16[512,1536]{1,0:T(8,128)(2,1)}, bf16[512,1536]{1,0:T(8,128)(2,1)}, bf16[1024,1536]{1,0:T(8,128)(2,1)}, bf16[1024,3072]{1,0:T(8,128)(2,1)}) custom-call(bf16[512,1536]{1,0:T(8,128)(2,1)} %collective-permute-done.3.refs_1_.x_ref, bf16[512,1536]{1,0:T(8,128)(2,1)} %copy-done.26, bf16[512,1536]{1,0:T(8,128)(2,1)} %copy.122.gate_ref, ...), custom_call_target="tpu_custom_call" | custom-call | flops 14495514624 | bytes 26738688 | tf_op jit(solution)/shard_map/experts/pallas_call | solution.py:551
  325.2 24.5 %experts.7 = (f32[512,1536]{1,0:T(8,128)}, f32[512,1536]{1,0:T(8,128)}, bf16[1024,1536]{1,0:T(8,128)(2,1)}, bf16[1024,3072]{1,0:T(8,128)(2,1)}) custom-call(bf16[512,1536]{1,0:T(8,128)(2,1)} %multiply_convert_fusion.x_ref.refs_0_, bf16[512,1536]{1,0:T(8,128)(2,1)} %copy-done.17, ...), custom_call_target="tpu_custom_call", output_to_operand_aliasing={{2}: (8, {}), {3}: (9, {})} | custom-call | flops 14495514624 | bytes 26738688 | tf_op jit(solution)/shard_map/experts/pallas_call | solution.py:551
  349.7 14.9 %gradient_parts.2 = bf16[2,768,2304]{2,1,0:T(8,128)(2,1)} custom-call(bf16[768,1024]{1,0:T(8,128)(2,1)} %get-tuple-element.171.refs_0_, bf16[768,1024]{1,0:T(8,128)(2,1)} %get-tuple-element.173.refs_1_, bf16[768,1024]{1,0:T(8,128)(2,1)} %get-tuple-element.174.refs_2_, bf16[768,1024]{1,0:T(8,128)(2,1)} %get-tuple-element.175.refs_3_, ...), custom_call_target="tpu_custom_call" | custom-call | flops 7247757312 | bytes 16515072 | tf_op jit(solution)/shard_map/gradient_parts/pallas_call | solution.py:711
  368.9 3.8 convolution_convert_fusion.6.do_ref
  372.6 3.7 collective-permute-done.8.refs_6_
  376.3 15.9 %gradient_parts.3 = (bf16[384,2304]{1,0:T(8,128)(2,1)}, bf16[384,2304]{1,0:T(8,128)(2,1)}, bf16[384,2304]{1,0:T(8,128)(2,1)}, bf16[384,2304]{1,0:T(8,128)(2,1)}) custom-call(bf16[768,1024]{1,0:T(8,128)(2,1)} %get-tuple-element.176.refs_4_.refs_0_, bf16[768,1024]{1,0:T(8,128)(2,1)} %get-tuple-element.177.refs_5_.refs_1_, ...), custom_call_target="tpu_custom_call" | custom-call | flops 7247757312 | bytes 16515072 | tf_op jit(solution)/shard_map/gradient_parts/pallas_call | solution.py:711
  396.3 3.1 turn.7
  399.5 29.9 %attend_back.1 = (bf16[512,1536]{1,0:T(8,128)(2,1)}, bf16[512,512]{1,0:T(8,128)(2,1)}, bf16[512,512]{1,0:T(8,128)(2,1)}, f32[512,512]{1,0:T(8,128)}) custom-call(s32[1]{0:T(128)} %bitcast.11.z_ref, s32[512,1]{1,0:T(8,128)} %copy.113.start_ref, bf16[512,1536]{1,0:T(8,128)(2,1)} %project_query.1.q_ref, bf16[512,1536]{1,0:T(8,128)(2,1)} %get-tuple-element.154.o_ref, ...), custom_call_target="tpu_custom_call" | custom-call | flops 12079595520 | bytes 9437184 | tf_op jit(solution)/shard_map/attend_back/pallas_call | solution.py:453
  429.3 3.8 collective-permute-done.10.fb_got
  433.2 34.6 %mix.1 = (bf16[384,1536]{1,0:T(8,128)(2,1)}, bf16[384,1536]{1,0:T(8,128)(2,1)}, bf16[384,1536]{1,0:T(8,128)(2,1)}, bf16[384,1536]{1,0:T(8,128)(2,1)}, bf16[512,5...) custom-call(bf16[512,1536]{1,0:T(8,128)(2,1)} %get-tuple-element.225.dq_ref, bf16[512,1536]{1,0:T(8,128)(2,1)} %get-tuple-element.154.o_ref, ...), custom_call_target="tpu_custom_call" | custom-call | tf_op jit(solution)/shard_map/mix/pallas_call | solution.py:846
  474.9 9.8 %project_back.1 = f32[512,1536]{1,0:T(8,128)} custom-call(s32[1]{0:T(128)} %bitcast.11.z_ref, bf16[512,1536]{1,0:T(8,128)(2,1)} %get-tuple-element.225.dq_ref, bf16[8,4,192,384]{3,2,1,0:T(8,128)(2,1)} %bitcast.89, bf16[512,512]{1,0:T(8,128)(2,1)} %pad_maximum_fusion.1.dkv_ref, bf16[1536,512]{1,0:T(8,128)(2,1)} %wkv_ref.1), custom_call_target="tpu_custom_call" | custom-call | flops 3221225472 | bytes 9437184 | tf_op jit(solution)/shard_map/project_back/pallas_call | solution.py:272
  484.7 4.2 multiply_reduce_fusion.1
  492.3 3.2 add_convert_fusion.2.s_keep
  495.6 3.8 convolution_convert_fusion.2
  499.4 4.6 convolution_convert_fusion.3
  505.6 112.9 %finish.1 = (bf16[8,64,1536]{2,1,0:T(8,128)(2,1)}, bf16[8,64,1536]{2,1,0:T(8,128)(2,1)}, f32[192,384]{1,0:T(8,128)}, f32[192,384]{1,0:T(8,128)}, f32[192,640]{1,0:T(8,128)}, /*index=5*/f32[2,192,2304]{2,1,0:T(8,128)}) custom-call(bf16[8,64,1536]{2,1,0:T(8,128)(2,1)} %bitcast.61, bf16[8,64,1536]{2,1,0:T(8,128)(2,1)} %bitcast.59, ...), custom_call_target="tpu_custom_call" | custom-call | tf_op jit(solution)/shard_map/finish/pallas_call | solution.py:1027
  622.0 3.7 convolution_convert_fusion
  630.7 5.7 assemble.1
  (225 shorter events, 85.9 us)
Async XLA Ops:
  7.2 9.7 %copy-start = (bf16[512,1536]{1,0:T(8,128)(2,1)S(1)}, bf16[512,1536]{1,0:T(8,128)(2,1)}, u32[]{:S(2)}) copy-start(bf16[512,1536]{1,0:T(8,128)(2,1)} %param.19) | copy-start | bytes 4718596
  7.2 140.0 %all-gather.6.cloned.1.call-start = ((), (), s32[]{:S(2)}) async-start(), calls=%async_computation | async-start | bytes 5308416 | tf_op jit(solution)/shard_map/all_gather | solution.py:1201
  8.4 8.5 %copy-start.45 = (s32[512]{0:T(512)}, s32[512]{0:T(512)S(1)}, u32[]{:S(2)}) copy-start(s32[512]{0:T(512)S(1)} %get-tuple-element.304) | copy-start | bytes 6148
  53.0 126.2 %all-gather.8.cloned.1.call-start = ((), (), s32[]{:S(2)}) async-start(), calls=%async_computation.1 | async-start | bytes 5308416 | tf_op jit(solution)/shard_map/all_gather | solution.py:1201
  53.8 244.5 %all-gather.10.cloned.1.call-start = ((), (), s32[]{:S(2)}) async-start(), calls=%async_computation.2 | async-start | bytes 5308416 | tf_op jit(solution)/shard_map/all_gather | solution.py:1201
  56.2 80.9 %collective-permute-start = (bf16[192,1536]{1,0:T(8,128)(2,1)}, bf16[192,1536]{1,0:T(8,128)(2,1)}, u32[]{:S(2)}, u32[]{:S(2)}) collective-permute-start(bf16[192,1536]{1,0:T(8,128)(2,1)} %get-tuple-element.141), channel_id=1, source_target_pairs={{0,2},{1,3},{2,0},{3,1},{4,6},{5,7},{6,4},{7,5},{8,10},{9,11},{10,... | collective-permute-start | bytes 1769480 | tf_op jit(solution)/shard_map/ppermute | solution.py:1187
  59.3 77.7 %collective-permute-start.1 = (bf16[192,1536]{1,0:T(8,128)(2,1)}, bf16[192,1536]{1,0:T(8,128)(2,1)}, u32[]{:S(2)}, u32[]{:S(2)}) collective-permute-start(bf16[192,1536]{1,0:T(8,128)(2,1)} %get-tuple-element.142), channel_id=1, source_target_pairs={{0,2},{1,3},{2,0},{3,1},{4,6},{5,7},{6,4},{7,5},{8,10},{9,11},{10,... | collective-permute-start | bytes 1769480 | tf_op jit(solution)/shard_map/ppermute | solution.py:1187
  72.1 65.5 %copy-start.2 = (bf16[512,1536]{1,0:T(8,128)(2,1)}, bf16[512,1536]{1,0:T(8,128)(2,1)S(1)}, u32[]{:S(2)}) copy-start(bf16[512,1536]{1,0:T(8,128)(2,1)S(1)} %multiply_convert_fusion.1.x_ref.refs_0_) | copy-start | bytes 4718596
  137.1 163.3 %all-gather.12.cloned.1.call-start = ((), (), s32[]{:S(2)}) async-start(), calls=%async_computation.3 | async-start | bytes 5308416 | tf_op jit(solution)/shard_map/all_gather | solution.py:1201
  137.7 162.7 %all-gather.14.cloned.1.call-start = ((), (), s32[]{:S(2)}) async-start(), calls=%async_computation.4 | async-start | bytes 5308416 | tf_op jit(solution)/shard_map/all_gather | solution.py:1201
  140.1 14.9 %copy-start.17 = (bf16[512,1536]{1,0:T(8,128)(2,1)}, bf16[512,1536]{1,0:T(8,128)(2,1)S(1)}, u32[]{:S(2)}) copy-start(bf16[512,1536]{1,0:T(8,128)(2,1)S(1)} %convolution_convert_fusion.4.dy_ref.refs_0_) | copy-start | bytes 4718596
  140.1 36.8 %collective-permute-start.2 = (bf16[512,1536]{1,0:T(8,128)(2,1)S(1)}, bf16[512,1536]{1,0:T(8,128)(2,1)S(1)}, u32[]{:S(2)}, u32[]{:S(2)}) collective-permute-start(bf16[512,1536]{1,0:T(8,128)(2,1)S(1)} %convolution_convert_fusion.4.dy_ref.refs_0_), channel_id=1, source_target_pairs={{0,1},{1,0},{2,3},{3,2},{4,5},{5,4},{6,7},{7,6},{8,9},{9,8},{10,11... | collective-permute-start | bytes 4718600 | tf_op jit(solution)/shard_map/ppermute | solution.py:1187
  155.0 22.0 %copy-start.30 = (bf16[512,8]{1,0:T(8,128)(2,1)S(1)}, bf16[512,8]{1,0:T(8,128)(2,1)}, u32[]{:S(2)}) copy-start(bf16[512,8]{1,0:T(8,128)(2,1)} %copy-done.29) | copy-start | bytes 24580
  155.1 22.4 %copy-start.38 = (bf16[512,8]{0,1:T(8,128)(2,1)S(1)}, bf16[512,8]{0,1:T(8,128)(2,1)}, u32[]{:S(2)}) copy-start(bf16[512,8]{0,1:T(8,128)(2,1)} %copy-done.37) | copy-start | bytes 24580
  189.9 35.1 %collective-permute-start.3 = (bf16[512,1536]{1,0:T(8,128)(2,1)}, bf16[512,1536]{1,0:T(8,128)(2,1)}, u32[]{:S(2)}, u32[]{:S(2)}) collective-permute-start(bf16[512,1536]{1,0:T(8,128)(2,1)} %multiply_convert_fusion.x_ref.refs_0_), channel_id=1, source_target_pairs={{0,1},{1,0},{2,3},{3,2},{4,5},{5,4},{6,7},{7,6},{8,9},{9,8},{10,11... | collective-permute-start | bytes 4718600 | tf_op jit(solution)/shard_map/ppermute | solution.py:1187
  218.9 11.4 %copy-start.28 = (bf16[192,1536]{1,0:T(8,128)(2,1)S(1)}, bf16[192,1536]{1,0:T(8,128)(2,1)}, u32[]{:S(2)}) copy-start(bf16[192,1536]{1,0:T(8,128)(2,1)} %constant_dynamic-slice_fusion.8) | copy-start | bytes 1769476
  230.3 26.4 %collective-permute-start.4 = (bf16[192,1536]{1,0:T(8,128)(2,1)S(1)}, bf16[192,1536]{1,0:T(8,128)(2,1)}, u32[]{:S(2)}, u32[]{:S(2)}) collective-permute-start(bf16[192,1536]{1,0:T(8,128)(2,1)S(1)} %copy-done.28), channel_id=1, source_target_pairs={{0,2},{1,3},{2,0},{3,1},{4,6},{5,7},{6,4},{7,5},{8,10},{9,11},{10,... | collective-permute-start | bytes 1769480 | tf_op jit(solution)/shard_map/ppermute | solution.py:1187
  298.3 66.2 %collective-permute-start.6 = (bf16[384,2304]{1,0:T(8,128)(2,1)}, bf16[384,2304]{1,0:T(8,128)(2,1)}, u32[]{:S(2)}, u32[]{:S(2)}) collective-permute-start(bf16[384,2304]{1,0:T(8,128)(2,1)} %get-tuple-element.208), channel_id=1, source_target_pairs={{0,8},{4,12},{8,0},{12,4},{16,24},{20,28},{24,16},{28,20},{1,9},{5... | collective-permute-start | bytes 5308424 | tf_op jit(solution)/shard_map/ppermute | solution.py:1190
  298.4 66.2 %collective-permute-start.7 = (bf16[384,2304]{1,0:T(8,128)(2,1)}, bf16[384,2304]{1,0:T(8,128)(2,1)}, u32[]{:S(2)}, u32[]{:S(2)}) collective-permute-start(bf16[384,2304]{1,0:T(8,128)(2,1)} %get-tuple-element.210), channel_id=1, source_target_pairs={{0,16},{4,20},{8,24},{12,28},{16,0},{20,4},{24,8},{28,12},{1,17},{... | collective-permute-start | bytes 5308424 | tf_op jit(solution)/shard_map/ppermute | solution.py:1190
  325.2 39.4 %collective-permute-start.5 = (bf16[512,1536]{1,0:T(8,128)(2,1)}, bf16[512,1536]{1,0:T(8,128)(2,1)S(1)}, u32[]{:S(2)}, u32[]{:S(2)}) collective-permute-start(bf16[512,1536]{1,0:T(8,128)(2,1)} %get-tuple-element.204), channel_id=1, source_target_pairs={{0,1},{1,0},{2,3},{3,2},{4,5},{5,4},{6,7},{7,6},{8,9},{9,8},{10,11... | collective-permute-start | bytes 4718600 | tf_op jit(solution)/shard_map/ppermute | solution.py:1187
  349.7 15.0 %copy-start.14 = (f32[512,1536]{1,0:T(8,128)S(1)}, f32[512,1536]{1,0:T(8,128)}, u32[]{:S(2)}) copy-start(f32[512,1536]{1,0:T(8,128)} %get-tuple-element.202) | copy-start | bytes 9437188
  364.6 11.7 %collective-permute-start.8 = (bf16[2,768,2304]{2,1,0:T(8,128)(2,1)}, bf16[2,768,2304]{2,1,0:T(8,128)(2,1)}, u32[]{:S(2)}, u32[]{:S(2)}) collective-permute-start(bf16[2,768,2304]{2,1,0:T(8,128)(2,1)} %gradient_parts.2), channel_id=1, source_target_pairs={{0,4},{4,0},{8,12},{12,8},{16,20},{20,16},{24,28},{28,24},{1,5},{5... | collective-permute-start | bytes 21233672 | tf_op jit(solution)/shard_map/ppermute | solution.py:1190
  392.2 41.0 %collective-permute-start.10 = (bf16[384,2304]{1,0:T(8,128)(2,1)}, bf16[384,2304]{1,0:T(8,128)(2,1)}, u32[]{:S(2)}, u32[]{:S(2)}) collective-permute-start(bf16[384,2304]{1,0:T(8,128)(2,1)} %get-tuple-element.224), channel_id=1, source_target_pairs={{0,16},{4,20},{8,24},{12,28},{16,0},{20,4},{24,8},{28,12},{1,17},{... | collective-permute-start | bytes 5308424 | tf_op jit(solution)/shard_map/ppermute | solution.py:1190
  392.3 40.9 %collective-permute-start.9 = (bf16[384,2304]{1,0:T(8,128)(2,1)}, bf16[384,2304]{1,0:T(8,128)(2,1)}, u32[]{:S(2)}, u32[]{:S(2)}) collective-permute-start(bf16[384,2304]{1,0:T(8,128)(2,1)} %get-tuple-element.222), channel_id=1, source_target_pairs={{0,8},{4,12},{8,0},{12,4},{16,24},{20,28},{24,16},{28,20},{1,9},{5... | collective-permute-start | bytes 5308424 | tf_op jit(solution)/shard_map/ppermute | solution.py:1190
  394.3 73.6 %collective-permute-start.11 = (bf16[512,1536]{1,0:T(8,128)(2,1)}, bf16[512,1536]{1,0:T(8,128)(2,1)}, u32[]{:S(2)}, u32[]{:S(2)}) collective-permute-start(bf16[512,1536]{1,0:T(8,128)(2,1)} %get-tuple-element.238), channel_id=1, source_target_pairs={{0,1},{1,0},{2,3},{3,2},{4,5},{5,4},{6,7},{7,6},{8,9},{9,8},{10,11... | collective-permute-start | bytes 4718600 | tf_op jit(solution)/shard_map/ppermute | solution.py:1187
  433.2 34.6 %copy-start.27 = (f32[512,512]{1,0:T(8,128)S(1)}, f32[512,512]{1,0:T(8,128)}, u32[]{:S(2)}) copy-start(f32[512,512]{1,0:T(8,128)} %get-tuple-element.226) | copy-start | bytes 3145732
  470.8 157.1 %collective-permute-start.12 = (bf16[192,2304]{1,0:T(8,128)(2,1)}, bf16[192,2304]{1,0:T(8,128)(2,1)}, u32[]{:S(2)}, u32[]{:S(2)}) collective-permute-start(bf16[192,2304]{1,0:T(8,128)(2,1)} %get-tuple-element.279), channel_id=1, source_target_pairs={{0,2},{1,3},{2,0},{3,1},{4,6},{5,7},{6,4},{7,5},{8,10},{9,11},{10,... | collective-permute-start | bytes 2654216 | tf_op jit(solution)/shard_map/ppermute | solution.py:1187
  472.4 155.5 %collective-permute-start.13 = (bf16[192,2304]{1,0:T(8,128)(2,1)}, bf16[192,2304]{1,0:T(8,128)(2,1)}, u32[]{:S(2)}, u32[]{:S(2)}) collective-permute-start(bf16[192,2304]{1,0:T(8,128)(2,1)} %get-tuple-element.280), channel_id=1, source_target_pairs={{0,2},{1,3},{2,0},{3,1},{4,6},{5,7},{6,4},{7,5},{8,10},{9,11},{10,... | collective-permute-start | bytes 2654216 | tf_op jit(solution)/shard_map/ppermute | solution.py:1187
  474.8 9.8 %copy-start.36 = (f32[1536]{0:T(1024)S(1)}, f32[1536]{0:T(1024)}, u32[]{:S(2)}) copy-start(f32[1536]{0:T(1024)} %param.20) | copy-start | bytes 18436
  474.8 9.8 %copy-start.42 = (f32[512]{0:T(512)S(1)}, f32[512]{0:T(512)}, u32[]{:S(2)}) copy-start(f32[512]{0:T(512)} %copy-done.41) | copy-start | bytes 6148
  505.6 116.4 %copy-start.46 = (s32[512]{0:T(512)S(1)}, s32[512]{0:T(512)}, u32[]{:S(2)}) copy-start(s32[512]{0:T(512)} %copy-done.45) | copy-start | bytes 6148
  630.7 7.2 %copy-start.1 = (bf16[512,1536]{1,0:T(8,128)(2,1)S(1)}, bf16[512,1536]{1,0:T(8,128)(2,1)}, u32[]{:S(2)}) copy-start(bf16[512,1536]{1,0:T(8,128)(2,1)} %param.19) | copy-start | bytes 4718596
  (39 other events, 139.7 us)
Sparse Core Ops, SparseCore 0:
  53.1 54.1 all-gather.5
  109.2 38.4 all-gather.7
  149.6 38.9 all-gather.9
  190.3 38.9 all-gather.11
  256.9 36.7 all-gather.13

commit v5 on v4

--- a/solution.py
+++ b/solution.py
@@ -874,18 +874,11 @@
     o_send,
     s_send,
     s_keep,
-    a_keep,
-    a_got,
-    b_keep,
-    b_got,
     back_ref,
     back_out_ref,
     q_ref,
     o_ref,
     s_ref,
-    own_ref,
-    own_half,
-    own_last,
     q_got,
     o_got,
     q_half,
@@ -956,13 +949,6 @@
     total = s_keep2 + s_got2[...].astype(F32)
     s_quarter[...] = total[rows:].astype(BF16)
     s_three = start(s_quarter, s_last, 6, two)
-    own_copies = []
-    for side, (keep, got, to) in enumerate(((a_keep, a_got, four), (b_keep, b_got, two))):
-        total = keep[...].astype(F32) + got[...].astype(F32)
-        own_ref[side] = total[:rows]
-        own_half[side] = total[rows:].astype(BF16)
-        own_copies.append(start(own_half.at[side], own_last.at[side], 12 + side, to))
-    total = s_keep2 + s_got2[...].astype(F32)
     deals = []
     for i, (src, dst) in enumerate(((dx_ref, back_ref), (out_ref, back_out_ref))):
         for p in range(1, count):
@@ -1009,14 +995,11 @@
     o_ref[...] = total[:, part:]
     k_far.wait()
     s_ref[...] = s_own + k_got[1].astype(F32)
-    for side, copy in enumerate(own_copies):
-        copy.wait()
-        own_ref[side] += own_last[side].astype(F32)
     for copy in deals:
         copy.wait()
 
 
-def finish(dx, out, q_keep, q_send, o_keep, o_send, s_send, s_keep, own, z_count):
+def finish(dx, out, q_keep, q_send, o_keep, o_send, s_send, s_keep, z_count):
     count = dx.shape[0]
     rows = q_keep.shape[0] // 2
     columns = q_keep.shape[1]
@@ -1026,19 +1009,16 @@
     dma = pltpu.SemaphoreType.DMA
     return pl.pallas_call(
         finish_kernel,
-        in_specs=[vmem] * 12,
-        out_specs=[vmem] * 6,
+        in_specs=[vmem] * 8,
+        out_specs=[vmem] * 5,
         out_shape=[
             jax.ShapeDtypeStruct(dx.shape, BF16),
             jax.ShapeDtypeStruct(dx.shape, BF16),
             jax.ShapeDtypeStruct((rows, part), F32),
             jax.ShapeDtypeStruct((rows, part), F32),
             jax.ShapeDtypeStruct((rows, small), F32),
-            jax.ShapeDtypeStruct((2, rows, own[0].shape[1]), F32),
         ],
         scratch_shapes=[
-            pltpu.VMEM((2, rows, own[0].shape[1]), BF16),
-            pltpu.VMEM((2, rows, own[0].shape[1]), BF16),
             pltpu.VMEM((2 * rows, columns), BF16),
             pltpu.VMEM((2 * rows, columns), BF16),
             pltpu.VMEM((rows, columns), BF16),
@@ -1064,12 +1044,13 @@
             vmem_limit_bytes=56 * 2**20, collective_id=0, has_side_effects=True
         ),
         name="finish",
-    )(dx, out, q_keep, q_send, o_keep, o_send, s_send, s_keep, *own)
-
-
-def assemble_kernel(own_ref, far_ref, gate_ref, up_ref, down_ref):
+    )(dx, out, q_keep, q_send, o_keep, o_send, s_send, s_keep)
+
+
+def assemble_kernel(a_keep, a_got, b_keep, b_got, far_ref, gate_ref, up_ref, down_ref):
     count, rows, columns = gate_ref.shape
-    a, b = [own_ref[side] + far_ref[side].astype(F32) for side in (0, 1)]
+    a = a_keep[...] + a_got[...].astype(F32) + far_ref[0].astype(F32)
+    b = b_keep[...] + b_got[...].astype(F32) + far_ref[1].astype(F32)
     gate = jnp.concatenate([a[:, :512], a[:, 1024:1536], b[:, 512:1024]], axis=1)
     up = jnp.concatenate([a[:, 512:1024], b[:, :512], b[:, 1024:1536]], axis=1)
     down = jnp.concatenate([a[:, 1536:], b[:, 1536:]], axis=1)
@@ -1083,18 +1064,18 @@
 
 
 def assemble(own, far_sum, count):
-    _, rows, columns = own.shape
+    rows, columns = own[0].shape
     part = columns * 2 // (3 * count)
     vmem = pl.BlockSpec(memory_space=pltpu.VMEM)
     wide = jax.ShapeDtypeStruct((count, rows, part), F32)
     return pl.pallas_call(
         assemble_kernel,
-        in_specs=[vmem] * 2,
+        in_specs=[vmem] * 5,
         out_specs=[vmem] * 3,
         out_shape=[wide, wide, jax.ShapeDtypeStruct((count, part, rows), F32)],
         compiler_params=params(),
         name="assemble",
-    )(own, far_sum)
+    )(*own, far_sum)
 
 
 def turn_kernel(orders, d_ref, *refs):
@@ -1345,6 +1326,14 @@
     def first_moves(parts):
         return parts[0], dp_move(parts[1], xy[0]), parts[2], dp_move(parts[3], yx[0])
 
+    def second_moves(moved):
+        halves = []
+        for keep, got, bit in ((*moved[:2], xy[1]), (*moved[2:], yx[1])):
+            x = keep.astype(F32) + got.astype(F32)
+            half = x.shape[0] // 2
+            halves += [x[:half], dp_move(x[half:].astype(BF16), bit)]
+        return halves
+
     def expert_lefts(n_a, d_a, keep):
         return n_a[keep], d_a[keep], n_a[2 + keep], d_a[2 + keep]
 
@@ -1385,6 +1374,7 @@
         far_sent = gradient_parts(EXPERT_JOBS, expert_lefts(n2_a, dy_a, 0), far_grads)
         dnn_moved, far_sent, *own = tie(dnn_moved, far_sent, *own)
         got = dp_move(far_sent, 1)
+        own = second_moves(own)
     yn, dnn_moved = tie(yn, dnn_moved)
     yn_moved = z_move(yn, near)
     dn2 = dn2 + dnn_moved.astype(F32)
@@ -1398,7 +1388,8 @@
     do = mm_nt(dhb, wo).astype(BF16)
     if halving:
         far_w = gradient_parts(EXPERT_JOBS, expert_lefts(n2_a, dy_a, 1), far_grads, got)
-        do, *far_w = tie(do, *far_w)
+        do, *both = tie(do, *far_w, *own)
+        far_w, own = both[:4], both[4:]
         far_w = first_moves(far_w)
     dq, dkv_two, dkv_one, dkv = attend_back(
         z_arg, start, q, o, do, lse, cos_full, sin_full, kvs, kv_heads
@@ -1409,8 +1400,7 @@
         *parts, dkv_sum, far_sum = mix(
             dq, o, (n1_t[0], n1_t[1], *dhb_t), dkv_one, dkv_two, far_w
         )
-        far_sum = [z_move(part, far) for part in jnp.split(far_sum.reshape(-1, far_sum.shape[2]), 2, axis=0)]
-        far_sum = jnp.concatenate(far_sum, axis=0).reshape(2, out_w, -1)
+        far_sum = z_move(far_sum, far)
         dkv_sum, yn_moved = tie(dkv_sum, yn_moved)
     else:
         dkv_one = z_move(dkv_one, [(b, a) for a, b in up_one])
@@ -1440,7 +1430,9 @@
     result = h + y + yn_moved.astype(F32)
     result_out = mm_tn(unpack, result.astype(BF16)).astype(BF16)
 
-    if not halving:
+    if halving:
+        sum_gate, sum_up, sum_down = assemble(own, far_sum, experts_n)
+    else:
         lefts = (n2_a[0], dy_a[0])
         far_sums = [dp_sum(mm(a, b).astype(BF16)) for a, b in zip(lefts, far_grads[::-1])]
         own_sums = [dp_sum(mm(a, b).astype(BF16)) for a, b in zip(lefts, own_grads[::-1])]
@@ -1470,16 +1462,14 @@
             (mm(left, dkv_wide) + column).astype(BF16) for left, column in zip(n1_t[2:], columns)
         ]
         dx_out = mm_tn(unpack, dx.astype(BF16)).astype(BF16).reshape(dp_count, share, width)
-        back, back_out, sum_query, sum_out, small, own_sum = finish(
+        back, back_out, sum_query, sum_out, small = finish(
             dx_out,
             result_out.reshape(dp_count, share, width),
             *parts,
             kv_send,
             kv_keep,
-            own,
             tensor_count,
         )
-        sum_gate, sum_up, sum_down = assemble(own_sum, far_sum, experts_n)
         grad_tokens = mm_tn(pack, back.reshape(rows, width)).astype(BF16)
         outputs = mm_tn(pack, back_out.reshape(rows, width)).astype(BF16)
     else:

time: 655 us -> 641 us (0.979); the launches traced: 645 us -> 638 us
  Pallas kernels: 494 us -> 477 us
    pallas_call x2, Pallas kernels: 119 us -> 100 us  [the longest x1 94.1 us: finish(): pl.pallas_call(finish_kernel, in_specs=[vmem] * 8, out_specs=[vmem] * 5,...]
    pallas_call x1, Pallas kernels: 7.82 us -> 19.5 us  [project_query(): pl.pallas_call(project_query_kernel, grid_spec=pltpu.PrefetchScalarGridSp...]
    pallas_call x1, Pallas kernels: 36.2 us -> 27.7 us  [gradients(): pl.pallas_call(functools.partial(gradient_kernel, jobs, len(keep_lefts),...]
  transfers between devices with their start and end apart: 19 -> 20, of which waited for: 5 -> 5; matrix products, arithmetic and copies ran while one was open for 12% -> 14% of each run, Pallas kernels for 69% -> 69%
where the time goes in v5:
time: 641 us; the launch traced here: 638 us
  Pallas kernels  477 us (74%)
  local copies, waits for them, and re-layouts  43.3 us (7%)
  matrix products  40 us (6%)
  other arithmetic  25.7 us (4%)
  starting transfers between devices  19.3 us (3%)
  waiting for transfers between devices  18.4 us (3%)
  between operations  14.8 us (2%)
    pallas_call x4, Pallas kernels, experts(): pl.pallas_call(functools.partial(expert_kernel, chunk, before is None, la...  94.7 us
    pallas_call x1, Pallas kernels, finish(): pl.pallas_call(finish_kernel, in_specs=[vmem] * 8, out_specs=[vmem] * 5,...  94.1 us
    pallas_call x1, Pallas kernels, keyval(): pl.pallas_call(keyval_kernel, in_specs=[vmem] * 7, out_specs=[vmem] * 6,...  60.9 us
    pallas_call x1, Pallas kernels, mix(): pl.pallas_call(mix_kernel, in_specs=[vmem] * 12, out_specs=[vmem] * 6, ou...  33.8 us
    pallas_call x2, Pallas kernels, gradient_parts(): pl.pallas_call(functools.partial(part_kernel, jobs, len(lefts), len(right...  30.7 us
    pallas_call x1, Pallas kernels, open_moves(): pl.pallas_call(open_kernel, in_specs=[vmem] * 3, out_specs=[vmem] * 3, ou...  30.5 us
    pallas_call x1, Pallas kernels, attend_back(): pl.pallas_call(functools.partial(attend_back_kernel, kv_heads), grid_spec...  29.9 us
    pallas_call x1, Pallas kernels, gradients(): pl.pallas_call(functools.partial(gradient_kernel, jobs, len(keep_lefts),...  27.7 us
  transfers between devices with their start and end apart: 20, of which 5 were waited for; matrix products, arithmetic and copies ran while one was open for 14% of the time, Pallas kernels for 69%

profile of v5, /device:TPU:0, one launch (start us, length us, event | category | flops | bytes accessed | tf_op | source)
XLA Modules:
  0.0 638.0 jit_solution(10246736557710039145)
XLA Ops:
  10.5 3.8 concatenate.24
  20.9 30.5 %open_moves.1 = (bf16[8,64,1664]{2,1,0:T(8,128)(2,1)S(1)}, bf16[4,192,384]{2,1,0:T(8,128)(2,1)S(1)}, bf16[4,48,1536]{2,1,0:T(8,128)(2,1)S(1)}) custom-call(bf16[8,64,1664]{2,1,0:T(8,128)(2,1)S(1)} %bitcast.51, bf16[192,384]{1,0:T(8,128)(2,1)S(1)} %constant_dynamic-slice_fusion.12.q_ref, bf16[48,1536]{1,0:T(8,128)(2,1)S(1)} %constant_dynamic-slice_fusion.11.o_ref), custom_call_target="tpu_custom_call" | custom-call | tf_op jit(solution)/shard_map/open_moves/pallas_call | solution.py:99
  56.2 3.2 collective-permute-start
  60.8 2.9 fusion.8
  72.6 60.9 %keyval.1 = (bf16[512,512]{1,0:T(8,128)(2,1)S(1)}, bf16[512,512]{1,0:T(8,128)(2,1)S(1)}, bf16[512,512]{1,0:T(8,128)(2,1)S(1)}, f32[4,8,128]{2,1,0:T(8,128)S(1)},...) custom-call(bf16[512,1536]{1,0:T(8,128)(2,1)S(1)} %multiply_convert_fusion.1.x_ref.refs_0_, ...), custom_call_target="tpu_custom_call" | custom-call | tf_op jit(solution)/shard_map/keyval/pallas_call | solution.py:194
  143.7 3.6 turn.5
  147.3 19.5 %project_query.1.q_ref = bf16[512,1536]{1,0:T(8,128)(2,1)} custom-call(s32[1]{0:T(128)} %bitcast.11.z_ref, bf16[512,1536]{1,0:T(8,128)(2,1)} %copy-done.2, bf16[8,4,192,384]{3,2,1,0:T(8,128)(2,1)} %bitcast.82, f32[512,128]{1,0:T(8,128)} %copy-done.7, f32[512,128]{1,0:T(8,128)} %copy-done.3), custom_call_target="tpu_custom_call" | custom-call | flops 2415919104 | bytes 7864320 | tf_op jit(solution)/shard_map/project_query/pallas_call | solution.py:228
  166.8 21.7 %attend.1 = (bf16[512,1536]{1,0:T(8,128)(2,1)}, f32[12,512,1]{2,1,0:T(8,128)}) custom-call(s32[1]{0:T(128)} %bitcast.11.z_ref, s32[512,1]{1,0:T(8,128)} %copy.113.start_ref, bf16[512,1536]{1,0:T(8,128)(2,1)} %project_query.1.q_ref, bf16[512,512]{1,0:T(8,128)(2,1)} %copy-done.13, bf16[512,512]{1,0:T(8,128)(2,1)} %copy-done.12, bf16[512,512]{1,0:T(8,128)(2,1)} %copy-done.11), custom_call_target="tpu_custom_call" | custom-call | flops 4831838208 | bytes 6291456 | tf_op jit(solution)/shard_map/attend/pallas_call | solution.py:348
  193.6 6.4 %multiply_reduce_fusion.4 = (f32[512]{0:T(512)S(1)}, f32[512,1536]{1,0:T(8,128)S(1)}) fusion(bf16[512,1536]{1,0:T(8,128)(2,1)S(1)} %copy-done.25, bf16[1536,1536]{1,0:T(8,128)(2,1)S(1)} %bitcast.59, f32[512,1664]{1,0:T(8,128)} %fusion.8), kind=kOutput, calls=%fused_computation.12 | convolution fusion | flops 2418277888 | bytes 12584960 | tf_op jit(solution)/shard_map/dot_general | solution.py:22
  207.1 22.8 %experts.4 = (f32[512,1536]{1,0:T(8,128)}, f32[512,1536]{1,0:T(8,128)}, bf16[1024,1536]{1,0:T(8,128)(2,1)}, bf16[1024,3072]{1,0:T(8,128)(2,1)}) custom-call(bf16[512,1536]{1,0:T(8,128)(2,1)} %multiply_convert_fusion.x_ref.refs_0_, bf16[512,1536]{1,0:T(8,128)(2,1)} %copy-done.17, bf16[512,1536]{1,0:T(8,128)(2,1)} %copy.119.gate_ref, ...), custom_call_target="tpu_custom_call" | custom-call | flops 14495514624 | bytes 26738688 | tf_op jit(solution)/shard_map/experts/pallas_call | solution.py:551
  230.0 6.9 %collective-permute-done.3.refs_1_.x_ref = bf16[512,1536]{1,0:T(8,128)(2,1)} collective-permute-done((bf16[512,1536]{1,0:T(8,128)(2,1)}, bf16[512,1536]{1,0:T(8,128)(2,1)}, u32[]{:S(2)}, u32[]{:S(2)}) %collective-permute-start.3) | collective-permute-done | bytes 1572896 | tf_op jit(solution)/shard_map/ppermute | solution.py:1168
  236.9 5.3 turn.4
  244.4 22.7 %experts.5 = (f32[512,1536]{1,0:T(8,128)}, f32[512,1536]{1,0:T(8,128)}, bf16[1024,1536]{1,0:T(8,128)(2,1)}, bf16[1024,3072]{1,0:T(8,128)(2,1)}) custom-call(bf16[512,1536]{1,0:T(8,128)(2,1)} %collective-permute-done.3.refs_1_.x_ref, bf16[512,1536]{1,0:T(8,128)(2,1)} %copy-done.26, ...), custom_call_target="tpu_custom_call", output_to_operand_aliasing={{2}: (6, {}), {3}: (7, {})} | custom-call | flops 14495514624 | bytes 26738688 | tf_op jit(solution)/shard_map/experts/pallas_call | solution.py:551
  268.9 5.4 turn.6
  274.2 27.7 %gradients.1 = (bf16[384,2304]{1,0:T(8,128)(2,1)}, bf16[384,2304]{1,0:T(8,128)(2,1)}, bf16[384,2304]{1,0:T(8,128)(2,1)}, bf16[384,2304]{1,0:T(8,128)(2,1)}) custom-call(bf16[768,1024]{1,0:T(8,128)(2,1)} %get-tuple-element.174.refs_0_, bf16[768,1024]{1,0:T(8,128)(2,1)} %get-tuple-element.176.refs_1_, bf16[768,1024]{1,0:T(8,128)(2,1)} %get-tuple-element.177.refs_2_, ...), custom_call_target="tpu_custom_call" | custom-call | flops 1000000000 | bytes 1000000 | tf_op jit(solution)/shard_map/gradients/pallas_call | solution.py:647
  305.7 24.8 %experts.6 = (bf16[512,1536]{1,0:T(8,128)(2,1)}, bf16[512,1536]{1,0:T(8,128)(2,1)}, bf16[1024,1536]{1,0:T(8,128)(2,1)}, bf16[1024,3072]{1,0:T(8,128)(2,1)}) custom-call(bf16[512,1536]{1,0:T(8,128)(2,1)} %collective-permute-done.3.refs_1_.x_ref, bf16[512,1536]{1,0:T(8,128)(2,1)} %copy-done.26, bf16[512,1536]{1,0:T(8,128)(2,1)} %copy.122.gate_ref, ...), custom_call_target="tpu_custom_call" | custom-call | flops 14495514624 | bytes 26738688 | tf_op jit(solution)/shard_map/experts/pallas_call | solution.py:551
  332.7 24.4 %experts.7 = (f32[512,1536]{1,0:T(8,128)}, f32[512,1536]{1,0:T(8,128)}, bf16[1024,1536]{1,0:T(8,128)(2,1)}, bf16[1024,3072]{1,0:T(8,128)(2,1)}) custom-call(bf16[512,1536]{1,0:T(8,128)(2,1)} %multiply_convert_fusion.x_ref.refs_0_, bf16[512,1536]{1,0:T(8,128)(2,1)} %copy-done.17, ...), custom_call_target="tpu_custom_call", output_to_operand_aliasing={{2}: (8, {}), {3}: (9, {})} | custom-call | flops 14495514624 | bytes 26738688 | tf_op jit(solution)/shard_map/experts/pallas_call | solution.py:551
  357.1 14.5 %gradient_parts.2 = bf16[2,768,2304]{2,1,0:T(8,128)(2,1)} custom-call(bf16[768,1024]{1,0:T(8,128)(2,1)} %get-tuple-element.174.refs_0_, bf16[768,1024]{1,0:T(8,128)(2,1)} %get-tuple-element.176.refs_1_, bf16[768,1024]{1,0:T(8,128)(2,1)} %get-tuple-element.177.refs_2_, bf16[768,1024]{1,0:T(8,128)(2,1)} %get-tuple-element.178.refs_3_, ...), custom_call_target="tpu_custom_call" | custom-call | flops 7247757312 | bytes 16515072 | tf_op jit(solution)/shard_map/gradient_parts/pallas_call | solution.py:711
  385.2 3.7 convolution_convert_fusion.6.do_ref
  391.6 16.2 %gradient_parts.3 = (bf16[384,2304]{1,0:T(8,128)(2,1)}, bf16[384,2304]{1,0:T(8,128)(2,1)}, bf16[384,2304]{1,0:T(8,128)(2,1)}, bf16[384,2304]{1,0:T(8,128)(2,1)}) custom-call(bf16[768,1024]{1,0:T(8,128)(2,1)} %get-tuple-element.179.refs_4_.refs_0_, bf16[768,1024]{1,0:T(8,128)(2,1)} %get-tuple-element.180.refs_5_.refs_1_, ...), custom_call_target="tpu_custom_call" | custom-call | flops 7247757312 | bytes 16515072 | tf_op jit(solution)/shard_map/gradient_parts/pallas_call | solution.py:711
  409.4 3.1 turn.7
  412.5 29.9 %attend_back.1 = (bf16[512,1536]{1,0:T(8,128)(2,1)}, bf16[512,512]{1,0:T(8,128)(2,1)}, bf16[512,512]{1,0:T(8,128)(2,1)}, f32[512,512]{1,0:T(8,128)}) custom-call(s32[1]{0:T(128)} %bitcast.11.z_ref, s32[512,1]{1,0:T(8,128)} %copy.113.start_ref, bf16[512,1536]{1,0:T(8,128)(2,1)} %project_query.1.q_ref, bf16[512,1536]{1,0:T(8,128)(2,1)} %get-tuple-element.157.o_ref, ...), custom_call_target="tpu_custom_call" | custom-call | flops 12079595520 | bytes 9437184 | tf_op jit(solution)/shard_map/attend_back/pallas_call | solution.py:453
  442.4 6.1 collective-permute-done.11.fa_got
  449.4 33.8 %mix.1 = (bf16[384,1536]{1,0:T(8,128)(2,1)}, bf16[384,1536]{1,0:T(8,128)(2,1)}, bf16[384,1536]{1,0:T(8,128)(2,1)}, bf16[384,1536]{1,0:T(8,128)(2,1)}, bf16[512,5...) custom-call(bf16[512,1536]{1,0:T(8,128)(2,1)} %get-tuple-element.232.dq_ref, bf16[512,1536]{1,0:T(8,128)(2,1)} %get-tuple-element.157.o_ref, ...), custom_call_target="tpu_custom_call" | custom-call | tf_op jit(solution)/shard_map/mix/pallas_call | solution.py:846
  488.4 9.8 %project_back.1 = f32[512,1536]{1,0:T(8,128)} custom-call(s32[1]{0:T(128)} %bitcast.11.z_ref, bf16[512,1536]{1,0:T(8,128)(2,1)} %get-tuple-element.232.dq_ref, bf16[8,4,192,384]{3,2,1,0:T(8,128)(2,1)} %bitcast.83, bf16[512,512]{1,0:T(8,128)(2,1)} %pad_maximum_fusion.dkv_ref, bf16[1536,512]{1,0:T(8,128)(2,1)} %wkv_ref.1), custom_call_target="tpu_custom_call" | custom-call | flops 3221225472 | bytes 9437184 | tf_op jit(solution)/shard_map/project_back/pallas_call | solution.py:272
  498.2 3.7 multiply_reduce_fusion.1
  507.1 3.1 add_convert_fusion.2.s_keep
  512.0 3.8 convolution_convert_fusion.2
  515.7 4.5 convolution_convert_fusion.3
  520.2 94.1 %finish.1 = (bf16[8,64,1536]{2,1,0:T(8,128)(2,1)}, bf16[8,64,1536]{2,1,0:T(8,128)(2,1)}, f32[192,384]{1,0:T(8,128)}, f32[192,384]{1,0:T(8,128)}, f32[192,640]{1,0:T(8,128)}) custom-call(bf16[8,64,1536]{2,1,0:T(8,128)(2,1)} %bitcast.55, bf16[8,64,1536]{2,1,0:T(8,128)(2,1)} %bitcast.54, bf16[384,1536]{1,0:T(8,128)(2,1)} %get-tuple-element.249.q_keep, ...), custom_call_target="tpu_custom_call" | custom-call | tf_op jit(solution)/shard_map/finish/pallas_call | solution.py:1010
  617.8 3.7 convolution_convert_fusion
  623.7 6.2 assemble.1
  (233 shorter events, 94.9 us)
Async XLA Ops:
  7.2 9.7 %copy-start = (bf16[512,1536]{1,0:T(8,128)(2,1)S(1)}, bf16[512,1536]{1,0:T(8,128)(2,1)}, u32[]{:S(2)}) copy-start(bf16[512,1536]{1,0:T(8,128)(2,1)} %param.19) | copy-start | bytes 4718596
  7.2 140.1 %all-gather.6.cloned.1.call-start = ((), (), s32[]{:S(2)}) async-start(), calls=%async_computation | async-start | bytes 5308416 | tf_op jit(solution)/shard_map/all_gather | solution.py:1182
  8.4 8.5 %copy-start.46 = (s32[512]{0:T(512)}, s32[512]{0:T(512)S(1)}, u32[]{:S(2)}) copy-start(s32[512]{0:T(512)S(1)} %get-tuple-element.308) | copy-start | bytes 6148
  53.0 137.8 %all-gather.8.cloned.1.call-start = ((), (), s32[]{:S(2)}) async-start(), calls=%async_computation.1 | async-start | bytes 5308416 | tf_op jit(solution)/shard_map/all_gather | solution.py:1182
  53.8 248.1 %all-gather.10.cloned.1.call-start = ((), (), s32[]{:S(2)}) async-start(), calls=%async_computation.2 | async-start | bytes 5308416 | tf_op jit(solution)/shard_map/all_gather | solution.py:1182
  56.2 81.0 %collective-permute-start = (bf16[192,1536]{1,0:T(8,128)(2,1)}, bf16[192,1536]{1,0:T(8,128)(2,1)}, u32[]{:S(2)}, u32[]{:S(2)}) collective-permute-start(bf16[192,1536]{1,0:T(8,128)(2,1)} %get-tuple-element.144), channel_id=1, source_target_pairs={{0,2},{1,3},{2,0},{3,1},{4,6},{5,7},{6,4},{7,5},{8,10},{9,11},{10,... | collective-permute-start | bytes 1769480 | tf_op jit(solution)/shard_map/ppermute | solution.py:1168
  59.3 77.8 %collective-permute-start.1 = (bf16[192,1536]{1,0:T(8,128)(2,1)}, bf16[192,1536]{1,0:T(8,128)(2,1)}, u32[]{:S(2)}, u32[]{:S(2)}) collective-permute-start(bf16[192,1536]{1,0:T(8,128)(2,1)} %get-tuple-element.145), channel_id=1, source_target_pairs={{0,2},{1,3},{2,0},{3,1},{4,6},{5,7},{6,4},{7,5},{8,10},{9,11},{10,... | collective-permute-start | bytes 1769480 | tf_op jit(solution)/shard_map/ppermute | solution.py:1168
  72.2 65.5 %copy-start.2 = (bf16[512,1536]{1,0:T(8,128)(2,1)}, bf16[512,1536]{1,0:T(8,128)(2,1)S(1)}, u32[]{:S(2)}) copy-start(bf16[512,1536]{1,0:T(8,128)(2,1)S(1)} %multiply_convert_fusion.1.x_ref.refs_0_) | copy-start | bytes 4718596
  137.2 167.0 %all-gather.12.cloned.1.call-start = ((), (), s32[]{:S(2)}) async-start(), calls=%async_computation.3 | async-start | bytes 5308416 | tf_op jit(solution)/shard_map/all_gather | solution.py:1182
  137.8 167.9 %all-gather.14.cloned.1.call-start = ((), (), s32[]{:S(2)}) async-start(), calls=%async_computation.4 | async-start | bytes 5308416 | tf_op jit(solution)/shard_map/all_gather | solution.py:1182
  140.2 26.6 %copy-start.17 = (bf16[512,1536]{1,0:T(8,128)(2,1)}, bf16[512,1536]{1,0:T(8,128)(2,1)S(1)}, u32[]{:S(2)}) copy-start(bf16[512,1536]{1,0:T(8,128)(2,1)S(1)} %convolution_convert_fusion.4.dy_ref.refs_0_) | copy-start | bytes 4718596
  140.2 48.3 %collective-permute-start.2 = (bf16[512,1536]{1,0:T(8,128)(2,1)S(1)}, bf16[512,1536]{1,0:T(8,128)(2,1)S(1)}, u32[]{:S(2)}, u32[]{:S(2)}) collective-permute-start(bf16[512,1536]{1,0:T(8,128)(2,1)S(1)} %convolution_convert_fusion.4.dy_ref.refs_0_), channel_id=1, source_target_pairs={{0,1},{1,0},{2,3},{3,2},{4,5},{5,4},{6,7},{7,6},{8,9},{9,8},{10,11... | collective-permute-start | bytes 4718600 | tf_op jit(solution)/shard_map/ppermute | solution.py:1168
  166.8 21.8 %copy-start.30 = (bf16[512,8]{1,0:T(8,128)(2,1)S(1)}, bf16[512,8]{1,0:T(8,128)(2,1)}, u32[]{:S(2)}) copy-start(bf16[512,8]{1,0:T(8,128)(2,1)} %copy-done.29) | copy-start | bytes 24580
  166.8 22.3 %copy-start.39 = (bf16[512,8]{0,1:T(8,128)(2,1)S(1)}, bf16[512,8]{0,1:T(8,128)(2,1)}, u32[]{:S(2)}) copy-start(bf16[512,8]{0,1:T(8,128)(2,1)} %copy-done.38) | copy-start | bytes 24580
  201.5 35.4 %collective-permute-start.3 = (bf16[512,1536]{1,0:T(8,128)(2,1)}, bf16[512,1536]{1,0:T(8,128)(2,1)}, u32[]{:S(2)}, u32[]{:S(2)}) collective-permute-start(bf16[512,1536]{1,0:T(8,128)(2,1)} %multiply_convert_fusion.x_ref.refs_0_), channel_id=1, source_target_pairs={{0,1},{1,0},{2,3},{3,2},{4,5},{5,4},{6,7},{7,6},{8,9},{9,8},{10,11... | collective-permute-start | bytes 4718600 | tf_op jit(solution)/shard_map/ppermute | solution.py:1168
  230.0 12.2 %copy-start.28 = (bf16[192,1536]{1,0:T(8,128)(2,1)S(1)}, bf16[192,1536]{1,0:T(8,128)(2,1)}, u32[]{:S(2)}) copy-start(bf16[192,1536]{1,0:T(8,128)(2,1)} %constant_dynamic-slice_fusion.8) | copy-start | bytes 1769476
  242.1 26.7 %collective-permute-start.4 = (bf16[192,1536]{1,0:T(8,128)(2,1)S(1)}, bf16[192,1536]{1,0:T(8,128)(2,1)}, u32[]{:S(2)}, u32[]{:S(2)}) collective-permute-start(bf16[192,1536]{1,0:T(8,128)(2,1)S(1)} %copy-done.28), channel_id=1, source_target_pairs={{0,2},{1,3},{2,0},{3,1},{4,6},{5,7},{6,4},{7,5},{8,10},{9,11},{10,... | collective-permute-start | bytes 1769480 | tf_op jit(solution)/shard_map/ppermute | solution.py:1168
  301.9 69.7 %collective-permute-start.6 = (bf16[384,2304]{1,0:T(8,128)(2,1)}, bf16[384,2304]{1,0:T(8,128)(2,1)}, u32[]{:S(2)}, u32[]{:S(2)}) collective-permute-start(bf16[384,2304]{1,0:T(8,128)(2,1)} %get-tuple-element.211), channel_id=1, source_target_pairs={{0,8},{4,12},{8,0},{12,4},{16,24},{20,28},{24,16},{28,20},{1,9},{5... | collective-permute-start | bytes 5308424 | tf_op jit(solution)/shard_map/ppermute | solution.py:1171
  302.0 69.6 %collective-permute-start.7 = (bf16[384,2304]{1,0:T(8,128)(2,1)}, bf16[384,2304]{1,0:T(8,128)(2,1)}, u32[]{:S(2)}, u32[]{:S(2)}) collective-permute-start(bf16[384,2304]{1,0:T(8,128)(2,1)} %get-tuple-element.213), channel_id=1, source_target_pairs={{0,16},{4,20},{8,24},{12,28},{16,0},{20,4},{24,8},{28,12},{1,17},{... | collective-permute-start | bytes 5308424 | tf_op jit(solution)/shard_map/ppermute | solution.py:1171
  330.5 41.1 %collective-permute-start.5 = (bf16[512,1536]{1,0:T(8,128)(2,1)}, bf16[512,1536]{1,0:T(8,128)(2,1)S(1)}, u32[]{:S(2)}, u32[]{:S(2)}) collective-permute-start(bf16[512,1536]{1,0:T(8,128)(2,1)} %get-tuple-element.207), channel_id=1, source_target_pairs={{0,1},{1,0},{2,3},{3,2},{4,5},{5,4},{6,7},{7,6},{8,9},{9,8},{10,11... | collective-permute-start | bytes 4718600 | tf_op jit(solution)/shard_map/ppermute | solution.py:1168
  371.6 20.0 %collective-permute-start.8 = (bf16[2,768,2304]{2,1,0:T(8,128)(2,1)}, bf16[2,768,2304]{2,1,0:T(8,128)(2,1)}, u32[]{:S(2)}, u32[]{:S(2)}) collective-permute-start(bf16[2,768,2304]{2,1,0:T(8,128)(2,1)} %gradient_parts.2), channel_id=1, source_target_pairs={{0,4},{4,0},{8,12},{12,8},{16,20},{20,16},{24,28},{28,24},{1,5},{5... | collective-permute-start | bytes 21233672 | tf_op jit(solution)/shard_map/ppermute | solution.py:1171
  375.2 32.6 %collective-permute-start.10 = (bf16[192,2304]{1,0:T(8,128)(2,1)}, bf16[192,2304]{1,0:T(8,128)(2,1)}, u32[]{:S(2)}, u32[]{:S(2)}) collective-permute-start(bf16[192,2304]{1,0:T(8,128)(2,1)} %slice.158), channel_id=1, source_target_pairs={{0,8},{4,12},{8,0},{12,4},{16,24},{20,28},{24,16},{28,20},{1,9},{5... | collective-permute-start | bytes 2654216 | tf_op jit(solution)/shard_map/ppermute | solution.py:1171
  379.2 28.6 %collective-permute-start.9 = (bf16[192,2304]{1,0:T(8,128)(2,1)}, bf16[192,2304]{1,0:T(8,128)(2,1)}, u32[]{:S(2)}, u32[]{:S(2)}) collective-permute-start(bf16[192,2304]{1,0:T(8,128)(2,1)} %slice.159), channel_id=1, source_target_pairs={{0,16},{4,20},{8,24},{12,28},{16,0},{20,4},{24,8},{28,12},{1,17},{... | collective-permute-start | bytes 2654216 | tf_op jit(solution)/shard_map/ppermute | solution.py:1171
  407.8 40.7 %collective-permute-start.11 = (bf16[384,2304]{1,0:T(8,128)(2,1)}, bf16[384,2304]{1,0:T(8,128)(2,1)}, u32[]{:S(2)}, u32[]{:S(2)}) collective-permute-start(bf16[384,2304]{1,0:T(8,128)(2,1)} %get-tuple-element.229), channel_id=1, source_target_pairs={{0,8},{4,12},{8,0},{12,4},{16,24},{20,28},{24,16},{28,20},{1,9},{5... | collective-permute-start | bytes 5308424 | tf_op jit(solution)/shard_map/ppermute | solution.py:1171
  409.0 40.3 %collective-permute-start.12 = (bf16[384,2304]{1,0:T(8,128)(2,1)}, bf16[384,2304]{1,0:T(8,128)(2,1)}, u32[]{:S(2)}, u32[]{:S(2)}) collective-permute-start(bf16[384,2304]{1,0:T(8,128)(2,1)} %get-tuple-element.231), channel_id=1, source_target_pairs={{0,16},{4,20},{8,24},{12,28},{16,0},{20,4},{24,8},{28,12},{1,17},{... | collective-permute-start | bytes 5308424 | tf_op jit(solution)/shard_map/ppermute | solution.py:1171
  409.1 74.1 %collective-permute-start.13 = (bf16[512,1536]{1,0:T(8,128)(2,1)}, bf16[512,1536]{1,0:T(8,128)(2,1)}, u32[]{:S(2)}, u32[]{:S(2)}) collective-permute-start(bf16[512,1536]{1,0:T(8,128)(2,1)} %get-tuple-element.245), channel_id=1, source_target_pairs={{0,1},{1,0},{2,3},{3,2},{4,5},{5,4},{6,7},{7,6},{8,9},{9,8},{10,11... | collective-permute-start | bytes 4718600 | tf_op jit(solution)/shard_map/ppermute | solution.py:1168
  449.4 33.8 %copy-start.27 = (f32[512,512]{1,0:T(8,128)S(1)}, f32[512,512]{1,0:T(8,128)}, u32[]{:S(2)}) copy-start(f32[512,512]{1,0:T(8,128)} %get-tuple-element.233) | copy-start | bytes 3145732
  484.7 139.0 %collective-permute-start.14 = (bf16[2,192,2304]{2,1,0:T(8,128)(2,1)}, bf16[2,192,2304]{2,1,0:T(8,128)(2,1)}, u32[]{:S(2)}, u32[]{:S(2)}) collective-permute-start(bf16[2,192,2304]{2,1,0:T(8,128)(2,1)} %get-tuple-element.264), channel_id=1, source_target_pairs={{0,2},{1,3},{2,0},{3,1},{4,6},{5,7},{6,4},{7,5},{8,10},{9,11},{10,... | collective-permute-start | bytes 5308424 | tf_op jit(solution)/shard_map/ppermute | solution.py:1168
  488.4 9.8 %copy-start.37 = (f32[1536]{0:T(1024)S(1)}, f32[1536]{0:T(1024)}, u32[]{:S(2)}) copy-start(f32[1536]{0:T(1024)} %param.20) | copy-start | bytes 18436
  488.4 9.8 %copy-start.43 = (f32[512]{0:T(512)S(1)}, f32[512]{0:T(512)}, u32[]{:S(2)}) copy-start(f32[512]{0:T(512)} %copy-done.42) | copy-start | bytes 6148
  520.2 97.6 %copy-start.47 = (s32[512]{0:T(512)S(1)}, s32[512]{0:T(512)}, u32[]{:S(2)}) copy-start(s32[512]{0:T(512)} %copy-done.46) | copy-start | bytes 6148
  621.5 9.8 %copy-start.1 = (bf16[512,1536]{1,0:T(8,128)(2,1)S(1)}, bf16[512,1536]{1,0:T(8,128)(2,1)}, u32[]{:S(2)}) copy-start(bf16[512,1536]{1,0:T(8,128)(2,1)} %param.19) | copy-start | bytes 4718596
  (41 other events, 148.4 us)
Sparse Core Ops, SparseCore 0:
  53.1 54.2 all-gather.5
  109.3 38.4 all-gather.7
  149.7 38.8 all-gather.9
  190.4 38.9 all-gather.11
  269.0 36.6 all-gather.13

commit v6 on v5

--- a/solution.py
+++ b/solution.py
@@ -1213,7 +1213,7 @@
     def piece(w, count):
         return lax.dynamic_slice_in_dim(w, member * count, count, 0)
 
-    wg_piece, wu_piece, wd_piece = [piece(w, hidden_piece) for w in (wg_own, wu_own, wd_own)]
+    wg_piece, wu_piece = [piece(w, hidden_piece) for w in (wg_own, wu_own)]
     packed_dy = mm(pack, cotangent).astype(BF16)
     packed, packed_dy = tie(packed, packed_dy)
     arrived, wq_z, wo_z = open_moves(
@@ -1285,24 +1285,7 @@
     dy_near = z_move(dy_rows, near)
     kvs = (kv_two, kv_one, kv)
     o, lse = attend(z_arg, start, q, kvs, kv_heads)
-    o, wd_piece, dy_near, counts, weight, marks_near = tie(
-        o, wd_piece, dy_near, counts, weight, marks_near
-    )
-
-    def kept_gates(routed, weight, at):
-        block = (z - 1 - jnp.arange(tensor_count, dtype=jnp.int32)) % tensor_count
-        base = jnp.sum(
-            jnp.where((block < at)[:, None], counts[:, 0, :experts_n], 0.0), axis=0
-        )
-        position = mm(lower, routed.astype(BF16)) + base[None, :]
-        weight = jnp.where(position < capacity, weight, 0.0).astype(BF16)
-        return row_major(jnp.repeat(weight, part_hidden, axis=1))
-
-    gate_own = kept_gates(routed, weight, z)
-    marks_near = marks_near.astype(F32)
-    gate_near = kept_gates(
-        marks_near[:, :experts_n], marks_near[:, experts_n : 2 * experts_n], z + 1 - 2 * (z % 2)
-    )
+    o, dy_near = tie(o, dy_near)
     wg_far = team_gather(wg_moved)
     wu_far = team_gather(wu_moved)
     h = x_rows + mm(o, wo)
@@ -1338,11 +1321,29 @@
         return n_a[keep], d_a[keep], n_a[2 + keep], d_a[2 + keep]
 
     xy, yx = (2, 4), (4, 2)
+    n2, counts, weight, marks_near = tie(n2, counts, weight, marks_near)
     n2_near = z_move(n2, near)
+
+    def kept_gates(routed, weight, at):
+        block = (z - 1 - jnp.arange(tensor_count, dtype=jnp.int32)) % tensor_count
+        base = jnp.sum(
+            jnp.where((block < at)[:, None], counts[:, 0, :experts_n], 0.0), axis=0
+        )
+        position = mm(lower, routed.astype(BF16)) + base[None, :]
+        weight = jnp.where(position < capacity, weight, 0.0).astype(BF16)
+        return row_major(jnp.repeat(weight, part_hidden, axis=1))
+
+    gate_own = kept_gates(routed, weight, z)
+    marks_near = marks_near.astype(F32)
+    gate_near = kept_gates(
+        marks_near[:, :experts_n], marks_near[:, experts_n : 2 * experts_n], z + 1 - 2 * (z % 2)
+    )
     y, dn2, *own_grads = experts(0, n2, dy_rows, gate_own, wg_own, wu_own, wd_own)
-    n2_near, y, wd_piece = tie(n2_near, y, wd_piece)
+    y, n1 = tie(y, n1)
+    n1_t = turned((n1,), *orders_a, *orders_b)
+    n2_near, y, wd_source = tie(n2_near, y, wd_own)
+    wd_piece = piece(wd_source, hidden_piece)
     n2_a = turned((n2, n2_near), *orders_a, *orders_b)
-    n1_t = turned((n1,), *orders_a, *orders_b)
     dy_near, *turns = tie(dy_near, *n2_a, *n1_t)
     n2_a, n1_t = turns[:4], turns[4:]
     wd_moved = z_move(wd_piece, far)

time: 641 us -> 653 us (1.019)
    pallas_call x4, Pallas kernels: 17.3 us -> 30.3 us  [turn(): pl.pallas_call(functools.partial(turn_kernel, orders), grid_spec=pltpu.Pr...]
    pallas_call x1, Pallas kernels: 19.5 us -> 7.88 us  [project_query(): pl.pallas_call(project_query_kernel, grid_spec=pltpu.PrefetchScalarGridSp...]
  transfers between devices with their start and end apart: 20 -> 20, of which waited for: 5 -> 6; matrix products, arithmetic and copies ran while one was open for 14% -> 14% of each run, Pallas kernels for 69% -> 69%
where the time goes in v6:
time: 653 us; the launch traced here: 645 us
  Pallas kernels  483 us (74%)
  local copies, waits for them, and re-layouts  45.8 us (7%)
  matrix products  39.8 us (6%)
  other arithmetic  26.2 us (4%)
  waiting for transfers between devices  18.6 us (3%)
  starting transfers between devices  17 us (3%)
  between operations  15 us (2%)
    pallas_call x1, Pallas kernels, finish(): pl.pallas_call(finish_kernel, in_specs=[vmem] * 8, out_specs=[vmem] * 5,...  97.3 us
    pallas_call x4, Pallas kernels, experts(): pl.pallas_call(functools.partial(expert_kernel, chunk, before is None, la...  95.5 us
    pallas_call x1, Pallas kernels, keyval(): pl.pallas_call(keyval_kernel, in_specs=[vmem] * 7, out_specs=[vmem] * 6,...  60.9 us
    pallas_call x1, Pallas kernels, mix(): pl.pallas_call(mix_kernel, in_specs=[vmem] * 12, out_specs=[vmem] * 6, ou...  34.9 us
    pallas_call x2, Pallas kernels, gradient_parts(): pl.pallas_call(functools.partial(part_kernel, jobs, len(lefts), len(right...  30.5 us
    pallas_call x1, Pallas kernels, open_moves(): pl.pallas_call(open_kernel, in_specs=[vmem] * 3, out_specs=[vmem] * 3, ou...  30.5 us
    pallas_call x4, Pallas kernels, turn(): pl.pallas_call(functools.partial(turn_kernel, orders), grid_spec=pltpu.Pr...  30.3 us
    pallas_call x1, Pallas kernels, attend_back(): pl.pallas_call(functools.partial(attend_back_kernel, kv_heads), grid_spec...  29.9 us
  transfers between devices with their start and end apart: 20, of which 6 were waited for; matrix products, arithmetic and copies ran while one was open for 14% of the time, Pallas kernels for 69%

profile of v6, /device:TPU:0, one launch (start us, length us, event | category | flops | bytes accessed | tf_op | source)
XLA Modules:
  0.0 645.2 jit_solution(3710394487360278223)
XLA Ops:
  10.5 3.8 concatenate.24
  20.9 30.5 %open_moves.1 = (bf16[8,64,1664]{2,1,0:T(8,128)(2,1)S(1)}, bf16[4,192,384]{2,1,0:T(8,128)(2,1)S(1)}, bf16[4,48,1536]{2,1,0:T(8,128)(2,1)S(1)}) custom-call(bf16[8,64,1664]{2,1,0:T(8,128)(2,1)S(1)} %bitcast.51, bf16[192,384]{1,0:T(8,128)(2,1)S(1)} %constant_dynamic-slice_fusion.12.q_ref, bf16[48,1536]{1,0:T(8,128)(2,1)S(1)} %constant_dynamic-slice_fusion.11.o_ref), custom_call_target="tpu_custom_call" | custom-call | tf_op jit(solution)/shard_map/open_moves/pallas_call | solution.py:99
  56.1 3.2 collective-permute-start
  72.6 60.9 %keyval.1 = (bf16[512,512]{1,0:T(8,128)(2,1)S(1)}, bf16[512,512]{1,0:T(8,128)(2,1)S(1)}, bf16[512,512]{1,0:T(8,128)(2,1)S(1)}, f32[4,8,128]{2,1,0:T(8,128)S(1)},...) custom-call(bf16[512,1536]{1,0:T(8,128)(2,1)S(1)} %multiply_convert_fusion.1.x_ref.refs_0_, ...), custom_call_target="tpu_custom_call" | custom-call | tf_op jit(solution)/shard_map/keyval/pallas_call | solution.py:194
  141.7 7.9 %project_query.1.q_ref = bf16[512,1536]{1,0:T(8,128)(2,1)} custom-call(s32[1]{0:T(128)} %bitcast.11.z_ref, bf16[512,1536]{1,0:T(8,128)(2,1)} %copy-done.2, bf16[8,4,192,384]{3,2,1,0:T(8,128)(2,1)} %bitcast.82, f32[512,128]{1,0:T(8,128)} %copy-done.7, f32[512,128]{1,0:T(8,128)} %copy-done.3), custom_call_target="tpu_custom_call" | custom-call | flops 2415919104 | bytes 7864320 | tf_op jit(solution)/shard_map/project_query/pallas_call | solution.py:228
  149.5 21.7 %attend.1 = (bf16[512,1536]{1,0:T(8,128)(2,1)}, f32[12,512,1]{2,1,0:T(8,128)}) custom-call(s32[1]{0:T(128)} %bitcast.11.z_ref, s32[512,1]{1,0:T(8,128)} %copy.113.start_ref, bf16[512,1536]{1,0:T(8,128)(2,1)} %project_query.1.q_ref, bf16[512,512]{1,0:T(8,128)(2,1)} %copy-done.13, bf16[512,512]{1,0:T(8,128)(2,1)} %copy-done.12, bf16[512,512]{1,0:T(8,128)(2,1)} %copy-done.11), custom_call_target="tpu_custom_call" | custom-call | flops 4831838208 | bytes 6291456 | tf_op jit(solution)/shard_map/attend/pallas_call | solution.py:348
  171.2 4.2 collective-permute-done.2.refs_1_.dy_ref
  175.4 3.3 copy.114
  178.8 6.2 multiply_reduce_fusion.4
  196.6 23.4 %experts.4 = (f32[512,1536]{1,0:T(8,128)}, f32[512,1536]{1,0:T(8,128)}, bf16[1024,1536]{1,0:T(8,128)(2,1)}, bf16[1024,3072]{1,0:T(8,128)(2,1)}) custom-call(bf16[512,1536]{1,0:T(8,128)(2,1)} %multiply_convert_fusion.x_ref.refs_0_, bf16[512,1536]{1,0:T(8,128)(2,1)} %copy-done.17, bf16[512,1536]{1,0:T(8,128)(2,1)} %copy.119.gate_ref, ...), custom_call_target="tpu_custom_call" | custom-call | flops 14495514624 | bytes 26738688 | tf_op jit(solution)/shard_map/experts/pallas_call | solution.py:551
  220.1 3.6 turn.5
  223.7 3.4 collective-permute-done.3.refs_1_.x_ref
  227.1 18.2 %turn.4 = (bf16[768,1024]{1,0:T(8,128)(2,1)}, bf16[768,1024]{1,0:T(8,128)(2,1)}, bf16[768,1024]{1,0:T(8,128)(2,1)}, bf16[768,1024]{1,0:T(8,128)(2,1)}) custom-call(s32[1]{0:T(128)} %bitcast.19.d_ref, bf16[512,1536]{1,0:T(8,128)(2,1)} %multiply_convert_fusion.x_ref.refs_0_, bf16[512,1536]{1,0:T(8,128)(2,1)} %collective-permute-done.3.refs_1_.x_ref), custom_call_target="tpu_custom_call" | custom-call | bytes 9437184 | tf_op jit(solution)/shard_map/turn/pallas_call | solution.py:1102
  248.1 22.7 %experts.5 = (f32[512,1536]{1,0:T(8,128)}, f32[512,1536]{1,0:T(8,128)}, bf16[1024,1536]{1,0:T(8,128)(2,1)}, bf16[1024,3072]{1,0:T(8,128)(2,1)}) custom-call(bf16[512,1536]{1,0:T(8,128)(2,1)} %collective-permute-done.3.refs_1_.x_ref, bf16[512,1536]{1,0:T(8,128)(2,1)} %copy-done.26, ...), custom_call_target="tpu_custom_call", output_to_operand_aliasing={{2}: (6, {}), {3}: (7, {})} | custom-call | flops 14495514624 | bytes 26738688 | tf_op jit(solution)/shard_map/experts/pallas_call | solution.py:551
  272.3 5.3 turn.6
  277.7 27.5 %gradients.1 = (bf16[384,2304]{1,0:T(8,128)(2,1)}, bf16[384,2304]{1,0:T(8,128)(2,1)}, bf16[384,2304]{1,0:T(8,128)(2,1)}, bf16[384,2304]{1,0:T(8,128)(2,1)}) custom-call(bf16[768,1024]{1,0:T(8,128)(2,1)} %get-tuple-element.178.refs_0_, bf16[768,1024]{1,0:T(8,128)(2,1)} %get-tuple-element.180.refs_1_, bf16[768,1024]{1,0:T(8,128)(2,1)} %get-tuple-element.181.refs_2_, ...), custom_call_target="tpu_custom_call" | custom-call | flops 1000000000 | bytes 1000000 | tf_op jit(solution)/shard_map/gradients/pallas_call | solution.py:647
  309.4 24.8 %experts.6 = (bf16[512,1536]{1,0:T(8,128)(2,1)}, bf16[512,1536]{1,0:T(8,128)(2,1)}, bf16[1024,1536]{1,0:T(8,128)(2,1)}, bf16[1024,3072]{1,0:T(8,128)(2,1)}) custom-call(bf16[512,1536]{1,0:T(8,128)(2,1)} %collective-permute-done.3.refs_1_.x_ref, bf16[512,1536]{1,0:T(8,128)(2,1)} %copy-done.26, bf16[512,1536]{1,0:T(8,128)(2,1)} %copy.122.gate_ref, ...), custom_call_target="tpu_custom_call" | custom-call | flops 14495514624 | bytes 26738688 | tf_op jit(solution)/shard_map/experts/pallas_call | solution.py:551
  336.0 24.5 %experts.7 = (f32[512,1536]{1,0:T(8,128)}, f32[512,1536]{1,0:T(8,128)}, bf16[1024,1536]{1,0:T(8,128)(2,1)}, bf16[1024,3072]{1,0:T(8,128)(2,1)}) custom-call(bf16[512,1536]{1,0:T(8,128)(2,1)} %multiply_convert_fusion.x_ref.refs_0_, bf16[512,1536]{1,0:T(8,128)(2,1)} %copy-done.17, ...), custom_call_target="tpu_custom_call", output_to_operand_aliasing={{2}: (8, {}), {3}: (9, {})} | custom-call | flops 14495514624 | bytes 26738688 | tf_op jit(solution)/shard_map/experts/pallas_call | solution.py:551
  360.5 14.4 %gradient_parts.2 = bf16[2,768,2304]{2,1,0:T(8,128)(2,1)} custom-call(bf16[768,1024]{1,0:T(8,128)(2,1)} %get-tuple-element.178.refs_0_, bf16[768,1024]{1,0:T(8,128)(2,1)} %get-tuple-element.180.refs_1_, bf16[768,1024]{1,0:T(8,128)(2,1)} %get-tuple-element.181.refs_2_, bf16[768,1024]{1,0:T(8,128)(2,1)} %get-tuple-element.182.refs_3_, ...), custom_call_target="tpu_custom_call" | custom-call | flops 7247757312 | bytes 16515072 | tf_op jit(solution)/shard_map/gradient_parts/pallas_call | solution.py:711
  389.5 3.7 convolution_convert_fusion.6.do_ref
  395.9 16.0 %gradient_parts.3 = (bf16[384,2304]{1,0:T(8,128)(2,1)}, bf16[384,2304]{1,0:T(8,128)(2,1)}, bf16[384,2304]{1,0:T(8,128)(2,1)}, bf16[384,2304]{1,0:T(8,128)(2,1)}) custom-call(bf16[768,1024]{1,0:T(8,128)(2,1)} %get-tuple-element.183.refs_4_.refs_0_, bf16[768,1024]{1,0:T(8,128)(2,1)} %get-tuple-element.184.refs_5_.refs_1_, ...), custom_call_target="tpu_custom_call" | custom-call | flops 7247757312 | bytes 16515072 | tf_op jit(solution)/shard_map/gradient_parts/pallas_call | solution.py:711
  417.2 29.9 %attend_back.1 = (bf16[512,1536]{1,0:T(8,128)(2,1)}, bf16[512,512]{1,0:T(8,128)(2,1)}, bf16[512,512]{1,0:T(8,128)(2,1)}, f32[512,512]{1,0:T(8,128)}) custom-call(s32[1]{0:T(128)} %bitcast.11.z_ref, s32[512,1]{1,0:T(8,128)} %copy.113.start_ref, bf16[512,1536]{1,0:T(8,128)(2,1)} %project_query.1.q_ref, bf16[512,1536]{1,0:T(8,128)(2,1)} %get-tuple-element.157.o_ref, ...), custom_call_target="tpu_custom_call" | custom-call | flops 12079595520 | bytes 9437184 | tf_op jit(solution)/shard_map/attend_back/pallas_call | solution.py:453
  447.1 5.7 collective-permute-done.11.fa_got
  454.1 34.9 %mix.1 = (bf16[384,1536]{1,0:T(8,128)(2,1)}, bf16[384,1536]{1,0:T(8,128)(2,1)}, bf16[384,1536]{1,0:T(8,128)(2,1)}, bf16[384,1536]{1,0:T(8,128)(2,1)}, bf16[512,5...) custom-call(bf16[512,1536]{1,0:T(8,128)(2,1)} %get-tuple-element.236.dq_ref, bf16[512,1536]{1,0:T(8,128)(2,1)} %get-tuple-element.157.o_ref, ...), custom_call_target="tpu_custom_call" | custom-call | tf_op jit(solution)/shard_map/mix/pallas_call | solution.py:846
  492.0 9.9 %project_back.1 = f32[512,1536]{1,0:T(8,128)} custom-call(s32[1]{0:T(128)} %bitcast.11.z_ref, bf16[512,1536]{1,0:T(8,128)(2,1)} %get-tuple-element.236.dq_ref, bf16[8,4,192,384]{3,2,1,0:T(8,128)(2,1)} %bitcast.83, bf16[512,512]{1,0:T(8,128)(2,1)} %pad_maximum_fusion.dkv_ref, bf16[1536,512]{1,0:T(8,128)(2,1)} %wkv_ref.1), custom_call_target="tpu_custom_call" | custom-call | flops 3221225472 | bytes 9437184 | tf_op jit(solution)/shard_map/project_back/pallas_call | solution.py:272
  501.8 3.7 multiply_reduce_fusion.1
  510.7 3.1 add_convert_fusion.2.s_keep
  515.6 3.8 convolution_convert_fusion.2
  519.4 4.5 convolution_convert_fusion.3
  523.8 97.3 %finish.1 = (bf16[8,64,1536]{2,1,0:T(8,128)(2,1)}, bf16[8,64,1536]{2,1,0:T(8,128)(2,1)}, f32[192,384]{1,0:T(8,128)}, f32[192,384]{1,0:T(8,128)}, f32[192,640]{1,0:T(8,128)}) custom-call(bf16[8,64,1536]{2,1,0:T(8,128)(2,1)} %bitcast.55, bf16[8,64,1536]{2,1,0:T(8,128)(2,1)} %bitcast.54, bf16[384,1536]{1,0:T(8,128)(2,1)} %get-tuple-element.253.q_keep, ...), custom_call_target="tpu_custom_call" | custom-call | tf_op jit(solution)/shard_map/finish/pallas_call | solution.py:1010
  624.7 3.7 convolution_convert_fusion
  630.6 6.2 assemble.1
  (239 shorter events, 98.3 us)
Async XLA Ops:
  7.2 9.7 %copy-start = (bf16[512,1536]{1,0:T(8,128)(2,1)S(1)}, bf16[512,1536]{1,0:T(8,128)(2,1)}, u32[]{:S(2)}) copy-start(bf16[512,1536]{1,0:T(8,128)(2,1)} %param.19) | copy-start | bytes 4718596
  7.2 134.5 %all-gather.6.cloned.1.call-start = ((), (), s32[]{:S(2)}) async-start(), calls=%async_computation | async-start | bytes 5308416 | tf_op jit(solution)/shard_map/all_gather | solution.py:1182
  8.4 8.4 %copy-start.48 = (s32[512]{0:T(512)}, s32[512]{0:T(512)S(1)}, u32[]{:S(2)}) copy-start(s32[512]{0:T(512)S(1)} %get-tuple-element.312) | copy-start | bytes 6148
  53.0 122.4 %all-gather.8.cloned.1.call-start = ((), (), s32[]{:S(2)}) async-start(), calls=%async_computation.1 | async-start | bytes 5308416 | tf_op jit(solution)/shard_map/all_gather | solution.py:1182
  53.7 251.5 %all-gather.10.cloned.1.call-start = ((), (), s32[]{:S(2)}) async-start(), calls=%async_computation.2 | async-start | bytes 5308416 | tf_op jit(solution)/shard_map/all_gather | solution.py:1182
  56.1 80.9 %collective-permute-start = (bf16[192,1536]{1,0:T(8,128)(2,1)}, bf16[192,1536]{1,0:T(8,128)(2,1)}, u32[]{:S(2)}, u32[]{:S(2)}) collective-permute-start(bf16[192,1536]{1,0:T(8,128)(2,1)} %get-tuple-element.146), channel_id=1, source_target_pairs={{0,2},{1,3},{2,0},{3,1},{4,6},{5,7},{6,4},{7,5},{8,10},{9,11},{10,... | collective-permute-start | bytes 1769480 | tf_op jit(solution)/shard_map/ppermute | solution.py:1168
  59.3 77.8 %collective-permute-start.1 = (bf16[192,1536]{1,0:T(8,128)(2,1)}, bf16[192,1536]{1,0:T(8,128)(2,1)}, u32[]{:S(2)}, u32[]{:S(2)}) collective-permute-start(bf16[192,1536]{1,0:T(8,128)(2,1)} %get-tuple-element.147), channel_id=1, source_target_pairs={{0,2},{1,3},{2,0},{3,1},{4,6},{5,7},{6,4},{7,5},{8,10},{9,11},{10,... | collective-permute-start | bytes 1769480 | tf_op jit(solution)/shard_map/ppermute | solution.py:1168
  72.2 65.5 %copy-start.2 = (bf16[512,1536]{1,0:T(8,128)(2,1)}, bf16[512,1536]{1,0:T(8,128)(2,1)S(1)}, u32[]{:S(2)}) copy-start(bf16[512,1536]{1,0:T(8,128)(2,1)S(1)} %multiply_convert_fusion.1.x_ref.refs_0_) | copy-start | bytes 4718596
  137.1 171.2 %all-gather.12.cloned.1.call-start = ((), (), s32[]{:S(2)}) async-start(), calls=%async_computation.3 | async-start | bytes 5308416 | tf_op jit(solution)/shard_map/all_gather | solution.py:1182
  137.7 171.7 %all-gather.14.cloned.1.call-start = ((), (), s32[]{:S(2)}) async-start(), calls=%async_computation.4 | async-start | bytes 5308416 | tf_op jit(solution)/shard_map/all_gather | solution.py:1182
  140.2 9.3 %copy-start.17 = (bf16[512,1536]{1,0:T(8,128)(2,1)}, bf16[512,1536]{1,0:T(8,128)(2,1)S(1)}, u32[]{:S(2)}) copy-start(bf16[512,1536]{1,0:T(8,128)(2,1)S(1)} %convolution_convert_fusion.4.dy_ref.refs_0_) | copy-start | bytes 4718596
  140.2 35.2 %collective-permute-start.2 = (bf16[512,1536]{1,0:T(8,128)(2,1)S(1)}, bf16[512,1536]{1,0:T(8,128)(2,1)S(1)}, u32[]{:S(2)}, u32[]{:S(2)}) collective-permute-start(bf16[512,1536]{1,0:T(8,128)(2,1)S(1)} %convolution_convert_fusion.4.dy_ref.refs_0_), channel_id=1, source_target_pairs={{0,1},{1,0},{2,3},{3,2},{4,5},{5,4},{6,7},{7,6},{8,9},{9,8},{10,11... | collective-permute-start | bytes 4718600 | tf_op jit(solution)/shard_map/ppermute | solution.py:1168
  178.8 6.8 %copy-start.34 = (f32[1536]{0:T(1024)S(1)}, f32[1536]{0:T(1024)}, u32[]{:S(2)}) copy-start(f32[1536]{0:T(1024)} %param.24) | copy-start | bytes 18436
  192.5 34.6 %collective-permute-start.3 = (bf16[512,1536]{1,0:T(8,128)(2,1)}, bf16[512,1536]{1,0:T(8,128)(2,1)}, u32[]{:S(2)}, u32[]{:S(2)}) collective-permute-start(bf16[512,1536]{1,0:T(8,128)(2,1)} %multiply_convert_fusion.x_ref.refs_0_), channel_id=1, source_target_pairs={{0,1},{1,0},{2,3},{3,2},{4,5},{5,4},{6,7},{7,6},{8,9},{9,8},{10,11... | collective-permute-start | bytes 4718600 | tf_op jit(solution)/shard_map/ppermute | solution.py:1168
  246.4 25.9 %collective-permute-start.4 = (bf16[192,1536]{1,0:T(8,128)(2,1)S(1)}, bf16[192,1536]{1,0:T(8,128)(2,1)}, u32[]{:S(2)}, u32[]{:S(2)}) collective-permute-start(bf16[192,1536]{1,0:T(8,128)(2,1)S(1)} %constant_dynamic-slice_fusion.8), channel_id=1, source_target_pairs={{0,2},{1,3},{2,0},{3,1},{4,6},{5,7},{6,4},{7,5},{8,10},{9,11},{10,... | collective-permute-start | bytes 1769480 | tf_op jit(solution)/shard_map/ppermute | solution.py:1168
  305.3 69.7 %collective-permute-start.6 = (bf16[384,2304]{1,0:T(8,128)(2,1)}, bf16[384,2304]{1,0:T(8,128)(2,1)}, u32[]{:S(2)}, u32[]{:S(2)}) collective-permute-start(bf16[384,2304]{1,0:T(8,128)(2,1)} %get-tuple-element.215), channel_id=1, source_target_pairs={{0,8},{4,12},{8,0},{12,4},{16,24},{20,28},{24,16},{28,20},{1,9},{5... | collective-permute-start | bytes 5308424 | tf_op jit(solution)/shard_map/ppermute | solution.py:1171
  305.9 69.0 %collective-permute-start.7 = (bf16[384,2304]{1,0:T(8,128)(2,1)}, bf16[384,2304]{1,0:T(8,128)(2,1)}, u32[]{:S(2)}, u32[]{:S(2)}) collective-permute-start(bf16[384,2304]{1,0:T(8,128)(2,1)} %get-tuple-element.217), channel_id=1, source_target_pairs={{0,16},{4,20},{8,24},{12,28},{16,0},{20,4},{24,8},{28,12},{1,17},{... | collective-permute-start | bytes 5308424 | tf_op jit(solution)/shard_map/ppermute | solution.py:1171
  334.2 40.7 %collective-permute-start.5 = (bf16[512,1536]{1,0:T(8,128)(2,1)}, bf16[512,1536]{1,0:T(8,128)(2,1)S(1)}, u32[]{:S(2)}, u32[]{:S(2)}) collective-permute-start(bf16[512,1536]{1,0:T(8,128)(2,1)} %get-tuple-element.211), channel_id=1, source_target_pairs={{0,1},{1,0},{2,3},{3,2},{4,5},{5,4},{6,7},{7,6},{8,9},{9,8},{10,11... | collective-permute-start | bytes 4718600 | tf_op jit(solution)/shard_map/ppermute | solution.py:1168
  375.0 20.9 %collective-permute-start.8 = (bf16[2,768,2304]{2,1,0:T(8,128)(2,1)}, bf16[2,768,2304]{2,1,0:T(8,128)(2,1)}, u32[]{:S(2)}, u32[]{:S(2)}) collective-permute-start(bf16[2,768,2304]{2,1,0:T(8,128)(2,1)} %gradient_parts.2), channel_id=1, source_target_pairs={{0,4},{4,0},{8,12},{12,8},{16,20},{20,16},{24,28},{28,24},{1,5},{5... | collective-permute-start | bytes 21233672 | tf_op jit(solution)/shard_map/ppermute | solution.py:1171
  378.6 6.8 %copy-start.45 = (f32[512]{0:T(512)S(1)}, f32[512]{0:T(512)}, u32[]{:S(2)}) copy-start(f32[512]{0:T(512)} %copy-done.44) | copy-start | bytes 6148
  378.6 33.4 %collective-permute-start.10 = (bf16[192,2304]{1,0:T(8,128)(2,1)}, bf16[192,2304]{1,0:T(8,128)(2,1)}, u32[]{:S(2)}, u32[]{:S(2)}) collective-permute-start(bf16[192,2304]{1,0:T(8,128)(2,1)} %slice.158), channel_id=1, source_target_pairs={{0,8},{4,12},{8,0},{12,4},{16,24},{20,28},{24,16},{28,20},{1,9},{5... | collective-permute-start | bytes 2654216 | tf_op jit(solution)/shard_map/ppermute | solution.py:1171
  382.7 29.3 %collective-permute-start.9 = (bf16[192,2304]{1,0:T(8,128)(2,1)}, bf16[192,2304]{1,0:T(8,128)(2,1)}, u32[]{:S(2)}, u32[]{:S(2)}) collective-permute-start(bf16[192,2304]{1,0:T(8,128)(2,1)} %slice.159), channel_id=1, source_target_pairs={{0,16},{4,20},{8,24},{12,28},{16,0},{20,4},{24,8},{28,12},{1,17},{... | collective-permute-start | bytes 2654216 | tf_op jit(solution)/shard_map/ppermute | solution.py:1171
  412.0 40.8 %collective-permute-start.11 = (bf16[384,2304]{1,0:T(8,128)(2,1)}, bf16[384,2304]{1,0:T(8,128)(2,1)}, u32[]{:S(2)}, u32[]{:S(2)}) collective-permute-start(bf16[384,2304]{1,0:T(8,128)(2,1)} %get-tuple-element.233), channel_id=1, source_target_pairs={{0,8},{4,12},{8,0},{12,4},{16,24},{20,28},{24,16},{28,20},{1,9},{5... | collective-permute-start | bytes 5308424 | tf_op jit(solution)/shard_map/ppermute | solution.py:1171
  413.7 40.3 %collective-permute-start.12 = (bf16[384,2304]{1,0:T(8,128)(2,1)}, bf16[384,2304]{1,0:T(8,128)(2,1)}, u32[]{:S(2)}, u32[]{:S(2)}) collective-permute-start(bf16[384,2304]{1,0:T(8,128)(2,1)} %get-tuple-element.235), channel_id=1, source_target_pairs={{0,16},{4,20},{8,24},{12,28},{16,0},{20,4},{24,8},{28,12},{1,17},{... | collective-permute-start | bytes 5308424 | tf_op jit(solution)/shard_map/ppermute | solution.py:1171
  413.7 75.3 %collective-permute-start.13 = (bf16[512,1536]{1,0:T(8,128)(2,1)}, bf16[512,1536]{1,0:T(8,128)(2,1)}, u32[]{:S(2)}, u32[]{:S(2)}) collective-permute-start(bf16[512,1536]{1,0:T(8,128)(2,1)} %get-tuple-element.249), channel_id=1, source_target_pairs={{0,1},{1,0},{2,3},{3,2},{4,5},{5,4},{6,7},{7,6},{8,9},{9,8},{10,11... | collective-permute-start | bytes 4718600 | tf_op jit(solution)/shard_map/ppermute | solution.py:1168
  454.1 34.9 %copy-start.27 = (f32[512,512]{1,0:T(8,128)S(1)}, f32[512,512]{1,0:T(8,128)}, u32[]{:S(2)}) copy-start(f32[512,512]{1,0:T(8,128)} %get-tuple-element.237) | copy-start | bytes 3145732
  490.5 140.1 %collective-permute-start.14 = (bf16[2,192,2304]{2,1,0:T(8,128)(2,1)}, bf16[2,192,2304]{2,1,0:T(8,128)(2,1)}, u32[]{:S(2)}, u32[]{:S(2)}) collective-permute-start(bf16[2,192,2304]{2,1,0:T(8,128)(2,1)} %get-tuple-element.268), channel_id=1, source_target_pairs={{0,2},{1,3},{2,0},{3,1},{4,6},{5,7},{6,4},{7,5},{8,10},{9,11},{10,... | collective-permute-start | bytes 5308424 | tf_op jit(solution)/shard_map/ppermute | solution.py:1168
  492.0 9.9 %copy-start.37 = (f32[1536]{0:T(1024)S(1)}, f32[1536]{0:T(1024)}, u32[]{:S(2)}) copy-start(f32[1536]{0:T(1024)} %param.20) | copy-start | bytes 18436
  492.0 9.9 %copy-start.43 = (f32[512]{0:T(512)S(1)}, f32[512]{0:T(512)}, u32[]{:S(2)}) copy-start(f32[512]{0:T(512)} %copy-done.42) | copy-start | bytes 6148
  523.8 100.9 %copy-start.49 = (s32[512]{0:T(512)S(1)}, s32[512]{0:T(512)}, u32[]{:S(2)}) copy-start(s32[512]{0:T(512)} %copy-done.48) | copy-start | bytes 6148
  628.4 9.8 %copy-start.1 = (bf16[512,1536]{1,0:T(8,128)(2,1)S(1)}, bf16[512,1536]{1,0:T(8,128)(2,1)}, u32[]{:S(2)}) copy-start(bf16[512,1536]{1,0:T(8,128)(2,1)} %param.19) | copy-start | bytes 4718596
  630.6 6.9 %copy-start.32 = (f32[192,384]{1,0:T(8,128)S(1)}, f32[192,384]{1,0:T(8,128)}, u32[]{:S(2)}) copy-start(f32[192,384]{1,0:T(8,128)} %get-tuple-element.263) | copy-start | bytes 884740
  (44 other events, 151.3 us)
Sparse Core Ops, SparseCore 0:
  53.1 54.2 all-gather.5
  109.8 38.4 all-gather.7
  150.2 38.9 all-gather.9
  190.9 38.9 all-gather.11
  272.5 36.9 all-gather.13

commit v7 on v5

--- a/solution.py
+++ b/solution.py
@@ -1340,9 +1340,10 @@
     xy, yx = (2, 4), (4, 2)
     n2_near = z_move(n2, near)
     y, dn2, *own_grads = experts(0, n2, dy_rows, gate_own, wg_own, wu_own, wd_own)
+    y, n1 = tie(y, n1)
+    n1_t = turned((n1,), *orders_a, *orders_b)
     n2_near, y, wd_piece = tie(n2_near, y, wd_piece)
     n2_a = turned((n2, n2_near), *orders_a, *orders_b)
-    n1_t = turned((n1,), *orders_a, *orders_b)
     dy_near, *turns = tie(dy_near, *n2_a, *n1_t)
     n2_a, n1_t = turns[:4], turns[4:]
     wd_moved = z_move(wd_piece, far)

time: 641 us -> 646 us (level)
    pallas_call x4, Pallas kernels: 17.3 us -> 30.1 us  [turn(): pl.pallas_call(functools.partial(turn_kernel, orders), grid_spec=pltpu.Pr...]
    pallas_call x1, Pallas kernels: 19.5 us -> 7.89 us  [project_query(): pl.pallas_call(project_query_kernel, grid_spec=pltpu.PrefetchScalarGridSp...]
  transfers between devices with their start and end apart: 20 -> 20, of which waited for: 5 -> 6; matrix products, arithmetic and copies ran while one was open for 14% -> 14% of each run, Pallas kernels for 69% -> 70%
where the time goes in v7:
time: 646 us; the launch traced here: 638 us
  Pallas kernels  481 us (74%)
  local copies, waits for them, and re-layouts  43.5 us (7%)
  matrix products  40 us (6%)
  other arithmetic  25.7 us (4%)
  waiting for transfers between devices  17 us (3%)
  starting transfers between devices  15.6 us (2%)
  between operations  15 us (2%)
    pallas_call x1, Pallas kernels, finish(): pl.pallas_call(finish_kernel, in_specs=[vmem] * 8, out_specs=[vmem] * 5,...  97 us
    pallas_call x4, Pallas kernels, experts(): pl.pallas_call(functools.partial(expert_kernel, chunk, before is None, la...  94.8 us
    pallas_call x1, Pallas kernels, keyval(): pl.pallas_call(keyval_kernel, in_specs=[vmem] * 7, out_specs=[vmem] * 6,...  60.9 us
    pallas_call x1, Pallas kernels, mix(): pl.pallas_call(mix_kernel, in_specs=[vmem] * 12, out_specs=[vmem] * 6, ou...  34.3 us
    pallas_call x1, Pallas kernels, open_moves(): pl.pallas_call(open_kernel, in_specs=[vmem] * 3, out_specs=[vmem] * 3, ou...  30.4 us
    pallas_call x2, Pallas kernels, gradient_parts(): pl.pallas_call(functools.partial(part_kernel, jobs, len(lefts), len(right...  30.4 us
    pallas_call x4, Pallas kernels, turn(): pl.pallas_call(functools.partial(turn_kernel, orders), grid_spec=pltpu.Pr...  30.1 us
    pallas_call x1, Pallas kernels, attend_back(): pl.pallas_call(functools.partial(attend_back_kernel, kv_heads), grid_spec...  29.9 us
  transfers between devices with their start and end apart: 20, of which 6 were waited for; matrix products, arithmetic and copies ran while one was open for 14% of the time, Pallas kernels for 70%

profile of v7, /device:TPU:0, one launch (start us, length us, event | category | flops | bytes accessed | tf_op | source)
XLA Modules:
  0.0 637.8 jit_solution(6005131821258845121)
XLA Ops:
  10.5 3.8 concatenate.24
  20.9 30.4 %open_moves.1 = (bf16[8,64,1664]{2,1,0:T(8,128)(2,1)S(1)}, bf16[4,192,384]{2,1,0:T(8,128)(2,1)S(1)}, bf16[4,48,1536]{2,1,0:T(8,128)(2,1)S(1)}) custom-call(bf16[8,64,1664]{2,1,0:T(8,128)(2,1)S(1)} %bitcast.51, bf16[192,384]{1,0:T(8,128)(2,1)S(1)} %constant_dynamic-slice_fusion.12.q_ref, bf16[48,1536]{1,0:T(8,128)(2,1)S(1)} %constant_dynamic-slice_fusion.11.o_ref), custom_call_target="tpu_custom_call" | custom-call | tf_op jit(solution)/shard_map/open_moves/pallas_call | solution.py:99
  56.1 3.2 collective-permute-start
  60.8 2.9 fusion.8
  72.6 60.9 %keyval.1 = (bf16[512,512]{1,0:T(8,128)(2,1)S(1)}, bf16[512,512]{1,0:T(8,128)(2,1)S(1)}, bf16[512,512]{1,0:T(8,128)(2,1)S(1)}, f32[4,8,128]{2,1,0:T(8,128)S(1)},...) custom-call(bf16[512,1536]{1,0:T(8,128)(2,1)S(1)} %multiply_convert_fusion.1.x_ref.refs_0_, ...), custom_call_target="tpu_custom_call" | custom-call | tf_op jit(solution)/shard_map/keyval/pallas_call | solution.py:194
  143.6 7.9 %project_query.1.q_ref = bf16[512,1536]{1,0:T(8,128)(2,1)} custom-call(s32[1]{0:T(128)} %bitcast.11.z_ref, bf16[512,1536]{1,0:T(8,128)(2,1)} %copy-done.2, bf16[8,4,192,384]{3,2,1,0:T(8,128)(2,1)} %bitcast.82, f32[512,128]{1,0:T(8,128)} %copy-done.7, f32[512,128]{1,0:T(8,128)} %copy-done.3), custom_call_target="tpu_custom_call" | custom-call | flops 2415919104 | bytes 7864320 | tf_op jit(solution)/shard_map/project_query/pallas_call | solution.py:228
  151.5 21.7 %attend.1 = (bf16[512,1536]{1,0:T(8,128)(2,1)}, f32[12,512,1]{2,1,0:T(8,128)}) custom-call(s32[1]{0:T(128)} %bitcast.11.z_ref, s32[512,1]{1,0:T(8,128)} %copy.113.start_ref, bf16[512,1536]{1,0:T(8,128)(2,1)} %project_query.1.q_ref, bf16[512,512]{1,0:T(8,128)(2,1)} %copy-done.13, bf16[512,512]{1,0:T(8,128)(2,1)} %copy-done.12, bf16[512,512]{1,0:T(8,128)(2,1)} %copy-done.11), custom_call_target="tpu_custom_call" | custom-call | flops 4831838208 | bytes 6291456 | tf_op jit(solution)/shard_map/attend/pallas_call | solution.py:348
  180.6 6.3 multiply_reduce_fusion.4
  188.8 22.8 %experts.4 = (f32[512,1536]{1,0:T(8,128)}, f32[512,1536]{1,0:T(8,128)}, bf16[1024,1536]{1,0:T(8,128)(2,1)}, bf16[1024,3072]{1,0:T(8,128)(2,1)}) custom-call(bf16[512,1536]{1,0:T(8,128)(2,1)} %multiply_convert_fusion.x_ref.refs_0_, bf16[512,1536]{1,0:T(8,128)(2,1)} %copy-done.17, bf16[512,1536]{1,0:T(8,128)(2,1)} %copy.119.gate_ref, ...), custom_call_target="tpu_custom_call" | custom-call | flops 14495514624 | bytes 26738688 | tf_op jit(solution)/shard_map/experts/pallas_call | solution.py:551
  216.0 3.6 turn.5
  219.7 3.3 collective-permute-done.3.refs_1_.x_ref
  222.9 18.1 %turn.4 = (bf16[768,1024]{1,0:T(8,128)(2,1)}, bf16[768,1024]{1,0:T(8,128)(2,1)}, bf16[768,1024]{1,0:T(8,128)(2,1)}, bf16[768,1024]{1,0:T(8,128)(2,1)}) custom-call(s32[1]{0:T(128)} %bitcast.20.d_ref, bf16[512,1536]{1,0:T(8,128)(2,1)} %multiply_convert_fusion.x_ref.refs_0_, bf16[512,1536]{1,0:T(8,128)(2,1)} %collective-permute-done.3.refs_1_.x_ref), custom_call_target="tpu_custom_call" | custom-call | bytes 9437184 | tf_op jit(solution)/shard_map/turn/pallas_call | solution.py:1102
  241.9 22.6 %experts.5 = (f32[512,1536]{1,0:T(8,128)}, f32[512,1536]{1,0:T(8,128)}, bf16[1024,1536]{1,0:T(8,128)(2,1)}, bf16[1024,3072]{1,0:T(8,128)(2,1)}) custom-call(bf16[512,1536]{1,0:T(8,128)(2,1)} %collective-permute-done.3.refs_1_.x_ref, bf16[512,1536]{1,0:T(8,128)(2,1)} %copy-done.26, ...), custom_call_target="tpu_custom_call", output_to_operand_aliasing={{2}: (6, {}), {3}: (7, {})} | custom-call | flops 14495514624 | bytes 26738688 | tf_op jit(solution)/shard_map/experts/pallas_call | solution.py:551
  266.6 5.3 turn.6
  271.9 27.5 %gradients.1 = (bf16[384,2304]{1,0:T(8,128)(2,1)}, bf16[384,2304]{1,0:T(8,128)(2,1)}, bf16[384,2304]{1,0:T(8,128)(2,1)}, bf16[384,2304]{1,0:T(8,128)(2,1)}) custom-call(bf16[768,1024]{1,0:T(8,128)(2,1)} %get-tuple-element.178.refs_0_, bf16[768,1024]{1,0:T(8,128)(2,1)} %get-tuple-element.180.refs_1_, bf16[768,1024]{1,0:T(8,128)(2,1)} %get-tuple-element.181.refs_2_, ...), custom_call_target="tpu_custom_call" | custom-call | flops 1000000000 | bytes 1000000 | tf_op jit(solution)/shard_map/gradients/pallas_call | solution.py:647
  303.2 24.9 %experts.6 = (bf16[512,1536]{1,0:T(8,128)(2,1)}, bf16[512,1536]{1,0:T(8,128)(2,1)}, bf16[1024,1536]{1,0:T(8,128)(2,1)}, bf16[1024,3072]{1,0:T(8,128)(2,1)}) custom-call(bf16[512,1536]{1,0:T(8,128)(2,1)} %collective-permute-done.3.refs_1_.x_ref, bf16[512,1536]{1,0:T(8,128)(2,1)} %copy-done.26, bf16[512,1536]{1,0:T(8,128)(2,1)} %copy.122.gate_ref, ...), custom_call_target="tpu_custom_call" | custom-call | flops 14495514624 | bytes 26738688 | tf_op jit(solution)/shard_map/experts/pallas_call | solution.py:551
  329.9 24.4 %experts.7 = (f32[512,1536]{1,0:T(8,128)}, f32[512,1536]{1,0:T(8,128)}, bf16[1024,1536]{1,0:T(8,128)(2,1)}, bf16[1024,3072]{1,0:T(8,128)(2,1)}) custom-call(bf16[512,1536]{1,0:T(8,128)(2,1)} %multiply_convert_fusion.x_ref.refs_0_, bf16[512,1536]{1,0:T(8,128)(2,1)} %copy-done.17, ...), custom_call_target="tpu_custom_call", output_to_operand_aliasing={{2}: (8, {}), {3}: (9, {})} | custom-call | flops 14495514624 | bytes 26738688 | tf_op jit(solution)/shard_map/experts/pallas_call | solution.py:551
  354.3 14.4 %gradient_parts.2 = bf16[2,768,2304]{2,1,0:T(8,128)(2,1)} custom-call(bf16[768,1024]{1,0:T(8,128)(2,1)} %get-tuple-element.178.refs_0_, bf16[768,1024]{1,0:T(8,128)(2,1)} %get-tuple-element.180.refs_1_, bf16[768,1024]{1,0:T(8,128)(2,1)} %get-tuple-element.181.refs_2_, bf16[768,1024]{1,0:T(8,128)(2,1)} %get-tuple-element.182.refs_3_, ...), custom_call_target="tpu_custom_call" | custom-call | flops 7247757312 | bytes 16515072 | tf_op jit(solution)/shard_map/gradient_parts/pallas_call | solution.py:711
  382.3 3.8 convolution_convert_fusion.6.do_ref
  388.7 16.0 %gradient_parts.3 = (bf16[384,2304]{1,0:T(8,128)(2,1)}, bf16[384,2304]{1,0:T(8,128)(2,1)}, bf16[384,2304]{1,0:T(8,128)(2,1)}, bf16[384,2304]{1,0:T(8,128)(2,1)}) custom-call(bf16[768,1024]{1,0:T(8,128)(2,1)} %get-tuple-element.183.refs_4_.refs_0_, bf16[768,1024]{1,0:T(8,128)(2,1)} %get-tuple-element.184.refs_5_.refs_1_, ...), custom_call_target="tpu_custom_call" | custom-call | flops 7247757312 | bytes 16515072 | tf_op jit(solution)/shard_map/gradient_parts/pallas_call | solution.py:711
  406.5 3.1 turn.7
  409.6 29.9 %attend_back.1 = (bf16[512,1536]{1,0:T(8,128)(2,1)}, bf16[512,512]{1,0:T(8,128)(2,1)}, bf16[512,512]{1,0:T(8,128)(2,1)}, f32[512,512]{1,0:T(8,128)}) custom-call(s32[1]{0:T(128)} %bitcast.11.z_ref, s32[512,1]{1,0:T(8,128)} %copy.113.start_ref, bf16[512,1536]{1,0:T(8,128)(2,1)} %project_query.1.q_ref, bf16[512,1536]{1,0:T(8,128)(2,1)} %get-tuple-element.159.o_ref, ...), custom_call_target="tpu_custom_call" | custom-call | flops 12079595520 | bytes 9437184 | tf_op jit(solution)/shard_map/attend_back/pallas_call | solution.py:453
  439.5 6.2 collective-permute-done.11.fa_got
  446.3 34.3 %mix.1 = (bf16[384,1536]{1,0:T(8,128)(2,1)}, bf16[384,1536]{1,0:T(8,128)(2,1)}, bf16[384,1536]{1,0:T(8,128)(2,1)}, bf16[384,1536]{1,0:T(8,128)(2,1)}, bf16[512,5...) custom-call(bf16[512,1536]{1,0:T(8,128)(2,1)} %get-tuple-element.236.dq_ref, bf16[512,1536]{1,0:T(8,128)(2,1)} %get-tuple-element.159.o_ref, ...), custom_call_target="tpu_custom_call" | custom-call | tf_op jit(solution)/shard_map/mix/pallas_call | solution.py:846
  484.9 9.8 %project_back.1 = f32[512,1536]{1,0:T(8,128)} custom-call(s32[1]{0:T(128)} %bitcast.11.z_ref, bf16[512,1536]{1,0:T(8,128)(2,1)} %get-tuple-element.236.dq_ref, bf16[8,4,192,384]{3,2,1,0:T(8,128)(2,1)} %bitcast.83, bf16[512,512]{1,0:T(8,128)(2,1)} %pad_maximum_fusion.dkv_ref, bf16[1536,512]{1,0:T(8,128)(2,1)} %wkv_ref.1), custom_call_target="tpu_custom_call" | custom-call | flops 3221225472 | bytes 9437184 | tf_op jit(solution)/shard_map/project_back/pallas_call | solution.py:272
  494.8 3.7 multiply_reduce_fusion.1
  503.6 3.1 add_convert_fusion.2.s_keep
  508.5 3.8 convolution_convert_fusion.2
  512.3 4.5 convolution_convert_fusion.3
  516.8 97.0 %finish.1 = (bf16[8,64,1536]{2,1,0:T(8,128)(2,1)}, bf16[8,64,1536]{2,1,0:T(8,128)(2,1)}, f32[192,384]{1,0:T(8,128)}, f32[192,384]{1,0:T(8,128)}, f32[192,640]{1,0:T(8,128)}) custom-call(bf16[8,64,1536]{2,1,0:T(8,128)(2,1)} %bitcast.55, bf16[8,64,1536]{2,1,0:T(8,128)(2,1)} %bitcast.54, bf16[384,1536]{1,0:T(8,128)(2,1)} %get-tuple-element.253.q_keep, ...), custom_call_target="tpu_custom_call" | custom-call | tf_op jit(solution)/shard_map/finish/pallas_call | solution.py:1010
  617.3 3.7 convolution_convert_fusion
  623.2 6.2 assemble.1
  (233 shorter events, 93.7 us)
Async XLA Ops:
  7.2 9.7 %copy-start = (bf16[512,1536]{1,0:T(8,128)(2,1)S(1)}, bf16[512,1536]{1,0:T(8,128)(2,1)}, u32[]{:S(2)}) copy-start(bf16[512,1536]{1,0:T(8,128)(2,1)} %param.19) | copy-start | bytes 4718596
  7.2 136.4 %all-gather.6.cloned.1.call-start = ((), (), s32[]{:S(2)}) async-start(), calls=%async_computation | async-start | bytes 5308416 | tf_op jit(solution)/shard_map/all_gather | solution.py:1182
  8.4 8.5 %copy-start.46 = (s32[512]{0:T(512)}, s32[512]{0:T(512)S(1)}, u32[]{:S(2)}) copy-start(s32[512]{0:T(512)S(1)} %get-tuple-element.312) | copy-start | bytes 6148
  53.0 124.7 %all-gather.8.cloned.1.call-start = ((), (), s32[]{:S(2)}) async-start(), calls=%async_computation.1 | async-start | bytes 5308416 | tf_op jit(solution)/shard_map/all_gather | solution.py:1182
  53.8 245.7 %all-gather.10.cloned.1.call-start = ((), (), s32[]{:S(2)}) async-start(), calls=%async_computation.2 | async-start | bytes 5308416 | tf_op jit(solution)/shard_map/all_gather | solution.py:1182
  56.1 81.0 %collective-permute-start = (bf16[192,1536]{1,0:T(8,128)(2,1)}, bf16[192,1536]{1,0:T(8,128)(2,1)}, u32[]{:S(2)}, u32[]{:S(2)}) collective-permute-start(bf16[192,1536]{1,0:T(8,128)(2,1)} %get-tuple-element.146), channel_id=1, source_target_pairs={{0,2},{1,3},{2,0},{3,1},{4,6},{5,7},{6,4},{7,5},{8,10},{9,11},{10,... | collective-permute-start | bytes 1769480 | tf_op jit(solution)/shard_map/ppermute | solution.py:1168
  59.3 77.8 %collective-permute-start.1 = (bf16[192,1536]{1,0:T(8,128)(2,1)}, bf16[192,1536]{1,0:T(8,128)(2,1)}, u32[]{:S(2)}, u32[]{:S(2)}) collective-permute-start(bf16[192,1536]{1,0:T(8,128)(2,1)} %get-tuple-element.147), channel_id=1, source_target_pairs={{0,2},{1,3},{2,0},{3,1},{4,6},{5,7},{6,4},{7,5},{8,10},{9,11},{10,... | collective-permute-start | bytes 1769480 | tf_op jit(solution)/shard_map/ppermute | solution.py:1168
  72.2 65.5 %copy-start.2 = (bf16[512,1536]{1,0:T(8,128)(2,1)}, bf16[512,1536]{1,0:T(8,128)(2,1)S(1)}, u32[]{:S(2)}) copy-start(bf16[512,1536]{1,0:T(8,128)(2,1)S(1)} %multiply_convert_fusion.1.x_ref.refs_0_) | copy-start | bytes 4718596
  137.1 164.6 %all-gather.12.cloned.1.call-start = ((), (), s32[]{:S(2)}) async-start(), calls=%async_computation.3 | async-start | bytes 5308416 | tf_op jit(solution)/shard_map/all_gather | solution.py:1182
  137.7 165.5 %all-gather.14.cloned.1.call-start = ((), (), s32[]{:S(2)}) async-start(), calls=%async_computation.4 | async-start | bytes 5308416 | tf_op jit(solution)/shard_map/all_gather | solution.py:1182
  140.2 11.3 %copy-start.17 = (bf16[512,1536]{1,0:T(8,128)(2,1)}, bf16[512,1536]{1,0:T(8,128)(2,1)S(1)}, u32[]{:S(2)}) copy-start(bf16[512,1536]{1,0:T(8,128)(2,1)S(1)} %convolution_convert_fusion.4.dy_ref.refs_0_) | copy-start | bytes 4718596
  140.3 35.2 %collective-permute-start.2 = (bf16[512,1536]{1,0:T(8,128)(2,1)S(1)}, bf16[512,1536]{1,0:T(8,128)(2,1)S(1)}, u32[]{:S(2)}, u32[]{:S(2)}) collective-permute-start(bf16[512,1536]{1,0:T(8,128)(2,1)S(1)} %convolution_convert_fusion.4.dy_ref.refs_0_), channel_id=1, source_target_pairs={{0,1},{1,0},{2,3},{3,2},{4,5},{5,4},{6,7},{7,6},{8,9},{9,8},{10,11... | collective-permute-start | bytes 4718600 | tf_op jit(solution)/shard_map/ppermute | solution.py:1168
  151.5 24.0 %copy-start.30 = (bf16[512,8]{1,0:T(8,128)(2,1)S(1)}, bf16[512,8]{1,0:T(8,128)(2,1)}, u32[]{:S(2)}) copy-start(bf16[512,8]{1,0:T(8,128)(2,1)} %copy-done.29) | copy-start | bytes 24580
  151.5 24.5 %copy-start.39 = (bf16[512,8]{0,1:T(8,128)(2,1)S(1)}, bf16[512,8]{0,1:T(8,128)(2,1)}, u32[]{:S(2)}) copy-start(bf16[512,8]{0,1:T(8,128)(2,1)} %copy-done.38) | copy-start | bytes 24580
  188.4 34.5 %collective-permute-start.3 = (bf16[512,1536]{1,0:T(8,128)(2,1)}, bf16[512,1536]{1,0:T(8,128)(2,1)}, u32[]{:S(2)}, u32[]{:S(2)}) collective-permute-start(bf16[512,1536]{1,0:T(8,128)(2,1)} %multiply_convert_fusion.x_ref.refs_0_), channel_id=1, source_target_pairs={{0,1},{1,0},{2,3},{3,2},{4,5},{5,4},{6,7},{7,6},{8,9},{9,8},{10,11... | collective-permute-start | bytes 4718600 | tf_op jit(solution)/shard_map/ppermute | solution.py:1168
  216.0 25.0 %copy-start.28 = (bf16[192,1536]{1,0:T(8,128)(2,1)S(1)}, bf16[192,1536]{1,0:T(8,128)(2,1)}, u32[]{:S(2)}) copy-start(bf16[192,1536]{1,0:T(8,128)(2,1)} %constant_dynamic-slice_fusion.8) | copy-start | bytes 1769476
  241.1 25.5 %collective-permute-start.4 = (bf16[192,1536]{1,0:T(8,128)(2,1)S(1)}, bf16[192,1536]{1,0:T(8,128)(2,1)}, u32[]{:S(2)}, u32[]{:S(2)}) collective-permute-start(bf16[192,1536]{1,0:T(8,128)(2,1)S(1)} %copy-done.28), channel_id=1, source_target_pairs={{0,2},{1,3},{2,0},{3,1},{4,6},{5,7},{6,4},{7,5},{8,10},{9,11},{10,... | collective-permute-start | bytes 1769480 | tf_op jit(solution)/shard_map/ppermute | solution.py:1168
  299.5 69.3 %collective-permute-start.6 = (bf16[384,2304]{1,0:T(8,128)(2,1)}, bf16[384,2304]{1,0:T(8,128)(2,1)}, u32[]{:S(2)}, u32[]{:S(2)}) collective-permute-start(bf16[384,2304]{1,0:T(8,128)(2,1)} %get-tuple-element.215), channel_id=1, source_target_pairs={{0,8},{4,12},{8,0},{12,4},{16,24},{20,28},{24,16},{28,20},{1,9},{5... | collective-permute-start | bytes 5308424 | tf_op jit(solution)/shard_map/ppermute | solution.py:1171
  299.6 69.2 %collective-permute-start.7 = (bf16[384,2304]{1,0:T(8,128)(2,1)}, bf16[384,2304]{1,0:T(8,128)(2,1)}, u32[]{:S(2)}, u32[]{:S(2)}) collective-permute-start(bf16[384,2304]{1,0:T(8,128)(2,1)} %get-tuple-element.217), channel_id=1, source_target_pairs={{0,16},{4,20},{8,24},{12,28},{16,0},{20,4},{24,8},{28,12},{1,17},{... | collective-permute-start | bytes 5308424 | tf_op jit(solution)/shard_map/ppermute | solution.py:1171
  328.1 40.7 %collective-permute-start.5 = (bf16[512,1536]{1,0:T(8,128)(2,1)}, bf16[512,1536]{1,0:T(8,128)(2,1)S(1)}, u32[]{:S(2)}, u32[]{:S(2)}) collective-permute-start(bf16[512,1536]{1,0:T(8,128)(2,1)} %get-tuple-element.211), channel_id=1, source_target_pairs={{0,1},{1,0},{2,3},{3,2},{4,5},{5,4},{6,7},{7,6},{8,9},{9,8},{10,11... | collective-permute-start | bytes 4718600 | tf_op jit(solution)/shard_map/ppermute | solution.py:1168
  368.8 19.9 %collective-permute-start.8 = (bf16[2,768,2304]{2,1,0:T(8,128)(2,1)}, bf16[2,768,2304]{2,1,0:T(8,128)(2,1)}, u32[]{:S(2)}, u32[]{:S(2)}) collective-permute-start(bf16[2,768,2304]{2,1,0:T(8,128)(2,1)} %gradient_parts.2), channel_id=1, source_target_pairs={{0,4},{4,0},{8,12},{12,8},{16,20},{20,16},{24,28},{28,24},{1,5},{5... | collective-permute-start | bytes 21233672 | tf_op jit(solution)/shard_map/ppermute | solution.py:1171
  372.4 32.3 %collective-permute-start.10 = (bf16[192,2304]{1,0:T(8,128)(2,1)}, bf16[192,2304]{1,0:T(8,128)(2,1)}, u32[]{:S(2)}, u32[]{:S(2)}) collective-permute-start(bf16[192,2304]{1,0:T(8,128)(2,1)} %slice.158), channel_id=1, source_target_pairs={{0,8},{4,12},{8,0},{12,4},{16,24},{20,28},{24,16},{28,20},{1,9},{5... | collective-permute-start | bytes 2654216 | tf_op jit(solution)/shard_map/ppermute | solution.py:1171
  376.6 28.1 %collective-permute-start.9 = (bf16[192,2304]{1,0:T(8,128)(2,1)}, bf16[192,2304]{1,0:T(8,128)(2,1)}, u32[]{:S(2)}, u32[]{:S(2)}) collective-permute-start(bf16[192,2304]{1,0:T(8,128)(2,1)} %slice.159), channel_id=1, source_target_pairs={{0,16},{4,20},{8,24},{12,28},{16,0},{20,4},{24,8},{28,12},{1,17},{... | collective-permute-start | bytes 2654216 | tf_op jit(solution)/shard_map/ppermute | solution.py:1171
  404.7 41.0 %collective-permute-start.11 = (bf16[384,2304]{1,0:T(8,128)(2,1)}, bf16[384,2304]{1,0:T(8,128)(2,1)}, u32[]{:S(2)}, u32[]{:S(2)}) collective-permute-start(bf16[384,2304]{1,0:T(8,128)(2,1)} %get-tuple-element.233), channel_id=1, source_target_pairs={{0,8},{4,12},{8,0},{12,4},{16,24},{20,28},{24,16},{28,20},{1,9},{5... | collective-permute-start | bytes 5308424 | tf_op jit(solution)/shard_map/ppermute | solution.py:1171
  405.9 40.5 %collective-permute-start.12 = (bf16[384,2304]{1,0:T(8,128)(2,1)}, bf16[384,2304]{1,0:T(8,128)(2,1)}, u32[]{:S(2)}, u32[]{:S(2)}) collective-permute-start(bf16[384,2304]{1,0:T(8,128)(2,1)} %get-tuple-element.235), channel_id=1, source_target_pairs={{0,16},{4,20},{8,24},{12,28},{16,0},{20,4},{24,8},{28,12},{1,17},{... | collective-permute-start | bytes 5308424 | tf_op jit(solution)/shard_map/ppermute | solution.py:1171
  406.2 74.4 %collective-permute-start.13 = (bf16[512,1536]{1,0:T(8,128)(2,1)}, bf16[512,1536]{1,0:T(8,128)(2,1)}, u32[]{:S(2)}, u32[]{:S(2)}) collective-permute-start(bf16[512,1536]{1,0:T(8,128)(2,1)} %get-tuple-element.249), channel_id=1, source_target_pairs={{0,1},{1,0},{2,3},{3,2},{4,5},{5,4},{6,7},{7,6},{8,9},{9,8},{10,11... | collective-permute-start | bytes 4718600 | tf_op jit(solution)/shard_map/ppermute | solution.py:1168
  446.3 34.3 %copy-start.27 = (f32[512,512]{1,0:T(8,128)S(1)}, f32[512,512]{1,0:T(8,128)}, u32[]{:S(2)}) copy-start(f32[512,512]{1,0:T(8,128)} %get-tuple-element.237) | copy-start | bytes 3145732
  482.1 141.1 %collective-permute-start.14 = (bf16[2,192,2304]{2,1,0:T(8,128)(2,1)}, bf16[2,192,2304]{2,1,0:T(8,128)(2,1)}, u32[]{:S(2)}, u32[]{:S(2)}) collective-permute-start(bf16[2,192,2304]{2,1,0:T(8,128)(2,1)} %get-tuple-element.268), channel_id=1, source_target_pairs={{0,2},{1,3},{2,0},{3,1},{4,6},{5,7},{6,4},{7,5},{8,10},{9,11},{10,... | collective-permute-start | bytes 5308424 | tf_op jit(solution)/shard_map/ppermute | solution.py:1168
  484.9 9.8 %copy-start.37 = (f32[1536]{0:T(1024)S(1)}, f32[1536]{0:T(1024)}, u32[]{:S(2)}) copy-start(f32[1536]{0:T(1024)} %param.20) | copy-start | bytes 18436
  484.9 9.8 %copy-start.43 = (f32[512]{0:T(512)S(1)}, f32[512]{0:T(512)}, u32[]{:S(2)}) copy-start(f32[512]{0:T(512)} %copy-done.42) | copy-start | bytes 6148
  516.8 100.6 %copy-start.47 = (s32[512]{0:T(512)S(1)}, s32[512]{0:T(512)}, u32[]{:S(2)}) copy-start(s32[512]{0:T(512)} %copy-done.46) | copy-start | bytes 6148
  621.0 9.8 %copy-start.1 = (bf16[512,1536]{1,0:T(8,128)(2,1)S(1)}, bf16[512,1536]{1,0:T(8,128)(2,1)}, u32[]{:S(2)}) copy-start(bf16[512,1536]{1,0:T(8,128)(2,1)} %param.19) | copy-start | bytes 4718596
  (41 other events, 146.6 us)
Sparse Core Ops, SparseCore 0:
  53.1 54.2 all-gather.5
  109.9 38.4 all-gather.7
  150.3 38.9 all-gather.9
  191.0 38.9 all-gather.11
  266.7 36.4 all-gather.13
